TPU v7x, 128 devices: a whole 4x4x4 slice. The times are simulated.
128 devices in a mesh: group: 2 (over x_lo), dp: 8 (over z, x_hi), mp: 8 (over y, core).
Axes of the slice: x: 4 (x_hi: 2, x_lo: 2; x = x_hi * 2 + x_lo), y: 4, z: 4, core: 2. Of those that a mesh axis runs over, the one named last changes fastest.
Arguments:
- latent_noise: bfloat16 [8, 768, 2432], P('dp', 'mp'), may hold values from -6 to 6
- timestep: int32 [8], P('dp'), may hold values from 0 to 49
- reward_slot: int32 [8], replicated, may hold values from 0 to 7, each once
- target: bfloat16 [8, 768, 1280], P('dp', 'mp'), may hold values from -6 to 6
- modulation: float32 [50, 3, 2432], replicated, may hold values from -3 to 3
- w_in: bfloat16 [2432, 9728], P(('group', 'dp'), 'mp'), may hold values from -0.125 to 0.125
- w_out_t: bfloat16 [2432, 9728], P(('group', 'dp'), 'mp'), may hold values from -0.0625 to 0.0625
- w_final: bfloat16 [2432, 64], replicated, may hold values from -0.125 to 0.125
- w_dec1: bfloat16 [64, 2048], replicated, may hold values from -0.75 to 0.75
- w_dec2: bfloat16 [2048, 768], replicated, may hold values from -0.125 to 0.125
- w_patch: bfloat16 [768, 1280], replicated, may hold values from -0.21875 to 0.21875
- w_v1: bfloat16 [1280, 5120], P(None, 'mp'), may hold values from -0.15625 to 0.15625
- w_v2: bfloat16 [5120, 1280], P('mp'), may hold values from -0.078125 to 0.078125
Outputs:
- grad_in: float32 [2432, 9728], P(('group', 'dp'), 'mp')
- grad_out_t: float32 [2432, 9728], P(('group', 'dp'), 'mp')
Inputs may be any that keep to these rules, and one draw needn't show every extreme that they name: `reward_slot`: each reward slot scores exactly one image.
All inputs are finite; a program needn't handle non-finite values.
Results may differ from a plain program's by a relative error of at most 0.025.
Values may be sent and summed in bfloat16 or wider, within the bound.
No kernel may reach another device: no remote copies, remote signals or barrier semaphores. Data moves between devices by JAX's collectives and lax.ppermute only.
A program may use at most 128 MiB of HBM per device.

v0:
```python
import math

import jax
import jax.numpy as jnp
from jax import lax
from jax.sharding import PartitionSpec as P


def passed_along(value, axis, steps):
    count = lax.axis_size(axis)
    leading, last = (max(0, -steps), min(count, count - steps))
    return lax.ppermute(value, axis, [(source, source + steps) for source in range(leading, last)])


def layer_norm(values):
    mean = jnp.mean(values, axis=-1, keepdims=True)
    centred = values - mean
    variance = jnp.mean(centred * centred, axis=-1, keepdims=True)
    return centred * lax.rsqrt(variance + 1e-06)


def gelu_tanh(values):
    return jax.nn.gelu(values, approximate=True)


def gelu_back(values, cotangent):
    _, pullback = jax.vjp(gelu_tanh, values)
    return pullback(cotangent)[0]


def silu_back(values, cotangent):
    _, pullback = jax.vjp(jax.nn.silu, values)
    return pullback(cotangent)[0]


def norm_back(values, cotangent):
    _, pullback = jax.vjp(layer_norm, values)
    return pullback(cotangent)[0]


def matmul(left, right):
    return jnp.dot(left, right, preferred_element_type=jnp.float32)


def matmul_nt(left, right):
    return lax.dot_general(
        left, right, (((1,), (1,)), ((), ())), preferred_element_type=jnp.float32
    )


def matmul_tn(left, right):
    return lax.dot_general(
        left, right, (((0,), (0,)), ((), ())), preferred_element_type=jnp.float32
    )


def on_device(
    latent_noise,
    timestep,
    reward_slot,
    target,
    modulation,
    w_in,
    w_out_t,
    w_final,
    w_dec1,
    w_dec2,
    w_patch,
    w_v1,
    w_v2,
):
    tok_dev = latent_noise.shape[1]
    mp_size = lax.axis_size("mp")
    dp_size = lax.axis_size("dp")
    rows = tok_dev * mp_size
    scale = 1.0 / math.sqrt(dp_size * rows)
    is_gen = lax.axis_index("group") == 0
    is_reward = jnp.logical_not(is_gen)
    my_image = lax.axis_index("dp")
    image_ids = lax.iota(jnp.int32, dp_size)
    my_slot = jnp.sum(jnp.where(image_ids == my_image, reward_slot, 0))
    full_in, full_out = (
        lax.all_gather(w_in, ("group", "dp"), axis=0, tiled=True),
        lax.all_gather(w_out_t, ("group", "dp"), axis=0, tiled=True),
    )
    pick_step = (lax.iota(jnp.int32, modulation.shape[0]) == timestep[0]).astype(jnp.float32)
    modulate = jnp.tensordot(pick_step, modulation, axes=1, precision=lax.Precision.HIGHEST)
    noise_rows = latent_noise[0]
    modulated = (
        layer_norm(noise_rows.astype(jnp.float32)) * (1.0 + modulate[1]) + modulate[0]
    ).astype(jnp.bfloat16)
    token_rows = lax.all_gather(modulated, "mp", axis=0, tiled=True)
    width_ff = full_in.shape[1]
    width_d = full_in.shape[0]

    def generator_forward():
        pre_act = matmul(token_rows, full_in)
        hidden = gelu_tanh(pre_act).astype(jnp.bfloat16)
        return (pre_act, hidden, matmul_nt(hidden, full_out))

    def quiet_forward():
        return (
            jnp.zeros((rows, width_ff), jnp.float32),
            jnp.zeros((rows, width_ff), jnp.bfloat16),
            jnp.zeros((rows, width_d), jnp.float32),
        )

    pre_act, hidden, block_part = lax.cond(is_gen, generator_forward, quiet_forward)
    block_out = lax.psum_scatter(
        block_part.astype(jnp.bfloat16), "mp", scatter_dimension=0, tiled=True
    ).astype(jnp.float32)
    state = (noise_rows.astype(jnp.float32) + modulate[2] * block_out).astype(jnp.bfloat16)
    latent = matmul(state, w_final).astype(jnp.bfloat16)
    dec_pre = matmul(latent, w_dec1)
    dec_act = jax.nn.silu(dec_pre).astype(jnp.bfloat16)
    pixels = matmul(dec_act, w_dec2).astype(jnp.bfloat16)
    arrived = passed_along(pixels[None], "group", 1)
    every = lax.all_gather(arrived, "dp", axis=0, tiled=True)
    pick_image = (reward_slot == my_image).astype(jnp.bfloat16)
    patches = jnp.einsum("i,itp->tp", pick_image, every, preferred_element_type=jnp.float32).astype(
        jnp.bfloat16
    )
    embedded = matmul(patches, w_patch)
    normed_patch = layer_norm(embedded).astype(jnp.bfloat16)
    patch_rows = lax.all_gather(normed_patch, "mp", axis=0, tiled=True)
    width_ef = w_v1.shape[1]
    width_e = w_v1.shape[0]

    def reward_forward():
        vit_pre = matmul(patch_rows, w_v1)
        vit_hidden = gelu_tanh(vit_pre).astype(jnp.bfloat16)
        return (vit_pre, matmul(vit_hidden, w_v2))

    def quiet_reward():
        return (jnp.zeros((rows, width_ef), jnp.float32), jnp.zeros((rows, width_e), jnp.float32))

    vit_pre, vit_part = lax.cond(is_reward, reward_forward, quiet_reward)
    vit_out = lax.psum_scatter(
        vit_part.astype(jnp.bfloat16), "mp", scatter_dimension=0, tiled=True
    ).astype(jnp.float32)
    features = embedded + vit_out
    feature_grad = ((features - target[0].astype(jnp.float32)) * scale).astype(jnp.bfloat16)
    grad_rows = lax.all_gather(feature_grad, "mp", axis=0, tiled=True)

    def reward_backward():
        vit_hidden_grad = matmul_nt(grad_rows, w_v2)
        vit_pre_grad = gelu_back(vit_pre, vit_hidden_grad).astype(jnp.bfloat16)
        return matmul_nt(vit_pre_grad, w_v1)

    def quiet_back():
        return jnp.zeros((rows, width_e), jnp.float32)

    norm_part = lax.cond(is_reward, reward_backward, quiet_back)
    norm_grad = lax.psum_scatter(
        norm_part.astype(jnp.bfloat16), "mp", scatter_dimension=0, tiled=True
    ).astype(jnp.float32)
    embed_grad = (feature_grad.astype(jnp.float32) + norm_back(embedded, norm_grad)).astype(
        jnp.bfloat16
    )
    pixel_grad = matmul_nt(embed_grad, w_patch).astype(jnp.bfloat16)
    returned = passed_along(pixel_grad[None], "group", -1)
    every_grad = lax.all_gather(returned, "dp", axis=0, tiled=True)
    pick_slot = (image_ids == my_slot).astype(jnp.bfloat16)
    pixel_back = jnp.einsum(
        "i,itp->tp", pick_slot, every_grad, preferred_element_type=jnp.float32
    ).astype(jnp.bfloat16)
    decode_grad = matmul_nt(pixel_back, w_dec2)
    dec_pre_grad = silu_back(dec_pre, decode_grad).astype(jnp.bfloat16)
    latent_grad = matmul_nt(dec_pre_grad, w_dec1).astype(jnp.bfloat16)
    state_grad = matmul_nt(latent_grad, w_final)
    block_grad = (modulate[2] * state_grad).astype(jnp.bfloat16)
    block_rows = lax.all_gather(block_grad, "mp", axis=0, tiled=True)

    def generator_backward():
        hidden_grad = matmul(block_rows, full_out)
        pre_grad = gelu_back(pre_act, hidden_grad).astype(jnp.bfloat16)
        return (matmul_tn(token_rows, pre_grad), matmul_tn(block_rows, hidden))

    def quiet_terms():
        return (
            jnp.zeros((width_d, width_ff), jnp.float32),
            jnp.zeros((width_d, width_ff), jnp.float32),
        )

    term_in, term_out = lax.cond(is_gen, generator_backward, quiet_terms)
    grad_in, grad_out_t = (
        lax.psum_scatter(
            term_in.astype(jnp.bfloat16), ("group", "dp"), scatter_dimension=0, tiled=True
        ).astype(jnp.float32),
        lax.psum_scatter(
            term_out.astype(jnp.bfloat16), ("group", "dp"), scatter_dimension=0, tiled=True
        ).astype(jnp.float32),
    )
    return (grad_in, grad_out_t)


def solution(mesh):
    placed = (
        P("dp", "mp", None),
        P("dp"),
        P(),
        P("dp", "mp", None),
        P(),
        P(("group", "dp"), "mp"),
        P(("group", "dp"), "mp"),
        P(),
        P(),
        P(),
        P(),
        P(None, "mp"),
        P("mp", None),
    )
    return jax.shard_map(
        on_device,
        mesh=mesh,
        in_specs=placed,
        out_specs=(P(("group", "dp"), "mp"), P(("group", "dp"), "mp")),
        check_vma=False,
    )
```

profile of v0, /device:TPU:8, one launch (start us, length us, event | category | flops | bytes accessed | tf_op | source)
XLA Modules:
  0.0 1064.1 jit_solution(7455250480961245618)
XLA Ops:
  15.6 30.0 %all-gather.9.cloned.1.call-done = bf16[768,2432]{1,0:T(8,128)(2,1)} async-done(((bf16[96,2432]{1,0:T(8,128)(2,1)}), bf16[768,2432]{1,0:T(8,128)(2,1)}) %all-gather.9.cloned.1.call-update) | async-done | bytes 3735568 | tf_op jit(solution)/shard_map/all_gather | solution.py:92
  45.7 162.2 %all-gather.11.cloned.1.call-done = bf16[2432,1216]{1,0:T(8,128)(2,1)} async-done(((bf16[152,1216]{1,0:T(8,128)(2,1)}), bf16[2432,1216]{1,0:T(8,128)(2,1)}) %all-gather.11.cloned.1.call-update) | async-done | bytes 5914640 | tf_op jit(solution)/shard_map/all_gather | solution.py:83
  207.8 159.4 %all-gather.13.cloned.1.call-done = bf16[2432,1216]{1,0:T(8,128)(2,1)} async-done(((bf16[152,1216]{1,0:T(8,128)(2,1)}), bf16[2432,1216]{1,0:T(8,128)(2,1)}) %all-gather.13.cloned.1.call-update) | async-done | bytes 5914640 | tf_op jit(solution)/shard_map/all_gather | solution.py:84
  367.2 20.7 %conditional.4 = (f32[768,1216]{0,1:T(8,128)}, bf16[768,1216]{0,1:T(8,128)(2,1)}, bf16[768,2432]{1,0:T(8,128)(2,1)}) conditional(s32[]{:T(128)} %convert_element_type.111, () %tuple.41, (bf16[768,2432]{1,0:T(8,128)(2,1)}, bf16[2432,1216]{1,0:T(8,128)(2,1)}, bf16[2432,1216]{1,0:T(8,128)(2,1)}) %tuple.42), branch_computations={%region_3.4_spmd, %region_4.5_spmd} | conditional | flops 9093267456 | bytes 50430004 | solution.py:108
  367.2 12.2 %fusion.7 = (bf16[768,1216]{0,1:T(8,128)(2,1)}, f32[768,1216]{0,1:T(8,128)}) fusion(bf16[768,2432]{1,0:T(8,128)(2,1)} %get-tuple-element.24, bf16[2432,1216]{1,0:T(8,128)(2,1)} %get-tuple-element.34), kind=kOutput, calls=%fused_computation.8 | convolution fusion | flops 4550836224 | bytes 15253504 | tf_op jit(solution)/shard_map/cond/branch_1_fun/dot_general | solution.py:42
  379.5 8.5 fusion.118
  388.2 30.2 %reduce-scatter.10.cloned.1.call-done = bf16[96,2432]{1,0:T(8,128)(2,1)} async-done(((bf16[768,2432]{1,0:T(8,128)(2,1)}), bf16[96,2432]{1,0:T(8,128)(2,1)}) %reduce-scatter.10.cloned.1.call-update) | async-done | bytes 466960 | tf_op jit(solution)/shard_map/reduce_scatter | solution.py:109
  418.4 2.9 fusion.72
  423.1 3.4 collective-permute-start
  426.4 3.3 collective-permute-done
  430.5 49.8 %all-gather.15.cloned.1.call-done = bf16[8,96,768]{2,1,0:T(8,128)(2,1)} async-done(((bf16[1,96,768]{2,1,0:T(8,128)(2,1)}), bf16[8,96,768]{2,1,0:T(8,128)(2,1)}) %all-gather.15.cloned.1.call-update) | async-done | bytes 1179664 | tf_op jit(solution)/shard_map/all_gather | solution.py:118
  486.1 22.5 %all-gather.17.cloned.1.call-done = bf16[768,1280]{1,0:T(8,128)(2,1)} async-done(((bf16[96,1280]{1,0:T(8,128)(2,1)}), bf16[768,1280]{1,0:T(8,128)(2,1)}) %all-gather.17.cloned.1.call-update) | async-done | bytes 1966096 | tf_op jit(solution)/shard_map/all_gather | solution.py:125
  508.6 2.8 conditional.5
  511.5 38.7 %reduce-scatter.12.cloned.1.call-done = bf16[96,1280]{1,0:T(8,128)(2,1)} async-done(((bf16[768,1280]{1,0:T(8,128)(2,1)}), bf16[96,1280]{1,0:T(8,128)(2,1)}) %reduce-scatter.12.cloned.1.call-update) | async-done | bytes 245776 | tf_op jit(solution)/shard_map/reduce_scatter | solution.py:138
  552.1 26.1 %all-gather.19.cloned.1.call-done = bf16[768,1280]{1,0:T(8,128)(2,1)} async-done(((bf16[96,1280]{1,0:T(8,128)(2,1)}), bf16[768,1280]{1,0:T(8,128)(2,1)}) %all-gather.19.cloned.1.call-update) | async-done | bytes 1966096 | tf_op jit(solution)/shard_map/all_gather | solution.py:143
  579.8 38.2 %reduce-scatter.14.cloned.1.call-done = bf16[96,1280]{1,0:T(8,128)(2,1)} async-done(((bf16[768,1280]{1,0:T(8,128)(2,1)}), bf16[96,1280]{1,0:T(8,128)(2,1)}) %reduce-scatter.14.cloned.1.call-update) | async-done | bytes 245776 | tf_op jit(solution)/shard_map/reduce_scatter | solution.py:154
  620.8 2.6 fusion.68
  624.7 5.7 collective-permute-done.1
  632.1 48.7 %all-gather.21.cloned.1.call-done = bf16[8,96,768]{2,1,0:T(8,128)(2,1)} async-done(((bf16[1,96,768]{2,1,0:T(8,128)(2,1)}), bf16[8,96,768]{2,1,0:T(8,128)(2,1)}) %all-gather.21.cloned.1.call-update) | async-done | bytes 1179664 | tf_op jit(solution)/shard_map/all_gather | solution.py:162
  680.7 2.7 fusion.62
  685.4 3.0 fusion.61
  688.5 28.0 %all-gather.23.cloned.1.call-done = bf16[768,2432]{1,0:T(8,128)(2,1)} async-done(((bf16[96,2432]{1,0:T(8,128)(2,1)}), bf16[768,2432]{1,0:T(8,128)(2,1)}) %all-gather.23.cloned.1.call-update) | async-done | bytes 3735568 | tf_op jit(solution)/shard_map/all_gather | solution.py:172
  716.6 30.8 %conditional.7 = (bf16[2432,1216]{0,1:T(8,128)(2,1)}, bf16[2432,1216]{0,1:T(8,128)(2,1)}) conditional(s32[]{:T(128)} %convert_element_type.111, () %tuple.40, (bf16[768,2432]{1,0:T(8,128)(2,1)}, bf16[2432,1216]{1,0:T(8,128)(2,1)}, f32[768,1216]{0,1:T(8,128)}, bf16[768,2432]{1,0:T(8,128)(2,1)}, bf16[768,1216]{0,1:T(8,128)(2,1)}) %tuple.47), branch_computations={%region_16.17_spmd, %region_17.18_spmd} | conditional | flops 13645971456 | bytes 34553872 | solution.py:185
  716.6 9.1 fusion.120
  725.7 21.7 %convolution_bitcast_fusion = bf16[2432,1216]{0,1:T(8,128)(2,1)} fusion(bf16[768,2432]{1,0:T(8,128)(2,1)} %get-tuple-element.46, f32[768,1216]{0,1:T(8,128)} %get-tuple-element.45, bf16[768,2432]{1,0:T(8,128)(2,1)} %get-tuple-element.43, bf16[2432,1216]{1,0:T(8,128)(2,1)} %get-tuple-element.44), kind=kOutput, calls=%fused_computation.43 | convolution fusion | flops 9103540224 | bytes 23035904 | tf_op jit(solution)/shard_map/cond/branch_1_fun/dot_general | solution.py:52
  747.4 9.4 copy.33
  756.9 9.4 copy.35
  766.3 138.0 %reduce-scatter.16.cloned.1.call-done = bf16[152,1216]{1,0:T(8,128)(2,1)} async-done(((bf16[2432,1216]{1,0:T(8,128)(2,1)}), bf16[152,1216]{1,0:T(8,128)(2,1)}) %reduce-scatter.16.cloned.1.call-update) | async-done | bytes 369680
  904.3 2.2 copy.34
  906.5 2.2 copy.25
  908.7 144.7 %reduce-scatter.18.cloned.1.call-done = bf16[152,1216]{1,0:T(8,128)(2,1)} async-done(((bf16[2432,1216]{1,0:T(8,128)(2,1)}), bf16[152,1216]{1,0:T(8,128)(2,1)}) %reduce-scatter.18.cloned.1.call-update) | async-done | bytes 369680
  1055.4 2.2 copy.26
  (78 shorter events, 33.7 us)
Async XLA Ops:
  7.2 414.1 %copy-start = (bf16[2048,768]{1,0:T(8,128)(2,1)S(1)}, bf16[2048,768]{1,0:T(8,128)(2,1)}, u32[]{:S(2)}) copy-start(bf16[2048,768]{1,0:T(8,128)(2,1)} %param.30) | copy-start | bytes 9437188
  7.2 38.5 %all-gather.9.cloned.1.call-start = ((), (), s32[]{:S(2)}) async-start(), calls=%async_computation.5 | async-start | bytes 4202496 | tf_op jit(solution)/shard_map/all_gather | solution.py:92
  7.2 5.7 copy-start.3
  14.1 193.8 %all-gather.11.cloned.1.call-start = ((), (), s32[]{:S(2)}) async-start(), calls=%async_computation.6 | async-start | bytes 6615040 | tf_op jit(solution)/shard_map/all_gather | solution.py:83
  14.8 352.4 %all-gather.13.cloned.1.call-start = ((), (), s32[]{:S(2)}) async-start(), calls=%async_computation.7 | async-start | bytes 6615040 | tf_op jit(solution)/shard_map/all_gather | solution.py:84
  15.5 402.8 %reduce-scatter.10.cloned.1.call-start = ((), (), s32[]{:S(2)}) async-start(), calls=%async_computation.8 | async-start | bytes 4202496 | tf_op jit(solution)/shard_map/reduce_scatter | solution.py:109
  367.2 12.2 %copy-start.11 = (bf16[2432,1216]{1,0:T(8,128)(2,1)S(1)}, bf16[2432,1216]{1,0:T(8,128)(2,1)}, u32[]{:S(2)}) copy-start(bf16[2432,1216]{1,0:T(8,128)(2,1)} %get-tuple-element.35) | copy-start | bytes 17743876 | tf_op jit(solution)/shard_map/cond
  387.9 30.5 %copy-start.5 = (bf16[2432,64]{0,1:T(8,128)(2,1)S(1)}, bf16[2432,64]{0,1:T(8,128)(2,1)}, u32[]{:S(2)}) copy-start(bf16[2432,64]{0,1:T(8,128)(2,1)} %param.28) | copy-start | bytes 933892
  387.9 92.3 %all-gather.15.cloned.1.call-start = ((), (), s32[]{:S(2)}) async-start(), calls=%async_computation.9 | async-start | bytes 1327104 | tf_op jit(solution)/shard_map/all_gather | solution.py:118
  421.3 59.0 %copy-start.10 = (s32[8]{0:T(128)S(1)}, s32[8]{0:T(128)}, u32[]{:S(2)}) copy-start(s32[8]{0:T(128)} %param.23) | copy-start | bytes 100
  423.1 6.7 collective-permute-start
  429.7 0.7 copy-start.8
  430.4 78.2 %all-gather.17.cloned.1.call-start = ((), (), s32[]{:S(2)}) async-start(), calls=%async_computation.10 | async-start | bytes 2211840 | tf_op jit(solution)/shard_map/all_gather | solution.py:125
  484.5 0.8 copy-start.2
  486.1 64.1 %reduce-scatter.12.cloned.1.call-start = ((), (), s32[]{:S(2)}) async-start(), calls=%async_computation.11 | async-start | bytes 2211840 | tf_op jit(solution)/shard_map/reduce_scatter | solution.py:138
  511.4 38.8 %copy-start.7 = (bf16[1,96,1280]{2,1,0:T(8,128)(2,1)S(1)}, bf16[1,96,1280]{2,1,0:T(8,128)(2,1)}, u32[]{:S(2)}) copy-start(bf16[1,96,1280]{2,1,0:T(8,128)(2,1)} %param.24) | copy-start | bytes 737284
  511.5 66.8 %all-gather.19.cloned.1.call-start = ((), (), s32[]{:S(2)}) async-start(), calls=%async_computation.12 | async-start | bytes 2211840 | tf_op jit(solution)/shard_map/all_gather | solution.py:143
  552.1 65.9 %reduce-scatter.14.cloned.1.call-start = ((), (), s32[]{:S(2)}) async-start(), calls=%async_computation.13 | async-start | bytes 2211840 | tf_op jit(solution)/shard_map/reduce_scatter | solution.py:154
  579.7 41.1 %copy-start.4 = (bf16[96,1280]{1,0:T(8,128)(2,1)S(1)}, bf16[96,1280]{1,0:T(8,128)(2,1)}, u32[]{:S(2)}) copy-start(bf16[96,1280]{1,0:T(8,128)(2,1)} %fusion.83) | copy-start | bytes 737284
  579.7 101.0 %all-gather.21.cloned.1.call-start = ((), (), s32[]{:S(2)}) async-start(), calls=%async_computation.14 | async-start | bytes 1327104 | tf_op jit(solution)/shard_map/all_gather | solution.py:162
  623.4 7.0 collective-permute-start.1
  630.5 0.7 copy-start.9
  631.1 85.4 %all-gather.23.cloned.1.call-start = ((), (), s32[]{:S(2)}) async-start(), calls=%async_computation.15 | async-start | bytes 4202496 | tf_op jit(solution)/shard_map/all_gather | solution.py:172
  683.5 2.0 copy-start.6
  688.5 215.8 %reduce-scatter.16.cloned.1.call-start = ((), (), s32[]{:S(2)}) async-start(), calls=%async_computation.16 | async-start | bytes 6615040
  756.8 296.5 %reduce-scatter.18.cloned.1.call-start = ((), (), s32[]{:S(2)}) async-start(), calls=%async_computation.17 | async-start | bytes 6615040
  904.3 153.3 %copy-start.1 = (bf16[2048,768]{1,0:T(8,128)(2,1)S(1)}, bf16[2048,768]{1,0:T(8,128)(2,1)}, u32[]{:S(2)}) copy-start(bf16[2048,768]{1,0:T(8,128)(2,1)} %param.30) | copy-start | bytes 9437188
Sparse Core Ops, SparseCore 0:
  14.2 31.4 all-gather.8
  47.3 160.4 all-gather.10
  209.5 157.7 all-gather.12
  388.1 30.2 reduce-scatter.9
  430.5 49.6 all-gather.14
  486.2 22.3 all-gather.16
  511.6 38.5 reduce-scatter.11
  552.6 25.6 all-gather.18
  580.8 37.1 reduce-scatter.13
  631.3 49.3 all-gather.20
  688.6 27.9 all-gather.22
  756.9 147.3 reduce-scatter.15
  906.7 146.6 reduce-scatter.17
where the time goes:
time: 1070 us; the launch traced here: 1060 us
  waiting for transfers between devices  927 us (87%)
  matrix products  72.8 us (7%)
  local copies, waits for them, and re-layouts  33.5 us (3%)
  between operations  14.9 us (1%)
    unnamed x15, waiting for transfers between devices  284 us
    all_gather x1, waiting for transfers between devices, on_device(): lax.all_gather(w_in, ('group', 'dp'), axis=0, tiled=True)  162 us
    all_gather x1, waiting for transfers between devices, on_device(): lax.all_gather(w_out_t, ('group', 'dp'), axis=0, tiled=True)  159 us
    all_gather x1, waiting for transfers between devices, on_device(): every = lax.all_gather(arrived, 'dp', axis=0, tiled=True)  49.8 us
    all_gather x1, waiting for transfers between devices, on_device(): every_grad = lax.all_gather(returned, 'dp', axis=0, tiled=True)  48.7 us
    reduce_scatter x1, waiting for transfers between devices, on_device(): lax.psum_scatter(vit_part.astype(jnp.bfloat16), 'mp', scatter_dimension=0...  38.7 us
    reduce_scatter x1, waiting for transfers between devices, on_device(): lax.psum_scatter(norm_part.astype(jnp.bfloat16), 'mp', scatter_dimension=...  38.2 us
    dot_general x2, matrix products, matmul_tn(): lax.dot_general(left, right, (((0,), (0,)), ((), ())), preferred_element_...  30.8 us
  transfers between devices with their start and end apart: 15, of which 15 were waited for; matrix products, arithmetic and copies ran while one was open for 1% of the time, Pallas kernels for 0%

commit v1 on v0

v1 whole, which is shorter than its diff:
```python
import math

import jax
import jax.numpy as jnp
from jax import lax
from jax.sharding import Mesh
from jax.sharding import PartitionSpec as P

BF16 = jnp.bfloat16
F32 = jnp.float32
AXES = ("near", "z", "far", "y", "core")
IMAGE = ("z", "far")
ROWS_AT = ("near", "z", "far")
TOKENS_AT = ("near", "y", "core")


def layer_norm(values):
    mean = jnp.mean(values, axis=-1, keepdims=True)
    centred = values - mean
    variance = jnp.mean(centred * centred, axis=-1, keepdims=True)
    return centred * lax.rsqrt(variance + 1e-06)


def gelu_tanh(values):
    return jax.nn.gelu(values, approximate=True)


def with_slope(function, values):
    result, pullback = jax.vjp(function, values)
    return result, pullback(jnp.ones_like(values))[0]


def norm_back(values, cotangent):
    _, pullback = jax.vjp(layer_norm, values)
    return pullback(cotangent)[0]


def matmul(left, right):
    return jnp.dot(left, right, preferred_element_type=F32)


def matmul_nt(left, right):
    return lax.dot_general(left, right, (((1,), (1,)), ((), ())), preferred_element_type=F32)


def matmul_tn(left, right):
    return lax.dot_general(left, right, (((0,), (0,)), ((), ())), preferred_element_type=F32)


def turned(value, axis, steps):
    count = lax.axis_size(axis)
    return lax.ppermute(value, axis, [(at, (at + steps) % count) for at in range(count)])


def from_all(value, axis):
    count = lax.axis_size(axis)
    return [value] + [turned(value, axis, step) for step in range(1, count)]


def summed_back(blocks, axis):
    total = blocks[0]
    for step in range(1, len(blocks)):
        total = total + turned(blocks[step].astype(BF16), axis, -step).astype(F32)
    return total


def exchanged(blocks, axis):
    return lax.all_to_all(blocks, axis, 0, 0, tiled=True)


def on_device(
    latent_noise,
    timestep,
    reward_slot,
    target,
    modulation,
    w_in,
    w_out_t,
    w_final,
    w_dec1,
    w_dec2,
    w_patch,
    w_v1,
    w_v2,
):
    tok_dev = latent_noise.shape[1]
    n_near, n_y, n_core = (lax.axis_size(axis) for axis in TOKENS_AT)
    n_images = lax.axis_size("z") * lax.axis_size("far")
    n_rows = n_near * n_images
    n_tokens = n_near * n_y * n_core
    mine = tok_dev // n_near
    rows = tok_dev * n_y * n_core
    d_dev, ff_mp = w_in.shape
    width_d = d_dev * n_rows
    half = ff_mp // n_near
    strip = ff_mp // n_rows
    lat = w_final.shape[1]
    scale = 1.0 / math.sqrt(n_images * rows)
    near = lax.axis_index("near")
    my_image = lax.axis_index(IMAGE)
    my_slot = reward_slot[my_image]

    split_in = jnp.moveaxis(w_in.reshape(d_dev, n_near, half), 1, 0)
    keep = lax.dynamic_index_in_dim(split_in, near, 0, keepdims=False)
    give = lax.dynamic_index_in_dim(split_in, 1 - near, 0, keepdims=False)
    got = turned(give, "near", 1)
    pair = jnp.stack([jnp.where(near == 0, keep, got), jnp.where(near == 0, got, keep)])
    full_in = jnp.zeros((n_near, n_images, d_dev, half), BF16)
    for step, block in enumerate(from_all(pair, IMAGE)):
        owner = (my_image - step) % n_images
        full_in = lax.dynamic_update_slice_in_dim(full_in, block[:, None], owner, 1)
    full_in = full_in.reshape(width_d, half)

    modulate = modulation[timestep[0]]
    noise_rows = latent_noise[0]
    modulated = (
        layer_norm(noise_rows.astype(F32)) * (1.0 + modulate[1]) + modulate[0]
    ).astype(BF16)
    token_rows = lax.all_gather(modulated, ("y", "core"), axis=0, tiled=True)

    strips = jnp.moveaxis(w_out_t.reshape(d_dev, n_rows, strip), 1, 0)
    steps_row = jnp.broadcast_to(timestep[0].astype(BF16), (n_rows, 8, strip))
    arrived = exchanged(jnp.concatenate([strips, steps_row], axis=1), ROWS_AT)
    strip_rows = arrived[:, :d_dev].reshape(width_d, strip)
    all_steps = arrived[:n_images, d_dev, 0].astype(jnp.int32)
    gates = modulation[all_steps, 2]
    gated_final = (gates.T[:, :, None] * w_final.astype(F32)[:, None, :]).astype(BF16)
    gated_final = gated_final.reshape(width_d, n_images * lat)
    through = matmul_tn(strip_rows, gated_final).astype(BF16)
    through = exchanged(jnp.moveaxis(through.reshape(strip, n_images, lat), 1, 0), IMAGE)
    through = through.reshape(half, lat)

    v1_both = (w_v1, turned(w_v1, "core", 1))
    v2_both = (w_v2, turned(w_v2, "core", 1))
    my_target = lax.dynamic_slice_in_dim(target[0], near * mine, mine, 0)
    goals = lax.all_gather(my_target, IMAGE, axis=0)
    goal = lax.dynamic_index_in_dim(goals, my_slot, 0, keepdims=False).astype(F32)

    pre_act = matmul(token_rows, full_in)
    hidden, hidden_slope = with_slope(gelu_tanh, pre_act)
    hidden = hidden.astype(BF16)
    latent_part = matmul(hidden, through)
    latent_part = jnp.moveaxis(latent_part.reshape(n_y * n_core, n_near, mine, lat), 1, 0)
    latent_parts = exchanged(latent_part.reshape(n_tokens, mine, lat), TOKENS_AT)
    my_noise = lax.dynamic_slice_in_dim(noise_rows, near * mine, mine, 0)
    latent = (matmul(my_noise, w_final) + jnp.sum(latent_parts, axis=0)).astype(BF16)

    dec_pre = matmul(latent, w_dec1)
    dec_act, dec_slope = with_slope(jax.nn.silu, dec_pre)
    pixels = matmul(dec_act.astype(BF16), w_dec2).astype(BF16)
    embedded = matmul(pixels, w_patch)
    normed = layer_norm(embedded).astype(BF16)

    patch_rows = jnp.concatenate(from_all(normed, "y"))
    slopes = []
    vit_part = 0.0
    for v1, v2 in zip(v1_both, v2_both):
        act, slope = with_slope(gelu_tanh, matmul(patch_rows, v1))
        slopes.append(slope)
        vit_part = vit_part + matmul(act.astype(BF16), v2)
    vit_out = summed_back(jnp.split(vit_part, n_y), "y")
    feature_grad = ((embedded + vit_out - goal) * scale).astype(BF16)

    grad_rows = jnp.concatenate(from_all(feature_grad, "y"))
    norm_part = 0.0
    for v1, v2, slope in zip(v1_both, v2_both, slopes):
        vit_pre_grad = (slope * matmul_nt(grad_rows, v2)).astype(BF16)
        norm_part = norm_part + matmul_nt(vit_pre_grad, v1)
    norm_grad = summed_back(jnp.split(norm_part, n_y), "y")
    embed_grad = (feature_grad.astype(F32) + norm_back(embedded, norm_grad)).astype(BF16)
    pixel_grad = matmul_nt(embed_grad, w_patch).astype(BF16)
    dec_pre_grad = (dec_slope * matmul_nt(pixel_grad, w_dec2)).astype(BF16)
    latent_grad = matmul_nt(dec_pre_grad, w_dec1).astype(BF16)

    spread = jnp.broadcast_to(latent_grad, (n_tokens, mine, lat))
    latent_rows = exchanged(spread, TOKENS_AT).reshape(n_near, n_y * n_core, mine, lat)
    latent_rows = jnp.moveaxis(latent_rows, 0, 1).reshape(rows, lat)

    inner = matmul_tn(latent_rows, hidden).astype(BF16)
    inner = exchanged(jnp.moveaxis(inner.reshape(lat, n_images, strip), 1, 0), IMAGE)
    out_strip = matmul(gated_final, inner.reshape(n_images * lat, strip)).astype(BF16)
    out_strips = exchanged(out_strip.reshape(n_rows, d_dev, strip), ROWS_AT)
    grad_out_t = jnp.moveaxis(out_strips, 0, 1).reshape(d_dev, ff_mp).astype(F32)

    pre_grad = (hidden_slope * matmul_nt(latent_rows, through)).astype(BF16)
    term_in = matmul_tn(token_rows, pre_grad).astype(BF16)
    terms = exchanged(term_in.reshape(n_rows, d_dev, half), ROWS_AT)
    grad_in = jnp.sum(terms.reshape(n_near, n_images, d_dev, half).astype(F32), axis=1)
    grad_in = jnp.moveaxis(grad_in, 0, 1).reshape(d_dev, ff_mp)
    return (grad_in, grad_out_t)


def solution(mesh):
    n_group, n_dp, n_mp = (mesh.shape[axis] for axis in ("group", "dp", "mp"))
    fine = Mesh(mesh.devices.reshape(n_group, n_dp // 2, 2, n_mp // 2, 2), AXES)
    tokens = ("y", "core")
    weights = P(ROWS_AT, tokens)
    placed = (
        P(IMAGE, tokens, None),
        P(IMAGE),
        P(),
        P(IMAGE, tokens, None),
        P(),
        weights,
        weights,
        P(),
        P(),
        P(),
        P(),
        P(None, tokens),
        P(tokens, None),
    )
    return jax.shard_map(
        on_device, mesh=fine, in_specs=placed, out_specs=(weights, weights), check_vma=False
    )
```

time: 1070 us -> 353 us (0.33)
  waiting for transfers between devices: 927 us -> 67.4 us
  starting transfers between devices: 5.58 us -> 85.6 us
  blocking collectives: 0 us -> 51.1 us
  local copies, waits for them, and re-layouts: 33.5 us -> 58.1 us
  matrix products: 72.8 us -> 48.5 us
  other arithmetic: 10.2 us -> 21.7 us
    all_gather x8 -> x1, waiting for transfers between devices: 527 us -> 0.01 us  [on_device(): token_rows = lax.all_gather(modulated, ('y', 'core'), axis=0, tiled=True)]
    unnamed x15 -> x1, waiting for transfers between devices: 284 us -> 0.02 us
    reduce_scatter x3 -> x0, waiting for transfers between devices: 107 us -> none  [the longest x1 38.7 us: on_device(): lax.psum_scatter(vit_part.astype(jnp.bfloat16), 'mp', scatter_dimension=0...]
    all_to_all x0 -> x6, waiting for transfers between devices: none -> 56.4 us  [exchanged(): return lax.all_to_all(blocks, axis, 0, 0, tiled=True)]
    all_to_all x0 -> x6, starting transfers between devices: none -> 48.1 us  [exchanged(): return lax.all_to_all(blocks, axis, 0, 0, tiled=True)]
    all_gather x0 -> x1, blocking collectives: none -> 39.8 us  [on_device(): goals = lax.all_gather(my_target, IMAGE, axis=0)]
    ppermute x2 -> x22, starting transfers between devices: 4.65 us -> 37.4 us  [turned(): lax.ppermute(value, axis, [(at, (at + steps) % count) for at in range(cou...]
    unnamed x28 -> x30, local copies, waits for them, and re-layouts: 29.3 us -> 6.32 us
  transfers between devices with their start and end apart: 15 -> 29, of which waited for: 15 -> 11; matrix products, arithmetic and copies ran while one was open for 1% -> 20% of each run, Pallas kernels for 0% -> 0%
where the time goes in v1:
time: 353 us; the launch traced here: 350 us
  starting transfers between devices  85.6 us (24%)
  waiting for transfers between devices  67.4 us (19%)
  local copies, waits for them, and re-layouts  58.1 us (16%)
  blocking collectives  51.1 us (14%)
  matrix products  48.5 us (14%)
  other arithmetic  21.7 us (6%)
  between operations  17.3 us (5%)
    all_to_all x6, waiting for transfers between devices, exchanged(): return lax.all_to_all(blocks, axis, 0, 0, tiled=True)  56.4 us
    all_to_all x6, starting transfers between devices, exchanged(): return lax.all_to_all(blocks, axis, 0, 0, tiled=True)  48.1 us
    all_gather x1, blocking collectives, on_device(): goals = lax.all_gather(my_target, IMAGE, axis=0)  39.8 us
    ppermute x22, starting transfers between devices, turned(): lax.ppermute(value, axis, [(at, (at + steps) % count) for at in range(cou...  37.4 us
    dot_general x9, matrix products, matmul(): return jnp.dot(left, right, preferred_element_type=F32)  24.6 us
    dot_general x4, matrix products, matmul_nt(): lax.dot_general(left, right, (((1,), (1,)), ((), ())), preferred_element_...  12.8 us
    all_to_all x1, blocking collectives, exchanged(): return lax.all_to_all(blocks, axis, 0, 0, tiled=True)  11.4 us
    dot_general x3, matrix products, matmul_tn(): lax.dot_general(left, right, (((0,), (0,)), ((), ())), preferred_element_...  11.1 us
  transfers between devices with their start and end apart: 29, of which 11 were waited for; matrix products, arithmetic and copies ran while one was open for 20% of the time, Pallas kernels for 0%

profile of v1, /device:TPU:8, one launch (start us, length us, event | category | flops | bytes accessed | tf_op | source)
XLA Modules:
  0.0 349.6 jit_solution(4912313151971310633)
XLA Ops:
  19.1 2.9 reshape.147
  24.3 7.6 %all-to-all-start = ((bf16[16,160,76]{2,1,0:T(8,128)(2,1)}), bf16[16,160,76]{2,1,0:T(8,128)(2,1)}, u32[]{:S(2)}, u32[]{:S(2)}) async-start(bf16[16,160,76]{2,1,0:T(8,128)(2,1)} %concatenate.12.clone), calls=%async_computation | async-start | bytes 1310720 | tf_op jit(solution)/shard_map/all_to_all | solution.py:68
  34.9 3.3 collective-permute-start.1
  43.7 4.4 %collective-permute-start.5 = (bf16[2,152,608]{2,1,0:T(8,128)(2,1)}, bf16[2,152,608]{2,1,0:T(8,128)(2,1)}, u32[]{:S(2)}, u32[]{:S(2)}) collective-permute-start(bf16[2,152,608]{2,1,0:T(8,128)(2,1)} %pad_maximum_fusion.2), channel_id=1, source_target_pairs={{0,40},{8,48},{16,56},{24,0},{32,8},{40,16},{48,24},{56,32},{1,41}... | collective-permute-start | bytes 1109000 | tf_op jit(solution)/shard_map/ppermute | solution.py:52
  58.7 20.3 %all-to-all-start.1 = ((bf16[8,76,64]{1,2,0:T(8,128)(2,1)}), bf16[8,76,64]{1,2,0:T(8,128)(2,1)}, u32[]{:S(2)}, u32[]{:S(2)}) async-start(bf16[8,76,64]{1,2,0:T(8,128)(2,1)} %copy.102), calls=%async_computation.1 | async-start | bytes 262144 | tf_op jit(solution)/shard_map/all_to_all | solution.py:68
  81.6 6.3 %all-to-all-done.1 = bf16[8,76,64]{1,2,0:T(8,128)(2,1)} async-done(((bf16[8,76,64]{1,2,0:T(8,128)(2,1)}), bf16[8,76,64]{1,2,0:T(8,128)(2,1)}, u32[]{:S(2)}, u32[]{:S(2)}) %all-to-all-start.1) | async-done | bytes 77856 | tf_op jit(solution)/shard_map/all_to_all | solution.py:68
  102.0 7.6 %multiply_convert_fusion.1 = (bf16[768,608]{0,1:T(8,128)(2,1)}, f32[768,608]{0,1:T(8,128)}) fusion(bf16[768,2432]{1,0:T(8,128)(2,1)} %all-gather.2.cloned.1.call-done, bf16[2432,608]{1,0:T(8,128)(2,1)} %bitcast.20), kind=kOutput, calls=%fused_computation.20 | convolution fusion | flops 2275418112 | bytes 9494528 | tf_op jit(solution)/shard_map/dot_general | solution.py:39
  114.5 4.9 %all-to-all-start.2 = ((f32[16,1,3072]{2,1,0:T(1,128)}), f32[16,1,3072]{2,1,0:T(1,128)S(1)}, u32[]{:S(2)}, u32[]{:S(2)}) async-start(f32[16,1,3072]{2,1,0:T(1,128)} %reshape.174), calls=%async_computation.2 | async-start | bytes 393216 | tf_op jit(solution)/shard_map/all_to_all | solution.py:68
  119.9 4.5 %all-to-all-done.2 = f32[16,1,3072]{2,1,0:T(1,128)S(1)} async-done(((f32[16,1,3072]{2,1,0:T(1,128)}), f32[16,1,3072]{2,1,0:T(1,128)S(1)}, u32[]{:S(2)}, u32[]{:S(2)}) %all-to-all-start.2) | async-done | bytes 196640 | tf_op jit(solution)/shard_map/all_to_all | solution.py:68
  130.7 3.0 fusion.150
  134.0 2.5 collective-permute-start.10
  136.5 3.0 collective-permute-start.9
  147.9 3.0 fusion.151
  151.6 3.6 %collective-permute-start.13 = (bf16[48,1280]{1,0:T(8,128)(2,1)}, bf16[48,1280]{1,0:T(8,128)(2,1)}, u32[]{:S(2)}, u32[]{:S(2)}) collective-permute-start(bf16[48,1280]{1,0:T(8,128)(2,1)} %get-tuple-element.13), channel_id=1, source_target_pairs={{0,6},{2,0},{4,2},{6,4},{1,7},{3,1},{5,3},{7,5},{8,14},{10,8},{12,... | collective-permute-start | bytes 368648 | tf_op jit(solution)/shard_map/ppermute | solution.py:52
  157.3 39.8 %all_gather.8 = bf16[8,48,1280]{2,1,0:T(8,128)(2,1)} all-gather(bf16[1,48,1280]{2,1,0:T(8,128)(2,1)S(1)} %constant_dynamic-slice_fusion), channel_id=1, replica_groups=mesh['near'=2,'z'=4,'far'=2,'y'=4,'core'=2] {'z','far'}, dimensions={0}, use_global_device_ids=true | all-gather | bytes 1105920 | tf_op jit(solution)/shard_map/all_gather | solution.py:136
  205.8 3.6 %collective-permute-done.17 = bf16[48,1280]{1,0:T(8,128)(2,1)S(1)} collective-permute-done((bf16[48,1280]{1,0:T(8,128)(2,1)S(1)}, bf16[48,1280]{1,0:T(8,128)(2,1)S(1)}, u32[]{:S(2)}, u32[]{:S(2)}) %collective-permute-start.17) | collective-permute-done | bytes 122912 | tf_op jit(solution)/shard_map/ppermute | solution.py:52
  210.0 4.7 %fusion.12 = f32[192,1280]{1,0:T(8,128)} fusion(bf16[1280,640]{1,0:T(8,128)(2,1)} %param.24, bf16[640,1280]{1,0:T(8,128)(2,1)} %param.25, f32[192,640]{1,0:T(8,128)} %copy-done.7, bf16[48,1280]{1,0:T(8,128)(2,1)} %collective-permute-done.18, bf16[48,1280]{1,0:T(8,128)(2,1)} %copy-done.10, bf16[48,1280]{1,0:T(8,128)(2,1)} %copy-done.9, ...), kind=kOutput, calls=%fused_computation.27 | convolution fusion | flops 633446400 | bytes 5242880 | tf_op jit(solution)/shard_map/dot_general | solution.py:43
  214.7 5.1 %fusion.152 = (bf16[192,1280]{1,0:T(8,128)(2,1)}, f32[192,1280]{1,0:T(8,128)}) fusion(f32[192,1280]{1,0:T(8,128)} %fusion.12, bf16[1280,640]{1,0:T(8,128)(2,1)} %collective-permute-done.11, f32[192,640]{1,0:T(8,128)} %copy-done.6, bf16[640,1280]{1,0:T(8,128)(2,1)} %collective-permute-done.12, bf16[48,1280]{1,0:T(8,128)(2,1)} %collective-permute-done.18, ...), kind=kOutput, calls=%fused_computation.205 | convolution fusion | flops 633937920 | bytes 6717440 | tf_op jit(solution)/shard_map/dot_general | solution.py:43
  221.1 2.7 collective-permute-start.20
  223.8 2.5 collective-permute-start.21
  235.5 11.4 %all_to_all.35 = bf16[16,2,1536]{2,1,0:T(2,128)(2,1)S(1)} all-to-all(bf16[16,2,1536]{2,1,0:T(2,128)(2,1)} %reshape.176), channel_id=1, replica_groups=mesh['near'=2,'z'=4,'far'=2,'y'=4,'core'=2] {'near','y','core'}, dimensions={0} | all-to-all | bytes 196608 | tf_op jit(solution)/shard_map/all_to_all | solution.py:68
  252.3 3.9 %all-to-all-start.5 = ((bf16[8,64,76]{2,1,0:T(8,128)(2,1)}), bf16[8,64,76]{2,1,0:T(8,128)(2,1)S(1)}, u32[]{:S(2)}, u32[]{:S(2)}) async-start(bf16[8,64,76]{2,1,0:T(8,128)(2,1)} %bitcast.138), calls=%async_computation.5 | async-start | bytes 262144 | tf_op jit(solution)/shard_map/all_to_all | solution.py:68
  256.4 8.0 %all-to-all-done.5 = bf16[8,64,76]{2,1,0:T(8,128)(2,1)S(1)} async-done(((bf16[8,64,76]{2,1,0:T(8,128)(2,1)}), bf16[8,64,76]{2,1,0:T(8,128)(2,1)S(1)}, u32[]{:S(2)}, u32[]{:S(2)}) %all-to-all-start.5) | async-done | bytes 77856 | tf_op jit(solution)/shard_map/all_to_all | solution.py:68
  264.5 2.4 fusion
  268.9 4.3 %all-to-all-start.6 = ((bf16[16,152,76]{2,1,0:T(8,128)(2,1)}), bf16[16,152,76]{2,1,0:T(8,128)(2,1)}, u32[]{:S(2)}, u32[]{:S(2)}) async-start(bf16[16,152,76]{2,1,0:T(8,128)(2,1)} %bitcast.148), calls=%async_computation.6 | async-start | bytes 1245184 | tf_op jit(solution)/shard_map/all_to_all | solution.py:68
  273.2 8.0 %convolution_convert_fusion = bf16[2432,608]{0,1:T(8,128)(2,1)} fusion(bf16[768,2432]{1,0:T(8,128)(2,1)} %all-gather.2.cloned.1.call-done, f32[768,608]{0,1:T(8,128)} %get-tuple-element.19, bf16[768,64]{0,1:T(8,128)(2,1)S(1)} %copy-done.8, bf16[608,64]{0,1:T(8,128)(2,1)S(1)} %reshape.150), kind=kOutput, calls=%fused_computation.3 | convolution fusion | flops 2341335040 | bytes 8736768 | tf_op jit(solution)/shard_map/dot_general | solution.py:47
  281.2 5.5 %copy.106 = bf16[2432,608]{1,0:T(8,128)(2,1)} copy(bf16[2432,608]{0,1:T(8,128)(2,1)} %convolution_convert_fusion) | data formatting | bytes 5914624 | tf_op jit(solution)/shard_map/convert_element_type | solution.py:186
  286.7 7.1 %all-to-all-start.4 = ((bf16[16,152,608]{2,1,0:T(8,128)(2,1)}), bf16[16,152,608]{2,1,0:T(8,128)(2,1)}, u32[]{:S(2)}, u32[]{:S(2)}) async-start(bf16[16,152,608]{2,1,0:T(8,128)(2,1)} %bitcast.143), calls=%async_computation.4 | async-start | bytes 6225920 | tf_op jit(solution)/shard_map/all_to_all | solution.py:68
  296.2 2.7 reshape.161
  298.9 37.6 %all-to-all-done.4 = bf16[16,152,608]{2,1,0:T(8,128)(2,1)} async-done(((bf16[16,152,608]{2,1,0:T(8,128)(2,1)}), bf16[16,152,608]{2,1,0:T(8,128)(2,1)}, u32[]{:S(2)}, u32[]{:S(2)}) %all-to-all-start.4) | async-done | bytes 2957344 | tf_op jit(solution)/shard_map/all_to_all | solution.py:68
  336.5 2.4 convert_reduce_fusion
  340.3 2.5 reshape.155
  (138 shorter events, 101.3 us)
Async XLA Ops:
  7.2 123.6 %copy-start = (bf16[2048,768]{1,0:T(8,128)(2,1)S(1)}, bf16[2048,768]{1,0:T(8,128)(2,1)}, u32[]{:S(2)}) copy-start(bf16[2048,768]{1,0:T(8,128)(2,1)} %param.22) | copy-start | bytes 9437188
  7.2 94.9 %all-gather.2.cloned.1.call-start = ((), (), s32[]{:S(2)}) async-start(), calls=%async_computation.7 | async-start | bytes 4202496 | tf_op jit(solution)/shard_map/all_gather | solution.py:119
  17.6 15.4 %collective-permute-start = (bf16[152,608]{1,0:T(8,128)(2,1)}, bf16[152,608]{1,0:T(8,128)(2,1)}, u32[]{:S(2)}, u32[]{:S(2)}) collective-permute-start(bf16[152,608]{1,0:T(8,128)(2,1)} %bitcast.137), channel_id=1, source_target_pairs={{0,64},{64,0},{1,65},{65,1},{2,66},{66,2},{3,67},{67,3},{4,68},{68... | collective-permute-start | bytes 554504 | tf_op jit(solution)/shard_map/ppermute | solution.py:52
  24.3 23.9 %all-to-all-start = ((bf16[16,160,76]{2,1,0:T(8,128)(2,1)}), bf16[16,160,76]{2,1,0:T(8,128)(2,1)}, u32[]{:S(2)}, u32[]{:S(2)}) async-start(bf16[16,160,76]{2,1,0:T(8,128)(2,1)} %concatenate.12.clone), calls=%async_computation | async-start | bytes 1310720 | tf_op jit(solution)/shard_map/all_to_all | solution.py:68
  34.9 54.2 %collective-permute-start.1 = (bf16[2,152,608]{2,1,0:T(8,128)(2,1)}, bf16[2,152,608]{2,1,0:T(8,128)(2,1)}, u32[]{:S(2)}, u32[]{:S(2)}) collective-permute-start(bf16[2,152,608]{2,1,0:T(8,128)(2,1)} %pad_maximum_fusion.2), channel_id=1, source_target_pairs={{0,8},{8,16},{16,24},{24,32},{32,40},{40,48},{48,56},{56,0},{1,9},... | collective-permute-start | bytes 1109000 | tf_op jit(solution)/shard_map/ppermute | solution.py:52
  38.2 53.6 %collective-permute-start.2 = (bf16[2,152,608]{2,1,0:T(8,128)(2,1)}, bf16[2,152,608]{2,1,0:T(8,128)(2,1)}, u32[]{:S(2)}, u32[]{:S(2)}) collective-permute-start(bf16[2,152,608]{2,1,0:T(8,128)(2,1)} %pad_maximum_fusion.2), channel_id=1, source_target_pairs={{0,16},{8,24},{16,32},{24,40},{32,48},{40,56},{48,0},{56,8},{1,17}... | collective-permute-start | bytes 1109000 | tf_op jit(solution)/shard_map/ppermute | solution.py:52
  39.6 54.4 %collective-permute-start.3 = (bf16[2,152,608]{2,1,0:T(8,128)(2,1)}, bf16[2,152,608]{2,1,0:T(8,128)(2,1)}, u32[]{:S(2)}, u32[]{:S(2)}) collective-permute-start(bf16[2,152,608]{2,1,0:T(8,128)(2,1)} %pad_maximum_fusion.2), channel_id=1, source_target_pairs={{0,24},{8,32},{16,40},{24,48},{32,56},{40,0},{48,8},{56,16},{1,25}... | collective-permute-start | bytes 1109000 | tf_op jit(solution)/shard_map/ppermute | solution.py:52
  41.6 54.1 %collective-permute-start.4 = (bf16[2,152,608]{2,1,0:T(8,128)(2,1)}, bf16[2,152,608]{2,1,0:T(8,128)(2,1)}, u32[]{:S(2)}, u32[]{:S(2)}) collective-permute-start(bf16[2,152,608]{2,1,0:T(8,128)(2,1)} %pad_maximum_fusion.2), channel_id=1, source_target_pairs={{0,32},{8,40},{16,48},{24,56},{32,0},{40,8},{48,16},{56,24},{1,33}... | collective-permute-start | bytes 1109000 | tf_op jit(solution)/shard_map/ppermute | solution.py:52
  43.7 53.8 %collective-permute-start.5 = (bf16[2,152,608]{2,1,0:T(8,128)(2,1)}, bf16[2,152,608]{2,1,0:T(8,128)(2,1)}, u32[]{:S(2)}, u32[]{:S(2)}) collective-permute-start(bf16[2,152,608]{2,1,0:T(8,128)(2,1)} %pad_maximum_fusion.2), channel_id=1, source_target_pairs={{0,40},{8,48},{16,56},{24,0},{32,8},{40,16},{48,24},{56,32},{1,41}... | collective-permute-start | bytes 1109000 | tf_op jit(solution)/shard_map/ppermute | solution.py:52
  58.7 29.2 %all-to-all-start.1 = ((bf16[8,76,64]{1,2,0:T(8,128)(2,1)}), bf16[8,76,64]{1,2,0:T(8,128)(2,1)}, u32[]{:S(2)}, u32[]{:S(2)}) async-start(bf16[8,76,64]{1,2,0:T(8,128)(2,1)} %copy.102), calls=%async_computation.1 | async-start | bytes 262144 | tf_op jit(solution)/shard_map/all_to_all | solution.py:68
  89.1 10.3 %collective-permute-start.6 = (bf16[2,152,608]{2,1,0:T(8,128)(2,1)}, bf16[2,152,608]{2,1,0:T(8,128)(2,1)S(1)}, u32[]{:S(2)}, u32[]{:S(2)}) collective-permute-start(bf16[2,152,608]{2,1,0:T(8,128)(2,1)} %pad_maximum_fusion.2), channel_id=1, source_target_pairs={{0,48},{8,56},{16,0},{24,8},{32,16},{40,24},{48,32},{56,40},{1,49}... | collective-permute-start | bytes 1109000 | tf_op jit(solution)/shard_map/ppermute | solution.py:52
  91.8 9.4 %collective-permute-start.7 = (bf16[2,152,608]{2,1,0:T(8,128)(2,1)}, bf16[2,152,608]{2,1,0:T(8,128)(2,1)S(1)}, u32[]{:S(2)}, u32[]{:S(2)}) collective-permute-start(bf16[2,152,608]{2,1,0:T(8,128)(2,1)} %pad_maximum_fusion.2), channel_id=1, source_target_pairs={{0,56},{8,0},{16,8},{24,16},{32,24},{40,32},{48,40},{56,48},{1,57}... | collective-permute-start | bytes 1109000 | tf_op jit(solution)/shard_map/ppermute | solution.py:52
  114.5 10.0 %all-to-all-start.2 = ((f32[16,1,3072]{2,1,0:T(1,128)}), f32[16,1,3072]{2,1,0:T(1,128)S(1)}, u32[]{:S(2)}, u32[]{:S(2)}) async-start(f32[16,1,3072]{2,1,0:T(1,128)} %reshape.174), calls=%async_computation.2 | async-start | bytes 393216 | tf_op jit(solution)/shard_map/all_to_all | solution.py:68
  119.4 25.6 %collective-permute-start.11 = (bf16[1280,640]{1,0:T(8,128)(2,1)}, bf16[1280,640]{1,0:T(8,128)(2,1)}, u32[]{:S(2)}, u32[]{:S(2)}) collective-permute-start(bf16[1280,640]{1,0:T(8,128)(2,1)} %param.24), channel_id=1, source_target_pairs={{0,1},{1,0},{2,3},{3,2},{4,5},{5,4},{6,7},{7,6},{8,9},{9,8},{10,11... | collective-permute-start | bytes 4915208 | tf_op jit(solution)/shard_map/ppermute | solution.py:52
  119.5 28.3 %collective-permute-start.12 = (bf16[640,1280]{1,0:T(8,128)(2,1)}, bf16[640,1280]{1,0:T(8,128)(2,1)}, u32[]{:S(2)}, u32[]{:S(2)}) collective-permute-start(bf16[640,1280]{1,0:T(8,128)(2,1)} %param.25), channel_id=1, source_target_pairs={{0,1},{1,0},{2,3},{3,2},{4,5},{5,4},{6,7},{7,6},{8,9},{9,8},{10,11... | collective-permute-start | bytes 4915208 | tf_op jit(solution)/shard_map/ppermute | solution.py:52
  134.0 6.5 %collective-permute-start.10 = (bf16[48,1280]{1,0:T(8,128)(2,1)S(1)}, bf16[48,1280]{1,0:T(8,128)(2,1)S(1)}, u32[]{:S(2)}, u32[]{:S(2)}) collective-permute-start(bf16[48,1280]{1,0:T(8,128)(2,1)S(1)} %multiply_convert_fusion.7), channel_id=1, source_target_pairs={{0,6},{2,0},{4,2},{6,4},{1,7},{3,1},{5,3},{7,5},{8,14},{10,8},{12,... | collective-permute-start | bytes 368648 | tf_op jit(solution)/shard_map/ppermute | solution.py:52
  136.5 6.0 %collective-permute-start.8 = (bf16[48,1280]{1,0:T(8,128)(2,1)S(1)}, bf16[48,1280]{1,0:T(8,128)(2,1)S(1)}, u32[]{:S(2)}, u32[]{:S(2)}) collective-permute-start(bf16[48,1280]{1,0:T(8,128)(2,1)S(1)} %multiply_convert_fusion.7), channel_id=1, source_target_pairs={{0,2},{2,4},{4,6},{6,0},{1,3},{3,5},{5,7},{7,1},{8,10},{10,12},{12... | collective-permute-start | bytes 368648 | tf_op jit(solution)/shard_map/ppermute | solution.py:52
  136.5 6.4 %collective-permute-start.9 = (bf16[48,1280]{1,0:T(8,128)(2,1)S(1)}, bf16[48,1280]{1,0:T(8,128)(2,1)S(1)}, u32[]{:S(2)}, u32[]{:S(2)}) collective-permute-start(bf16[48,1280]{1,0:T(8,128)(2,1)S(1)} %multiply_convert_fusion.7), channel_id=1, source_target_pairs={{0,4},{2,6},{4,0},{6,2},{1,5},{3,7},{5,1},{7,3},{8,12},{10,14},{12... | collective-permute-start | bytes 368648 | tf_op jit(solution)/shard_map/ppermute | solution.py:52
  147.9 49.2 %copy-start.11 = (s32[8]{0:T(128)S(1)}, s32[8]{0:T(128)}, u32[]{:S(2)}) copy-start(s32[8]{0:T(128)} %param.15) | copy-start | bytes 100
  151.6 47.9 %collective-permute-start.13 = (bf16[48,1280]{1,0:T(8,128)(2,1)}, bf16[48,1280]{1,0:T(8,128)(2,1)}, u32[]{:S(2)}, u32[]{:S(2)}) collective-permute-start(bf16[48,1280]{1,0:T(8,128)(2,1)} %get-tuple-element.13), channel_id=1, source_target_pairs={{0,6},{2,0},{4,2},{6,4},{1,7},{3,1},{5,3},{7,5},{8,14},{10,8},{12,... | collective-permute-start | bytes 368648 | tf_op jit(solution)/shard_map/ppermute | solution.py:52
  155.2 44.4 %collective-permute-start.14 = (bf16[48,1280]{1,0:T(8,128)(2,1)}, bf16[48,1280]{1,0:T(8,128)(2,1)}, u32[]{:S(2)}, u32[]{:S(2)}) collective-permute-start(bf16[48,1280]{1,0:T(8,128)(2,1)} %get-tuple-element.15), channel_id=1, source_target_pairs={{0,4},{2,6},{4,0},{6,2},{1,5},{3,7},{5,1},{7,3},{8,12},{10,14},{12... | collective-permute-start | bytes 368648 | tf_op jit(solution)/shard_map/ppermute | solution.py:52
  155.4 44.2 %collective-permute-start.15 = (bf16[48,1280]{1,0:T(8,128)(2,1)S(1)}, bf16[48,1280]{1,0:T(8,128)(2,1)}, u32[]{:S(2)}, u32[]{:S(2)}) collective-permute-start(bf16[48,1280]{1,0:T(8,128)(2,1)S(1)} %get-tuple-element.14), channel_id=1, source_target_pairs={{0,2},{2,4},{4,6},{6,0},{1,3},{3,5},{5,7},{7,1},{8,10},{10,12},{12... | collective-permute-start | bytes 368648 | tf_op jit(solution)/shard_map/ppermute | solution.py:52
  200.9 4.9 %collective-permute-start.16 = (bf16[48,1280]{1,0:T(8,128)(2,1)S(1)}, bf16[48,1280]{1,0:T(8,128)(2,1)S(1)}, u32[]{:S(2)}, u32[]{:S(2)}) collective-permute-start(bf16[48,1280]{1,0:T(8,128)(2,1)S(1)} %fusion.68), channel_id=1, source_target_pairs={{0,2},{2,4},{4,6},{6,0},{1,3},{3,5},{5,7},{7,1},{8,10},{10,12},{12... | collective-permute-start | bytes 368648 | tf_op jit(solution)/shard_map/ppermute | solution.py:52
  202.9 6.4 %collective-permute-start.17 = (bf16[48,1280]{1,0:T(8,128)(2,1)S(1)}, bf16[48,1280]{1,0:T(8,128)(2,1)S(1)}, u32[]{:S(2)}, u32[]{:S(2)}) collective-permute-start(bf16[48,1280]{1,0:T(8,128)(2,1)S(1)} %fusion.68), channel_id=1, source_target_pairs={{0,4},{2,6},{4,0},{6,2},{1,5},{3,7},{5,1},{7,3},{8,12},{10,14},{12... | collective-permute-start | bytes 368648 | tf_op jit(solution)/shard_map/ppermute | solution.py:52
  203.2 6.9 %collective-permute-start.18 = (bf16[48,1280]{1,0:T(8,128)(2,1)S(1)}, bf16[48,1280]{1,0:T(8,128)(2,1)}, u32[]{:S(2)}, u32[]{:S(2)}) collective-permute-start(bf16[48,1280]{1,0:T(8,128)(2,1)S(1)} %fusion.68), channel_id=1, source_target_pairs={{0,6},{2,0},{4,2},{6,4},{1,7},{3,1},{5,3},{7,5},{8,14},{10,8},{12,... | collective-permute-start | bytes 368648 | tf_op jit(solution)/shard_map/ppermute | solution.py:52
  220.9 5.3 %collective-permute-start.19 = (bf16[48,1280]{1,0:T(8,128)(2,1)S(1)}, bf16[48,1280]{1,0:T(8,128)(2,1)S(1)}, u32[]{:S(2)}, u32[]{:S(2)}) collective-permute-start(bf16[48,1280]{1,0:T(8,128)(2,1)S(1)} %get-tuple-element.10), channel_id=1, source_target_pairs={{0,6},{2,0},{4,2},{6,4},{1,7},{3,1},{5,3},{7,5},{8,14},{10,8},{12,... | collective-permute-start | bytes 368648 | tf_op jit(solution)/shard_map/ppermute | solution.py:52
  221.1 6.9 %collective-permute-start.20 = (bf16[48,1280]{1,0:T(8,128)(2,1)S(1)}, bf16[48,1280]{1,0:T(8,128)(2,1)S(1)}, u32[]{:S(2)}, u32[]{:S(2)}) collective-permute-start(bf16[48,1280]{1,0:T(8,128)(2,1)S(1)} %get-tuple-element.12), channel_id=1, source_target_pairs={{0,4},{2,6},{4,0},{6,2},{1,5},{3,7},{5,1},{7,3},{8,12},{10,14},{12... | collective-permute-start | bytes 368648 | tf_op jit(solution)/shard_map/ppermute | solution.py:52
  223.8 5.5 %collective-permute-start.21 = (bf16[48,1280]{1,0:T(8,128)(2,1)S(1)}, bf16[48,1280]{1,0:T(8,128)(2,1)S(1)}, u32[]{:S(2)}, u32[]{:S(2)}) collective-permute-start(bf16[48,1280]{1,0:T(8,128)(2,1)S(1)} %get-tuple-element.11), channel_id=1, source_target_pairs={{0,2},{2,4},{4,6},{6,0},{1,3},{3,5},{5,7},{7,1},{8,10},{10,12},{12... | collective-permute-start | bytes 368648 | tf_op jit(solution)/shard_map/ppermute | solution.py:52
  234.7 21.6 %copy-start.5 = (bf16[8,76,64]{1,0,2:T(8,128)(2,1)S(1)}, bf16[8,76,64]{1,0,2:T(8,128)(2,1)}, u32[]{:S(2)}) copy-start(bf16[8,76,64]{1,0,2:T(8,128)(2,1)} %copy-done.4) | copy-start | bytes 233476
  252.3 12.1 %all-to-all-start.5 = ((bf16[8,64,76]{2,1,0:T(8,128)(2,1)}), bf16[8,64,76]{2,1,0:T(8,128)(2,1)S(1)}, u32[]{:S(2)}, u32[]{:S(2)}) async-start(bf16[8,64,76]{2,1,0:T(8,128)(2,1)} %bitcast.138), calls=%async_computation.5 | async-start | bytes 262144 | tf_op jit(solution)/shard_map/all_to_all | solution.py:68
  268.9 17.7 %all-to-all-start.6 = ((bf16[16,152,76]{2,1,0:T(8,128)(2,1)}), bf16[16,152,76]{2,1,0:T(8,128)(2,1)}, u32[]{:S(2)}, u32[]{:S(2)}) async-start(bf16[16,152,76]{2,1,0:T(8,128)(2,1)} %bitcast.148), calls=%async_computation.6 | async-start | bytes 1245184 | tf_op jit(solution)/shard_map/all_to_all | solution.py:68
  286.7 49.8 %all-to-all-start.4 = ((bf16[16,152,608]{2,1,0:T(8,128)(2,1)}), bf16[16,152,608]{2,1,0:T(8,128)(2,1)}, u32[]{:S(2)}, u32[]{:S(2)}) async-start(bf16[16,152,608]{2,1,0:T(8,128)(2,1)} %bitcast.143), calls=%async_computation.4 | async-start | bytes 6225920 | tf_op jit(solution)/shard_map/all_to_all | solution.py:68
  (9 other events, 62.1 us)
Sparse Core Ops, SparseCore 0:
  14.0 31.4 all-gather.1

commit v2 on v1

--- a/solution.py
+++ b/solution.py
@@ -101,15 +101,8 @@
     my_slot = reward_slot[my_image]
 
     split_in = jnp.moveaxis(w_in.reshape(d_dev, n_near, half), 1, 0)
-    keep = lax.dynamic_index_in_dim(split_in, near, 0, keepdims=False)
-    give = lax.dynamic_index_in_dim(split_in, 1 - near, 0, keepdims=False)
-    got = turned(give, "near", 1)
-    pair = jnp.stack([jnp.where(near == 0, keep, got), jnp.where(near == 0, got, keep)])
-    full_in = jnp.zeros((n_near, n_images, d_dev, half), BF16)
-    for step, block in enumerate(from_all(pair, IMAGE)):
-        owner = (my_image - step) % n_images
-        full_in = lax.dynamic_update_slice_in_dim(full_in, block[:, None], owner, 1)
-    full_in = full_in.reshape(width_d, half)
+    split_in = jnp.broadcast_to(split_in[:, None], (n_near, n_images, d_dev, half))
+    full_in = exchanged(split_in.reshape(n_rows, d_dev, half), ROWS_AT).reshape(width_d, half)
 
     modulate = modulation[timestep[0]]
     noise_rows = latent_noise[0]
@@ -127,31 +120,46 @@
     gated_final = (gates.T[:, :, None] * w_final.astype(F32)[:, None, :]).astype(BF16)
     gated_final = gated_final.reshape(width_d, n_images * lat)
     through = matmul_tn(strip_rows, gated_final).astype(BF16)
-    through = exchanged(jnp.moveaxis(through.reshape(strip, n_images, lat), 1, 0), IMAGE)
-    through = through.reshape(half, lat)
+    through = jnp.moveaxis(through.reshape(strip, n_images, lat), 1, 0)
+    through, full_in = lax.optimization_barrier((through, full_in))
+    through = exchanged(through, IMAGE).reshape(half, lat)
 
     v1_both = (w_v1, turned(w_v1, "core", 1))
     v2_both = (w_v2, turned(w_v2, "core", 1))
     my_target = lax.dynamic_slice_in_dim(target[0], near * mine, mine, 0)
-    goals = lax.all_gather(my_target, IMAGE, axis=0)
-    goal = lax.dynamic_index_in_dim(goals, my_slot, 0, keepdims=False).astype(F32)
 
     pre_act = matmul(token_rows, full_in)
     hidden, hidden_slope = with_slope(gelu_tanh, pre_act)
     hidden = hidden.astype(BF16)
-    latent_part = matmul(hidden, through)
-    latent_part = jnp.moveaxis(latent_part.reshape(n_y * n_core, n_near, mine, lat), 1, 0)
-    latent_parts = exchanged(latent_part.reshape(n_tokens, mine, lat), TOKENS_AT)
-    my_noise = lax.dynamic_slice_in_dim(noise_rows, near * mine, mine, 0)
-    latent = (matmul(my_noise, w_final) + jnp.sum(latent_parts, axis=0)).astype(BF16)
+    n_mp = n_y * n_core
+    own_part = matmul(noise_rows, w_final).reshape(1, n_near, mine, lat)
+    here = (lax.iota(jnp.int32, n_mp) == lax.axis_index(("y", "core")))[:, None]
+    here = here & (lax.iota(jnp.int32, n_near) == near)[None]
+    latent_part = matmul(hidden, through).reshape(n_mp, n_near, mine, lat)
+    latent_part = (latent_part + jnp.where(here[:, :, None, None], own_part, 0.0)).astype(BF16)
+    my_target, latent_part = lax.optimization_barrier((my_target, latent_part))
+    latent_part = latent_part.reshape(n_y, n_core, n_near, mine, lat).transpose(2, 1, 0, 3, 4)
+    latent_part = jnp.broadcast_to(latent_part[:, None], (n_near, n_y) + latent_part.shape[1:])
+    latent_parts = exchanged(latent_part.reshape(n_tokens, n_y * mine, lat), TOKENS_AT)
+    latents = jnp.sum(latent_parts.astype(F32), axis=0).astype(BF16)
+    goals = exchanged(jnp.broadcast_to(my_target, (n_images,) + my_target.shape), IMAGE)
+    goal = lax.dynamic_index_in_dim(goals, my_slot, 0, keepdims=False).astype(F32)
+    my_y = lax.axis_index("y")
+    latent = jnp.concatenate(
+        [
+            lax.dynamic_slice_in_dim(latents, (my_y - step) % n_y * mine, mine, 0)
+            for step in range(n_y)
+        ]
+    )
 
     dec_pre = matmul(latent, w_dec1)
     dec_act, dec_slope = with_slope(jax.nn.silu, dec_pre)
     pixels = matmul(dec_act.astype(BF16), w_dec2).astype(BF16)
     embedded = matmul(pixels, w_patch)
-    normed = layer_norm(embedded).astype(BF16)
-
-    patch_rows = jnp.concatenate(from_all(normed, "y"))
+    patch_rows = layer_norm(embedded).astype(BF16)
+    embedded = embedded[:mine]
+    dec_slope = dec_slope[:mine]
+
     slopes = []
     vit_part = 0.0
     for v1, v2 in zip(v1_both, v2_both):
@@ -176,17 +184,17 @@
     latent_rows = exchanged(spread, TOKENS_AT).reshape(n_near, n_y * n_core, mine, lat)
     latent_rows = jnp.moveaxis(latent_rows, 0, 1).reshape(rows, lat)
 
+    pre_grad = (hidden_slope * matmul_nt(latent_rows, through)).astype(BF16)
+    term_in = matmul_tn(token_rows, pre_grad).astype(BF16)
+    terms = exchanged(term_in.reshape(n_rows, d_dev, half), ROWS_AT)
+    grad_in = jnp.sum(terms.reshape(n_near, n_images, d_dev, half).astype(F32), axis=1)
+    grad_in = jnp.moveaxis(grad_in, 0, 1).reshape(d_dev, ff_mp)
+
     inner = matmul_tn(latent_rows, hidden).astype(BF16)
     inner = exchanged(jnp.moveaxis(inner.reshape(lat, n_images, strip), 1, 0), IMAGE)
     out_strip = matmul(gated_final, inner.reshape(n_images * lat, strip)).astype(BF16)
     out_strips = exchanged(out_strip.reshape(n_rows, d_dev, strip), ROWS_AT)
     grad_out_t = jnp.moveaxis(out_strips, 0, 1).reshape(d_dev, ff_mp).astype(F32)
-
-    pre_grad = (hidden_slope * matmul_nt(latent_rows, through)).astype(BF16)
-    term_in = matmul_tn(token_rows, pre_grad).astype(BF16)
-    terms = exchanged(term_in.reshape(n_rows, d_dev, half), ROWS_AT)
-    grad_in = jnp.sum(terms.reshape(n_near, n_images, d_dev, half).astype(F32), axis=1)
-    grad_in = jnp.moveaxis(grad_in, 0, 1).reshape(d_dev, ff_mp)
     return (grad_in, grad_out_t)
 
 

time: 353 us -> 327 us (0.926)
  waiting for transfers between devices: 67.4 us -> 113 us
  blocking collectives: 51.1 us -> 11.2 us
  starting transfers between devices: 85.6 us -> 64.7 us
  local copies, waits for them, and re-layouts: 58.1 us -> 45.6 us
  matrix products: 48.5 us -> 52.1 us
    all_to_all x6 -> x8, waiting for transfers between devices: 56.4 us -> 104 us  [exchanged(): return lax.all_to_all(blocks, axis, 0, 0, tiled=True)]
    all_gather x1 -> x0, blocking collectives: 39.8 us -> none  [on_device(): goals = lax.all_gather(my_target, IMAGE, axis=0)]
    ppermute x22 -> x11, starting transfers between devices: 37.4 us -> 18.6 us  [turned(): lax.ppermute(value, axis, [(at, (at + steps) % count) for at in range(cou...]
    dynamic_update_slice x7 -> x0, local copies, waits for them, and re-layouts: 10.5 us -> none  [on_device(): full_in = lax.dynamic_update_slice_in_dim(full_in, block[:, None], owner, 1)]
    dot_general x9 -> x10, matrix products: 24.6 us -> 28.8 us  [matmul(): return jnp.dot(left, right, preferred_element_type=F32)]
    ppermute x22 -> x11, waiting for transfers between devices: 10.9 us -> 8.78 us  [turned(): lax.ppermute(value, axis, [(at, (at + steps) % count) for at in range(cou...]
    all_to_all x6 -> x8, starting transfers between devices: 48.1 us -> 46 us  [exchanged(): return lax.all_to_all(blocks, axis, 0, 0, tiled=True)]
  transfers between devices with their start and end apart: 29 -> 20, of which waited for: 11 -> 12; matrix products, arithmetic and copies ran while one was open for 20% -> 19% of each run, Pallas kernels for 0% -> 0%
where the time goes in v2:
time: 327 us; the launch traced here: 323 us
  waiting for transfers between devices  113 us (35%)
  starting transfers between devices  64.7 us (20%)
  matrix products  52.1 us (16%)
  local copies, waits for them, and re-layouts  45.6 us (14%)
  other arithmetic  19.5 us (6%)
  between operations  17.2 us (5%)
  blocking collectives  11.2 us (3%)
    all_to_all x8, waiting for transfers between devices, exchanged(): return lax.all_to_all(blocks, axis, 0, 0, tiled=True)  104 us
    all_to_all x8, starting transfers between devices, exchanged(): return lax.all_to_all(blocks, axis, 0, 0, tiled=True)  46 us
    dot_general x10, matrix products, matmul(): return jnp.dot(left, right, preferred_element_type=F32)  28.8 us
    ppermute x11, starting transfers between devices, turned(): lax.ppermute(value, axis, [(at, (at + steps) % count) for at in range(cou...  18.6 us
    dot_general x4, matrix products, matmul_nt(): lax.dot_general(left, right, (((1,), (1,)), ((), ())), preferred_element_...  12.8 us
    all_to_all x1, blocking collectives, exchanged(): return lax.all_to_all(blocks, axis, 0, 0, tiled=True)  11.2 us
    dot_general x3, matrix products, matmul_tn(): lax.dot_general(left, right, (((0,), (0,)), ((), ())), preferred_element_...  10.5 us
    ppermute x11, waiting for transfers between devices, turned(): lax.ppermute(value, axis, [(at, (at + steps) % count) for at in range(cou...  8.78 us
  transfers between devices with their start and end apart: 20, of which 12 were waited for; matrix products, arithmetic and copies ran while one was open for 19% of the time, Pallas kernels for 0%

profile of v2, /device:TPU:8, one launch (start us, length us, event | category | flops | bytes accessed | tf_op | source)
XLA Modules:
  0.0 323.0 jit_solution(8226177147583110138)
XLA Ops:
  18.1 7.9 %all-to-all-start = ((bf16[16,160,76]{2,1,0:T(8,128)(2,1)}), bf16[16,160,76]{2,1,0:T(8,128)(2,1)}, u32[]{:S(2)}, u32[]{:S(2)}) async-start(bf16[16,160,76]{2,1,0:T(8,128)(2,1)} %concatenate.12.clone), calls=%async_computation | async-start | bytes 1310720 | tf_op jit(solution)/shard_map/all_to_all | solution.py:68
  28.3 10.1 %all-to-all-done = bf16[16,160,76]{2,1,0:T(8,128)(2,1)} async-done(((bf16[16,160,76]{2,1,0:T(8,128)(2,1)}), bf16[16,160,76]{2,1,0:T(8,128)(2,1)}, u32[]{:S(2)}, u32[]{:S(2)}) %all-to-all-start) | async-done | bytes 389152 | tf_op jit(solution)/shard_map/all_to_all | solution.py:68
  38.4 2.9 broadcast_in_dim.34
  41.3 4.6 %all-to-all-start.1 = ((bf16[16,152,608]{2,1,0:T(8,128)(2,1)}), bf16[16,152,608]{2,1,0:T(8,128)(2,1)}, u32[]{:S(2)}, u32[]{:S(2)}) async-start(bf16[16,152,608]{2,1,0:T(8,128)(2,1)} %bitcast.102), calls=%async_computation.1 | async-start | bytes 6225920 | tf_op jit(solution)/shard_map/all_to_all | solution.py:68
  55.8 33.1 %all-to-all-done.1 = bf16[16,152,608]{2,1,0:T(8,128)(2,1)} async-done(((bf16[16,152,608]{2,1,0:T(8,128)(2,1)}), bf16[16,152,608]{2,1,0:T(8,128)(2,1)}, u32[]{:S(2)}, u32[]{:S(2)}) %all-to-all-start.1) | async-done | bytes 2957344 | tf_op jit(solution)/shard_map/all_to_all | solution.py:68
  89.7 5.8 %all-to-all-start.2 = ((bf16[8,76,64]{1,2,0:T(8,128)(2,1)}), bf16[8,76,64]{1,2,0:T(8,128)(2,1)S(1)}, u32[]{:S(2)}, u32[]{:S(2)}) async-start(bf16[8,76,64]{1,2,0:T(8,128)(2,1)} %copy.70), calls=%async_computation.2 | async-start | bytes 262144 | tf_op jit(solution)/shard_map/all_to_all | solution.py:68
  95.6 8.1 %all-to-all-done.2 = bf16[8,76,64]{1,2,0:T(8,128)(2,1)S(1)} async-done(((bf16[8,76,64]{1,2,0:T(8,128)(2,1)}), bf16[8,76,64]{1,2,0:T(8,128)(2,1)S(1)}, u32[]{:S(2)}, u32[]{:S(2)}) %all-to-all-start.2) | async-done | bytes 77856 | tf_op jit(solution)/shard_map/all_to_all | solution.py:68
  104.0 7.5 %multiply_convert_fusion.1 = (bf16[768,608]{0,1:T(8,128)(2,1)}, f32[768,608]{0,1:T(8,128)}) fusion(bf16[768,2432]{1,0:T(8,128)(2,1)} %all-gather.2.cloned.1.call-done, bf16[2432,608]{1,0:T(8,128)(2,1)} %bitcast.10), kind=kOutput, calls=%fused_computation.20 | convolution fusion | flops 2275418112 | bytes 9494528 | tf_op jit(solution)/shard_map/dot_general | solution.py:39
  118.7 5.4 %all-to-all-start.3 = ((bf16[16,192,64]{1,2,0:T(8,128)(2,1)}), bf16[16,192,64]{1,2,0:T(8,128)(2,1)}, u32[]{:S(2)}, u32[]{:S(2)}) async-start(bf16[16,192,64]{1,2,0:T(8,128)(2,1)} %copy.73), calls=%async_computation.3 | async-start | bytes 1048576 | tf_op jit(solution)/shard_map/all_to_all | solution.py:68
  124.6 7.0 %all-to-all-done.3 = bf16[16,192,64]{1,2,0:T(8,128)(2,1)} async-done(((bf16[16,192,64]{1,2,0:T(8,128)(2,1)}), bf16[16,192,64]{1,2,0:T(8,128)(2,1)}, u32[]{:S(2)}, u32[]{:S(2)}) %all-to-all-start.3) | async-done | bytes 393248 | tf_op jit(solution)/shard_map/all_to_all | solution.py:68
  132.7 4.4 %all-to-all-start.4 = ((bf16[8,48,1280]{2,1,0:T(8,128)(2,1)}), bf16[8,48,1280]{2,1,0:T(8,128)(2,1)}, u32[]{:S(2)}, u32[]{:S(2)}) async-start(bf16[8,48,1280]{2,1,0:T(8,128)(2,1)} %broadcast_in_dim.40), calls=%async_computation.4 | async-start | bytes 1966080 | tf_op jit(solution)/shard_map/all_to_all | solution.py:68
  138.4 3.3 %add_divide_fusion = (f32[192,2048]{1,0:T(8,128)}, f32[192,2048]{1,0:T(8,128)}) fusion(bf16[64,2048]{1,0:T(8,128)(2,1)} %param.21, bf16[48,64]{0,1:T(8,128)(2,1)S(1)} %get-tuple-element.27, bf16[48,64]{0,1:T(8,128)(2,1)S(1)} %get-tuple-element.28, bf16[48,64]{0,1:T(8,128)(2,1)S(1)} %get-tuple-element.29, bf16[48,64]{0,1:T(8,128)(2,1)S(1)} %get-tuple-element.26), kind=kOutput, calls=%fused_computation.22 | convolution fusion | flops 51609600 | bytes 3432448 | tf_op jit(solution)/shard_map/dot_general | solution.py:39
  141.6 4.5 %fusion.148 = (f32[192]{0:T(256)S(1)}, f32[192,1280]{1,0:T(8,128)}) fusion(bf16[768,1280]{1,0:T(8,128)(2,1)} %param.23, bf16[2048,768]{1,0:T(8,128)(2,1)S(1)} %copy-done, f32[192,2048]{1,0:T(8,128)} %get-tuple-element.41), kind=kOutput, calls=%fused_computation.202 | convolution fusion | flops 983826240 | bytes 7668480 | tf_op jit(solution)/shard_map/dot_general | solution.py:39
  153.6 3.2 fusion.149
  157.6 3.5 %collective-permute-start.2 = (bf16[48,1280]{1,0:T(8,128)(2,1)}, bf16[48,1280]{1,0:T(8,128)(2,1)S(1)}, u32[]{:S(2)}, u32[]{:S(2)}) collective-permute-start(bf16[48,1280]{1,0:T(8,128)(2,1)} %get-tuple-element.23), channel_id=1, source_target_pairs={{0,6},{2,0},{4,2},{6,4},{1,7},{3,1},{5,3},{7,5},{8,14},{10,8},{12,... | collective-permute-start | bytes 368648 | tf_op jit(solution)/shard_map/ppermute | solution.py:52
  161.1 3.0 collective-permute-start.3
  169.2 4.3 %collective-permute-start.7 = (bf16[48,1280]{1,0:T(8,128)(2,1)S(1)}, bf16[48,1280]{1,0:T(8,128)(2,1)S(1)}, u32[]{:S(2)}, u32[]{:S(2)}) collective-permute-start(bf16[48,1280]{1,0:T(8,128)(2,1)S(1)} %get-tuple-element.18), channel_id=1, source_target_pairs={{0,6},{2,0},{4,2},{6,4},{1,7},{3,1},{5,3},{7,5},{8,14},{10,8},{12,... | collective-permute-start | bytes 368648 | tf_op jit(solution)/shard_map/ppermute | solution.py:52
  177.0 2.9 collective-permute-done.6
  180.6 4.6 %fusion.13 = f32[192,1280]{1,0:T(8,128)} fusion(bf16[1280,640]{1,0:T(8,128)(2,1)} %param.24, bf16[640,1280]{1,0:T(8,128)(2,1)} %param.25, f32[192,640]{1,0:T(8,128)} %copy-done.4, bf16[48,1280]{1,0:T(8,128)(2,1)S(1)} %collective-permute-done.7, bf16[48,1280]{1,0:T(8,128)(2,1)} %copy-done.12, bf16[48,1280]{1,0:T(8,128)(2,1)} %collective-permute-done.5, ...), kind=kOutput, calls=%fused_computation.31 | convolution fusion | flops 633446400 | bytes 5242880 | tf_op jit(solution)/shard_map/dot_general | solution.py:43
  185.2 5.0 %fusion.150 = (bf16[192,1280]{1,0:T(8,128)(2,1)}, f32[192,1280]{1,0:T(8,128)}) fusion(f32[192,1280]{1,0:T(8,128)} %fusion.13, bf16[1280,640]{1,0:T(8,128)(2,1)} %collective-permute-done, f32[192,640]{1,0:T(8,128)} %copy-done.3, bf16[640,1280]{1,0:T(8,128)(2,1)} %collective-permute-done.1, bf16[48,1280]{1,0:T(8,128)(2,1)S(1)} %collective-permute-done.7, ...), kind=kOutput, calls=%fused_computation.204 | convolution fusion | flops 633937920 | bytes 6717440 | tf_op jit(solution)/shard_map/dot_general | solution.py:43
  193.5 3.6 %collective-permute-start.9 = (bf16[48,1280]{1,0:T(8,128)(2,1)S(1)}, bf16[48,1280]{1,0:T(8,128)(2,1)S(1)}, u32[]{:S(2)}, u32[]{:S(2)}) collective-permute-start(bf16[48,1280]{1,0:T(8,128)(2,1)S(1)} %get-tuple-element.22), channel_id=1, source_target_pairs={{0,4},{2,6},{4,0},{6,2},{1,5},{3,7},{5,1},{7,3},{8,12},{10,14},{12... | collective-permute-start | bytes 368648 | tf_op jit(solution)/shard_map/ppermute | solution.py:52
  203.3 2.4 fusion.15
  206.6 11.2 %all_to_all.45 = bf16[16,2,1536]{2,1,0:T(2,128)(2,1)S(1)} all-to-all(bf16[16,2,1536]{2,1,0:T(2,128)(2,1)} %reshape.236), channel_id=1, replica_groups=mesh['near'=2,'z'=4,'far'=2,'y'=4,'core'=2] {'near','y','core'}, dimensions={0} | all-to-all | bytes 196608 | tf_op jit(solution)/shard_map/all_to_all | solution.py:68
  223.2 6.5 %all-to-all-start.7 = ((bf16[8,64,76]{2,1,0:T(8,128)(2,1)}), bf16[8,64,76]{2,1,0:T(8,128)(2,1)S(1)}, u32[]{:S(2)}, u32[]{:S(2)}) async-start(bf16[8,64,76]{2,1,0:T(8,128)(2,1)} %bitcast.97), calls=%async_computation.7 | async-start | bytes 262144 | tf_op jit(solution)/shard_map/all_to_all | solution.py:68
  229.8 8.0 %all-to-all-done.7 = bf16[8,64,76]{2,1,0:T(8,128)(2,1)S(1)} async-done(((bf16[8,64,76]{2,1,0:T(8,128)(2,1)}), bf16[8,64,76]{2,1,0:T(8,128)(2,1)S(1)}, u32[]{:S(2)}, u32[]{:S(2)}) %all-to-all-start.7) | async-done | bytes 77856 | tf_op jit(solution)/shard_map/all_to_all | solution.py:68
  242.4 4.3 %all-to-all-start.8 = ((bf16[16,152,76]{2,1,0:T(8,128)(2,1)}), bf16[16,152,76]{2,1,0:T(8,128)(2,1)}, u32[]{:S(2)}, u32[]{:S(2)}) async-start(bf16[16,152,76]{2,1,0:T(8,128)(2,1)} %bitcast.110), calls=%async_computation.8 | async-start | bytes 1245184 | tf_op jit(solution)/shard_map/all_to_all | solution.py:68
  246.6 8.0 %convolution_convert_fusion = bf16[2432,608]{0,1:T(8,128)(2,1)} fusion(bf16[768,2432]{1,0:T(8,128)(2,1)} %all-gather.2.cloned.1.call-done, f32[768,608]{0,1:T(8,128)} %get-tuple-element.33, bf16[768,64]{0,1:T(8,128)(2,1)S(1)} %copy-done.8, bf16[608,64]{0,1:T(8,128)(2,1)S(1)} %reshape.209), kind=kOutput, calls=%fused_computation.3 | convolution fusion | flops 2341335040 | bytes 8736768 | tf_op jit(solution)/shard_map/dot_general | solution.py:47
  254.6 5.5 %copy.75 = bf16[2432,608]{1,0:T(8,128)(2,1)} copy(bf16[2432,608]{0,1:T(8,128)(2,1)} %convolution_convert_fusion) | data formatting | bytes 5914624 | tf_op jit(solution)/shard_map/convert_element_type | solution.py:188
  260.1 7.1 %all-to-all-start.6 = ((bf16[16,152,608]{2,1,0:T(8,128)(2,1)}), bf16[16,152,608]{2,1,0:T(8,128)(2,1)}, u32[]{:S(2)}, u32[]{:S(2)}) async-start(bf16[16,152,608]{2,1,0:T(8,128)(2,1)} %bitcast.103), calls=%async_computation.6 | async-start | bytes 6225920 | tf_op jit(solution)/shard_map/all_to_all | solution.py:68
  269.6 2.7 reshape.222
  272.3 37.6 %all-to-all-done.6 = bf16[16,152,608]{2,1,0:T(8,128)(2,1)} async-done(((bf16[16,152,608]{2,1,0:T(8,128)(2,1)}), bf16[16,152,608]{2,1,0:T(8,128)(2,1)}, u32[]{:S(2)}, u32[]{:S(2)}) %all-to-all-start.6) | async-done | bytes 2957344 | tf_op jit(solution)/shard_map/all_to_all | solution.py:68
  313.7 2.5 reshape.216
  (116 shorter events, 74.9 us)
Async XLA Ops:
  7.2 134.5 %copy-start = (bf16[2048,768]{1,0:T(8,128)(2,1)S(1)}, bf16[2048,768]{1,0:T(8,128)(2,1)}, u32[]{:S(2)}) copy-start(bf16[2048,768]{1,0:T(8,128)(2,1)} %param.22) | copy-start | bytes 9437188
  7.2 6.8 %copy-start.9 = (bf16[152,1216]{1,0:T(8,128)(2,1)S(1)}, bf16[152,1216]{1,0:T(8,128)(2,1)}, u32[]{:S(2)}) copy-start(bf16[152,1216]{1,0:T(8,128)(2,1)} %param.19) | copy-start | bytes 1108996
  7.2 96.8 %all-gather.2.cloned.1.call-start = ((), (), s32[]{:S(2)}) async-start(), calls=%async_computation.9 | async-start | bytes 4202496 | tf_op jit(solution)/shard_map/all_gather | solution.py:112
  18.1 20.3 %all-to-all-start = ((bf16[16,160,76]{2,1,0:T(8,128)(2,1)}), bf16[16,160,76]{2,1,0:T(8,128)(2,1)}, u32[]{:S(2)}, u32[]{:S(2)}) async-start(bf16[16,160,76]{2,1,0:T(8,128)(2,1)} %concatenate.12.clone), calls=%async_computation | async-start | bytes 1310720 | tf_op jit(solution)/shard_map/all_to_all | solution.py:68
  41.3 4.6 %copy-start.6 = (bf16[2432,64]{0,1:T(8,128)(2,1)S(1)}, bf16[2432,64]{0,1:T(8,128)(2,1)}, u32[]{:S(2)}) copy-start(bf16[2432,64]{0,1:T(8,128)(2,1)} %param.20) | copy-start | bytes 933892
  41.3 47.5 %all-to-all-start.1 = ((bf16[16,152,608]{2,1,0:T(8,128)(2,1)}), bf16[16,152,608]{2,1,0:T(8,128)(2,1)}, u32[]{:S(2)}, u32[]{:S(2)}) async-start(bf16[16,152,608]{2,1,0:T(8,128)(2,1)} %bitcast.102), calls=%async_computation.1 | async-start | bytes 6225920 | tf_op jit(solution)/shard_map/all_to_all | solution.py:68
  52.1 2.6 copy-start.10
  89.7 14.0 %all-to-all-start.2 = ((bf16[8,76,64]{1,2,0:T(8,128)(2,1)}), bf16[8,76,64]{1,2,0:T(8,128)(2,1)S(1)}, u32[]{:S(2)}, u32[]{:S(2)}) async-start(bf16[8,76,64]{1,2,0:T(8,128)(2,1)} %copy.70), calls=%async_computation.2 | async-start | bytes 262144 | tf_op jit(solution)/shard_map/all_to_all | solution.py:68
  115.4 16.3 %copy-start.7 = (bf16[48,1280]{1,0:T(8,128)(2,1)S(1)}, bf16[48,1280]{1,0:T(8,128)(2,1)}, u32[]{:S(2)}) copy-start(bf16[48,1280]{1,0:T(8,128)(2,1)} %dynamic-slice_bitcast_fusion) | copy-start | bytes 368644
  118.7 12.9 %all-to-all-start.3 = ((bf16[16,192,64]{1,2,0:T(8,128)(2,1)}), bf16[16,192,64]{1,2,0:T(8,128)(2,1)}, u32[]{:S(2)}, u32[]{:S(2)}) async-start(bf16[16,192,64]{1,2,0:T(8,128)(2,1)} %copy.73), calls=%async_computation.3 | async-start | bytes 1048576 | tf_op jit(solution)/shard_map/all_to_all | solution.py:68
  124.1 26.7 %collective-permute-start = (bf16[1280,640]{1,0:T(8,128)(2,1)}, bf16[1280,640]{1,0:T(8,128)(2,1)}, u32[]{:S(2)}, u32[]{:S(2)}) collective-permute-start(bf16[1280,640]{1,0:T(8,128)(2,1)} %param.24), channel_id=1, source_target_pairs={{0,1},{1,0},{2,3},{3,2},{4,5},{5,4},{6,7},{7,6},{8,9},{9,8},{10,11... | collective-permute-start | bytes 4915208 | tf_op jit(solution)/shard_map/ppermute | solution.py:52
  124.2 29.4 %collective-permute-start.1 = (bf16[640,1280]{1,0:T(8,128)(2,1)}, bf16[640,1280]{1,0:T(8,128)(2,1)}, u32[]{:S(2)}, u32[]{:S(2)}) collective-permute-start(bf16[640,1280]{1,0:T(8,128)(2,1)} %param.25), channel_id=1, source_target_pairs={{0,1},{1,0},{2,3},{3,2},{4,5},{5,4},{6,7},{7,6},{8,9},{9,8},{10,11... | collective-permute-start | bytes 4915208 | tf_op jit(solution)/shard_map/ppermute | solution.py:52
  132.7 35.1 %all-to-all-start.4 = ((bf16[8,48,1280]{2,1,0:T(8,128)(2,1)}), bf16[8,48,1280]{2,1,0:T(8,128)(2,1)}, u32[]{:S(2)}, u32[]{:S(2)}) async-start(bf16[8,48,1280]{2,1,0:T(8,128)(2,1)} %broadcast_in_dim.40), calls=%async_computation.4 | async-start | bytes 1966080 | tf_op jit(solution)/shard_map/all_to_all | solution.py:68
  146.2 3.9 %copy-start.5 = (bf16[640,1280]{1,0:T(8,128)(2,1)S(1)}, bf16[640,1280]{1,0:T(8,128)(2,1)}, u32[]{:S(2)}) copy-start(bf16[640,1280]{1,0:T(8,128)(2,1)} %param.25) | copy-start | bytes 4915204
  150.1 3.4 %copy-start.4 = (f32[192,640]{1,0:T(8,128)}, f32[192,640]{1,0:T(8,128)S(1)}, u32[]{:S(2)}) copy-start(f32[192,640]{1,0:T(8,128)S(1)} %fusion.144) | copy-start | bytes 1474564
  150.1 1.4 copy-start.1
  153.5 3.2 %copy-start.3 = (f32[192,640]{1,0:T(8,128)}, f32[192,640]{1,0:T(8,128)S(1)}, u32[]{:S(2)}) copy-start(f32[192,640]{1,0:T(8,128)S(1)} %fusion.143) | copy-start | bytes 1474564
  153.6 10.6 %copy-start.13 = (s32[8]{0:T(128)S(1)}, s32[8]{0:T(128)}, u32[]{:S(2)}) copy-start(s32[8]{0:T(128)} %param.15) | copy-start | bytes 100
  157.6 9.1 %collective-permute-start.2 = (bf16[48,1280]{1,0:T(8,128)(2,1)}, bf16[48,1280]{1,0:T(8,128)(2,1)S(1)}, u32[]{:S(2)}, u32[]{:S(2)}) collective-permute-start(bf16[48,1280]{1,0:T(8,128)(2,1)} %get-tuple-element.23), channel_id=1, source_target_pairs={{0,6},{2,0},{4,2},{6,4},{1,7},{3,1},{5,3},{7,5},{8,14},{10,8},{12,... | collective-permute-start | bytes 368648 | tf_op jit(solution)/shard_map/ppermute | solution.py:52
  161.1 6.0 %collective-permute-start.4 = (bf16[48,1280]{1,0:T(8,128)(2,1)}, bf16[48,1280]{1,0:T(8,128)(2,1)S(1)}, u32[]{:S(2)}, u32[]{:S(2)}) collective-permute-start(bf16[48,1280]{1,0:T(8,128)(2,1)} %get-tuple-element.24), channel_id=1, source_target_pairs={{0,2},{2,4},{4,6},{6,0},{1,3},{3,5},{5,7},{7,1},{8,10},{10,12},{12... | collective-permute-start | bytes 368648 | tf_op jit(solution)/shard_map/ppermute | solution.py:52
  161.1 6.7 %collective-permute-start.3 = (bf16[48,1280]{1,0:T(8,128)(2,1)}, bf16[48,1280]{1,0:T(8,128)(2,1)}, u32[]{:S(2)}, u32[]{:S(2)}) collective-permute-start(bf16[48,1280]{1,0:T(8,128)(2,1)} %get-tuple-element.25), channel_id=1, source_target_pairs={{0,4},{2,6},{4,0},{6,2},{1,5},{3,7},{5,1},{7,3},{8,12},{10,14},{12... | collective-permute-start | bytes 368648 | tf_op jit(solution)/shard_map/ppermute | solution.py:52
  169.2 7.7 %collective-permute-start.7 = (bf16[48,1280]{1,0:T(8,128)(2,1)S(1)}, bf16[48,1280]{1,0:T(8,128)(2,1)S(1)}, u32[]{:S(2)}, u32[]{:S(2)}) collective-permute-start(bf16[48,1280]{1,0:T(8,128)(2,1)S(1)} %get-tuple-element.18), channel_id=1, source_target_pairs={{0,6},{2,0},{4,2},{6,4},{1,7},{3,1},{5,3},{7,5},{8,14},{10,8},{12,... | collective-permute-start | bytes 368648 | tf_op jit(solution)/shard_map/ppermute | solution.py:52
  173.5 6.4 %collective-permute-start.6 = (bf16[48,1280]{1,0:T(8,128)(2,1)S(1)}, bf16[48,1280]{1,0:T(8,128)(2,1)S(1)}, u32[]{:S(2)}, u32[]{:S(2)}) collective-permute-start(bf16[48,1280]{1,0:T(8,128)(2,1)S(1)} %get-tuple-element.18), channel_id=1, source_target_pairs={{0,4},{2,6},{4,0},{6,2},{1,5},{3,7},{5,1},{7,3},{8,12},{10,14},{12... | collective-permute-start | bytes 368648 | tf_op jit(solution)/shard_map/ppermute | solution.py:52
  173.5 7.0 %collective-permute-start.5 = (bf16[48,1280]{1,0:T(8,128)(2,1)S(1)}, bf16[48,1280]{1,0:T(8,128)(2,1)}, u32[]{:S(2)}, u32[]{:S(2)}) collective-permute-start(bf16[48,1280]{1,0:T(8,128)(2,1)S(1)} %get-tuple-element.18), channel_id=1, source_target_pairs={{0,2},{2,4},{4,6},{6,0},{1,3},{3,5},{5,7},{7,1},{8,10},{10,12},{12... | collective-permute-start | bytes 368648 | tf_op jit(solution)/shard_map/ppermute | solution.py:52
  190.2 12.3 %copy-start.2 = (bf16[768,1280]{1,0:T(8,128)(2,1)S(1)}, bf16[768,1280]{1,0:T(8,128)(2,1)}, u32[]{:S(2)}) copy-start(bf16[768,1280]{1,0:T(8,128)(2,1)} %param.23) | copy-start | bytes 5898244
  191.4 5.7 %collective-permute-start.8 = (bf16[48,1280]{1,0:T(8,128)(2,1)S(1)}, bf16[48,1280]{1,0:T(8,128)(2,1)S(1)}, u32[]{:S(2)}, u32[]{:S(2)}) collective-permute-start(bf16[48,1280]{1,0:T(8,128)(2,1)S(1)} %get-tuple-element.20), channel_id=1, source_target_pairs={{0,6},{2,0},{4,2},{6,4},{1,7},{3,1},{5,3},{7,5},{8,14},{10,8},{12,... | collective-permute-start | bytes 368648 | tf_op jit(solution)/shard_map/ppermute | solution.py:52
  193.4 5.7 %collective-permute-start.10 = (bf16[48,1280]{1,0:T(8,128)(2,1)S(1)}, bf16[48,1280]{1,0:T(8,128)(2,1)S(1)}, u32[]{:S(2)}, u32[]{:S(2)}) collective-permute-start(bf16[48,1280]{1,0:T(8,128)(2,1)S(1)} %get-tuple-element.21), channel_id=1, source_target_pairs={{0,2},{2,4},{4,6},{6,0},{1,3},{3,5},{5,7},{7,1},{8,10},{10,12},{12... | collective-permute-start | bytes 368648 | tf_op jit(solution)/shard_map/ppermute | solution.py:52
  193.5 6.4 %collective-permute-start.9 = (bf16[48,1280]{1,0:T(8,128)(2,1)S(1)}, bf16[48,1280]{1,0:T(8,128)(2,1)S(1)}, u32[]{:S(2)}, u32[]{:S(2)}) collective-permute-start(bf16[48,1280]{1,0:T(8,128)(2,1)S(1)} %get-tuple-element.22), channel_id=1, source_target_pairs={{0,4},{2,6},{4,0},{6,2},{1,5},{3,7},{5,1},{7,3},{8,12},{10,14},{12... | collective-permute-start | bytes 368648 | tf_op jit(solution)/shard_map/ppermute | solution.py:52
  223.2 14.7 %all-to-all-start.7 = ((bf16[8,64,76]{2,1,0:T(8,128)(2,1)}), bf16[8,64,76]{2,1,0:T(8,128)(2,1)S(1)}, u32[]{:S(2)}, u32[]{:S(2)}) async-start(bf16[8,64,76]{2,1,0:T(8,128)(2,1)} %bitcast.97), calls=%async_computation.7 | async-start | bytes 262144 | tf_op jit(solution)/shard_map/all_to_all | solution.py:68
  229.8 16.8 %copy-start.8 = (bf16[768,64]{0,1:T(8,128)(2,1)S(1)}, bf16[768,64]{0,1:T(8,128)(2,1)}, u32[]{:S(2)}) copy-start(bf16[768,64]{0,1:T(8,128)(2,1)} %reshape.214) | copy-start | bytes 294916
  242.4 17.8 %all-to-all-start.8 = ((bf16[16,152,76]{2,1,0:T(8,128)(2,1)}), bf16[16,152,76]{2,1,0:T(8,128)(2,1)}, u32[]{:S(2)}, u32[]{:S(2)}) async-start(bf16[16,152,76]{2,1,0:T(8,128)(2,1)} %bitcast.110), calls=%async_computation.8 | async-start | bytes 1245184 | tf_op jit(solution)/shard_map/all_to_all | solution.py:68
  260.1 49.8 %all-to-all-start.6 = ((bf16[16,152,608]{2,1,0:T(8,128)(2,1)}), bf16[16,152,608]{2,1,0:T(8,128)(2,1)}, u32[]{:S(2)}, u32[]{:S(2)}) async-start(bf16[16,152,608]{2,1,0:T(8,128)(2,1)} %bitcast.103), calls=%async_computation.6 | async-start | bytes 6225920 | tf_op jit(solution)/shard_map/all_to_all | solution.py:68
  (2 other events, 1.4 us)
Sparse Core Ops, SparseCore 0:
  14.0 31.4 all-gather.1

commit v3 on v2

--- a/solution.py
+++ b/solution.py
@@ -3,10 +3,14 @@
 import jax
 import jax.numpy as jnp
 from jax import lax
+from jax.experimental import pallas as pl
+from jax.experimental.pallas import tpu as pltpu
 from jax.sharding import Mesh
 from jax.sharding import PartitionSpec as P
 
 BF16 = jnp.bfloat16
+GELU_SCALE = math.sqrt(2.0 / math.pi)
+VMEM_BYTES = 56 * 1024 * 1024
 F32 = jnp.float32
 AXES = ("near", "z", "far", "y", "core")
 IMAGE = ("z", "far")
@@ -21,13 +25,18 @@
     return centred * lax.rsqrt(variance + 1e-06)
 
 
-def gelu_tanh(values):
-    return jax.nn.gelu(values, approximate=True)
-
-
-def with_slope(function, values):
-    result, pullback = jax.vjp(function, values)
-    return result, pullback(jnp.ones_like(values))[0]
+def gelu_and_slope(values):
+    inner = GELU_SCALE * (values + 0.044715 * values * values * values)
+    bent = jnp.tanh(inner)
+    half = 0.5 * (1.0 + bent)
+    rate = GELU_SCALE * (1.0 + 3 * 0.044715 * values * values)
+    return values * half, half + 0.5 * values * (1.0 - bent * bent) * rate
+
+
+def silu_and_slope(values):
+    gate = jax.nn.sigmoid(values)
+    result = values * gate
+    return result, gate + result * (1.0 - gate)
 
 
 def norm_back(values, cotangent):
@@ -58,14 +67,232 @@
 
 
 def summed_back(blocks, axis):
-    total = blocks[0]
+    total = blocks[0].astype(F32)
     for step in range(1, len(blocks)):
-        total = total + turned(blocks[step].astype(BF16), axis, -step).astype(F32)
+        total = total + turned(blocks[step], axis, -step).astype(F32)
     return total
+
+
+def by_turns(blocks, axis):
+    count = lax.axis_size(axis)
+    here = lax.axis_index(axis)
+    blocks = lax.optimization_barrier(blocks)
+    result = []
+    for step in range(count):
+        block = lax.dynamic_slice_in_dim(blocks, (here + step) % count, 1, 0)
+        result.append(turned(block, axis, step) if step else block)
+    return result
 
 
 def exchanged(blocks, axis):
     return lax.all_to_all(blocks, axis, 0, 0, tiled=True)
+
+
+def whole(array):
+    return pl.BlockSpec(array.shape, lambda step: (0,) * len(array.shape))
+
+
+def call(kernel, grid, in_specs, out_specs, out_shape, scratch, flops, moved, *operands):
+    return pl.pallas_call(
+        kernel,
+        grid=(grid,),
+        in_specs=in_specs,
+        out_specs=out_specs,
+        out_shape=out_shape,
+        scratch_shapes=scratch,
+        compiler_params=pltpu.CompilerParams(vmem_limit_bytes=VMEM_BYTES),
+        cost_estimate=pl.CostEstimate(flops=flops, bytes_accessed=moved, transcendentals=0),
+    )(*operands)
+
+
+def block_forward_kernel(tokens, weights, through, hidden, slope, latent):
+    act, rate = gelu_and_slope(matmul(tokens[...], weights[...]))
+    act = act.astype(BF16)
+    hidden[...] = act
+    slope[...] = rate.astype(BF16)
+    latent[...] = matmul(act, through[...])
+
+
+def block_forward(tokens, weights, through):
+    rows, width = tokens.shape
+    columns, lat = through.shape
+    tile = rows // 4
+    by_rows = lambda last: pl.BlockSpec((tile, last), lambda step: (step, 0))
+    return call(
+        block_forward_kernel,
+        4,
+        [by_rows(width), whole(weights), whole(through)],
+        [by_rows(columns), by_rows(columns), by_rows(lat)],
+        [
+            jax.ShapeDtypeStruct((rows, columns), BF16),
+            jax.ShapeDtypeStruct((rows, columns), BF16),
+            jax.ShapeDtypeStruct((rows, lat), F32),
+        ],
+        [],
+        2 * rows * columns * width,
+        2 * (rows * width + width * columns + 2 * rows * columns),
+        tokens,
+        weights,
+        through,
+    )
+
+
+def block_backward_kernel(latent_grad, through, slope, tokens, term, pre_grad):
+    @pl.when(pl.program_id(0) == 0)
+    def _():
+        back = matmul_nt(latent_grad[...], through[...])
+        pre_grad[...] = (slope[...].astype(F32) * back).astype(BF16)
+
+    term[...] = matmul_tn(tokens[...], pre_grad[...]).astype(BF16)
+
+
+def block_backward(latent_grad, through, slope, tokens):
+    rows, width = tokens.shape
+    columns = slope.shape[1]
+    tile = min(640, width)
+    return call(
+        block_backward_kernel,
+        pl.cdiv(width, tile),
+        [
+            whole(latent_grad),
+            whole(through),
+            whole(slope),
+            pl.BlockSpec((rows, tile), lambda step: (0, step)),
+        ],
+        pl.BlockSpec((tile, columns), lambda step: (step, 0)),
+        jax.ShapeDtypeStruct((width, columns), BF16),
+        [pltpu.VMEM((rows, columns), BF16)],
+        2 * rows * columns * width,
+        2 * (rows * width + width * columns + rows * columns),
+        latent_grad,
+        through,
+        slope,
+        tokens,
+    )
+
+
+def decode_kernel(latent, w_dec1, w_dec2, w_patch, normed, embedded, slope, pixels):
+    step = pl.program_id(0)
+    act, rate = silu_and_slope(matmul(latent[...], w_dec1[...]))
+    slope[...] = rate[: slope.shape[0]]
+    part = matmul(act.astype(BF16), w_dec2[...])
+
+    @pl.when(step == 0)
+    def _():
+        pixels[...] = part
+
+    @pl.when(step > 0)
+    def _():
+        pixels[...] += part
+
+    @pl.when(step == pl.num_programs(0) - 1)
+    def _():
+        patches = matmul(pixels[...].astype(BF16), w_patch[...])
+        normed[...] = layer_norm(patches).astype(BF16)
+        embedded[...] = patches[: embedded.shape[0]]
+
+
+def decode(latent, w_dec1, w_dec2, w_patch, mine):
+    rows, lat = latent.shape
+    deep, pix = w_dec2.shape
+    width = w_patch.shape[1]
+    tile = min(512, deep)
+    return call(
+        decode_kernel,
+        deep // tile,
+        [
+            whole(latent),
+            pl.BlockSpec((lat, tile), lambda step: (0, step)),
+            pl.BlockSpec((tile, pix), lambda step: (step, 0)),
+            whole(w_patch),
+        ],
+        [
+            pl.BlockSpec((rows, width), lambda step: (0, 0)),
+            pl.BlockSpec((mine, width), lambda step: (0, 0)),
+            pl.BlockSpec((mine, tile), lambda step: (0, step)),
+        ],
+        [
+            jax.ShapeDtypeStruct((rows, width), BF16),
+            jax.ShapeDtypeStruct((mine, width), F32),
+            jax.ShapeDtypeStruct((mine, deep), F32),
+        ],
+        [pltpu.VMEM((rows, pix), F32)],
+        2 * rows * (lat * deep + deep * pix + pix * width),
+        2 * (deep * pix + pix * width),
+        latent,
+        w_dec1,
+        w_dec2,
+        w_patch,
+    )
+
+
+def reward_forward_kernel(normed, v1a, v1b, v2a, v2b, slope_a, slope_b, out, total):
+    step = pl.program_id(0)
+    part = 0.0
+    for v1, v2, slope in ((v1a, v2a, slope_a), (v1b, v2b, slope_b)):
+        act, rate = gelu_and_slope(matmul(normed[...], v1[...]))
+        slope[...] = rate
+        part = part + matmul(act.astype(BF16), v2[...])
+
+    @pl.when(step == 0)
+    def _():
+        total[...] = part
+
+    @pl.when(step > 0)
+    def _():
+        total[...] += part
+
+    @pl.when(step == pl.num_programs(0) - 1)
+    def _():
+        out[...] = total[...].astype(BF16)
+
+
+def reward_backward_kernel(grad, v1a, v1b, v2a, v2b, slope_a, slope_b, out, total):
+    step = pl.program_id(0)
+    part = 0.0
+    for v1, v2, slope in ((v1a, v2a, slope_a), (v1b, v2b, slope_b)):
+        back = (slope[...] * matmul_nt(grad[...], v2[...])).astype(BF16)
+        part = part + matmul_nt(back, v1[...])
+
+    @pl.when(step == 0)
+    def _():
+        total[...] = part
+
+    @pl.when(step > 0)
+    def _():
+        total[...] += part
+
+    @pl.when(step == pl.num_programs(0) - 1)
+    def _():
+        out[...] = total[...].astype(BF16)
+
+
+def reward(values, v1_both, v2_both, slopes=None):
+    rows, width = values.shape
+    hidden = v1_both[0].shape[1]
+    tile = min(128, hidden)
+    slope_spec = pl.BlockSpec((rows, tile), lambda step: (0, step))
+    slope_shape = jax.ShapeDtypeStruct((rows, hidden), F32)
+    out_spec = pl.BlockSpec((rows, width), lambda step: (0, 0))
+    out_shape = jax.ShapeDtypeStruct((rows, width), BF16)
+    v1_spec = pl.BlockSpec((width, tile), lambda step: (0, step))
+    v2_spec = pl.BlockSpec((tile, width), lambda step: (step, 0))
+    weight_specs = [whole(values), v1_spec, v1_spec, v2_spec, v2_spec]
+    forward = slopes is None
+    return call(
+        reward_forward_kernel if forward else reward_backward_kernel,
+        hidden // tile,
+        weight_specs + ([] if forward else [slope_spec] * 2),
+        [slope_spec] * 2 + [out_spec] if forward else out_spec,
+        [slope_shape] * 2 + [out_shape] if forward else out_shape,
+        [pltpu.VMEM((rows, width), F32)],
+        8 * rows * width * hidden,
+        8 * width * hidden,
+        values,
+        *v1_both,
+        *v2_both,
+        *(() if forward else slopes),
+    )
 
 
 def on_device(
@@ -100,20 +327,23 @@
     my_image = lax.axis_index(IMAGE)
     my_slot = reward_slot[my_image]
 
+    strips = jnp.moveaxis(w_out_t.reshape(d_dev, n_rows, strip), 1, 0)
+    steps_row = jnp.broadcast_to(timestep[0].astype(BF16), (n_rows, 8, strip))
+    strips = jnp.concatenate([strips, steps_row], axis=1)
     split_in = jnp.moveaxis(w_in.reshape(d_dev, n_near, half), 1, 0)
     split_in = jnp.broadcast_to(split_in[:, None], (n_near, n_images, d_dev, half))
-    full_in = exchanged(split_in.reshape(n_rows, d_dev, half), ROWS_AT).reshape(width_d, half)
+    split_in = split_in.reshape(n_rows, d_dev, half)
+    strips, split_in = lax.optimization_barrier((strips, split_in))
+    arrived = exchanged(strips, ROWS_AT)
+    arrived, split_in, noise_rows = lax.optimization_barrier((arrived, split_in, latent_noise[0]))
+    full_in = exchanged(split_in, ROWS_AT).reshape(width_d, half)
 
     modulate = modulation[timestep[0]]
-    noise_rows = latent_noise[0]
     modulated = (
         layer_norm(noise_rows.astype(F32)) * (1.0 + modulate[1]) + modulate[0]
     ).astype(BF16)
     token_rows = lax.all_gather(modulated, ("y", "core"), axis=0, tiled=True)
 
-    strips = jnp.moveaxis(w_out_t.reshape(d_dev, n_rows, strip), 1, 0)
-    steps_row = jnp.broadcast_to(timestep[0].astype(BF16), (n_rows, 8, strip))
-    arrived = exchanged(jnp.concatenate([strips, steps_row], axis=1), ROWS_AT)
     strip_rows = arrived[:, :d_dev].reshape(width_d, strip)
     all_steps = arrived[:n_images, d_dev, 0].astype(jnp.int32)
     gates = modulation[all_steps, 2]
@@ -121,21 +351,23 @@
     gated_final = gated_final.reshape(width_d, n_images * lat)
     through = matmul_tn(strip_rows, gated_final).astype(BF16)
     through = jnp.moveaxis(through.reshape(strip, n_images, lat), 1, 0)
-    through, full_in = lax.optimization_barrier((through, full_in))
-    through = exchanged(through, IMAGE).reshape(half, lat)
+    turns = by_turns(through, IMAGE)
+    through = jnp.zeros_like(through)
+    for step, block in enumerate(turns):
+        owner = (my_image - step) % n_images
+        through = lax.dynamic_update_slice_in_dim(through, block, owner, 0)
+    through = through.reshape(half, lat)
 
     v1_both = (w_v1, turned(w_v1, "core", 1))
     v2_both = (w_v2, turned(w_v2, "core", 1))
     my_target = lax.dynamic_slice_in_dim(target[0], near * mine, mine, 0)
 
-    pre_act = matmul(token_rows, full_in)
-    hidden, hidden_slope = with_slope(gelu_tanh, pre_act)
-    hidden = hidden.astype(BF16)
+    hidden, hidden_slope, latent_part = block_forward(token_rows, full_in, through)
     n_mp = n_y * n_core
     own_part = matmul(noise_rows, w_final).reshape(1, n_near, mine, lat)
     here = (lax.iota(jnp.int32, n_mp) == lax.axis_index(("y", "core")))[:, None]
     here = here & (lax.iota(jnp.int32, n_near) == near)[None]
-    latent_part = matmul(hidden, through).reshape(n_mp, n_near, mine, lat)
+    latent_part = latent_part.reshape(n_mp, n_near, mine, lat)
     latent_part = (latent_part + jnp.where(here[:, :, None, None], own_part, 0.0)).astype(BF16)
     my_target, latent_part = lax.optimization_barrier((my_target, latent_part))
     latent_part = latent_part.reshape(n_y, n_core, n_near, mine, lat).transpose(2, 1, 0, 3, 4)
@@ -152,28 +384,13 @@
         ]
     )
 
-    dec_pre = matmul(latent, w_dec1)
-    dec_act, dec_slope = with_slope(jax.nn.silu, dec_pre)
-    pixels = matmul(dec_act.astype(BF16), w_dec2).astype(BF16)
-    embedded = matmul(pixels, w_patch)
-    patch_rows = layer_norm(embedded).astype(BF16)
-    embedded = embedded[:mine]
-    dec_slope = dec_slope[:mine]
-
-    slopes = []
-    vit_part = 0.0
-    for v1, v2 in zip(v1_both, v2_both):
-        act, slope = with_slope(gelu_tanh, matmul(patch_rows, v1))
-        slopes.append(slope)
-        vit_part = vit_part + matmul(act.astype(BF16), v2)
+    patch_rows, embedded, dec_slope = decode(latent, w_dec1, w_dec2, w_patch, mine)
+    *slopes, vit_part = reward(patch_rows, v1_both, v2_both)
     vit_out = summed_back(jnp.split(vit_part, n_y), "y")
     feature_grad = ((embedded + vit_out - goal) * scale).astype(BF16)
 
     grad_rows = jnp.concatenate(from_all(feature_grad, "y"))
-    norm_part = 0.0
-    for v1, v2, slope in zip(v1_both, v2_both, slopes):
-        vit_pre_grad = (slope * matmul_nt(grad_rows, v2)).astype(BF16)
-        norm_part = norm_part + matmul_nt(vit_pre_grad, v1)
+    norm_part = reward(grad_rows, v1_both, v2_both, slopes)
     norm_grad = summed_back(jnp.split(norm_part, n_y), "y")
     embed_grad = (feature_grad.astype(F32) + norm_back(embedded, norm_grad)).astype(BF16)
     pixel_grad = matmul_nt(embed_grad, w_patch).astype(BF16)
@@ -184,17 +401,28 @@
     latent_rows = exchanged(spread, TOKENS_AT).reshape(n_near, n_y * n_core, mine, lat)
     latent_rows = jnp.moveaxis(latent_rows, 0, 1).reshape(rows, lat)
 
-    pre_grad = (hidden_slope * matmul_nt(latent_rows, through)).astype(BF16)
-    term_in = matmul_tn(token_rows, pre_grad).astype(BF16)
+    term_in = block_backward(latent_rows, through, hidden_slope, token_rows)
+    term_in, latent_rows = lax.optimization_barrier((term_in, latent_rows))
     terms = exchanged(term_in.reshape(n_rows, d_dev, half), ROWS_AT)
+
+    inner = matmul_tn(latent_rows, hidden).astype(BF16)
+    inner = by_turns(jnp.moveaxis(inner.reshape(lat, n_images, strip), 1, 0), IMAGE)
+    inner = jnp.concatenate(inner).reshape(n_images * lat, strip)
+    turned_gates = jnp.concatenate(
+        [
+            lax.dynamic_slice_in_dim(gates, (my_image - step) % n_images, 1, 0)
+            for step in range(n_images)
+        ]
+    )
+    turned_final = (turned_gates.T[:, :, None] * w_final.astype(F32)[:, None, :]).astype(BF16)
+    turned_final = turned_final.reshape(width_d, n_images * lat)
+    out_strip = matmul(turned_final, inner).astype(BF16)
+    out_strip, terms = lax.optimization_barrier((out_strip, terms))
+    out_strips = exchanged(out_strip.reshape(n_rows, d_dev, strip), ROWS_AT)
+    grad_out_t = jnp.moveaxis(out_strips, 0, 1).reshape(d_dev, ff_mp).astype(F32)
+
     grad_in = jnp.sum(terms.reshape(n_near, n_images, d_dev, half).astype(F32), axis=1)
     grad_in = jnp.moveaxis(grad_in, 0, 1).reshape(d_dev, ff_mp)
-
-    inner = matmul_tn(latent_rows, hidden).astype(BF16)
-    inner = exchanged(jnp.moveaxis(inner.reshape(lat, n_images, strip), 1, 0), IMAGE)
-    out_strip = matmul(gated_final, inner.reshape(n_images * lat, strip)).astype(BF16)
-    out_strips = exchanged(out_strip.reshape(n_rows, d_dev, strip), ROWS_AT)
-    grad_out_t = jnp.moveaxis(out_strips, 0, 1).reshape(d_dev, ff_mp).astype(F32)
     return (grad_in, grad_out_t)
 
 

time: 327 us -> 318 us (0.972)
  matrix products: 52.1 us -> 8.67 us
  Pallas kernels: 0 us -> 38.3 us
  starting transfers between devices: 64.7 us -> 87.2 us
  local copies, waits for them, and re-layouts: 45.6 us -> 35.7 us
  waiting for transfers between devices: 113 us -> 106 us
  other arithmetic: 19.5 us -> 13 us
    all_to_all x8 -> x6, waiting for transfers between devices: 104 us -> 26.5 us  [exchanged(): return lax.all_to_all(blocks, axis, 0, 0, tiled=True)]
    ppermute x11 -> x25, waiting for transfers between devices: 8.78 us -> 79.7 us  [turned(): lax.ppermute(value, axis, [(at, (at + steps) % count) for at in range(cou...]
    pallas_call x0 -> x5, Pallas kernels: none -> 38.3 us  [call(): pl.pallas_call(kernel, grid=(grid,), in_specs=in_specs, out_specs=out_spe...]
    ppermute x11 -> x25, starting transfers between devices: 18.6 us -> 47.5 us  [turned(): lax.ppermute(value, axis, [(at, (at + steps) % count) for at in range(cou...]
    dot_general x10 -> x2, matrix products: 28.8 us -> 2.68 us  [matmul(): return jnp.dot(left, right, preferred_element_type=F32)]
    dot_general x4 -> x2, matrix products: 12.8 us -> 2.99 us  [matmul_nt(): lax.dot_general(left, right, (((1,), (1,)), ((), ())), preferred_element_...]
    convert_element_type x2 -> x0, local copies, waits for them, and re-layouts: 7.74 us -> none  [the longest x1 5.51 us: on_device(): term_in = matmul_tn(token_rows, pre_grad).astype(BF16)]
    dot_general x3 -> x2, matrix products: 10.5 us -> 3.01 us  [matmul_tn(): lax.dot_general(left, right, (((0,), (0,)), ((), ())), preferred_element_...]
  transfers between devices with their start and end apart: 20 -> 32, of which waited for: 12 -> 16; matrix products, arithmetic and copies ran while one was open for 19% -> 11% of each run, Pallas kernels for 0% -> 7%
where the time goes in v3:
time: 318 us; the launch traced here: 316 us
  waiting for transfers between devices  106 us (33%)
  starting transfers between devices  87.2 us (27%)
  Pallas kernels  38.3 us (12%)
  local copies, waits for them, and re-layouts  35.7 us (11%)
  between operations  17.2 us (5%)
  other arithmetic  13 us (4%)
  blocking collectives  10.3 us (3%)
  matrix products  8.67 us (3%)
    ppermute x25, waiting for transfers between devices, turned(): lax.ppermute(value, axis, [(at, (at + steps) % count) for at in range(cou...  79.7 us
    ppermute x25, starting transfers between devices, turned(): lax.ppermute(value, axis, [(at, (at + steps) % count) for at in range(cou...  47.5 us
    all_to_all x6, starting transfers between devices, exchanged(): return lax.all_to_all(blocks, axis, 0, 0, tiled=True)  39.6 us
    pallas_call x5, Pallas kernels, call(): pl.pallas_call(kernel, grid=(grid,), in_specs=in_specs, out_specs=out_spe...  38.3 us
    all_to_all x6, waiting for transfers between devices, exchanged(): return lax.all_to_all(blocks, axis, 0, 0, tiled=True)  26.5 us
    all_to_all x1, blocking collectives, exchanged(): return lax.all_to_all(blocks, axis, 0, 0, tiled=True)  10.3 us
  transfers between devices with their start and end apart: 32, of which 16 were waited for; matrix products, arithmetic and copies ran while one was open for 11% of the time, Pallas kernels for 7%

profile of v3, /device:TPU:8, one launch (start us, length us, event | category | flops | bytes accessed | tf_op | source)
XLA Modules:
  0.0 316.5 jit_solution(15665810856900731783)
XLA Ops:
  15.1 7.9 %all-to-all-start = ((bf16[16,160,76]{1,2,0:T(8,128)(2,1)}), bf16[16,160,76]{1,2,0:T(8,128)(2,1)S(1)}, u32[]{:S(2)}, u32[]{:S(2)}) async-start(bf16[16,160,76]{1,2,0:T(8,128)(2,1)} %copy.97), calls=%async_computation | async-start | bytes 1310720 | tf_op jit(solution)/shard_map/all_to_all | solution.py:88
  24.0 11.3 %all-to-all-done = bf16[16,160,76]{1,2,0:T(8,128)(2,1)S(1)} async-done(((bf16[16,160,76]{1,2,0:T(8,128)(2,1)}), bf16[16,160,76]{1,2,0:T(8,128)(2,1)S(1)}, u32[]{:S(2)}, u32[]{:S(2)}) %all-to-all-start) | async-done | bytes 389152 | tf_op jit(solution)/shard_map/all_to_all | solution.py:88
  36.9 4.6 %all-to-all-start.1 = ((bf16[16,152,608]{2,1,0:T(8,128)(2,1)}), bf16[16,152,608]{2,1,0:T(8,128)(2,1)}, u32[]{:S(2)}, u32[]{:S(2)}) async-start(bf16[16,152,608]{2,1,0:T(8,128)(2,1)} %bitcast.3), calls=%async_computation.1 | async-start | bytes 6225920 | tf_op jit(solution)/shard_map/all_to_all | solution.py:88
  50.6 3.4 %collective-permute-start.3 = (bf16[1,76,64]{2,0,1:T(2,128)(2,1)S(1)}, bf16[1,76,64]{2,0,1:T(2,128)(2,1)S(1)}, u32[]{:S(2)}, u32[]{:S(2)}) collective-permute-start(bf16[1,76,64]{2,0,1:T(2,128)(2,1)S(1)} %get-tuple-element.61), channel_id=1, source_target_pairs={{0,32},{8,40},{16,48},{24,56},{32,0},{40,8},{48,16},{56,24},{1,33}... | collective-permute-start | bytes 29192 | tf_op jit(solution)/shard_map/ppermute | solution.py:61
  53.9 3.0 collective-permute-start.2
  56.9 26.8 %collective-permute-done.3 = bf16[1,76,64]{2,0,1:T(2,128)(2,1)S(1)} collective-permute-done((bf16[1,76,64]{2,0,1:T(2,128)(2,1)S(1)}, bf16[1,76,64]{2,0,1:T(2,128)(2,1)S(1)}, u32[]{:S(2)}, u32[]{:S(2)}) %collective-permute-start.3) | collective-permute-done | bytes 9760 | tf_op jit(solution)/shard_map/ppermute | solution.py:61
  85.8 4.0 %collective-permute-done.2 = bf16[1,76,64]{2,0,1:T(2,128)(2,1)S(1)} collective-permute-done((bf16[1,76,64]{2,0,1:T(2,128)(2,1)S(1)}, bf16[1,76,64]{2,0,1:T(2,128)(2,1)S(1)}, u32[]{:S(2)}, u32[]{:S(2)}) %collective-permute-start.2) | collective-permute-done | bytes 9760 | tf_op jit(solution)/shard_map/ppermute | solution.py:61
  94.7 3.3 %collective-permute-done.4 = bf16[1,76,64]{2,0,1:T(2,128)(2,1)S(1)} collective-permute-done((bf16[1,76,64]{2,0,1:T(2,128)(2,1)S(1)}, bf16[1,76,64]{2,0,1:T(2,128)(2,1)S(1)}, u32[]{:S(2)}, u32[]{:S(2)}) %collective-permute-start.4) | collective-permute-done | bytes 9760 | tf_op jit(solution)/shard_map/ppermute | solution.py:61
  99.9 7.7 %shard_map.140 = (bf16[768,608]{1,0:T(8,128)(2,1)}, bf16[768,608]{1,0:T(8,128)(2,1)}, f32[768,64]{1,0:T(8,128)}) custom-call(bf16[768,2432]{1,0:T(8,128)(2,1)} %all-gather.2.cloned.1.call-done.tokens, bf16[2432,608]{1,0:T(8,128)(2,1)} %bitcast.8.weights, bf16[608,64]{1,0:T(8,128)(2,1)} %copy.107.through), custom_call_target="tpu_custom_call" | custom-call | flops 2271215616 | bytes 8560640 | tf_op jit(solution)/shard_map/pallas_call | solution.py:96
  110.1 6.6 %all-to-all-start.2 = ((bf16[16,192,64]{1,2,0:T(8,128)(2,1)}), bf16[16,192,64]{1,2,0:T(8,128)(2,1)S(1)}, u32[]{:S(2)}, u32[]{:S(2)}) async-start(bf16[16,192,64]{1,2,0:T(8,128)(2,1)} %copy.110), calls=%async_computation.2 | async-start | bytes 1048576 | tf_op jit(solution)/shard_map/all_to_all | solution.py:88
  116.7 7.4 %all-to-all-done.2 = bf16[16,192,64]{1,2,0:T(8,128)(2,1)S(1)} async-done(((bf16[16,192,64]{1,2,0:T(8,128)(2,1)}), bf16[16,192,64]{1,2,0:T(8,128)(2,1)S(1)}, u32[]{:S(2)}, u32[]{:S(2)}) %all-to-all-start.2) | async-done | bytes 393248 | tf_op jit(solution)/shard_map/all_to_all | solution.py:88
  125.1 6.2 %all-to-all-start.3 = ((bf16[8,48,1280]{2,1,0:T(8,128)(2,1)}), bf16[8,48,1280]{2,1,0:T(8,128)(2,1)}, u32[]{:S(2)}, u32[]{:S(2)}) async-start(bf16[8,48,1280]{2,1,0:T(8,128)(2,1)} %broadcast_in_dim.70), calls=%async_computation.3 | async-start | bytes 1966080 | tf_op jit(solution)/shard_map/all_to_all | solution.py:88
  132.5 6.4 %shard_map.141 = (bf16[192,1280]{1,0:T(8,128)(2,1)}, f32[48,1280]{1,0:T(8,128)}, f32[48,2048]{1,0:T(8,128)}) custom-call(bf16[192,64]{1,0:T(8,128)(2,1)} %pad_maximum_fusion.1.latent, bf16[64,2048]{1,0:T(8,128)(2,1)} %w_dec1.1, bf16[2048,768]{1,0:T(8,128)(2,1)} %w_dec2.1, bf16[768,1280]{1,0:T(8,128)(2,1)} %w_patch.1), custom_call_target="tpu_custom_call" | custom-call | flops 1031798784 | bytes 5111808 | tf_op jit(solution)/shard_map/pallas_call | solution.py:96
  139.0 8.4 %shard_map.142 = (f32[192,640]{1,0:T(8,128)}, f32[192,640]{1,0:T(8,128)}, bf16[192,1280]{1,0:T(8,128)(2,1)}) custom-call(bf16[192,1280]{1,0:T(8,128)(2,1)} %get-tuple-element.31.normed, bf16[1280,640]{1,0:T(8,128)(2,1)} %v1a.3, bf16[1280,640]{1,0:T(8,128)(2,1)} %collective-permute-done.7.v1b, bf16[640,1280]{1,0:T(8,128)(2,1)} %v2a.3, ...), custom_call_target="tpu_custom_call" | custom-call | flops 1258291200 | bytes 6553600 | tf_op jit(solution)/shard_map/pallas_call | solution.py:96
  148.5 3.6 %collective-permute-start.9 = (bf16[48,1280]{1,0:T(8,128)(2,1)S(1)}, bf16[48,1280]{1,0:T(8,128)(2,1)S(1)}, u32[]{:S(2)}, u32[]{:S(2)}) collective-permute-start(bf16[48,1280]{1,0:T(8,128)(2,1)S(1)} %get-tuple-element.53), channel_id=1, source_target_pairs={{0,6},{2,0},{4,2},{6,4},{1,7},{3,1},{5,3},{7,5},{8,14},{10,8},{12,... | collective-permute-start | bytes 368648 | tf_op jit(solution)/shard_map/ppermute | solution.py:61
  152.1 3.0 collective-permute-start.10
  159.6 3.5 %collective-permute-start.14 = (bf16[48,1280]{1,0:T(8,128)(2,1)S(1)}, bf16[48,1280]{1,0:T(8,128)(2,1)S(1)}, u32[]{:S(2)}, u32[]{:S(2)}) collective-permute-start(bf16[48,1280]{1,0:T(8,128)(2,1)S(1)} %get-tuple-element.56), channel_id=1, source_target_pairs={{0,6},{2,0},{4,2},{6,4},{1,7},{3,1},{5,3},{7,5},{8,14},{10,8},{12,... | collective-permute-start | bytes 368648 | tf_op jit(solution)/shard_map/ppermute | solution.py:61
  166.5 3.0 collective-permute-done.13
  170.3 8.4 %shard_map.143 = bf16[192,1280]{1,0:T(8,128)(2,1)} custom-call(bf16[192,1280]{1,0:T(8,128)(2,1)} %pad_maximum_fusion.grad, bf16[1280,640]{1,0:T(8,128)(2,1)} %v1a.3, bf16[1280,640]{1,0:T(8,128)(2,1)} %collective-permute-done.7.v1b, bf16[640,1280]{1,0:T(8,128)(2,1)} %v2a.3, bf16[640,1280]{1,0:T(8,128)(2,1)} %collective-permute-done.8.v2b, ...), custom_call_target="tpu_custom_call" | custom-call | flops 1258291200 | bytes 6553600 | tf_op jit(solution)/shard_map/pallas_call | solution.py:96
  179.9 2.5 collective-permute-start.15
  182.3 3.3 %collective-permute-start.16 = (bf16[48,1280]{1,0:T(8,128)(2,1)S(1)}, bf16[48,1280]{1,0:T(8,128)(2,1)S(1)}, u32[]{:S(2)}, u32[]{:S(2)}) collective-permute-start(bf16[48,1280]{1,0:T(8,128)(2,1)S(1)} %get-tuple-element.52), channel_id=1, source_target_pairs={{0,4},{2,6},{4,0},{6,2},{1,5},{3,7},{5,1},{7,3},{8,12},{10,14},{12... | collective-permute-start | bytes 368648 | tf_op jit(solution)/shard_map/ppermute | solution.py:61
  194.2 10.3 %all_to_all.35 = bf16[16,2,1536]{2,1,0:T(2,128)(2,1)S(1)} all-to-all(bf16[16,2,1536]{2,1,0:T(2,128)(2,1)S(1)} %reshape.216), channel_id=1, replica_groups=mesh['near'=2,'z'=4,'far'=2,'y'=4,'core'=2] {'near','y','core'}, dimensions={0} | all-to-all | bytes 196608 | tf_op jit(solution)/shard_map/all_to_all | solution.py:88
  205.4 7.4 %shard_map.144 = bf16[2432,608]{1,0:T(8,128)(2,1)} custom-call(bf16[768,64]{1,0:T(8,128)(2,1)} %bitcast.79, bf16[608,64]{1,0:T(8,128)(2,1)} %copy.107.through, bf16[768,608]{1,0:T(8,128)(2,1)} %get-tuple-element.36.slope, bf16[768,2432]{1,0:T(8,128)(2,1)} %all-gather.2.cloned.1.call-done.tokens), custom_call_target="tpu_custom_call" | custom-call | flops 2271215616 | bytes 7626752 | tf_op jit(solution)/shard_map/pallas_call | solution.py:96
  212.8 7.0 %all-to-all-start.5 = ((bf16[16,152,608]{2,1,0:T(8,128)(2,1)}), bf16[16,152,608]{2,1,0:T(8,128)(2,1)S(1)}, u32[]{:S(2)}, u32[]{:S(2)}) async-start(bf16[16,152,608]{2,1,0:T(8,128)(2,1)} %bitcast.72), calls=%async_computation.5 | async-start | bytes 6225920 | tf_op jit(solution)/shard_map/all_to_all | solution.py:88
  223.7 3.4 %collective-permute-start.18 = (bf16[1,64,76]{2,1,0:T(8,128)(2,1)}, bf16[1,64,76]{2,1,0:T(8,128)(2,1)}, u32[]{:S(2)}, u32[]{:S(2)}) collective-permute-start(bf16[1,64,76]{2,1,0:T(8,128)(2,1)} %get-tuple-element.72), channel_id=1, source_target_pairs={{0,8},{8,16},{16,24},{24,32},{32,40},{40,48},{48,56},{56,0},{1,9},... | collective-permute-start | bytes 29192 | tf_op jit(solution)/shard_map/ppermute | solution.py:61
  235.1 2.7 collective-permute-start.21
  237.8 30.9 %collective-permute-done.18 = bf16[1,64,76]{2,1,0:T(8,128)(2,1)} collective-permute-done((bf16[1,64,76]{2,1,0:T(8,128)(2,1)}, bf16[1,64,76]{2,1,0:T(8,128)(2,1)}, u32[]{:S(2)}, u32[]{:S(2)}) %collective-permute-start.18) | collective-permute-done | bytes 9760 | tf_op jit(solution)/shard_map/ppermute | solution.py:61
  268.7 3.2 %collective-permute-start.19 = (bf16[1,64,76]{2,1,0:T(8,128)(2,1)}, bf16[1,64,76]{2,1,0:T(8,128)(2,1)S(1)}, u32[]{:S(2)}, u32[]{:S(2)}) collective-permute-start(bf16[1,64,76]{2,1,0:T(8,128)(2,1)} %get-tuple-element.71), channel_id=1, source_target_pairs={{0,16},{8,24},{16,32},{24,40},{32,48},{40,56},{48,0},{56,8},{1,17}... | collective-permute-start | bytes 29192 | tf_op jit(solution)/shard_map/ppermute | solution.py:61
  276.9 4.9 %collective-permute-done.20 = bf16[1,64,76]{2,1,0:T(8,128)(2,1)S(1)} collective-permute-done((bf16[1,64,76]{2,1,0:T(8,128)(2,1)}, bf16[1,64,76]{2,1,0:T(8,128)(2,1)S(1)}, u32[]{:S(2)}, u32[]{:S(2)}) %collective-permute-start.20) | collective-permute-done | bytes 9760 | tf_op jit(solution)/shard_map/ppermute | solution.py:61
  284.8 2.4 fusion
  289.3 7.4 %all-to-all-start.6 = ((bf16[16,152,76]{2,1,0:T(8,128)(2,1)}), bf16[16,152,76]{2,1,0:T(8,128)(2,1)}, u32[]{:S(2)}, u32[]{:S(2)}) async-start(bf16[16,152,76]{2,1,0:T(8,128)(2,1)} %bitcast.75), calls=%async_computation.6 | async-start | bytes 1245184 | tf_op jit(solution)/shard_map/all_to_all | solution.py:88
  299.0 7.8 %all-to-all-done.6 = bf16[16,152,76]{2,1,0:T(8,128)(2,1)} async-done(((bf16[16,152,76]{2,1,0:T(8,128)(2,1)}), bf16[16,152,76]{2,1,0:T(8,128)(2,1)}, u32[]{:S(2)}, u32[]{:S(2)}) %all-to-all-start.6) | async-done | bytes 369696 | tf_op jit(solution)/shard_map/all_to_all | solution.py:88
  (156 shorter events, 77.8 us)
Async XLA Ops:
  15.1 20.2 %all-to-all-start = ((bf16[16,160,76]{1,2,0:T(8,128)(2,1)}), bf16[16,160,76]{1,2,0:T(8,128)(2,1)S(1)}, u32[]{:S(2)}, u32[]{:S(2)}) async-start(bf16[16,160,76]{1,2,0:T(8,128)(2,1)} %copy.97), calls=%async_computation | async-start | bytes 1310720 | tf_op jit(solution)/shard_map/all_to_all | solution.py:88
  23.0 77.0 %all-gather.2.cloned.1.call-start = ((), (), s32[]{:S(2)}) async-start(), calls=%async_computation.7 | async-start | bytes 4202496 | tf_op jit(solution)/shard_map/all_gather | solution.py:345
  36.9 63.0 %all-to-all-start.1 = ((bf16[16,152,608]{2,1,0:T(8,128)(2,1)}), bf16[16,152,608]{2,1,0:T(8,128)(2,1)}, u32[]{:S(2)}, u32[]{:S(2)}) async-start(bf16[16,152,608]{2,1,0:T(8,128)(2,1)} %bitcast.3), calls=%async_computation.1 | async-start | bytes 6225920 | tf_op jit(solution)/shard_map/all_to_all | solution.py:88
  41.5 97.4 %collective-permute-start.7 = (bf16[1280,640]{1,0:T(8,128)(2,1)S(1)}, bf16[1280,640]{1,0:T(8,128)(2,1)}, u32[]{:S(2)}, u32[]{:S(2)}) collective-permute-start(bf16[1280,640]{1,0:T(8,128)(2,1)S(1)} %copy-done.4), channel_id=1, source_target_pairs={{0,1},{1,0},{2,3},{3,2},{4,5},{5,4},{6,7},{7,6},{8,9},{9,8},{10,11... | collective-permute-start | bytes 4915208 | tf_op jit(solution)/shard_map/ppermute | solution.py:61
  41.6 97.4 %collective-permute-start.8 = (bf16[640,1280]{1,0:T(8,128)(2,1)}, bf16[640,1280]{1,0:T(8,128)(2,1)}, u32[]{:S(2)}, u32[]{:S(2)}) collective-permute-start(bf16[640,1280]{1,0:T(8,128)(2,1)} %v2a.3), channel_id=1, source_target_pairs={{0,1},{1,0},{2,3},{3,2},{4,5},{5,4},{6,7},{7,6},{8,9},{9,8},{10,11... | collective-permute-start | bytes 4915208 | tf_op jit(solution)/shard_map/ppermute | solution.py:61
  50.6 33.1 %collective-permute-start.3 = (bf16[1,76,64]{2,0,1:T(2,128)(2,1)S(1)}, bf16[1,76,64]{2,0,1:T(2,128)(2,1)S(1)}, u32[]{:S(2)}, u32[]{:S(2)}) collective-permute-start(bf16[1,76,64]{2,0,1:T(2,128)(2,1)S(1)} %get-tuple-element.61), channel_id=1, source_target_pairs={{0,32},{8,40},{16,48},{24,56},{32,0},{40,8},{48,16},{56,24},{1,33}... | collective-permute-start | bytes 29192 | tf_op jit(solution)/shard_map/ppermute | solution.py:61
  53.9 35.9 %collective-permute-start.2 = (bf16[1,76,64]{2,0,1:T(2,128)(2,1)S(1)}, bf16[1,76,64]{2,0,1:T(2,128)(2,1)S(1)}, u32[]{:S(2)}, u32[]{:S(2)}) collective-permute-start(bf16[1,76,64]{2,0,1:T(2,128)(2,1)S(1)} %get-tuple-element.62), channel_id=1, source_target_pairs={{0,24},{8,32},{16,40},{24,48},{32,56},{40,0},{48,8},{56,16},{1,25}... | collective-permute-start | bytes 29192 | tf_op jit(solution)/shard_map/ppermute | solution.py:61
  56.9 33.0 %collective-permute-start.1 = (bf16[1,76,64]{2,0,1:T(2,128)(2,1)S(1)}, bf16[1,76,64]{2,0,1:T(2,128)(2,1)S(1)}, u32[]{:S(2)}, u32[]{:S(2)}) collective-permute-start(bf16[1,76,64]{2,0,1:T(2,128)(2,1)S(1)} %get-tuple-element.63), channel_id=1, source_target_pairs={{0,16},{8,24},{16,32},{24,40},{32,48},{40,56},{48,0},{56,8},{1,17}... | collective-permute-start | bytes 29192 | tf_op jit(solution)/shard_map/ppermute | solution.py:61
  83.7 7.9 %collective-permute-start = (bf16[1,76,64]{2,0,1:T(2,128)(2,1)S(1)}, bf16[1,76,64]{2,0,1:T(2,128)(2,1)S(1)}, u32[]{:S(2)}, u32[]{:S(2)}) collective-permute-start(bf16[1,76,64]{2,0,1:T(2,128)(2,1)S(1)} %get-tuple-element.64), channel_id=1, source_target_pairs={{0,8},{8,16},{16,24},{24,32},{32,40},{40,48},{48,56},{56,0},{1,9},... | collective-permute-start | bytes 29192 | tf_op jit(solution)/shard_map/ppermute | solution.py:61
  89.8 8.7 %collective-permute-start.6 = (bf16[1,76,64]{2,0,1:T(2,128)(2,1)S(1)}, bf16[1,76,64]{2,0,1:T(2,128)(2,1)S(1)}, u32[]{:S(2)}, u32[]{:S(2)}) collective-permute-start(bf16[1,76,64]{2,0,1:T(2,128)(2,1)S(1)} %get-tuple-element.58), channel_id=1, source_target_pairs={{0,56},{8,0},{16,8},{24,16},{32,24},{40,32},{48,40},{56,48},{1,57}... | collective-permute-start | bytes 29192 | tf_op jit(solution)/shard_map/ppermute | solution.py:61
  89.9 8.4 %collective-permute-start.5 = (bf16[1,76,64]{2,0,1:T(2,128)(2,1)S(1)}, bf16[1,76,64]{2,0,1:T(2,128)(2,1)S(1)}, u32[]{:S(2)}, u32[]{:S(2)}) collective-permute-start(bf16[1,76,64]{2,0,1:T(2,128)(2,1)S(1)} %get-tuple-element.59), channel_id=1, source_target_pairs={{0,48},{8,56},{16,0},{24,8},{32,16},{40,24},{48,32},{56,40},{1,49}... | collective-permute-start | bytes 29192 | tf_op jit(solution)/shard_map/ppermute | solution.py:61
  91.6 6.4 %collective-permute-start.4 = (bf16[1,76,64]{2,0,1:T(2,128)(2,1)S(1)}, bf16[1,76,64]{2,0,1:T(2,128)(2,1)S(1)}, u32[]{:S(2)}, u32[]{:S(2)}) collective-permute-start(bf16[1,76,64]{2,0,1:T(2,128)(2,1)S(1)} %get-tuple-element.60), channel_id=1, source_target_pairs={{0,40},{8,48},{16,56},{24,0},{32,8},{40,16},{48,24},{56,32},{1,41}... | collective-permute-start | bytes 29192 | tf_op jit(solution)/shard_map/ppermute | solution.py:61
  110.1 14.1 %all-to-all-start.2 = ((bf16[16,192,64]{1,2,0:T(8,128)(2,1)}), bf16[16,192,64]{1,2,0:T(8,128)(2,1)S(1)}, u32[]{:S(2)}, u32[]{:S(2)}) async-start(bf16[16,192,64]{1,2,0:T(8,128)(2,1)} %copy.110), calls=%async_computation.2 | async-start | bytes 1048576 | tf_op jit(solution)/shard_map/all_to_all | solution.py:88
  125.1 33.3 %all-to-all-start.3 = ((bf16[8,48,1280]{2,1,0:T(8,128)(2,1)}), bf16[8,48,1280]{2,1,0:T(8,128)(2,1)}, u32[]{:S(2)}, u32[]{:S(2)}) async-start(bf16[8,48,1280]{2,1,0:T(8,128)(2,1)} %broadcast_in_dim.70), calls=%async_computation.3 | async-start | bytes 1966080 | tf_op jit(solution)/shard_map/all_to_all | solution.py:88
  148.5 9.2 %collective-permute-start.9 = (bf16[48,1280]{1,0:T(8,128)(2,1)S(1)}, bf16[48,1280]{1,0:T(8,128)(2,1)S(1)}, u32[]{:S(2)}, u32[]{:S(2)}) collective-permute-start(bf16[48,1280]{1,0:T(8,128)(2,1)S(1)} %get-tuple-element.53), channel_id=1, source_target_pairs={{0,6},{2,0},{4,2},{6,4},{1,7},{3,1},{5,3},{7,5},{8,14},{10,8},{12,... | collective-permute-start | bytes 368648 | tf_op jit(solution)/shard_map/ppermute | solution.py:61
  152.1 5.6 %collective-permute-start.11 = (bf16[48,1280]{1,0:T(8,128)(2,1)S(1)}, bf16[48,1280]{1,0:T(8,128)(2,1)S(1)}, u32[]{:S(2)}, u32[]{:S(2)}) collective-permute-start(bf16[48,1280]{1,0:T(8,128)(2,1)S(1)} %get-tuple-element.54), channel_id=1, source_target_pairs={{0,2},{2,4},{4,6},{6,0},{1,3},{3,5},{5,7},{7,1},{8,10},{10,12},{12... | collective-permute-start | bytes 368648 | tf_op jit(solution)/shard_map/ppermute | solution.py:61
  152.1 6.4 %collective-permute-start.10 = (bf16[48,1280]{1,0:T(8,128)(2,1)S(1)}, bf16[48,1280]{1,0:T(8,128)(2,1)S(1)}, u32[]{:S(2)}, u32[]{:S(2)}) collective-permute-start(bf16[48,1280]{1,0:T(8,128)(2,1)S(1)} %get-tuple-element.55), channel_id=1, source_target_pairs={{0,4},{2,6},{4,0},{6,2},{1,5},{3,7},{5,1},{7,3},{8,12},{10,14},{12... | collective-permute-start | bytes 368648 | tf_op jit(solution)/shard_map/ppermute | solution.py:61
  159.6 6.9 %collective-permute-start.14 = (bf16[48,1280]{1,0:T(8,128)(2,1)S(1)}, bf16[48,1280]{1,0:T(8,128)(2,1)S(1)}, u32[]{:S(2)}, u32[]{:S(2)}) collective-permute-start(bf16[48,1280]{1,0:T(8,128)(2,1)S(1)} %get-tuple-element.56), channel_id=1, source_target_pairs={{0,6},{2,0},{4,2},{6,4},{1,7},{3,1},{5,3},{7,5},{8,14},{10,8},{12,... | collective-permute-start | bytes 368648 | tf_op jit(solution)/shard_map/ppermute | solution.py:61
  163.1 6.4 %collective-permute-start.13 = (bf16[48,1280]{1,0:T(8,128)(2,1)S(1)}, bf16[48,1280]{1,0:T(8,128)(2,1)S(1)}, u32[]{:S(2)}, u32[]{:S(2)}) collective-permute-start(bf16[48,1280]{1,0:T(8,128)(2,1)S(1)} %get-tuple-element.56), channel_id=1, source_target_pairs={{0,4},{2,6},{4,0},{6,2},{1,5},{3,7},{5,1},{7,3},{8,12},{10,14},{12... | collective-permute-start | bytes 368648 | tf_op jit(solution)/shard_map/ppermute | solution.py:61
  163.1 6.4 %collective-permute-start.12 = (bf16[48,1280]{1,0:T(8,128)(2,1)S(1)}, bf16[48,1280]{1,0:T(8,128)(2,1)S(1)}, u32[]{:S(2)}, u32[]{:S(2)}) collective-permute-start(bf16[48,1280]{1,0:T(8,128)(2,1)S(1)} %get-tuple-element.56), channel_id=1, source_target_pairs={{0,2},{2,4},{4,6},{6,0},{1,3},{3,5},{5,7},{7,1},{8,10},{10,12},{12... | collective-permute-start | bytes 368648 | tf_op jit(solution)/shard_map/ppermute | solution.py:61
  179.9 6.1 %collective-permute-start.15 = (bf16[48,1280]{1,0:T(8,128)(2,1)S(1)}, bf16[48,1280]{1,0:T(8,128)(2,1)S(1)}, u32[]{:S(2)}, u32[]{:S(2)}) collective-permute-start(bf16[48,1280]{1,0:T(8,128)(2,1)S(1)} %get-tuple-element.50), channel_id=1, source_target_pairs={{0,6},{2,0},{4,2},{6,4},{1,7},{3,1},{5,3},{7,5},{8,14},{10,8},{12,... | collective-permute-start | bytes 368648 | tf_op jit(solution)/shard_map/ppermute | solution.py:61
  182.3 4.9 %collective-permute-start.17 = (bf16[48,1280]{1,0:T(8,128)(2,1)S(1)}, bf16[48,1280]{1,0:T(8,128)(2,1)S(1)}, u32[]{:S(2)}, u32[]{:S(2)}) collective-permute-start(bf16[48,1280]{1,0:T(8,128)(2,1)S(1)} %get-tuple-element.51), channel_id=1, source_target_pairs={{0,2},{2,4},{4,6},{6,0},{1,3},{3,5},{5,7},{7,1},{8,10},{10,12},{12... | collective-permute-start | bytes 368648 | tf_op jit(solution)/shard_map/ppermute | solution.py:61
  182.3 6.4 %collective-permute-start.16 = (bf16[48,1280]{1,0:T(8,128)(2,1)S(1)}, bf16[48,1280]{1,0:T(8,128)(2,1)S(1)}, u32[]{:S(2)}, u32[]{:S(2)}) collective-permute-start(bf16[48,1280]{1,0:T(8,128)(2,1)S(1)} %get-tuple-element.52), channel_id=1, source_target_pairs={{0,4},{2,6},{4,0},{6,2},{1,5},{3,7},{5,1},{7,3},{8,12},{10,14},{12... | collective-permute-start | bytes 368648 | tf_op jit(solution)/shard_map/ppermute | solution.py:61
  212.8 74.4 %all-to-all-start.5 = ((bf16[16,152,608]{2,1,0:T(8,128)(2,1)}), bf16[16,152,608]{2,1,0:T(8,128)(2,1)S(1)}, u32[]{:S(2)}, u32[]{:S(2)}) async-start(bf16[16,152,608]{2,1,0:T(8,128)(2,1)} %bitcast.72), calls=%async_computation.5 | async-start | bytes 6225920 | tf_op jit(solution)/shard_map/all_to_all | solution.py:88
  223.7 45.0 %collective-permute-start.18 = (bf16[1,64,76]{2,1,0:T(8,128)(2,1)}, bf16[1,64,76]{2,1,0:T(8,128)(2,1)}, u32[]{:S(2)}, u32[]{:S(2)}) collective-permute-start(bf16[1,64,76]{2,1,0:T(8,128)(2,1)} %get-tuple-element.72), channel_id=1, source_target_pairs={{0,8},{8,16},{16,24},{24,32},{32,40},{40,48},{48,56},{56,0},{1,9},... | collective-permute-start | bytes 29192 | tf_op jit(solution)/shard_map/ppermute | solution.py:61
  228.5 55.6 %collective-permute-start.24 = (bf16[1,64,76]{2,1,0:T(8,128)(2,1)S(1)}, bf16[1,64,76]{2,1,0:T(8,128)(2,1)S(1)}, u32[]{:S(2)}, u32[]{:S(2)}) collective-permute-start(bf16[1,64,76]{2,1,0:T(8,128)(2,1)S(1)} %get-tuple-element.66), channel_id=1, source_target_pairs={{0,56},{8,0},{16,8},{24,16},{32,24},{40,32},{48,40},{56,48},{1,57}... | collective-permute-start | bytes 29192 | tf_op jit(solution)/shard_map/ppermute | solution.py:61
  230.8 52.7 %collective-permute-start.23 = (bf16[1,64,76]{2,1,0:T(8,128)(2,1)}, bf16[1,64,76]{2,1,0:T(8,128)(2,1)S(1)}, u32[]{:S(2)}, u32[]{:S(2)}) collective-permute-start(bf16[1,64,76]{2,1,0:T(8,128)(2,1)} %get-tuple-element.67), channel_id=1, source_target_pairs={{0,48},{8,56},{16,0},{24,8},{32,16},{40,24},{48,32},{56,40},{1,49}... | collective-permute-start | bytes 29192 | tf_op jit(solution)/shard_map/ppermute | solution.py:61
  232.7 50.2 %collective-permute-start.22 = (bf16[1,64,76]{2,1,0:T(8,128)(2,1)}, bf16[1,64,76]{2,1,0:T(8,128)(2,1)S(1)}, u32[]{:S(2)}, u32[]{:S(2)}) collective-permute-start(bf16[1,64,76]{2,1,0:T(8,128)(2,1)} %get-tuple-element.68), channel_id=1, source_target_pairs={{0,40},{8,48},{16,56},{24,0},{32,8},{40,16},{48,24},{56,32},{1,41}... | collective-permute-start | bytes 29192 | tf_op jit(solution)/shard_map/ppermute | solution.py:61
  235.1 47.2 %collective-permute-start.21 = (bf16[1,64,76]{2,1,0:T(8,128)(2,1)}, bf16[1,64,76]{2,1,0:T(8,128)(2,1)S(1)}, u32[]{:S(2)}, u32[]{:S(2)}) collective-permute-start(bf16[1,64,76]{2,1,0:T(8,128)(2,1)} %get-tuple-element.69), channel_id=1, source_target_pairs={{0,32},{8,40},{16,48},{24,56},{32,0},{40,8},{48,16},{56,24},{1,33}... | collective-permute-start | bytes 29192 | tf_op jit(solution)/shard_map/ppermute | solution.py:61
  268.7 5.2 %collective-permute-start.19 = (bf16[1,64,76]{2,1,0:T(8,128)(2,1)}, bf16[1,64,76]{2,1,0:T(8,128)(2,1)S(1)}, u32[]{:S(2)}, u32[]{:S(2)}) collective-permute-start(bf16[1,64,76]{2,1,0:T(8,128)(2,1)} %get-tuple-element.71), channel_id=1, source_target_pairs={{0,16},{8,24},{16,32},{24,40},{32,48},{40,56},{48,0},{56,8},{1,17}... | collective-permute-start | bytes 29192 | tf_op jit(solution)/shard_map/ppermute | solution.py:61
  273.9 7.9 %collective-permute-start.20 = (bf16[1,64,76]{2,1,0:T(8,128)(2,1)}, bf16[1,64,76]{2,1,0:T(8,128)(2,1)S(1)}, u32[]{:S(2)}, u32[]{:S(2)}) collective-permute-start(bf16[1,64,76]{2,1,0:T(8,128)(2,1)} %get-tuple-element.70), channel_id=1, source_target_pairs={{0,24},{8,32},{16,40},{24,48},{32,56},{40,0},{48,8},{56,16},{1,25}... | collective-permute-start | bytes 29192 | tf_op jit(solution)/shard_map/ppermute | solution.py:61
  289.3 17.5 %all-to-all-start.6 = ((bf16[16,152,76]{2,1,0:T(8,128)(2,1)}), bf16[16,152,76]{2,1,0:T(8,128)(2,1)}, u32[]{:S(2)}, u32[]{:S(2)}) async-start(bf16[16,152,76]{2,1,0:T(8,128)(2,1)} %bitcast.75), calls=%async_computation.6 | async-start | bytes 1245184 | tf_op jit(solution)/shard_map/all_to_all | solution.py:88
  (11 other events, 168.6 us)
Sparse Core Ops, SparseCore 0:
  37.0 27.1 all-gather.1

commit v4 on v3

--- a/solution.py
+++ b/solution.py
@@ -10,11 +10,13 @@
 
 BF16 = jnp.bfloat16
 GELU_SCALE = math.sqrt(2.0 / math.pi)
-VMEM_BYTES = 56 * 1024 * 1024
+VMEM_BYTES = 24 * 1024 * 1024
 F32 = jnp.float32
 AXES = ("near", "z", "far", "y", "core")
 IMAGE = ("z", "far")
 ROWS_AT = ("near", "z", "far")
+FAR_FIRST = ("far", "near", "z")
+PAIR_ROWS = ("near", "z")
 TOKENS_AT = ("near", "y", "core")
 
 
@@ -71,17 +73,6 @@
     for step in range(1, len(blocks)):
         total = total + turned(blocks[step], axis, -step).astype(F32)
     return total
-
-
-def by_turns(blocks, axis):
-    count = lax.axis_size(axis)
-    here = lax.axis_index(axis)
-    blocks = lax.optimization_barrier(blocks)
-    result = []
-    for step in range(count):
-        block = lax.dynamic_slice_in_dim(blocks, (here + step) % count, 1, 0)
-        result.append(turned(block, axis, step) if step else block)
-    return result
 
 
 def exchanged(blocks, axis):
@@ -105,69 +96,62 @@
     )(*operands)
 
 
-def block_forward_kernel(tokens, weights, through, hidden, slope, latent):
-    act, rate = gelu_and_slope(matmul(tokens[...], weights[...]))
-    act = act.astype(BF16)
-    hidden[...] = act
+def block_forward_kernel(tokens, weights, hidden, slope):
+    total = matmul(tokens[0], weights[0]) + matmul(tokens[1], weights[1])
+    act, rate = gelu_and_slope(total)
+    hidden[...] = act.astype(BF16)
     slope[...] = rate.astype(BF16)
-    latent[...] = matmul(act, through[...])
-
-
-def block_forward(tokens, weights, through):
-    rows, width = tokens.shape
-    columns, lat = through.shape
+
+
+def block_forward(tokens, weights):
+    parts, rows, width = tokens.shape
+    columns = weights.shape[2]
     tile = rows // 4
-    by_rows = lambda last: pl.BlockSpec((tile, last), lambda step: (step, 0))
     return call(
         block_forward_kernel,
         4,
-        [by_rows(width), whole(weights), whole(through)],
-        [by_rows(columns), by_rows(columns), by_rows(lat)],
-        [
-            jax.ShapeDtypeStruct((rows, columns), BF16),
-            jax.ShapeDtypeStruct((rows, columns), BF16),
-            jax.ShapeDtypeStruct((rows, lat), F32),
-        ],
+        [pl.BlockSpec((parts, tile, width), lambda step: (0, step, 0)), whole(weights)],
+        [pl.BlockSpec((tile, columns), lambda step: (step, 0))] * 2,
+        [jax.ShapeDtypeStruct((rows, columns), BF16)] * 2,
         [],
-        2 * rows * columns * width,
-        2 * (rows * width + width * columns + 2 * rows * columns),
+        2 * rows * columns * parts * width,
+        2 * (parts * rows * width + parts * width * columns + 2 * rows * columns),
         tokens,
         weights,
-        through,
-    )
-
-
-def block_backward_kernel(latent_grad, through, slope, tokens, term, pre_grad):
+    )
+
+
+def block_backward_kernel(grads, through, slope, tokens, grads2, through2, slope2, tokens2, term, pre, pre2):
     @pl.when(pl.program_id(0) == 0)
     def _():
-        back = matmul_nt(latent_grad[...], through[...])
-        pre_grad[...] = (slope[...].astype(F32) * back).astype(BF16)
-
-    term[...] = matmul_tn(tokens[...], pre_grad[...]).astype(BF16)
-
-
-def block_backward(latent_grad, through, slope, tokens):
-    rows, width = tokens.shape
-    columns = slope.shape[1]
+        back = matmul_nt(grads[...], through[...])
+        pre[...] = (slope[...].astype(F32) * back).astype(BF16)
+        back = matmul_nt(grads2[...], through2[...])
+        pre2[...] = (slope2[...].astype(F32) * back).astype(BF16)
+
+    total = matmul_tn(tokens[...], pre[...]) + matmul_tn(tokens2[...], pre2[...])
+    term[...] = total.astype(BF16)
+
+
+def block_backward(images):
+    rows, width = images[0][3].shape
+    columns = images[0][2].shape[1]
     tile = min(640, width)
+    cut = pl.BlockSpec((rows, tile), lambda step: (0, step))
+    specs = []
+    for grads, through, slope, _ in images:
+        specs += [whole(grads), whole(through), whole(slope), cut]
     return call(
         block_backward_kernel,
         pl.cdiv(width, tile),
-        [
-            whole(latent_grad),
-            whole(through),
-            whole(slope),
-            pl.BlockSpec((rows, tile), lambda step: (0, step)),
-        ],
+        specs,
         pl.BlockSpec((tile, columns), lambda step: (step, 0)),
         jax.ShapeDtypeStruct((width, columns), BF16),
-        [pltpu.VMEM((rows, columns), BF16)],
-        2 * rows * columns * width,
-        2 * (rows * width + width * columns + rows * columns),
-        latent_grad,
-        through,
-        slope,
-        tokens,
+        [pltpu.VMEM((rows, columns), BF16)] * 2,
+        4 * rows * columns * width,
+        2 * (2 * rows * width + width * columns + 2 * rows * columns),
+        *images[0],
+        *images[1],
     )
 
 
@@ -327,55 +311,61 @@
     my_image = lax.axis_index(IMAGE)
     my_slot = reward_slot[my_image]
 
-    strips = jnp.moveaxis(w_out_t.reshape(d_dev, n_rows, strip), 1, 0)
-    steps_row = jnp.broadcast_to(timestep[0].astype(BF16), (n_rows, 8, strip))
-    strips = jnp.concatenate([strips, steps_row], axis=1)
+    n_z, n_far = lax.axis_size("z"), lax.axis_size("far")
+    far = lax.axis_index("far")
+    wide = width_d // n_far
+
     split_in = jnp.moveaxis(w_in.reshape(d_dev, n_near, half), 1, 0)
-    split_in = jnp.broadcast_to(split_in[:, None], (n_near, n_images, d_dev, half))
+    split_in = jnp.broadcast_to(split_in[None, :, None], (n_far, n_near, n_z, d_dev, half))
     split_in = split_in.reshape(n_rows, d_dev, half)
-    strips, split_in = lax.optimization_barrier((strips, split_in))
-    arrived = exchanged(strips, ROWS_AT)
-    arrived, split_in, noise_rows = lax.optimization_barrier((arrived, split_in, latent_noise[0]))
-    full_in = exchanged(split_in, ROWS_AT).reshape(width_d, half)
+    split_in, noise_rows = lax.optimization_barrier((split_in, latent_noise[0]))
+    full_in = exchanged(split_in, FAR_FIRST).reshape(n_far, wide, half)
 
     modulate = modulation[timestep[0]]
     modulated = (
         layer_norm(noise_rows.astype(F32)) * (1.0 + modulate[1]) + modulate[0]
     ).astype(BF16)
-    token_rows = lax.all_gather(modulated, ("y", "core"), axis=0, tiled=True)
-
+    modulated = modulated.reshape(tok_dev, n_rows // n_far, n_far, d_dev)
+    modulated = jnp.moveaxis(modulated, 2, 0).reshape(n_far, tok_dev, wide)
+    token_rows = lax.all_gather(modulated, ("y", "core"), axis=1, tiled=True)
+
+    strips = jnp.moveaxis(w_out_t.reshape(d_dev, n_rows, strip), 1, 0)
+    steps_row = jnp.broadcast_to(timestep[0].astype(BF16), (n_rows, 8, strip))
+    strips = jnp.concatenate([strips, steps_row], axis=1)
+    strips, full_in = lax.optimization_barrier((strips, full_in))
+    arrived = exchanged(strips, ROWS_AT)
     strip_rows = arrived[:, :d_dev].reshape(width_d, strip)
     all_steps = arrived[:n_images, d_dev, 0].astype(jnp.int32)
     gates = modulation[all_steps, 2]
     gated_final = (gates.T[:, :, None] * w_final.astype(F32)[:, None, :]).astype(BF16)
-    gated_final = gated_final.reshape(width_d, n_images * lat)
-    through = matmul_tn(strip_rows, gated_final).astype(BF16)
-    through = jnp.moveaxis(through.reshape(strip, n_images, lat), 1, 0)
-    turns = by_turns(through, IMAGE)
-    through = jnp.zeros_like(through)
-    for step, block in enumerate(turns):
-        owner = (my_image - step) % n_images
-        through = lax.dynamic_update_slice_in_dim(through, block, owner, 0)
+    through = matmul_tn(strip_rows, gated_final.reshape(width_d, n_images * lat)).astype(BF16)
+    through = exchanged(jnp.moveaxis(through.reshape(strip, n_images, lat), 1, 0), IMAGE)
     through = through.reshape(half, lat)
 
     v1_both = (w_v1, turned(w_v1, "core", 1))
     v2_both = (w_v2, turned(w_v2, "core", 1))
-    my_target = lax.dynamic_slice_in_dim(target[0], near * mine, mine, 0)
-
-    hidden, hidden_slope, latent_part = block_forward(token_rows, full_in, through)
+
+    hidden, hidden_slope = block_forward(token_rows, full_in)
+    own_target, hidden = lax.optimization_barrier((target[0], hidden))
+    goals = lax.all_gather(own_target, IMAGE, axis=0)
+    goal = lax.dynamic_slice(goals, (my_slot, near * mine, 0), (1, mine, goals.shape[2]))[0]
+    goal = goal.astype(F32)
+    kept_rows = lax.dynamic_index_in_dim(token_rows, far, 0, keepdims=False)
+    far_rows = lax.dynamic_index_in_dim(token_rows, 1 - far, 0, keepdims=False)
+    far_rows, hidden_slope = lax.optimization_barrier((far_rows, hidden_slope))
+    far_rows = turned(far_rows, "far", 1)
+    far_slope = turned(hidden_slope, "far", 1)
+    far_through = turned(through, "far", 1)
     n_mp = n_y * n_core
     own_part = matmul(noise_rows, w_final).reshape(1, n_near, mine, lat)
     here = (lax.iota(jnp.int32, n_mp) == lax.axis_index(("y", "core")))[:, None]
     here = here & (lax.iota(jnp.int32, n_near) == near)[None]
-    latent_part = latent_part.reshape(n_mp, n_near, mine, lat)
+    latent_part = matmul(hidden, through).reshape(n_mp, n_near, mine, lat)
     latent_part = (latent_part + jnp.where(here[:, :, None, None], own_part, 0.0)).astype(BF16)
-    my_target, latent_part = lax.optimization_barrier((my_target, latent_part))
     latent_part = latent_part.reshape(n_y, n_core, n_near, mine, lat).transpose(2, 1, 0, 3, 4)
     latent_part = jnp.broadcast_to(latent_part[:, None], (n_near, n_y) + latent_part.shape[1:])
     latent_parts = exchanged(latent_part.reshape(n_tokens, n_y * mine, lat), TOKENS_AT)
     latents = jnp.sum(latent_parts.astype(F32), axis=0).astype(BF16)
-    goals = exchanged(jnp.broadcast_to(my_target, (n_images,) + my_target.shape), IMAGE)
-    goal = lax.dynamic_index_in_dim(goals, my_slot, 0, keepdims=False).astype(F32)
     my_y = lax.axis_index("y")
     latent = jnp.concatenate(
         [
@@ -397,33 +387,39 @@
     dec_pre_grad = (dec_slope * matmul_nt(pixel_grad, w_dec2)).astype(BF16)
     latent_grad = matmul_nt(dec_pre_grad, w_dec1).astype(BF16)
 
-    spread = jnp.broadcast_to(latent_grad, (n_tokens, mine, lat))
-    latent_rows = exchanged(spread, TOKENS_AT).reshape(n_near, n_y * n_core, mine, lat)
-    latent_rows = jnp.moveaxis(latent_rows, 0, 1).reshape(rows, lat)
-
-    term_in = block_backward(latent_rows, through, hidden_slope, token_rows)
-    term_in, latent_rows = lax.optimization_barrier((term_in, latent_rows))
-    terms = exchanged(term_in.reshape(n_rows, d_dev, half), ROWS_AT)
+    spread = jnp.broadcast_to(latent_grad, (n_far * n_tokens, mine, lat))
+    spread = exchanged(spread, ("far",) + TOKENS_AT)
+    spread = spread.reshape(n_far, n_near, n_y * n_core, mine, lat)
+    spread = jnp.moveaxis(spread, 1, 2).reshape(n_far, rows, lat)
+    latent_rows = lax.dynamic_index_in_dim(spread, far, 0, keepdims=False)
+    far_latent_rows = lax.dynamic_index_in_dim(spread, 1 - far, 0, keepdims=False)
 
     inner = matmul_tn(latent_rows, hidden).astype(BF16)
-    inner = by_turns(jnp.moveaxis(inner.reshape(lat, n_images, strip), 1, 0), IMAGE)
-    inner = jnp.concatenate(inner).reshape(n_images * lat, strip)
-    turned_gates = jnp.concatenate(
-        [
-            lax.dynamic_slice_in_dim(gates, (my_image - step) % n_images, 1, 0)
-            for step in range(n_images)
-        ]
-    )
-    turned_final = (turned_gates.T[:, :, None] * w_final.astype(F32)[:, None, :]).astype(BF16)
-    turned_final = turned_final.reshape(width_d, n_images * lat)
-    out_strip = matmul(turned_final, inner).astype(BF16)
-    out_strip, terms = lax.optimization_barrier((out_strip, terms))
-    out_strips = exchanged(out_strip.reshape(n_rows, d_dev, strip), ROWS_AT)
-    grad_out_t = jnp.moveaxis(out_strips, 0, 1).reshape(d_dev, ff_mp).astype(F32)
-
-    grad_in = jnp.sum(terms.reshape(n_near, n_images, d_dev, half).astype(F32), axis=1)
+    far_inner = turned(inner, "far", 1)
+    term_in = block_backward(
+        (
+            (latent_rows, through, hidden_slope, kept_rows),
+            (far_latent_rows, far_through, far_slope, far_rows),
+        )
+    )
+    both = jnp.concatenate([inner, far_inner])
+    both = jnp.broadcast_to(both, (n_near * n_z,) + both.shape)
+    sent = jnp.concatenate([term_in.reshape(n_near * n_z, d_dev, half), both], axis=1)
+    came = exchanged(sent, PAIR_ROWS).reshape(n_near, n_z, d_dev + 2 * lat, half)
+    grad_in = jnp.sum(came[:, :, :d_dev].astype(F32), axis=1)
     grad_in = jnp.moveaxis(grad_in, 0, 1).reshape(d_dev, ff_mp)
-    return (grad_in, grad_out_t)
+
+    at = lax.axis_index(ROWS_AT) * d_dev
+    my_final = lax.dynamic_slice_in_dim(w_final, at, d_dev, 0).astype(F32)
+    my_gates = lax.dynamic_slice_in_dim(gates, at, d_dev, 1).reshape(n_z, n_far, d_dev)
+    my_gates = jnp.where(far == 0, my_gates, my_gates[:, ::-1])
+    my_gated = my_gates.reshape(n_images, d_dev).T[:, :, None] * my_final[:, None, :]
+    my_gated = my_gated.astype(BF16).reshape(d_dev, n_images * lat)
+    outs = [
+        matmul(my_gated, came[at_near, :, d_dev:].reshape(n_images * lat, half))
+        for at_near in range(n_near)
+    ]
+    return (grad_in, jnp.concatenate(outs, axis=1))
 
 
 def solution(mesh):

time: 318 us -> 315 us (level)
  local copies, waits for them, and re-layouts: 35.7 us -> 68.6 us
  starting transfers between devices: 87.2 us -> 58.5 us
  waiting for transfers between devices: 106 us -> 119 us
  Pallas kernels: 38.3 us -> 26.4 us
  blocking collectives: 10.3 us -> 0 us
    all_to_all x6, waiting for transfers between devices: 26.5 us -> 84.5 us  [exchanged(): return lax.all_to_all(blocks, axis, 0, 0, tiled=True)]
    ppermute x25 -> x15, waiting for transfers between devices: 79.7 us -> 34.5 us  [turned(): lax.ppermute(value, axis, [(at, (at + steps) % count) for at in range(cou...]
    ppermute x25 -> x15, starting transfers between devices: 47.5 us -> 23.1 us  [turned(): lax.ppermute(value, axis, [(at, (at + steps) % count) for at in range(cou...]
    unnamed x34 -> x59, local copies, waits for them, and re-layouts: 5.13 us -> 23.2 us
    pallas_call x5, Pallas kernels: 38.3 us -> 26.4 us  [call(): pl.pallas_call(kernel, grid=(grid,), in_specs=in_specs, out_specs=out_spe...]
    all_to_all x1 -> x0, blocking collectives: 10.3 us -> none  [exchanged(): return lax.all_to_all(blocks, axis, 0, 0, tiled=True)]
    all_to_all x6, starting transfers between devices: 39.6 us -> 35.3 us  [exchanged(): return lax.all_to_all(blocks, axis, 0, 0, tiled=True)]
    squeeze x0 -> x1, local copies, waits for them, and re-layouts: none -> 4.29 us  [on_device(): kept_rows = lax.dynamic_index_in_dim(token_rows, far, 0, keepdims=False)]
  transfers between devices with their start and end apart: 32 -> 23, of which waited for: 16 -> 11; matrix products, arithmetic and copies ran while one was open for 11% -> 17% of each run, Pallas kernels for 7% -> 9%
where the time goes in v4:
time: 315 us; the launch traced here: 311 us
  waiting for transfers between devices  119 us (38%)
  local copies, waits for them, and re-layouts  68.6 us (22%)
  starting transfers between devices  58.5 us (19%)
  Pallas kernels  26.4 us (8%)
  between operations  17.2 us (5%)
  other arithmetic  12.8 us (4%)
  matrix products  8.1 us (3%)
    all_to_all x6, waiting for transfers between devices, exchanged(): return lax.all_to_all(blocks, axis, 0, 0, tiled=True)  84.5 us
    all_to_all x6, starting transfers between devices, exchanged(): return lax.all_to_all(blocks, axis, 0, 0, tiled=True)  35.3 us
    ppermute x15, waiting for transfers between devices, turned(): lax.ppermute(value, axis, [(at, (at + steps) % count) for at in range(cou...  34.5 us
    pallas_call x5, Pallas kernels, call(): pl.pallas_call(kernel, grid=(grid,), in_specs=in_specs, out_specs=out_spe...  26.4 us
    unnamed x59, local copies, waits for them, and re-layouts  23.2 us
    ppermute x15, starting transfers between devices, turned(): lax.ppermute(value, axis, [(at, (at + steps) % count) for at in range(cou...  23.1 us
  transfers between devices with their start and end apart: 23, of which 11 were waited for; matrix products, arithmetic and copies ran while one was open for 17% of the time, Pallas kernels for 9%

profile of v4, /device:TPU:8, one launch (start us, length us, event | category | flops | bytes accessed | tf_op | source)
XLA Modules:
  0.0 310.6 jit_solution(401025901472488865)
XLA Ops:
  16.8 7.9 %all-to-all-start = ((bf16[16,152,608]{2,1,0:T(8,128)(2,1)}), bf16[16,152,608]{2,1,0:T(8,128)(2,1)S(1)}, u32[]{:S(2)}, u32[]{:S(2)}) async-start(bf16[16,152,608]{2,1,0:T(8,128)(2,1)} %bitcast.86), calls=%async_computation | async-start | bytes 6225920 | tf_op jit(solution)/shard_map/all_to_all | solution.py:79
  25.3 3.0 reshape.207
  28.3 2.1 concatenate.21
  32.4 34.4 %all-to-all-done = bf16[16,152,608]{2,1,0:T(8,128)(2,1)S(1)} async-done(((bf16[16,152,608]{2,1,0:T(8,128)(2,1)}), bf16[16,152,608]{2,1,0:T(8,128)(2,1)S(1)}, u32[]{:S(2)}, u32[]{:S(2)}) %all-to-all-start) | async-done | bytes 2957344 | tf_op jit(solution)/shard_map/all_to_all | solution.py:79
  68.5 2.1 copy.99
  70.6 7.6 %all-to-all-start.1 = ((bf16[16,160,76]{2,1,0:T(8,128)(2,1)}), bf16[16,160,76]{2,1,0:T(8,128)(2,1)S(1)}, u32[]{:S(2)}, u32[]{:S(2)}) async-start(bf16[16,160,76]{2,1,0:T(8,128)(2,1)} %copy.99), calls=%async_computation.1 | async-start | bytes 1310720 | tf_op jit(solution)/shard_map/all_to_all | solution.py:79
  78.3 2.1 copy-done.3
  82.3 4.8 %shard_map.140 = (bf16[768,608]{1,0:T(8,128)(2,1)S(1)}, bf16[768,608]{1,0:T(8,128)(2,1)S(1)}) custom-call(bf16[2,768,1216]{2,1,0:T(8,128)(2,1)S(1)} %copy-done.3, bf16[2,1216,608]{2,1,0:T(8,128)(2,1)S(1)} %bitcast.78), custom_call_target="tpu_custom_call" | custom-call | flops 2271215616 | bytes 8560640 | tf_op jit(solution)/shard_map/pallas_call | solution.py:87
  93.3 6.2 %all-to-all-start.2 = ((bf16[8,76,64]{1,2,0:T(8,128)(2,1)}), bf16[8,76,64]{1,2,0:T(8,128)(2,1)S(1)}, u32[]{:S(2)}, u32[]{:S(2)}) async-start(bf16[8,76,64]{1,2,0:T(8,128)(2,1)} %copy.101), calls=%async_computation.2 | async-start | bytes 262144 | tf_op jit(solution)/shard_map/all_to_all | solution.py:79
  99.5 9.1 %all-to-all-done.2 = bf16[8,76,64]{1,2,0:T(8,128)(2,1)S(1)} async-done(((bf16[8,76,64]{1,2,0:T(8,128)(2,1)}), bf16[8,76,64]{1,2,0:T(8,128)(2,1)S(1)}, u32[]{:S(2)}, u32[]{:S(2)}) %all-to-all-start.2) | async-done | bytes 77856 | tf_op jit(solution)/shard_map/all_to_all | solution.py:79
  110.4 2.4 copy.105
  112.9 4.8 %all-to-all-start.3 = ((bf16[16,192,64]{1,2,0:T(8,128)(2,1)}), bf16[16,192,64]{1,2,0:T(8,128)(2,1)}, u32[]{:S(2)}, u32[]{:S(2)}) async-start(bf16[16,192,64]{1,2,0:T(8,128)(2,1)} %copy.105), calls=%async_computation.3 | async-start | bytes 1048576 | tf_op jit(solution)/shard_map/all_to_all | solution.py:79
  117.7 8.9 %all-to-all-done.3 = bf16[16,192,64]{1,2,0:T(8,128)(2,1)} async-done(((bf16[16,192,64]{1,2,0:T(8,128)(2,1)}), bf16[16,192,64]{1,2,0:T(8,128)(2,1)}, u32[]{:S(2)}, u32[]{:S(2)}) %all-to-all-start.3) | async-done | bytes 393248 | tf_op jit(solution)/shard_map/all_to_all | solution.py:79
  130.8 2.9 shard_map.141
  134.5 7.0 %shard_map.142 = (f32[192,640]{1,0:T(8,128)S(1)}, f32[192,640]{1,0:T(8,128)S(1)}, bf16[192,1280]{1,0:T(8,128)(2,1)S(1)}) custom-call(bf16[192,1280]{1,0:T(8,128)(2,1)S(1)} %get-tuple-element.26.normed, bf16[1280,640]{1,0:T(8,128)(2,1)} %v1a.3, bf16[1280,640]{1,0:T(8,128)(2,1)} %collective-permute-done.v1b, bf16[640,1280]{1,0:T(8,128)(2,1)} %v2a.3, ...), custom_call_target="tpu_custom_call" | custom-call | flops 1258291200 | bytes 6553600 | tf_op jit(solution)/shard_map/pallas_call | solution.py:87
  146.1 5.1 %collective-permute-start.3 = (bf16[48,1280]{1,0:T(8,128)(2,1)}, bf16[48,1280]{1,0:T(8,128)(2,1)}, u32[]{:S(2)}, u32[]{:S(2)}) collective-permute-start(bf16[48,1280]{1,0:T(8,128)(2,1)} %get-tuple-element.49), channel_id=1, source_target_pairs={{0,4},{2,6},{4,0},{6,2},{1,5},{3,7},{5,1},{7,3},{8,12},{10,14},{12... | collective-permute-start | bytes 368648 | tf_op jit(solution)/shard_map/ppermute | solution.py:63
  161.5 2.5 collective-permute-start.5
  164.0 4.3 %dynamic-slice_bitcast_fusion = (bf16[768,1216]{1,0:T(8,128)(2,1)}, bf16[1,768,1216]{2,1,0:T(8,128)(2,1)}) fusion(bf16[2,768,1216]{2,1,0:T(8,128)(2,1)} %all-gather.4.cloned.1.call-done.tokens, s32[]{:T(128)S(6)} %select_n.93, s32[]{:T(128)S(6)} %select_n.94), kind=kLoop, calls=%fused_computation.6 | loop fusion | bytes 7471112 | tf_op jit(solution)/shard_map/jit(dynamic_index_in_dim)/squeeze | solution.py:353
  168.3 4.0 %copy.112 = bf16[1,768,1216]{1,2,0:T(8,128)(2,1)} copy(bf16[1,768,1216]{2,1,0:T(8,128)(2,1)} %get-tuple-element.41) | data formatting | bytes 3735552 | tf_op jit(solution)/shard_map/jit(dynamic_index_in_dim)/dynamic_slice | solution.py:354
  172.3 2.2 copy.115
  174.5 3.5 %collective-permute-start.13 = (bf16[768,1216]{0,1:T(8,128)(2,1)}, bf16[768,1216]{0,1:T(8,128)(2,1)}, u32[]{:S(2)}, u32[]{:S(2)}) collective-permute-start(bf16[768,1216]{0,1:T(8,128)(2,1)} %bitcast.98), channel_id=1, source_target_pairs={{0,8},{8,0},{1,9},{9,1},{2,10},{10,2},{3,11},{11,3},{4,12},{12,4},... | collective-permute-start | bytes 5603336 | tf_op jit(solution)/shard_map/ppermute | solution.py:63
  181.2 6.8 %shard_map.143 = bf16[192,1280]{1,0:T(8,128)(2,1)S(1)} custom-call(bf16[192,1280]{1,0:T(8,128)(2,1)S(1)} %pad_maximum_fusion.2.grad, bf16[1280,640]{1,0:T(8,128)(2,1)} %v1a.3, bf16[1280,640]{1,0:T(8,128)(2,1)} %collective-permute-done.v1b, bf16[640,1280]{1,0:T(8,128)(2,1)} %v2a.3, bf16[640,1280]{1,0:T(8,128)(2,1)} %collective-permute-done.1.v2b, ...), custom_call_target="tpu_custom_call" | custom-call | flops 1258291200 | bytes 6553600 | tf_op jit(solution)/shard_map/pallas_call | solution.py:87
  198.0 2.3 fusion.9
  201.3 4.9 %all-to-all-start.4 = ((bf16[32,2,1536]{2,1,0:T(2,128)(2,1)}), bf16[32,2,1536]{2,1,0:T(2,128)(2,1)}, u32[]{:S(2)}, u32[]{:S(2)}) async-start(bf16[32,2,1536]{2,1,0:T(2,128)(2,1)} %reshape.235), calls=%async_computation.4 | async-start | bytes 393216 | tf_op jit(solution)/shard_map/all_to_all | solution.py:79
  206.5 3.1 collective-permute-start.11
  209.6 2.2 copy.117.slope2
  211.8 27.3 %collective-permute-done.13 = bf16[768,1216]{0,1:T(8,128)(2,1)} collective-permute-done((bf16[768,1216]{0,1:T(8,128)(2,1)}, bf16[768,1216]{0,1:T(8,128)(2,1)}, u32[]{:S(2)}, u32[]{:S(2)}) %collective-permute-start.13) | collective-permute-done | bytes 1867808 | tf_op jit(solution)/shard_map/ppermute | solution.py:63
  239.1 2.7 copy.118.tokens2
  243.9 2.1 copy.110
  254.0 4.9 %shard_map.144 = bf16[1216,608]{1,0:T(8,128)(2,1)S(1)} custom-call(bf16[768,64]{1,0:T(8,128)(2,1)S(1)} %bitcast.80, bf16[608,64]{1,0:T(8,128)(2,1)S(1)} %copy.116.through, bf16[768,608]{1,0:T(8,128)(2,1)S(1)} %copy-done.11, bf16[768,1216]{1,0:T(8,128)(2,1)S(1)} %copy-done.8, bf16[768,64]{1,0:T(8,128)(2,1)S(1)} %bitcast.81, ...), custom_call_target="tpu_custom_call" | custom-call | flops 2271215616 | bytes 7081984 | tf_op jit(solution)/shard_map/pallas_call | solution.py:87
  260.9 3.9 %all-to-all-start.5 = ((bf16[8,280,608]{2,1,0:T(8,128)(2,1)}), bf16[8,280,608]{2,1,0:T(8,128)(2,1)S(1)}, u32[]{:S(2)}, u32[]{:S(2)}) async-start(bf16[8,280,608]{2,1,0:T(8,128)(2,1)} %pad_maximum_fusion), calls=%async_computation.5 | async-start | bytes 5734400 | tf_op jit(solution)/shard_map/all_to_all | solution.py:79
  268.0 31.1 %all-to-all-done.5 = bf16[8,280,608]{2,1,0:T(8,128)(2,1)S(1)} async-done(((bf16[8,280,608]{2,1,0:T(8,128)(2,1)}), bf16[8,280,608]{2,1,0:T(8,128)(2,1)S(1)}, u32[]{:S(2)}, u32[]{:S(2)}) %all-to-all-start.5) | async-done | bytes 2723872 | tf_op jit(solution)/shard_map/all_to_all | solution.py:79
  (162 shorter events, 75.1 us)
Async XLA Ops:
  7.2 71.2 %all-gather.4.cloned.1.call-start = ((), (), s32[]{:S(2)}) async-start(), calls=%async_computation.6 | async-start | bytes 4423680 | tf_op jit(solution)/shard_map/all_gather | solution.py:330
  10.0 4.3 %copy-start.19 = (bf16[1,96,2432]{1,2,0:T(8,128)(2,1)}, bf16[1,96,2432]{1,2,0:T(8,128)(2,1)S(1)}, u32[]{:S(2)}) copy-start(bf16[1,96,2432]{1,2,0:T(8,128)(2,1)S(1)} %copy.96) | copy-start | bytes 1400836
  16.8 50.0 %all-to-all-start = ((bf16[16,152,608]{2,1,0:T(8,128)(2,1)}), bf16[16,152,608]{2,1,0:T(8,128)(2,1)S(1)}, u32[]{:S(2)}, u32[]{:S(2)}) async-start(bf16[16,152,608]{2,1,0:T(8,128)(2,1)} %bitcast.86), calls=%async_computation | async-start | bytes 6225920 | tf_op jit(solution)/shard_map/all_to_all | solution.py:79
  24.7 5.6 %copy-start.22 = (bf16[2432,64]{0,1:T(8,128)(2,1)S(1)}, bf16[2432,64]{0,1:T(8,128)(2,1)}, u32[]{:S(2)}) copy-start(bf16[2432,64]{0,1:T(8,128)(2,1)} %param.20) | copy-start | bytes 933892
  24.7 109.7 %collective-permute-start = (bf16[1280,640]{1,0:T(8,128)(2,1)}, bf16[1280,640]{1,0:T(8,128)(2,1)}, u32[]{:S(2)}, u32[]{:S(2)}) collective-permute-start(bf16[1280,640]{1,0:T(8,128)(2,1)} %v1a.3), channel_id=1, source_target_pairs={{0,1},{1,0},{2,3},{3,2},{4,5},{5,4},{6,7},{7,6},{8,9},{9,8},{10,11... | collective-permute-start | bytes 4915208 | tf_op jit(solution)/shard_map/ppermute | solution.py:63
  24.8 109.6 %collective-permute-start.1 = (bf16[640,1280]{1,0:T(8,128)(2,1)}, bf16[640,1280]{1,0:T(8,128)(2,1)}, u32[]{:S(2)}, u32[]{:S(2)}) collective-permute-start(bf16[640,1280]{1,0:T(8,128)(2,1)} %v2a.3), channel_id=1, source_target_pairs={{0,1},{1,0},{2,3},{3,2},{4,5},{5,4},{6,7},{7,6},{8,9},{9,8},{10,11... | collective-permute-start | bytes 4915208 | tf_op jit(solution)/shard_map/ppermute | solution.py:63
  70.6 18.5 %all-to-all-start.1 = ((bf16[16,160,76]{2,1,0:T(8,128)(2,1)}), bf16[16,160,76]{2,1,0:T(8,128)(2,1)S(1)}, u32[]{:S(2)}, u32[]{:S(2)}) async-start(bf16[16,160,76]{2,1,0:T(8,128)(2,1)} %copy.99), calls=%async_computation.1 | async-start | bytes 1310720 | tf_op jit(solution)/shard_map/all_to_all | solution.py:79
  78.2 78.2 %all-gather.6.cloned.1.call-start = ((), (), s32[]{:S(2)}) async-start(), calls=%async_computation.7 | async-start | bytes 2211840 | tf_op jit(solution)/shard_map/all_gather | solution.py:350
  78.3 2.1 copy-start.3
  88.1 20.8 %copy-start.4 = (bf16[768,608]{1,0:T(8,128)(2,1)}, bf16[768,608]{1,0:T(8,128)(2,1)S(1)}, u32[]{:S(2)}) copy-start(bf16[768,608]{1,0:T(8,128)(2,1)S(1)} %get-tuple-element.22) | copy-start | bytes 2801668
  91.4 17.5 %copy-start.24 = (f32[96,64]{1,0:T(8,128)S(1)}, f32[96,64]{1,0:T(8,128)}, u32[]{:S(2)}) copy-start(f32[96,64]{1,0:T(8,128)} %fusion.26) | copy-start | bytes 73732
  93.3 15.4 %all-to-all-start.2 = ((bf16[8,76,64]{1,2,0:T(8,128)(2,1)}), bf16[8,76,64]{1,2,0:T(8,128)(2,1)S(1)}, u32[]{:S(2)}, u32[]{:S(2)}) async-start(bf16[8,76,64]{1,2,0:T(8,128)(2,1)} %copy.101), calls=%async_computation.2 | async-start | bytes 262144 | tf_op jit(solution)/shard_map/all_to_all | solution.py:79
  109.4 18.9 %copy-start = (bf16[2048,768]{1,0:T(8,128)(2,1)S(1)}, bf16[2048,768]{1,0:T(8,128)(2,1)}, u32[]{:S(2)}) copy-start(bf16[2048,768]{1,0:T(8,128)(2,1)} %w_dec2.1) | copy-start | bytes 9437188
  112.9 13.7 %all-to-all-start.3 = ((bf16[16,192,64]{1,2,0:T(8,128)(2,1)}), bf16[16,192,64]{1,2,0:T(8,128)(2,1)}, u32[]{:S(2)}, u32[]{:S(2)}) async-start(bf16[16,192,64]{1,2,0:T(8,128)(2,1)} %copy.105), calls=%async_computation.3 | async-start | bytes 1048576 | tf_op jit(solution)/shard_map/all_to_all | solution.py:79
  134.5 16.7 %copy-start.25 = (s32[8]{0:T(128)S(1)}, s32[8]{0:T(128)}, u32[]{:S(2)}) copy-start(s32[8]{0:T(128)} %param.15) | copy-start | bytes 100
  144.6 9.1 %collective-permute-start.4 = (bf16[48,1280]{1,0:T(8,128)(2,1)}, bf16[48,1280]{1,0:T(8,128)(2,1)}, u32[]{:S(2)}, u32[]{:S(2)}) collective-permute-start(bf16[48,1280]{1,0:T(8,128)(2,1)} %get-tuple-element.48), channel_id=1, source_target_pairs={{0,2},{2,4},{4,6},{6,0},{1,3},{3,5},{5,7},{7,1},{8,10},{10,12},{12... | collective-permute-start | bytes 368648 | tf_op jit(solution)/shard_map/ppermute | solution.py:63
  146.1 9.1 %collective-permute-start.3 = (bf16[48,1280]{1,0:T(8,128)(2,1)}, bf16[48,1280]{1,0:T(8,128)(2,1)}, u32[]{:S(2)}, u32[]{:S(2)}) collective-permute-start(bf16[48,1280]{1,0:T(8,128)(2,1)} %get-tuple-element.49), channel_id=1, source_target_pairs={{0,4},{2,6},{4,0},{6,2},{1,5},{3,7},{5,1},{7,3},{8,12},{10,14},{12... | collective-permute-start | bytes 368648 | tf_op jit(solution)/shard_map/ppermute | solution.py:63
  151.2 5.2 %collective-permute-start.2 = (bf16[48,1280]{1,0:T(8,128)(2,1)}, bf16[48,1280]{1,0:T(8,128)(2,1)}, u32[]{:S(2)}, u32[]{:S(2)}) collective-permute-start(bf16[48,1280]{1,0:T(8,128)(2,1)} %get-tuple-element.47), channel_id=1, source_target_pairs={{0,6},{2,0},{4,2},{6,4},{1,7},{3,1},{5,3},{7,5},{8,14},{10,8},{12,... | collective-permute-start | bytes 368648 | tf_op jit(solution)/shard_map/ppermute | solution.py:63
  158.4 19.6 %collective-permute-start.7 = (bf16[48,1280]{1,0:T(8,128)(2,1)}, bf16[48,1280]{1,0:T(8,128)(2,1)}, u32[]{:S(2)}, u32[]{:S(2)}) collective-permute-start(bf16[48,1280]{1,0:T(8,128)(2,1)} %get-tuple-element.50), channel_id=1, source_target_pairs={{0,6},{2,0},{4,2},{6,4},{1,7},{3,1},{5,3},{7,5},{8,14},{10,8},{12,... | collective-permute-start | bytes 368648 | tf_op jit(solution)/shard_map/ppermute | solution.py:63
  160.3 17.8 %collective-permute-start.6 = (bf16[48,1280]{1,0:T(8,128)(2,1)}, bf16[48,1280]{1,0:T(8,128)(2,1)}, u32[]{:S(2)}, u32[]{:S(2)}) collective-permute-start(bf16[48,1280]{1,0:T(8,128)(2,1)} %get-tuple-element.50), channel_id=1, source_target_pairs={{0,4},{2,6},{4,0},{6,2},{1,5},{3,7},{5,1},{7,3},{8,12},{10,14},{12... | collective-permute-start | bytes 368648 | tf_op jit(solution)/shard_map/ppermute | solution.py:63
  161.5 16.6 %collective-permute-start.5 = (bf16[48,1280]{1,0:T(8,128)(2,1)}, bf16[48,1280]{1,0:T(8,128)(2,1)}, u32[]{:S(2)}, u32[]{:S(2)}) collective-permute-start(bf16[48,1280]{1,0:T(8,128)(2,1)} %get-tuple-element.50), channel_id=1, source_target_pairs={{0,2},{2,4},{4,6},{6,0},{1,3},{3,5},{5,7},{7,1},{8,10},{10,12},{12... | collective-permute-start | bytes 368648 | tf_op jit(solution)/shard_map/ppermute | solution.py:63
  174.5 35.1 %collective-permute-start.12 = (bf16[768,608]{0,1:T(8,128)(2,1)}, bf16[768,608]{0,1:T(8,128)(2,1)}, u32[]{:S(2)}, u32[]{:S(2)}) collective-permute-start(bf16[768,608]{0,1:T(8,128)(2,1)} %copy.115), channel_id=1, source_target_pairs={{0,8},{8,0},{1,9},{9,1},{2,10},{10,2},{3,11},{11,3},{4,12},{12,4},... | collective-permute-start | bytes 2801672 | tf_op jit(solution)/shard_map/ppermute | solution.py:63
  174.5 64.6 %collective-permute-start.13 = (bf16[768,1216]{0,1:T(8,128)(2,1)}, bf16[768,1216]{0,1:T(8,128)(2,1)}, u32[]{:S(2)}, u32[]{:S(2)}) collective-permute-start(bf16[768,1216]{0,1:T(8,128)(2,1)} %bitcast.98), channel_id=1, source_target_pairs={{0,8},{8,0},{1,9},{9,1},{2,10},{10,2},{3,11},{11,3},{4,12},{12,4},... | collective-permute-start | bytes 5603336 | tf_op jit(solution)/shard_map/ppermute | solution.py:63
  188.0 8.3 %copy-start.2 = (bf16[768,1280]{1,0:T(8,128)(2,1)S(1)}, bf16[768,1280]{1,0:T(8,128)(2,1)}, u32[]{:S(2)}) copy-start(bf16[768,1280]{1,0:T(8,128)(2,1)} %w_patch.1) | copy-start | bytes 5898244
  188.1 4.9 %collective-permute-start.10 = (bf16[48,1280]{1,0:T(8,128)(2,1)S(1)}, bf16[48,1280]{1,0:T(8,128)(2,1)S(1)}, u32[]{:S(2)}, u32[]{:S(2)}) collective-permute-start(bf16[48,1280]{1,0:T(8,128)(2,1)S(1)} %get-tuple-element.45), channel_id=1, source_target_pairs={{0,2},{2,4},{4,6},{6,0},{1,3},{3,5},{5,7},{7,1},{8,10},{10,12},{12... | collective-permute-start | bytes 368648 | tf_op jit(solution)/shard_map/ppermute | solution.py:63
  188.5 6.5 %collective-permute-start.9 = (bf16[48,1280]{1,0:T(8,128)(2,1)S(1)}, bf16[48,1280]{1,0:T(8,128)(2,1)S(1)}, u32[]{:S(2)}, u32[]{:S(2)}) collective-permute-start(bf16[48,1280]{1,0:T(8,128)(2,1)S(1)} %get-tuple-element.46), channel_id=1, source_target_pairs={{0,4},{2,6},{4,0},{6,2},{1,5},{3,7},{5,1},{7,3},{8,12},{10,14},{12... | collective-permute-start | bytes 368648 | tf_op jit(solution)/shard_map/ppermute | solution.py:63
  189.7 6.2 %collective-permute-start.8 = (bf16[48,1280]{1,0:T(8,128)(2,1)S(1)}, bf16[48,1280]{1,0:T(8,128)(2,1)S(1)}, u32[]{:S(2)}, u32[]{:S(2)}) collective-permute-start(bf16[48,1280]{1,0:T(8,128)(2,1)S(1)} %get-tuple-element.44), channel_id=1, source_target_pairs={{0,6},{2,0},{4,2},{6,4},{1,7},{3,1},{5,3},{7,5},{8,14},{10,8},{12,... | collective-permute-start | bytes 368648 | tf_op jit(solution)/shard_map/ppermute | solution.py:63
  201.3 40.5 %all-to-all-start.4 = ((bf16[32,2,1536]{2,1,0:T(2,128)(2,1)}), bf16[32,2,1536]{2,1,0:T(2,128)(2,1)}, u32[]{:S(2)}, u32[]{:S(2)}) async-start(bf16[32,2,1536]{2,1,0:T(2,128)(2,1)} %reshape.235), calls=%async_computation.4 | async-start | bytes 393216 | tf_op jit(solution)/shard_map/all_to_all | solution.py:79
  206.5 43.6 %collective-permute-start.11 = (bf16[608,64]{1,0:T(8,128)(2,1)S(1)}, bf16[608,64]{1,0:T(8,128)(2,1)S(1)}, u32[]{:S(2)}, u32[]{:S(2)}) collective-permute-start(bf16[608,64]{1,0:T(8,128)(2,1)S(1)} %copy.116.through), channel_id=1, source_target_pairs={{0,8},{8,0},{1,9},{9,1},{2,10},{10,2},{3,11},{11,3},{4,12},{12,4},... | collective-permute-start | bytes 233480 | tf_op jit(solution)/shard_map/ppermute | solution.py:63
  241.8 6.4 %copy-start.5 = (bf16[768,608]{1,0:T(8,128)(2,1)S(1)}, bf16[768,608]{1,0:T(8,128)(2,1)}, u32[]{:S(2)}) copy-start(bf16[768,608]{1,0:T(8,128)(2,1)} %copy-done.4) | copy-start | bytes 2801668
  248.6 10.3 %collective-permute-start.14 = (bf16[64,608]{1,0:T(8,128)(2,1)S(1)}, bf16[64,608]{1,0:T(8,128)(2,1)S(1)}, u32[]{:S(2)}, u32[]{:S(2)}) collective-permute-start(bf16[64,608]{1,0:T(8,128)(2,1)S(1)} %convolution_convert_fusion), channel_id=1, source_target_pairs={{0,8},{8,0},{1,9},{9,1},{2,10},{10,2},{3,11},{11,3},{4,12},{12,4},... | collective-permute-start | bytes 233480 | tf_op jit(solution)/shard_map/ppermute | solution.py:63
  260.9 38.1 %all-to-all-start.5 = ((bf16[8,280,608]{2,1,0:T(8,128)(2,1)}), bf16[8,280,608]{2,1,0:T(8,128)(2,1)S(1)}, u32[]{:S(2)}, u32[]{:S(2)}) async-start(bf16[8,280,608]{2,1,0:T(8,128)(2,1)} %pad_maximum_fusion), calls=%async_computation.5 | async-start | bytes 5734400 | tf_op jit(solution)/shard_map/all_to_all | solution.py:79
  (17 other events, 20.4 us)
Sparse Core Ops, SparseCore 0:
  17.0 32.2 all-gather.3
  88.2 54.9 all-gather.5

commit v5 on v4

--- a/solution.py
+++ b/solution.py
@@ -10,7 +10,8 @@
 
 BF16 = jnp.bfloat16
 GELU_SCALE = math.sqrt(2.0 / math.pi)
-VMEM_BYTES = 24 * 1024 * 1024
+MIB = 1024 * 1024
+SMALL, LARGE = 24 * MIB, 56 * MIB
 F32 = jnp.float32
 AXES = ("near", "z", "far", "y", "core")
 IMAGE = ("z", "far")
@@ -79,11 +80,18 @@
     return lax.all_to_all(blocks, axis, 0, 0, tiled=True)
 
 
+def lanes(columns):
+    return pl.cdiv(columns, 128) * 128
+
+
 def whole(array):
     return pl.BlockSpec(array.shape, lambda step: (0,) * len(array.shape))
 
 
-def call(kernel, grid, in_specs, out_specs, out_shape, scratch, flops, moved, *operands):
+SCALARS = pl.BlockSpec(memory_space=pltpu.SMEM)
+
+
+def call(kernel, grid, in_specs, out_specs, out_shape, scratch, flops, moved, limit, *operands):
     return pl.pallas_call(
         kernel,
         grid=(grid,),
@@ -91,72 +99,190 @@
         out_specs=out_specs,
         out_shape=out_shape,
         scratch_shapes=scratch,
-        compiler_params=pltpu.CompilerParams(vmem_limit_bytes=VMEM_BYTES),
+        compiler_params=pltpu.CompilerParams(vmem_limit_bytes=limit),
         cost_estimate=pl.CostEstimate(flops=flops, bytes_accessed=moved, transcendentals=0),
     )(*operands)
 
 
-def block_forward_kernel(tokens, weights, hidden, slope):
-    total = matmul(tokens[0], weights[0]) + matmul(tokens[1], weights[1])
+def block_forward_kernel(at, tokens, weights, hidden, slope):
+    far = at[0]
+    total = matmul(tokens[0], weights[far]) + matmul(tokens[1], weights[1 - far])
     act, rate = gelu_and_slope(total)
+    columns = act.shape[1]
     hidden[...] = act.astype(BF16)
-    slope[...] = rate.astype(BF16)
-
-
-def block_forward(tokens, weights):
+    slope[:, :columns] = rate.astype(BF16)
+    if slope.shape[1] > columns:
+        slope[:, columns:] = jnp.zeros((act.shape[0], slope.shape[1] - columns), BF16)
+
+
+def block_forward(at, tokens, weights):
     parts, rows, width = tokens.shape
     columns = weights.shape[2]
     tile = rows // 4
     return call(
         block_forward_kernel,
         4,
-        [pl.BlockSpec((parts, tile, width), lambda step: (0, step, 0)), whole(weights)],
-        [pl.BlockSpec((tile, columns), lambda step: (step, 0))] * 2,
-        [jax.ShapeDtypeStruct((rows, columns), BF16)] * 2,
+        [
+            SCALARS,
+            pl.BlockSpec((parts, tile, width), lambda step: (0, step, 0)),
+            whole(weights),
+        ],
+        [
+            pl.BlockSpec((tile, columns), lambda step: (step, 0)),
+            pl.BlockSpec((tile, lanes(columns)), lambda step: (step, 0)),
+        ],
+        [
+            jax.ShapeDtypeStruct((rows, columns), BF16),
+            jax.ShapeDtypeStruct((rows, lanes(columns)), BF16),
+        ],
         [],
         2 * rows * columns * parts * width,
         2 * (parts * rows * width + parts * width * columns + 2 * rows * columns),
+        LARGE,
+        at,
         tokens,
         weights,
     )
 
 
-def block_backward_kernel(grads, through, slope, tokens, grads2, through2, slope2, tokens2, term, pre, pre2):
+def latent_kernel(at, hidden, through, own_part, out, total):
+    n_near, n_y, n_core, _, mine, _ = out.shape
+    lat = through.shape[1]
+    near, place = at[1], at[2]
+    total[...] = matmul(hidden[...], through[...])
+    rows = pl.ds(pl.multiple_of((place * n_near + near) * mine, mine), mine)
+    total[rows] += own_part[pl.ds(pl.multiple_of(near * mine, mine), mine)]
+    for y in range(n_y):
+        for core in range(n_core):
+            for side in range(n_near):
+                start = ((y * n_core + core) * n_near + side) * mine
+                block = total[start : start + mine].astype(BF16)
+                for other in range(n_y):
+                    out[side, other, core, y // 2, :, y % 2 * lat : (y % 2 + 1) * lat] = block
+
+
+def latent_parts_of(at, hidden, through, own_part, shape):
+    rows, columns = hidden.shape
+    lat = through.shape[1]
+    return call(
+        latent_kernel,
+        1,
+        [SCALARS, whole(hidden), whole(through), whole(own_part)],
+        pl.BlockSpec(shape, lambda step: (0,) * len(shape)),
+        jax.ShapeDtypeStruct(shape, BF16),
+        [pltpu.VMEM((rows, lat), F32)],
+        2 * rows * columns * lat,
+        2 * rows * columns,
+        SMALL,
+        at,
+        hidden,
+        through,
+        own_part,
+    )
+
+
+def inner_kernel(at, spread, hidden, grads, far_grads, inner):
+    _, n_near, n_mp, mine, _ = spread.shape
+    for image, result in ((at[0], grads), (1 - at[0], far_grads)):
+        for place in range(n_mp):
+            for near in range(n_near):
+                start = (place * n_near + near) * mine
+                result[start : start + mine] = spread[image, near, place]
+    inner[...] = matmul_tn(grads[:, : inner.shape[0]], hidden[...]).astype(BF16)
+
+
+def inner_products(at, spread, hidden, lat):
+    rows, columns = hidden.shape
+    shapes = [
+        jax.ShapeDtypeStruct((rows, spread.shape[-1]), BF16),
+        jax.ShapeDtypeStruct((rows, spread.shape[-1]), BF16),
+        jax.ShapeDtypeStruct((lat, columns), BF16),
+    ]
+    return call(
+        inner_kernel,
+        1,
+        [SCALARS, whole(spread), whole(hidden)],
+        [whole(shape) for shape in shapes],
+        shapes,
+        [],
+        2 * rows * columns * lat,
+        2 * rows * columns,
+        SMALL,
+        at,
+        spread,
+        hidden,
+    )
+
+
+def block_backward_kernel(
+    grads, through, slope, tokens, grads2, through2, slope2, tokens2, term, pre, pre2
+):
     @pl.when(pl.program_id(0) == 0)
     def _():
-        back = matmul_nt(grads[...], through[...])
-        pre[...] = (slope[...].astype(F32) * back).astype(BF16)
-        back = matmul_nt(grads2[...], through2[...])
-        pre2[...] = (slope2[...].astype(F32) * back).astype(BF16)
-
-    total = matmul_tn(tokens[...], pre[...]) + matmul_tn(tokens2[...], pre2[...])
+        columns, lat = through.shape
+        for grad, via, rate, result in (
+            (grads, through, slope, pre),
+            (grads2, through2, slope2, pre2),
+        ):
+            back = matmul_nt(grad[:, :lat], via[...])
+            result[...] = (rate[:, :columns].astype(F32) * back).astype(BF16)
+
+    total = matmul_tn(tokens[0], pre[...]) + matmul_tn(tokens2[...], pre2[...])
     term[...] = total.astype(BF16)
 
 
-def block_backward(images):
-    rows, width = images[0][3].shape
-    columns = images[0][2].shape[1]
+def block_backward(grads, through, slope, tokens, grads2, through2, slope2, tokens2):
+    rows, width = tokens2.shape
+    columns = through.shape[0]
     tile = min(640, width)
-    cut = pl.BlockSpec((rows, tile), lambda step: (0, step))
-    specs = []
-    for grads, through, slope, _ in images:
-        specs += [whole(grads), whole(through), whole(slope), cut]
     return call(
         block_backward_kernel,
         pl.cdiv(width, tile),
-        specs,
+        [
+            whole(grads),
+            whole(through),
+            whole(slope),
+            pl.BlockSpec((1, rows, tile), lambda step: (0, 0, step)),
+            whole(grads2),
+            whole(through2),
+            whole(slope2),
+            pl.BlockSpec((rows, tile), lambda step: (0, step)),
+        ],
         pl.BlockSpec((tile, columns), lambda step: (step, 0)),
         jax.ShapeDtypeStruct((width, columns), BF16),
         [pltpu.VMEM((rows, columns), BF16)] * 2,
         4 * rows * columns * width,
         2 * (2 * rows * width + width * columns + 2 * rows * columns),
-        *images[0],
-        *images[1],
-    )
-
-
-def decode_kernel(latent, w_dec1, w_dec2, w_patch, normed, embedded, slope, pixels):
+        LARGE,
+        grads,
+        through,
+        slope,
+        tokens,
+        grads2,
+        through2,
+        slope2,
+        tokens2,
+    )
+
+
+def decode_kernel(at, parts, w_dec1, w_dec2, w_patch, normed, embedded, slope, pixels, total, latent):
     step = pl.program_id(0)
+
+    @pl.when(step == 0)
+    def _():
+        n_parts, pairs, mine, _ = parts.shape
+        count = total.shape[0]
+        lat = total.shape[2]
+        added = parts[0].astype(F32)
+        for source in range(1, n_parts):
+            added = added + parts[source].astype(F32)
+        for pair in range(pairs):
+            total[2 * pair] = added[pair, :, :lat]
+            total[2 * pair + 1] = added[pair, :, lat:]
+        for turn in range(count):
+            owner = lax.rem(at[3] - turn + count, count)
+            latent[turn * mine : (turn + 1) * mine] = total[owner].astype(BF16)
+
     act, rate = silu_and_slope(matmul(latent[...], w_dec1[...]))
     slope[...] = rate[: slope.shape[0]]
     part = matmul(act.astype(BF16), w_dec2[...])
@@ -176,8 +302,9 @@
         embedded[...] = patches[: embedded.shape[0]]
 
 
-def decode(latent, w_dec1, w_dec2, w_patch, mine):
-    rows, lat = latent.shape
+def decode(at, parts, w_dec1, w_dec2, w_patch, mine):
+    count, lat = 2 * parts.shape[1], parts.shape[3] // 2
+    rows = count * mine
     deep, pix = w_dec2.shape
     width = w_patch.shape[1]
     tile = min(512, deep)
@@ -185,7 +312,8 @@
         decode_kernel,
         deep // tile,
         [
-            whole(latent),
+            SCALARS,
+            whole(parts),
             pl.BlockSpec((lat, tile), lambda step: (0, step)),
             pl.BlockSpec((tile, pix), lambda step: (step, 0)),
             whole(w_patch),
@@ -200,10 +328,16 @@
             jax.ShapeDtypeStruct((mine, width), F32),
             jax.ShapeDtypeStruct((mine, deep), F32),
         ],
-        [pltpu.VMEM((rows, pix), F32)],
+        [
+            pltpu.VMEM((rows, pix), F32),
+            pltpu.VMEM((count, mine, lat), F32),
+            pltpu.VMEM((rows, lat), BF16),
+        ],
         2 * rows * (lat * deep + deep * pix + pix * width),
         2 * (deep * pix + pix * width),
-        latent,
+        SMALL,
+        at,
+        parts,
         w_dec1,
         w_dec2,
         w_patch,
@@ -254,7 +388,7 @@
 def reward(values, v1_both, v2_both, slopes=None):
     rows, width = values.shape
     hidden = v1_both[0].shape[1]
-    tile = min(128, hidden)
+    tile = hidden
     slope_spec = pl.BlockSpec((rows, tile), lambda step: (0, step))
     slope_shape = jax.ShapeDtypeStruct((rows, hidden), F32)
     out_spec = pl.BlockSpec((rows, width), lambda step: (0, 0))
@@ -272,6 +406,7 @@
         [pltpu.VMEM((rows, width), F32)],
         8 * rows * width * hidden,
         8 * width * hidden,
+        SMALL,
         values,
         *v1_both,
         *v2_both,
@@ -315,11 +450,17 @@
     far = lax.axis_index("far")
     wide = width_d // n_far
 
+    at = jnp.stack([far, near, lax.axis_index(("y", "core")), lax.axis_index("y")]).astype(jnp.int32)
+
+    strips = jnp.moveaxis(w_out_t.reshape(d_dev, n_rows, strip), 1, 0)
+    steps_row = jnp.broadcast_to(timestep[0].astype(BF16), (n_rows, 8, strip))
+    strips = jnp.concatenate([strips, steps_row], axis=1)
+    strips, w_in, noise_rows = lax.optimization_barrier((strips, w_in, latent_noise[0]))
+    arrived = exchanged(strips, ROWS_AT)
+
     split_in = jnp.moveaxis(w_in.reshape(d_dev, n_near, half), 1, 0)
     split_in = jnp.broadcast_to(split_in[None, :, None], (n_far, n_near, n_z, d_dev, half))
     split_in = split_in.reshape(n_rows, d_dev, half)
-    split_in, noise_rows = lax.optimization_barrier((split_in, latent_noise[0]))
-    full_in = exchanged(split_in, FAR_FIRST).reshape(n_far, wide, half)
 
     modulate = modulation[timestep[0]]
     modulated = (
@@ -327,57 +468,44 @@
     ).astype(BF16)
     modulated = modulated.reshape(tok_dev, n_rows // n_far, n_far, d_dev)
     modulated = jnp.moveaxis(modulated, 2, 0).reshape(n_far, tok_dev, wide)
+    modulated = jnp.where(far == 0, modulated, modulated[::-1])
+    modulated, split_in = lax.optimization_barrier((modulated, split_in))
     token_rows = lax.all_gather(modulated, ("y", "core"), axis=1, tiled=True)
-
-    strips = jnp.moveaxis(w_out_t.reshape(d_dev, n_rows, strip), 1, 0)
-    steps_row = jnp.broadcast_to(timestep[0].astype(BF16), (n_rows, 8, strip))
-    strips = jnp.concatenate([strips, steps_row], axis=1)
-    strips, full_in = lax.optimization_barrier((strips, full_in))
-    arrived = exchanged(strips, ROWS_AT)
+    far_rows = lax.all_gather(turned(modulated[1], "far", 1), ("y", "core"), axis=0, tiled=True)
+
+    arrived, split_in = lax.optimization_barrier((arrived, split_in))
+    full_in = exchanged(split_in, FAR_FIRST).reshape(n_far, wide, half)
+
     strip_rows = arrived[:, :d_dev].reshape(width_d, strip)
     all_steps = arrived[:n_images, d_dev, 0].astype(jnp.int32)
     gates = modulation[all_steps, 2]
     gated_final = (gates.T[:, :, None] * w_final.astype(F32)[:, None, :]).astype(BF16)
     through = matmul_tn(strip_rows, gated_final.reshape(width_d, n_images * lat)).astype(BF16)
-    through = exchanged(jnp.moveaxis(through.reshape(strip, n_images, lat), 1, 0), IMAGE)
-    through = through.reshape(half, lat)
+    through = jnp.moveaxis(through.reshape(strip, n_images, lat), 1, 0)
+    through, full_in, own_target = lax.optimization_barrier((through, full_in, target[0]))
+    through = exchanged(through, IMAGE).reshape(half, lat)
 
     v1_both = (w_v1, turned(w_v1, "core", 1))
     v2_both = (w_v2, turned(w_v2, "core", 1))
 
-    hidden, hidden_slope = block_forward(token_rows, full_in)
-    own_target, hidden = lax.optimization_barrier((target[0], hidden))
+    hidden, hidden_slope = block_forward(at, token_rows, full_in)
     goals = lax.all_gather(own_target, IMAGE, axis=0)
     goal = lax.dynamic_slice(goals, (my_slot, near * mine, 0), (1, mine, goals.shape[2]))[0]
     goal = goal.astype(F32)
-    kept_rows = lax.dynamic_index_in_dim(token_rows, far, 0, keepdims=False)
-    far_rows = lax.dynamic_index_in_dim(token_rows, 1 - far, 0, keepdims=False)
-    far_rows, hidden_slope = lax.optimization_barrier((far_rows, hidden_slope))
-    far_rows = turned(far_rows, "far", 1)
     far_slope = turned(hidden_slope, "far", 1)
     far_through = turned(through, "far", 1)
-    n_mp = n_y * n_core
-    own_part = matmul(noise_rows, w_final).reshape(1, n_near, mine, lat)
-    here = (lax.iota(jnp.int32, n_mp) == lax.axis_index(("y", "core")))[:, None]
-    here = here & (lax.iota(jnp.int32, n_near) == near)[None]
-    latent_part = matmul(hidden, through).reshape(n_mp, n_near, mine, lat)
-    latent_part = (latent_part + jnp.where(here[:, :, None, None], own_part, 0.0)).astype(BF16)
-    latent_part = latent_part.reshape(n_y, n_core, n_near, mine, lat).transpose(2, 1, 0, 3, 4)
-    latent_part = jnp.broadcast_to(latent_part[:, None], (n_near, n_y) + latent_part.shape[1:])
-    latent_parts = exchanged(latent_part.reshape(n_tokens, n_y * mine, lat), TOKENS_AT)
-    latents = jnp.sum(latent_parts.astype(F32), axis=0).astype(BF16)
-    my_y = lax.axis_index("y")
-    latent = jnp.concatenate(
-        [
-            lax.dynamic_slice_in_dim(latents, (my_y - step) % n_y * mine, mine, 0)
-            for step in range(n_y)
-        ]
-    )
-
-    patch_rows, embedded, dec_slope = decode(latent, w_dec1, w_dec2, w_patch, mine)
+    own_part = matmul(noise_rows, w_final)
+    shape = (n_near, n_y, n_core, n_y // 2, mine, 2 * lat)
+    latent_part = latent_parts_of(at, hidden, through, own_part, shape)
+    latent_parts = exchanged(latent_part.reshape(n_tokens, n_y // 2, mine, 2 * lat), TOKENS_AT)
+
+    patch_rows, embedded, dec_slope = decode(at, latent_parts, w_dec1, w_dec2, w_patch, mine)
     *slopes, vit_part = reward(patch_rows, v1_both, v2_both)
     vit_out = summed_back(jnp.split(vit_part, n_y), "y")
     feature_grad = ((embedded + vit_out - goal) * scale).astype(BF16)
+    feature_grad, far_slope, far_through = lax.optimization_barrier(
+        (feature_grad, far_slope, far_through)
+    )
 
     grad_rows = jnp.concatenate(from_all(feature_grad, "y"))
     norm_part = reward(grad_rows, v1_both, v2_both, slopes)
@@ -387,20 +515,22 @@
     dec_pre_grad = (dec_slope * matmul_nt(pixel_grad, w_dec2)).astype(BF16)
     latent_grad = matmul_nt(dec_pre_grad, w_dec1).astype(BF16)
 
-    spread = jnp.broadcast_to(latent_grad, (n_far * n_tokens, mine, lat))
+    latent_grad = jnp.pad(latent_grad, ((0, 0), (0, lanes(lat) - lat)))
+    spread = jnp.broadcast_to(latent_grad, (n_far * n_tokens,) + latent_grad.shape)
     spread = exchanged(spread, ("far",) + TOKENS_AT)
-    spread = spread.reshape(n_far, n_near, n_y * n_core, mine, lat)
-    spread = jnp.moveaxis(spread, 1, 2).reshape(n_far, rows, lat)
-    latent_rows = lax.dynamic_index_in_dim(spread, far, 0, keepdims=False)
-    far_latent_rows = lax.dynamic_index_in_dim(spread, 1 - far, 0, keepdims=False)
-
-    inner = matmul_tn(latent_rows, hidden).astype(BF16)
+    spread = spread.reshape((n_far, n_near, n_y * n_core) + latent_grad.shape)
+
+    latent_rows, far_latent_rows, inner = inner_products(at, spread, hidden, lat)
     far_inner = turned(inner, "far", 1)
     term_in = block_backward(
-        (
-            (latent_rows, through, hidden_slope, kept_rows),
-            (far_latent_rows, far_through, far_slope, far_rows),
-        )
+        latent_rows,
+        through,
+        hidden_slope,
+        token_rows,
+        far_latent_rows,
+        far_through,
+        far_slope,
+        far_rows,
     )
     both = jnp.concatenate([inner, far_inner])
     both = jnp.broadcast_to(both, (n_near * n_z,) + both.shape)
@@ -409,9 +539,9 @@
     grad_in = jnp.sum(came[:, :, :d_dev].astype(F32), axis=1)
     grad_in = jnp.moveaxis(grad_in, 0, 1).reshape(d_dev, ff_mp)
 
-    at = lax.axis_index(ROWS_AT) * d_dev
-    my_final = lax.dynamic_slice_in_dim(w_final, at, d_dev, 0).astype(F32)
-    my_gates = lax.dynamic_slice_in_dim(gates, at, d_dev, 1).reshape(n_z, n_far, d_dev)
+    first = lax.axis_index(ROWS_AT) * d_dev
+    my_final = lax.dynamic_slice_in_dim(w_final, first, d_dev, 0).astype(F32)
+    my_gates = lax.dynamic_slice_in_dim(gates, first, d_dev, 1).reshape(n_z, n_far, d_dev)
     my_gates = jnp.where(far == 0, my_gates, my_gates[:, ::-1])
     my_gated = my_gates.reshape(n_images, d_dev).T[:, :, None] * my_final[:, None, :]
     my_gated = my_gated.astype(BF16).reshape(d_dev, n_images * lat)

time: 315 us -> 277 us (0.88)
  local copies, waits for them, and re-layouts: 68.6 us -> 30.6 us
  blocking collectives: 0 us -> 36.9 us
  starting transfers between devices: 58.5 us -> 38.9 us
  waiting for transfers between devices: 119 us -> 103 us
  Pallas kernels: 26.4 us -> 31.4 us
  matrix products: 8.1 us -> 4.81 us
    all_to_all x0 -> x2, blocking collectives: none -> 36.9 us  [exchanged(): return lax.all_to_all(blocks, axis, 0, 0, tiled=True)]
    all_to_all x6 -> x4, starting transfers between devices: 35.3 us -> 17.1 us  [exchanged(): return lax.all_to_all(blocks, axis, 0, 0, tiled=True)]
    ppermute x15, waiting for transfers between devices: 34.5 us -> 21.8 us  [turned(): lax.ppermute(value, axis, [(at, (at + steps) % count) for at in range(cou...]
    unnamed x59 -> x57, local copies, waits for them, and re-layouts: 23.2 us -> 14.8 us
    dynamic_slice x6 -> x1, local copies, waits for them, and re-layouts: 6.76 us -> 0.79 us  [on_device(): lax.dynamic_slice_in_dim(gates, first, d_dev, 1).reshape(n_z, n_far, d_dev)]
    pallas_call x5 -> x7, Pallas kernels: 26.4 us -> 31.4 us  [call(): pl.pallas_call(kernel, grid=(grid,), in_specs=in_specs, out_specs=out_spe...]
    ppermute x2 -> x0, local copies, waits for them, and re-layouts: 4.88 us -> none  [turned(): lax.ppermute(value, axis, [(at, (at + steps) % count) for at in range(cou...]
    reshape x7 -> x4, local copies, waits for them, and re-layouts: 4.54 us -> 0.37 us  [the longest x2 0.22 us: on_device(): through = exchanged(through, IMAGE).reshape(half, lat)]
  transfers between devices with their start and end apart: 23 -> 22, of which waited for: 11 -> 13; matrix products, arithmetic and copies ran while one was open for 17% -> 6% of each run, Pallas kernels for 9% -> 11%
where the time goes in v5:
time: 277 us; the launch traced here: 274 us
  waiting for transfers between devices  103 us (37%)
  starting transfers between devices  38.9 us (14%)
  blocking collectives  36.9 us (13%)
  Pallas kernels  31.4 us (11%)
  local copies, waits for them, and re-layouts  30.6 us (11%)
  between operations  16.9 us (6%)
  other arithmetic  11.3 us (4%)
  matrix products  4.81 us (2%)
    all_to_all x4, waiting for transfers between devices, exchanged(): return lax.all_to_all(blocks, axis, 0, 0, tiled=True)  81.3 us
    all_to_all x2, blocking collectives, exchanged(): return lax.all_to_all(blocks, axis, 0, 0, tiled=True)  36.9 us
    pallas_call x7, Pallas kernels, call(): pl.pallas_call(kernel, grid=(grid,), in_specs=in_specs, out_specs=out_spe...  31.4 us
    ppermute x15, waiting for transfers between devices, turned(): lax.ppermute(value, axis, [(at, (at + steps) % count) for at in range(cou...  21.8 us
    ppermute x15, starting transfers between devices, turned(): lax.ppermute(value, axis, [(at, (at + steps) % count) for at in range(cou...  21.7 us
    all_to_all x4, starting transfers between devices, exchanged(): return lax.all_to_all(blocks, axis, 0, 0, tiled=True)  17.1 us
    unnamed x57, local copies, waits for them, and re-layouts  14.8 us
  transfers between devices with their start and end apart: 22, of which 13 were waited for; matrix products, arithmetic and copies ran while one was open for 6% of the time, Pallas kernels for 11%

profile of v5, /device:TPU:8, one launch (start us, length us, event | category | flops | bytes accessed | tf_op | source)
XLA Modules:
  0.0 274.0 jit_solution(13344543019920994325)
XLA Ops:
  7.2 2.1 reshape.157
  16.3 2.0 broadcast_in_dim.10
  18.5 20.7 %all_to_all.30 = bf16[16,160,76]{2,1,0:T(8,128)(2,1)S(1)} all-to-all(bf16[16,160,76]{2,1,0:T(8,128)(2,1)S(1)} %copy.56), channel_id=1, replica_groups=mesh['near'=2,'z'=4,'far'=2,'y'=4,'core'=2] {'near','z','far'}, dimensions={0} | all-to-all | bytes 778240 | tf_op jit(solution)/shard_map/all_to_all | solution.py:80
  39.2 4.7 %all-to-all-start.1 = ((bf16[16,152,608]{2,1,0:T(8,128)(2,1)}), bf16[16,152,608]{2,1,0:T(8,128)(2,1)}, u32[]{:S(2)}, u32[]{:S(2)}) async-start(bf16[16,152,608]{2,1,0:T(8,128)(2,1)} %bitcast.63), calls=%async_computation.1 | async-start | bytes 6225920 | tf_op jit(solution)/shard_map/all_to_all | solution.py:80
  47.3 37.6 %all-to-all-done.1 = bf16[16,152,608]{2,1,0:T(8,128)(2,1)} async-done(((bf16[16,152,608]{2,1,0:T(8,128)(2,1)}), bf16[16,152,608]{2,1,0:T(8,128)(2,1)}, u32[]{:S(2)}, u32[]{:S(2)}) %all-to-all-start.1) | async-done | bytes 2957344 | tf_op jit(solution)/shard_map/all_to_all | solution.py:80
  86.7 3.9 %all-to-all-start.2 = ((bf16[8,76,64]{1,2,0:T(8,128)(2,1)}), bf16[8,76,64]{1,2,0:T(8,128)(2,1)S(1)}, u32[]{:S(2)}, u32[]{:S(2)}) async-start(bf16[8,76,64]{1,2,0:T(8,128)(2,1)} %copy.58), calls=%async_computation.2 | async-start | bytes 262144 | tf_op jit(solution)/shard_map/all_to_all | solution.py:80
  91.3 7.6 %all-to-all-done.2 = bf16[8,76,64]{1,2,0:T(8,128)(2,1)S(1)} async-done(((bf16[8,76,64]{1,2,0:T(8,128)(2,1)}), bf16[8,76,64]{1,2,0:T(8,128)(2,1)S(1)}, u32[]{:S(2)}, u32[]{:S(2)}) %all-to-all-start.2) | async-done | bytes 77856 | tf_op jit(solution)/shard_map/all_to_all | solution.py:80
  99.2 8.0 %shard_map.140 = (bf16[768,608]{1,0:T(8,128)(2,1)}, bf16[768,640]{1,0:T(8,128)(2,1)}) custom-call(s32[4]{0:T(128)} %pad_add_fusion.at, bf16[2,768,1216]{2,1,0:T(8,128)(2,1)} %all-gather.5.cloned.1.call-done.tokens, bf16[2,1216,608]{2,1,0:T(8,128)(2,1)} %bitcast.17.weights), custom_call_target="tpu_custom_call" | custom-call | flops 2271215616 | bytes 8560640 | tf_op jit(solution)/shard_map/pallas_call | solution.py:95
  110.3 4.9 %all-to-all-start.3 = ((bf16[16,2,48,128]{3,2,1,0:T(8,128)(2,1)}), bf16[16,2,48,128]{3,2,1,0:T(8,128)(2,1)S(1)}, u32[]{:S(2)}, u32[]{:S(2)}) async-start(bf16[16,2,48,128]{3,2,1,0:T(8,128)(2,1)} %bitcast.57), calls=%async_computation.3 | async-start | bytes 786432 | tf_op jit(solution)/shard_map/all_to_all | solution.py:80
  115.2 1.7 slice_bitcast_fusion
  117.5 2.9 %collective-permute-start.5 = (bf16[768,640]{1,0:T(8,128)(2,1)}, bf16[768,640]{1,0:T(8,128)(2,1)}, u32[]{:S(2)}, u32[]{:S(2)}) collective-permute-start(bf16[768,640]{1,0:T(8,128)(2,1)} %get-tuple-element.41.slope), channel_id=1, source_target_pairs={{0,8},{8,0},{1,9},{9,1},{2,10},{10,2},{3,11},{11,3},{4,12},{12,4},... | collective-permute-start | bytes 2949128 | tf_op jit(solution)/shard_map/ppermute | solution.py:64
  120.4 4.1 %all-to-all-done.3.parts = bf16[16,2,48,128]{3,2,1,0:T(8,128)(2,1)S(1)} async-done(((bf16[16,2,48,128]{3,2,1,0:T(8,128)(2,1)}), bf16[16,2,48,128]{3,2,1,0:T(8,128)(2,1)S(1)}, u32[]{:S(2)}, u32[]{:S(2)}) %all-to-all-start.3) | async-done | bytes 393248 | tf_op jit(solution)/shard_map/all_to_all | solution.py:80
  125.2 1.5 copy-done.1
  128.7 3.7 %shard_map.142 = (bf16[192,1280]{1,0:T(8,128)(2,1)S(1)}, f32[48,1280]{1,0:T(8,128)S(1)}, f32[48,2048]{1,0:T(8,128)S(1)}) custom-call(s32[4]{0:T(128)S(1)} %copy-done.19, bf16[16,2,48,128]{3,2,1,0:T(8,128)(2,1)S(1)} %copy-done.6, bf16[64,2048]{1,0:T(8,128)(2,1)S(1)} %copy-done.10, bf16[2048,768]{1,0:T(8,128)(2,1)S(1)} %copy-done, bf16[768,1280]{1,0:T(8,128)(2,1)S(1)} %copy-done.1), custom_call_target="tpu_custom_call" | custom-call | flops 1031798784 | bytes 5111808 | tf_op jit(solution)/shard_map/pallas_call | solution.py:95
  133.2 5.0 %shard_map.143 = (f32[192,640]{1,0:T(8,128)S(1)}, f32[192,640]{1,0:T(8,128)S(1)}, bf16[192,1280]{1,0:T(8,128)(2,1)S(1)}) custom-call(bf16[192,1280]{1,0:T(8,128)(2,1)S(1)} %get-tuple-element.38.normed, bf16[1280,640]{1,0:T(8,128)(2,1)} %v1a.3, bf16[1280,640]{1,0:T(8,128)(2,1)} %collective-permute-done.v1b, bf16[640,1280]{1,0:T(8,128)(2,1)} %v2a.3, ...), custom_call_target="tpu_custom_call" | custom-call | flops 1258291200 | bytes 6553600 | tf_op jit(solution)/shard_map/pallas_call | solution.py:95
  141.3 1.6 collective-permute-start.4
  142.9 5.0 %collective-permute-start.3 = (bf16[48,1280]{1,0:T(8,128)(2,1)}, bf16[48,1280]{1,0:T(8,128)(2,1)}, u32[]{:S(2)}, u32[]{:S(2)}) collective-permute-start(bf16[48,1280]{1,0:T(8,128)(2,1)} %get-tuple-element.63), channel_id=1, source_target_pairs={{0,4},{2,6},{4,0},{6,2},{1,5},{3,7},{5,1},{7,3},{8,12},{10,14},{12... | collective-permute-start | bytes 368648 | tf_op jit(solution)/shard_map/ppermute | solution.py:64
  150.8 1.6 collective-permute-done.3
  155.1 6.5 %collective-permute-done.6.through2 = bf16[608,64]{1,0:T(8,128)(2,1)} collective-permute-done((bf16[608,64]{1,0:T(8,128)(2,1)S(1)}, bf16[608,64]{1,0:T(8,128)(2,1)}, u32[]{:S(2)}, u32[]{:S(2)}) %collective-permute-start.6) | collective-permute-done | bytes 77856 | tf_op jit(solution)/shard_map/ppermute | solution.py:64
  161.9 2.6 collective-permute-start.8
  164.5 1.8 collective-permute-start.7
  166.2 4.0 %collective-permute-done.9 = bf16[48,1280]{1,0:T(8,128)(2,1)S(1)} collective-permute-done((bf16[48,1280]{1,0:T(8,128)(2,1)S(1)}, bf16[48,1280]{1,0:T(8,128)(2,1)S(1)}, u32[]{:S(2)}, u32[]{:S(2)}) %collective-permute-start.9) | collective-permute-done | bytes 122912 | tf_op jit(solution)/shard_map/ppermute | solution.py:64
  170.2 2.7 collective-permute-done.8
  173.2 5.4 %shard_map.144 = bf16[192,1280]{1,0:T(8,128)(2,1)S(1)} custom-call(bf16[192,1280]{1,0:T(8,128)(2,1)S(1)} %pad_maximum_fusion.2.grad, bf16[1280,640]{1,0:T(8,128)(2,1)} %v1a.3, bf16[1280,640]{1,0:T(8,128)(2,1)} %collective-permute-done.v1b, bf16[640,1280]{1,0:T(8,128)(2,1)} %v2a.3, bf16[640,1280]{1,0:T(8,128)(2,1)} %collective-permute-done.1.v2b, ...), custom_call_target="tpu_custom_call" | custom-call | flops 1258291200 | bytes 6553600 | tf_op jit(solution)/shard_map/pallas_call | solution.py:95
  180.1 2.6 collective-permute-start.11
  184.5 3.2 %collective-permute-done.11 = bf16[48,1280]{1,0:T(8,128)(2,1)S(1)} collective-permute-done((bf16[48,1280]{1,0:T(8,128)(2,1)S(1)}, bf16[48,1280]{1,0:T(8,128)(2,1)S(1)}, u32[]{:S(2)}, u32[]{:S(2)}) %collective-permute-start.11) | collective-permute-done | bytes 122912 | tf_op jit(solution)/shard_map/ppermute | solution.py:64
  190.1 2.3 fusion.8
  192.5 16.2 %all_to_all.31 = bf16[32,48,128]{2,1,0:T(8,128)(2,1)S(1)} all-to-all(bf16[32,48,128]{2,1,0:T(8,128)(2,1)S(1)} %broadcast_in_dim.13), channel_id=1, replica_groups=mesh['near'=2,'z'=4,'far'=2,'y'=4,'core'=2] {'far','near','y','core'}, dimensions={0} | all-to-all | bytes 786432 | tf_op jit(solution)/shard_map/all_to_all | solution.py:80
  213.5 7.3 %shard_map.146 = bf16[1216,608]{1,0:T(8,128)(2,1)} custom-call(bf16[768,128]{1,0:T(8,128)(2,1)} %copy-done.17, bf16[608,64]{1,0:T(8,128)(2,1)} %copy-done.8, bf16[768,640]{1,0:T(8,128)(2,1)} %get-tuple-element.41.slope, bf16[2,768,1216]{2,1,0:T(8,128)(2,1)} %all-gather.5.cloned.1.call-done.tokens, bf16[768,128]{1,0:T(8,128)(2,1)} %copy-done.18, ...), custom_call_target="tpu_custom_call" | custom-call | flops 2271215616 | bytes 7081984 | tf_op jit(solution)/shard_map/pallas_call | solution.py:95
  222.2 1.8 pad_maximum_fusion
  224.0 3.6 %all-to-all-start.5 = ((bf16[8,280,608]{2,1,0:T(8,128)(2,1)}), bf16[8,280,608]{2,1,0:T(8,128)(2,1)S(1)}, u32[]{:S(2)}, u32[]{:S(2)}) async-start(bf16[8,280,608]{2,1,0:T(8,128)(2,1)} %pad_maximum_fusion), calls=%async_computation.5 | async-start | bytes 5734400 | tf_op jit(solution)/shard_map/all_to_all | solution.py:80
  230.8 31.9 %all-to-all-done.5 = bf16[8,280,608]{2,1,0:T(8,128)(2,1)S(1)} async-done(((bf16[8,280,608]{2,1,0:T(8,128)(2,1)}), bf16[8,280,608]{2,1,0:T(8,128)(2,1)S(1)}, u32[]{:S(2)}, u32[]{:S(2)}) %all-to-all-start.5) | async-done | bytes 2723872 | tf_op jit(solution)/shard_map/all_to_all | solution.py:80
  (145 shorter events, 46.7 us)
Async XLA Ops:
  7.2 92.0 %all-gather.5.cloned.1.call-start = ((), (), s32[]{:S(2)}) async-start(), calls=%async_computation.6 | async-start | bytes 4423680 | tf_op jit(solution)/shard_map/all_gather | solution.py:473
  39.1 4.8 %copy-start.22 = (bf16[16,160,76]{2,1,0:T(8,128)(2,1)}, bf16[16,160,76]{2,1,0:T(8,128)(2,1)S(1)}, u32[]{:S(2)}) copy-start(bf16[16,160,76]{2,1,0:T(8,128)(2,1)S(1)} %all_to_all.30) | copy-start | bytes 1167364
  39.1 4.7 %copy-start.24 = (bf16[2432,64]{0,1:T(8,128)(2,1)S(1)}, bf16[2432,64]{0,1:T(8,128)(2,1)}, u32[]{:S(2)}) copy-start(bf16[2432,64]{0,1:T(8,128)(2,1)} %param.20) | copy-start | bytes 933892
  39.2 45.8 %all-to-all-start.1 = ((bf16[16,152,608]{2,1,0:T(8,128)(2,1)}), bf16[16,152,608]{2,1,0:T(8,128)(2,1)}, u32[]{:S(2)}, u32[]{:S(2)}) async-start(bf16[16,152,608]{2,1,0:T(8,128)(2,1)} %bitcast.63), calls=%async_computation.1 | async-start | bytes 6225920 | tf_op jit(solution)/shard_map/all_to_all | solution.py:80
  43.8 107.0 %all-gather.9.cloned.1.call-start = ((), (), s32[]{:S(2)}) async-start(), calls=%async_computation.8 | async-start | bytes 2211840 | tf_op jit(solution)/shard_map/all_gather | solution.py:492
  85.0 48.2 %collective-permute-start = (bf16[1280,640]{1,0:T(8,128)(2,1)}, bf16[1280,640]{1,0:T(8,128)(2,1)}, u32[]{:S(2)}, u32[]{:S(2)}) collective-permute-start(bf16[1280,640]{1,0:T(8,128)(2,1)} %v1a.3), channel_id=1, source_target_pairs={{0,1},{1,0},{2,3},{3,2},{4,5},{5,4},{6,7},{7,6},{8,9},{9,8},{10,11... | collective-permute-start | bytes 4915208 | tf_op jit(solution)/shard_map/ppermute | solution.py:64
  85.1 48.1 %collective-permute-start.1 = (bf16[640,1280]{1,0:T(8,128)(2,1)}, bf16[640,1280]{1,0:T(8,128)(2,1)}, u32[]{:S(2)}, u32[]{:S(2)}) collective-permute-start(bf16[640,1280]{1,0:T(8,128)(2,1)} %v2a.3), channel_id=1, source_target_pairs={{0,1},{1,0},{2,3},{3,2},{4,5},{5,4},{6,7},{7,6},{8,9},{9,8},{10,11... | collective-permute-start | bytes 4915208 | tf_op jit(solution)/shard_map/ppermute | solution.py:64
  86.7 12.2 %all-to-all-start.2 = ((bf16[8,76,64]{1,2,0:T(8,128)(2,1)}), bf16[8,76,64]{1,2,0:T(8,128)(2,1)S(1)}, u32[]{:S(2)}, u32[]{:S(2)}) async-start(bf16[8,76,64]{1,2,0:T(8,128)(2,1)} %copy.58), calls=%async_computation.2 | async-start | bytes 262144 | tf_op jit(solution)/shard_map/all_to_all | solution.py:80
  99.1 8.1 %copy-start.8 = (bf16[608,64]{1,0:T(8,128)(2,1)}, bf16[608,64]{1,0:T(8,128)(2,1)S(1)}, u32[]{:S(2)}) copy-start(bf16[608,64]{1,0:T(8,128)(2,1)S(1)} %reshape.182.through) | copy-start | bytes 233476
  99.2 8.1 %copy-start.19 = (s32[4]{0:T(128)S(1)}, s32[4]{0:T(128)}, u32[]{:S(2)}) copy-start(s32[4]{0:T(128)} %pad_add_fusion.at) | copy-start | bytes 52
  99.2 26.1 %copy-start = (bf16[2048,768]{1,0:T(8,128)(2,1)S(1)}, bf16[2048,768]{1,0:T(8,128)(2,1)}, u32[]{:S(2)}) copy-start(bf16[2048,768]{1,0:T(8,128)(2,1)} %w_dec2.1) | copy-start | bytes 9437188
  110.3 14.2 %all-to-all-start.3 = ((bf16[16,2,48,128]{3,2,1,0:T(8,128)(2,1)}), bf16[16,2,48,128]{3,2,1,0:T(8,128)(2,1)S(1)}, u32[]{:S(2)}, u32[]{:S(2)}) async-start(bf16[16,2,48,128]{3,2,1,0:T(8,128)(2,1)} %bitcast.57), calls=%async_computation.3 | async-start | bytes 786432 | tf_op jit(solution)/shard_map/all_to_all | solution.py:80
  115.2 98.3 %all-gather.7.cloned.1.call-start = ((), (), s32[]{:S(2)}) async-start(), calls=%async_computation.7 | async-start | bytes 2211840 | tf_op jit(solution)/shard_map/all_gather | solution.py:474
  116.9 31.2 %collective-permute-start.13 = (bf16[96,1216]{1,0:T(8,128)(2,1)}, bf16[96,1216]{1,0:T(8,128)(2,1)}, u32[]{:S(2)}, u32[]{:S(2)}) collective-permute-start(bf16[96,1216]{1,0:T(8,128)(2,1)} %slice_bitcast_fusion), channel_id=1, source_target_pairs={{0,8},{8,0},{1,9},{9,1},{2,10},{10,2},{3,11},{11,3},{4,12},{12,4},... | collective-permute-start | bytes 700424 | tf_op jit(solution)/shard_map/ppermute | solution.py:64
  117.5 44.0 %collective-permute-start.5 = (bf16[768,640]{1,0:T(8,128)(2,1)}, bf16[768,640]{1,0:T(8,128)(2,1)}, u32[]{:S(2)}, u32[]{:S(2)}) collective-permute-start(bf16[768,640]{1,0:T(8,128)(2,1)} %get-tuple-element.41.slope), channel_id=1, source_target_pairs={{0,8},{8,0},{1,9},{9,1},{2,10},{10,2},{3,11},{11,3},{4,12},{12,4},... | collective-permute-start | bytes 2949128 | tf_op jit(solution)/shard_map/ppermute | solution.py:64
  133.2 14.9 %copy-start.27 = (s32[8]{0:T(128)S(1)}, s32[8]{0:T(128)}, u32[]{:S(2)}) copy-start(s32[8]{0:T(128)} %param.15) | copy-start | bytes 100
  133.2 17.5 %copy-start.9 = (bf16[608,64]{1,0:T(8,128)(2,1)S(1)}, bf16[608,64]{1,0:T(8,128)(2,1)}, u32[]{:S(2)}) copy-start(bf16[608,64]{1,0:T(8,128)(2,1)} %copy-done.8) | copy-start | bytes 233476
  141.3 9.5 %collective-permute-start.4 = (bf16[48,1280]{1,0:T(8,128)(2,1)}, bf16[48,1280]{1,0:T(8,128)(2,1)}, u32[]{:S(2)}, u32[]{:S(2)}) collective-permute-start(bf16[48,1280]{1,0:T(8,128)(2,1)} %get-tuple-element.62), channel_id=1, source_target_pairs={{0,2},{2,4},{4,6},{6,0},{1,3},{3,5},{5,7},{7,1},{8,10},{10,12},{12... | collective-permute-start | bytes 368648 | tf_op jit(solution)/shard_map/ppermute | solution.py:64
  142.9 9.5 %collective-permute-start.3 = (bf16[48,1280]{1,0:T(8,128)(2,1)}, bf16[48,1280]{1,0:T(8,128)(2,1)}, u32[]{:S(2)}, u32[]{:S(2)}) collective-permute-start(bf16[48,1280]{1,0:T(8,128)(2,1)} %get-tuple-element.63), channel_id=1, source_target_pairs={{0,4},{2,6},{4,0},{6,2},{1,5},{3,7},{5,1},{7,3},{8,12},{10,14},{12... | collective-permute-start | bytes 368648 | tf_op jit(solution)/shard_map/ppermute | solution.py:64
  148.0 5.8 %collective-permute-start.2 = (bf16[48,1280]{1,0:T(8,128)(2,1)}, bf16[48,1280]{1,0:T(8,128)(2,1)}, u32[]{:S(2)}, u32[]{:S(2)}) collective-permute-start(bf16[48,1280]{1,0:T(8,128)(2,1)} %get-tuple-element.61), channel_id=1, source_target_pairs={{0,6},{2,0},{4,2},{6,4},{1,7},{3,1},{5,3},{7,5},{8,14},{10,8},{12,... | collective-permute-start | bytes 368648 | tf_op jit(solution)/shard_map/ppermute | solution.py:64
  150.7 10.9 %collective-permute-start.6 = (bf16[608,64]{1,0:T(8,128)(2,1)S(1)}, bf16[608,64]{1,0:T(8,128)(2,1)}, u32[]{:S(2)}, u32[]{:S(2)}) collective-permute-start(bf16[608,64]{1,0:T(8,128)(2,1)S(1)} %copy-done.9), channel_id=1, source_target_pairs={{0,8},{8,0},{1,9},{9,1},{2,10},{10,2},{3,11},{11,3},{4,12},{12,4},... | collective-permute-start | bytes 233480 | tf_op jit(solution)/shard_map/ppermute | solution.py:64
  150.8 22.4 %copy-start.12 = (f32[192,640]{1,0:T(8,128)S(1)}, f32[192,640]{1,0:T(8,128)}, u32[]{:S(2)}) copy-start(f32[192,640]{1,0:T(8,128)} %copy-done.11) | copy-start | bytes 1474564
  150.8 22.4 %copy-start.14 = (f32[192,640]{1,0:T(8,128)S(1)}, f32[192,640]{1,0:T(8,128)}, u32[]{:S(2)}) copy-start(f32[192,640]{1,0:T(8,128)} %copy-done.13) | copy-start | bytes 1474564
  161.5 8.7 %collective-permute-start.9 = (bf16[48,1280]{1,0:T(8,128)(2,1)S(1)}, bf16[48,1280]{1,0:T(8,128)(2,1)S(1)}, u32[]{:S(2)}, u32[]{:S(2)}) collective-permute-start(bf16[48,1280]{1,0:T(8,128)(2,1)S(1)} %get-tuple-element.42), channel_id=1, source_target_pairs={{0,6},{2,0},{4,2},{6,4},{1,7},{3,1},{5,3},{7,5},{8,14},{10,8},{12,... | collective-permute-start | bytes 368648 | tf_op jit(solution)/shard_map/ppermute | solution.py:64
  161.9 11.0 %collective-permute-start.8 = (bf16[48,1280]{1,0:T(8,128)(2,1)S(1)}, bf16[48,1280]{1,0:T(8,128)(2,1)S(1)}, u32[]{:S(2)}, u32[]{:S(2)}) collective-permute-start(bf16[48,1280]{1,0:T(8,128)(2,1)S(1)} %get-tuple-element.42), channel_id=1, source_target_pairs={{0,4},{2,6},{4,0},{6,2},{1,5},{3,7},{5,1},{7,3},{8,12},{10,14},{12... | collective-permute-start | bytes 368648 | tf_op jit(solution)/shard_map/ppermute | solution.py:64
  164.5 8.7 %collective-permute-start.7 = (bf16[48,1280]{1,0:T(8,128)(2,1)S(1)}, bf16[48,1280]{1,0:T(8,128)(2,1)S(1)}, u32[]{:S(2)}, u32[]{:S(2)}) collective-permute-start(bf16[48,1280]{1,0:T(8,128)(2,1)S(1)} %get-tuple-element.42), channel_id=1, source_target_pairs={{0,2},{2,4},{4,6},{6,0},{1,3},{3,5},{5,7},{7,1},{8,10},{10,12},{12... | collective-permute-start | bytes 368648 | tf_op jit(solution)/shard_map/ppermute | solution.py:64
  178.6 10.8 %copy-start.2 = (bf16[768,1280]{1,0:T(8,128)(2,1)S(1)}, bf16[768,1280]{1,0:T(8,128)(2,1)}, u32[]{:S(2)}) copy-start(bf16[768,1280]{1,0:T(8,128)(2,1)} %w_patch.1) | copy-start | bytes 5898244
  178.7 5.8 %collective-permute-start.12 = (bf16[48,1280]{1,0:T(8,128)(2,1)S(1)}, bf16[48,1280]{1,0:T(8,128)(2,1)S(1)}, u32[]{:S(2)}, u32[]{:S(2)}) collective-permute-start(bf16[48,1280]{1,0:T(8,128)(2,1)S(1)} %get-tuple-element.59), channel_id=1, source_target_pairs={{0,2},{2,4},{4,6},{6,0},{1,3},{3,5},{5,7},{7,1},{8,10},{10,12},{12... | collective-permute-start | bytes 368648 | tf_op jit(solution)/shard_map/ppermute | solution.py:64
  180.1 7.6 %collective-permute-start.11 = (bf16[48,1280]{1,0:T(8,128)(2,1)S(1)}, bf16[48,1280]{1,0:T(8,128)(2,1)S(1)}, u32[]{:S(2)}, u32[]{:S(2)}) collective-permute-start(bf16[48,1280]{1,0:T(8,128)(2,1)S(1)} %get-tuple-element.60), channel_id=1, source_target_pairs={{0,4},{2,6},{4,0},{6,2},{1,5},{3,7},{5,1},{7,3},{8,12},{10,14},{12... | collective-permute-start | bytes 368648 | tf_op jit(solution)/shard_map/ppermute | solution.py:64
  182.7 6.3 %collective-permute-start.10 = (bf16[48,1280]{1,0:T(8,128)(2,1)S(1)}, bf16[48,1280]{1,0:T(8,128)(2,1)S(1)}, u32[]{:S(2)}, u32[]{:S(2)}) collective-permute-start(bf16[48,1280]{1,0:T(8,128)(2,1)S(1)} %get-tuple-element.58), channel_id=1, source_target_pairs={{0,6},{2,0},{4,2},{6,4},{1,7},{3,1},{5,3},{7,5},{8,14},{10,8},{12,... | collective-permute-start | bytes 368648 | tf_op jit(solution)/shard_map/ppermute | solution.py:64
  212.2 8.6 %collective-permute-start.14 = (bf16[64,608]{1,0:T(8,128)(2,1)S(1)}, bf16[64,608]{1,0:T(8,128)(2,1)S(1)}, u32[]{:S(2)}, u32[]{:S(2)}) collective-permute-start(bf16[64,608]{1,0:T(8,128)(2,1)S(1)} %get-tuple-element.49), channel_id=1, source_target_pairs={{0,8},{8,0},{1,9},{9,1},{2,10},{10,2},{3,11},{11,3},{4,12},{12,4},... | collective-permute-start | bytes 233480 | tf_op jit(solution)/shard_map/ppermute | solution.py:64
  224.0 38.7 %all-to-all-start.5 = ((bf16[8,280,608]{2,1,0:T(8,128)(2,1)}), bf16[8,280,608]{2,1,0:T(8,128)(2,1)S(1)}, u32[]{:S(2)}, u32[]{:S(2)}) async-start(bf16[8,280,608]{2,1,0:T(8,128)(2,1)} %pad_maximum_fusion), calls=%async_computation.5 | async-start | bytes 5734400 | tf_op jit(solution)/shard_map/all_to_all | solution.py:80
  (19 other events, 22.4 us)
Sparse Core Ops, SparseCore 0:
  18.4 32.2 all-gather.4
  85.1 62.2 all-gather.8
  149.1 23.6 all-gather.6

commit v6 on v5

--- a/solution.py
+++ b/solution.py
@@ -145,10 +145,45 @@
     )
 
 
-def latent_kernel(at, hidden, through, own_part, out, total):
+def through_kernel(w_out, gated, out):
+    n_near, n_images, part, _ = out.shape
+    lat = gated.shape[1] // n_images
+    total = matmul_tn(w_out[...], gated[...]).astype(BF16)
+    for near in range(n_near):
+        for image in range(n_images):
+            for side in range(2):
+                start = (2 * near + side) * part
+                block = total[start : start + part, image * lat : (image + 1) * lat]
+                out[near, image, :, side * lat : (side + 1) * lat] = block
+
+
+def through_terms(w_out, gated, n_near, n_images):
+    rows, columns = w_out.shape
+    shape = (n_near, n_images, columns // (2 * n_near), 2 * gated.shape[1] // n_images)
+    return call(
+        through_kernel,
+        1,
+        [whole(w_out), whole(gated)],
+        pl.BlockSpec(shape, lambda step: (0,) * len(shape)),
+        jax.ShapeDtypeStruct(shape, BF16),
+        [],
+        2 * rows * columns * gated.shape[1],
+        2 * rows * columns,
+        LARGE,
+        w_out,
+        gated,
+    )
+
+
+def latent_kernel(at, hidden, terms, own_part, out, through, total):
     n_near, n_y, n_core, _, mine, _ = out.shape
-    lat = through.shape[1]
+    part, lat = terms.shape[1], through.shape[1]
     near, place = at[1], at[2]
+    added = terms[0].astype(F32)
+    for source in range(1, terms.shape[0]):
+        added = added + terms[source].astype(F32)
+    through[:part] = added[:, :lat].astype(BF16)
+    through[part:] = added[:, lat:].astype(BF16)
     total[...] = matmul(hidden[...], through[...])
     rows = pl.ds(pl.multiple_of((place * n_near + near) * mine, mine), mine)
     total[rows] += own_part[pl.ds(pl.multiple_of(near * mine, mine), mine)]
@@ -161,22 +196,25 @@
                     out[side, other, core, y // 2, :, y % 2 * lat : (y % 2 + 1) * lat] = block
 
 
-def latent_parts_of(at, hidden, through, own_part, shape):
+def latent_parts_of(at, hidden, terms, own_part, shape):
     rows, columns = hidden.shape
-    lat = through.shape[1]
+    lat = terms.shape[2] // 2
     return call(
         latent_kernel,
         1,
-        [SCALARS, whole(hidden), whole(through), whole(own_part)],
-        pl.BlockSpec(shape, lambda step: (0,) * len(shape)),
-        jax.ShapeDtypeStruct(shape, BF16),
+        [SCALARS, whole(hidden), whole(terms), whole(own_part)],
+        [
+            pl.BlockSpec(shape, lambda step: (0,) * len(shape)),
+            pl.BlockSpec((columns, lat), lambda step: (0, 0)),
+        ],
+        [jax.ShapeDtypeStruct(shape, BF16), jax.ShapeDtypeStruct((columns, lat), BF16)],
         [pltpu.VMEM((rows, lat), F32)],
         2 * rows * columns * lat,
         2 * rows * columns,
-        SMALL,
+        LARGE,
         at,
         hidden,
-        through,
+        terms,
         own_part,
     )
 
@@ -439,7 +477,6 @@
     d_dev, ff_mp = w_in.shape
     width_d = d_dev * n_rows
     half = ff_mp // n_near
-    strip = ff_mp // n_rows
     lat = w_final.shape[1]
     scale = 1.0 / math.sqrt(n_images * rows)
     near = lax.axis_index("near")
@@ -452,16 +489,19 @@
 
     at = jnp.stack([far, near, lax.axis_index(("y", "core")), lax.axis_index("y")]).astype(jnp.int32)
 
-    strips = jnp.moveaxis(w_out_t.reshape(d_dev, n_rows, strip), 1, 0)
-    steps_row = jnp.broadcast_to(timestep[0].astype(BF16), (n_rows, 8, strip))
-    strips = jnp.concatenate([strips, steps_row], axis=1)
-    strips, w_in, noise_rows = lax.optimization_barrier((strips, w_in, latent_noise[0]))
-    arrived = exchanged(strips, ROWS_AT)
+    turned_steps = from_all(timestep, IMAGE)
+    images = lax.iota(jnp.int32, n_images)
+    all_steps = jnp.zeros_like(images)
+    for step, value in enumerate(turned_steps):
+        all_steps = jnp.where(images == (my_image - step) % n_images, value[0], all_steps)
 
     split_in = jnp.moveaxis(w_in.reshape(d_dev, n_near, half), 1, 0)
     split_in = jnp.broadcast_to(split_in[None, :, None], (n_far, n_near, n_z, d_dev, half))
     split_in = split_in.reshape(n_rows, d_dev, half)
-
+    split_in, all_steps = lax.optimization_barrier((split_in, all_steps))
+    full_in = exchanged(split_in, FAR_FIRST).reshape(n_far, wide, half)
+
+    noise_rows = latent_noise[0]
     modulate = modulation[timestep[0]]
     modulated = (
         layer_norm(noise_rows.astype(F32)) * (1.0 + modulate[1]) + modulate[0]
@@ -469,47 +509,50 @@
     modulated = modulated.reshape(tok_dev, n_rows // n_far, n_far, d_dev)
     modulated = jnp.moveaxis(modulated, 2, 0).reshape(n_far, tok_dev, wide)
     modulated = jnp.where(far == 0, modulated, modulated[::-1])
-    modulated, split_in = lax.optimization_barrier((modulated, split_in))
     token_rows = lax.all_gather(modulated, ("y", "core"), axis=1, tiled=True)
     far_rows = lax.all_gather(turned(modulated[1], "far", 1), ("y", "core"), axis=0, tiled=True)
 
-    arrived, split_in = lax.optimization_barrier((arrived, split_in))
-    full_in = exchanged(split_in, FAR_FIRST).reshape(n_far, wide, half)
-
-    strip_rows = arrived[:, :d_dev].reshape(width_d, strip)
-    all_steps = arrived[:n_images, d_dev, 0].astype(jnp.int32)
-    gates = modulation[all_steps, 2]
-    gated_final = (gates.T[:, :, None] * w_final.astype(F32)[:, None, :]).astype(BF16)
-    through = matmul_tn(strip_rows, gated_final.reshape(width_d, n_images * lat)).astype(BF16)
-    through = jnp.moveaxis(through.reshape(strip, n_images, lat), 1, 0)
-    through, full_in, own_target = lax.optimization_barrier((through, full_in, target[0]))
-    through = exchanged(through, IMAGE).reshape(half, lat)
+    first = lax.axis_index(ROWS_AT) * d_dev
+    my_final = lax.dynamic_slice_in_dim(w_final, first, d_dev, 0).astype(F32)
+    gates = jnp.stack(
+        [
+            lax.dynamic_slice(modulation, (all_steps[image], 2, first), (1, 1, d_dev))[0, 0]
+            for image in range(n_images)
+        ]
+    )
+    gated = (gates.T[:, :, None] * my_final[:, None, :]).astype(BF16)
+    terms = through_terms(w_out_t, gated.reshape(d_dev, n_images * lat), n_near, n_images)
+    terms = terms.reshape((n_rows,) + terms.shape[2:])
+    terms, full_in, own_target = lax.optimization_barrier((terms, full_in, target[0]))
+    terms = exchanged(terms, ROWS_AT)
 
     v1_both = (w_v1, turned(w_v1, "core", 1))
     v2_both = (w_v2, turned(w_v2, "core", 1))
 
     hidden, hidden_slope = block_forward(at, token_rows, full_in)
+    own_target = lax.dynamic_slice_in_dim(own_target, near * mine, mine, 0)
+    own_target = jnp.pad(own_target, ((0, mine // 6), (0, 0)))
     goals = lax.all_gather(own_target, IMAGE, axis=0)
-    goal = lax.dynamic_slice(goals, (my_slot, near * mine, 0), (1, mine, goals.shape[2]))[0]
+    goal = lax.dynamic_index_in_dim(goals, my_slot, 0, keepdims=False)[:mine]
     goal = goal.astype(F32)
     far_slope = turned(hidden_slope, "far", 1)
-    far_through = turned(through, "far", 1)
     own_part = matmul(noise_rows, w_final)
     shape = (n_near, n_y, n_core, n_y // 2, mine, 2 * lat)
-    latent_part = latent_parts_of(at, hidden, through, own_part, shape)
+    latent_part, through = latent_parts_of(at, hidden, terms, own_part, shape)
+    far_through = turned(through, "far", 1)
     latent_parts = exchanged(latent_part.reshape(n_tokens, n_y // 2, mine, 2 * lat), TOKENS_AT)
 
     patch_rows, embedded, dec_slope = decode(at, latent_parts, w_dec1, w_dec2, w_patch, mine)
     *slopes, vit_part = reward(patch_rows, v1_both, v2_both)
     vit_out = summed_back(jnp.split(vit_part, n_y), "y")
     feature_grad = ((embedded + vit_out - goal) * scale).astype(BF16)
-    feature_grad, far_slope, far_through = lax.optimization_barrier(
-        (feature_grad, far_slope, far_through)
-    )
 
     grad_rows = jnp.concatenate(from_all(feature_grad, "y"))
     norm_part = reward(grad_rows, v1_both, v2_both, slopes)
     norm_grad = summed_back(jnp.split(norm_part, n_y), "y")
+    norm_grad, far_slope, far_through = lax.optimization_barrier(
+        (norm_grad, far_slope, far_through)
+    )
     embed_grad = (feature_grad.astype(F32) + norm_back(embedded, norm_grad)).astype(BF16)
     pixel_grad = matmul_nt(embed_grad, w_patch).astype(BF16)
     dec_pre_grad = (dec_slope * matmul_nt(pixel_grad, w_dec2)).astype(BF16)
@@ -539,12 +582,8 @@
     grad_in = jnp.sum(came[:, :, :d_dev].astype(F32), axis=1)
     grad_in = jnp.moveaxis(grad_in, 0, 1).reshape(d_dev, ff_mp)
 
-    first = lax.axis_index(ROWS_AT) * d_dev
-    my_final = lax.dynamic_slice_in_dim(w_final, first, d_dev, 0).astype(F32)
-    my_gates = lax.dynamic_slice_in_dim(gates, first, d_dev, 1).reshape(n_z, n_far, d_dev)
-    my_gates = jnp.where(far == 0, my_gates, my_gates[:, ::-1])
-    my_gated = my_gates.reshape(n_images, d_dev).T[:, :, None] * my_final[:, None, :]
-    my_gated = my_gated.astype(BF16).reshape(d_dev, n_images * lat)
+    my_gated = gated.reshape(d_dev, n_z, n_far, lat)
+    my_gated = jnp.where(far == 0, my_gated, my_gated[:, :, ::-1]).reshape(d_dev, n_images * lat)
     outs = [
         matmul(my_gated, came[at_near, :, d_dev:].reshape(n_images * lat, half))
         for at_near in range(n_near)

time: 277 us -> 268 us (0.968)
  waiting for transfers between devices: 103 us -> 62.9 us
  between operations: 16.9 us -> 31.9 us
  starting transfers between devices: 38.9 us -> 53.7 us
  blocking collectives: 36.9 us -> 26.3 us
  other arithmetic: 11.3 us -> 19.4 us
  Pallas kernels: 31.4 us -> 37 us
  local copies, waits for them, and re-layouts: 30.6 us -> 27.7 us
    all_to_all x4 -> x3, waiting for transfers between devices: 81.3 us -> 47.6 us  [exchanged(): return lax.all_to_all(blocks, axis, 0, 0, tiled=True)]
    ppermute x15 -> x22, starting transfers between devices: 21.7 us -> 39.6 us  [turned(): lax.ppermute(value, axis, [(at, (at + steps) % count) for at in range(cou...]
    all_to_all x2, blocking collectives: 36.9 us -> 26.3 us  [exchanged(): return lax.all_to_all(blocks, axis, 0, 0, tiled=True)]
    ppermute x15 -> x22, waiting for transfers between devices: 21.8 us -> 15.1 us  [turned(): lax.ppermute(value, axis, [(at, (at + steps) % count) for at in range(cou...]
    select_n x1 -> x2, other arithmetic: 0.01 us -> 5.97 us  [the longest x1 4.48 us: on_device(): jnp.where(images == (my_image - step) % n_images, value[0], all_steps)]
    pallas_call x7 -> x8, Pallas kernels: 31.4 us -> 37 us  [call(): pl.pallas_call(kernel, grid=(grid,), in_specs=in_specs, out_specs=out_spe...]
    unnamed x57 -> x55, local copies, waits for them, and re-layouts: 14.8 us -> 9.27 us
    rev x1, local copies, waits for them, and re-layouts: 0.1 us -> 5.31 us  [on_device(): my_gated[:, :, ::-1]]
  transfers between devices with their start and end apart: 22 -> 28, of which waited for: 13 -> 10; matrix products, arithmetic and copies ran while one was open for 6% -> 12% of each run, Pallas kernels for 11% -> 14%
where the time goes in v6:
time: 268 us; the launch traced here: 265 us
  waiting for transfers between devices  62.9 us (23%)
  starting transfers between devices  53.7 us (20%)
  Pallas kernels  37 us (14%)
  between operations  31.9 us (12%)
  local copies, waits for them, and re-layouts  27.7 us (10%)
  blocking collectives  26.3 us (10%)
  other arithmetic  19.4 us (7%)
  matrix products  6.06 us (2%)
    all_to_all x3, waiting for transfers between devices, exchanged(): return lax.all_to_all(blocks, axis, 0, 0, tiled=True)  47.6 us
    ppermute x22, starting transfers between devices, turned(): lax.ppermute(value, axis, [(at, (at + steps) % count) for at in range(cou...  39.6 us
    pallas_call x8, Pallas kernels, call(): pl.pallas_call(kernel, grid=(grid,), in_specs=in_specs, out_specs=out_spe...  37 us
    all_to_all x2, blocking collectives, exchanged(): return lax.all_to_all(blocks, axis, 0, 0, tiled=True)  26.3 us
    ppermute x22, waiting for transfers between devices, turned(): lax.ppermute(value, axis, [(at, (at + steps) % count) for at in range(cou...  15.1 us
    all_to_all x3, starting transfers between devices, exchanged(): return lax.all_to_all(blocks, axis, 0, 0, tiled=True)  14 us
    unnamed x55, local copies, waits for them, and re-layouts  9.27 us
  transfers between devices with their start and end apart: 28, of which 10 were waited for; matrix products, arithmetic and copies ran while one was open for 12% of the time, Pallas kernels for 14%

profile of v6, /device:TPU:8, one launch (start us, length us, event | category | flops | bytes accessed | tf_op | source)
XLA Modules:
  0.0 265.0 jit_solution(18162304390580127661)
XLA Ops:
  14.1 3.1 %collective-permute-start.6 = (s32[1]{0:T(128)}, s32[1]{0:T(128)}, u32[]{:S(2)}, u32[]{:S(2)}) collective-permute-start(s32[1]{0:T(128)} %param.14), channel_id=1, source_target_pairs={{0,8},{8,16},{16,24},{24,32},{32,40},{40,48},{48,56},{56,0},{1,9},... | collective-permute-start | bytes 20 | tf_op jit(solution)/shard_map/ppermute | solution.py:64
  19.1 2.9 %collective-permute-start.4 = (s32[1]{0:T(128)}, s32[1]{0:T(128)}, u32[]{:S(2)}, u32[]{:S(2)}) collective-permute-start(s32[1]{0:T(128)} %param.14), channel_id=1, source_target_pairs={{0,24},{8,32},{16,40},{24,48},{32,56},{40,0},{48,8},{56,16},{1,25}... | collective-permute-start | bytes 20 | tf_op jit(solution)/shard_map/ppermute | solution.py:64
  23.2 5.4 %collective-permute-start.2 = (s32[1]{0:T(128)}, s32[1]{0:T(128)}, u32[]{:S(2)}, u32[]{:S(2)}) collective-permute-start(s32[1]{0:T(128)} %param.14), channel_id=1, source_target_pairs={{0,40},{8,48},{16,56},{24,0},{32,8},{40,16},{48,24},{56,32},{1,41}... | collective-permute-start | bytes 20 | tf_op jit(solution)/shard_map/ppermute | solution.py:64
  30.3 2.7 %collective-permute-done.1 = s32[1]{0:T(128)} collective-permute-done((s32[1]{0:T(128)}, s32[1]{0:T(128)}, u32[]{:S(2)}, u32[]{:S(2)}) %collective-permute-start.1) | collective-permute-done | bytes 36 | tf_op jit(solution)/shard_map/ppermute | solution.py:64
  33.0 2.4 collective-permute-done
  35.4 4.5 %compare_select_fusion.7 = s32[8]{0:T(128)S(1)} fusion(s32[]{:T(128)} %bitcast.82, s32[]{:T(128)S(6)} %select_n.134, s32[]{:T(128)} %bitcast.17, s32[]{:T(128)S(6)} %select_n.133, s32[]{:T(128)} %bitcast.16, s32[]{:T(128)S(6)} %select_n.132, s32[]{:T(128)} %bitcast.15, s32[]{:T(128)S(6)} %select_n.131, s32[]{:T(128)} %bitcast.14, s32[]{:T(128)S(6)} %select_n.130, ...), kind=kLoop, calls=%fused_computation.56 | loop fusion | flops 128 | bytes 96 | tf_op jit(solution)/shard_map/jit(_where)/select_n | solution.py:496
  41.9 4.6 %all-to-all-start = ((bf16[16,152,608]{2,1,0:T(8,128)(2,1)}), bf16[16,152,608]{2,1,0:T(8,128)(2,1)}, u32[]{:S(2)}, u32[]{:S(2)}) async-start(bf16[16,152,608]{2,1,0:T(8,128)(2,1)} %bitcast.10), calls=%async_computation | async-start | bytes 6225920 | tf_op jit(solution)/shard_map/all_to_all | solution.py:80
  64.6 3.2 %shard_map.140 = bf16[2,8,304,128]{3,2,1,0:T(8,128)(2,1)} custom-call(bf16[152,1216]{1,0:T(8,128)(2,1)} %w_out.1, bf16[152,512]{1,0:T(8,128)(2,1)} %convert_element_type.87.gated), custom_call_target="tpu_custom_call" | custom-call | flops 189267968 | bytes 369664 | tf_op jit(solution)/shard_map/pallas_call | solution.py:95
  67.8 17.4 %all-to-all-done = bf16[16,152,608]{2,1,0:T(8,128)(2,1)} async-done(((bf16[16,152,608]{2,1,0:T(8,128)(2,1)}), bf16[16,152,608]{2,1,0:T(8,128)(2,1)}, u32[]{:S(2)}, u32[]{:S(2)}) %all-to-all-start) | async-done | bytes 2957344 | tf_op jit(solution)/shard_map/all_to_all | solution.py:80
  85.2 5.8 %all-to-all-start.1 = ((bf16[16,304,128]{2,1,0:T(8,128)(2,1)}), bf16[16,304,128]{2,1,0:T(8,128)(2,1)}, u32[]{:S(2)}, u32[]{:S(2)}) async-start(bf16[16,304,128]{2,1,0:T(8,128)(2,1)} %bitcast.88), calls=%async_computation.1 | async-start | bytes 2490368 | tf_op jit(solution)/shard_map/all_to_all | solution.py:80
  93.9 8.0 %shard_map.141 = (bf16[768,608]{1,0:T(8,128)(2,1)}, bf16[768,640]{1,0:T(8,128)(2,1)}) custom-call(s32[4]{0:T(128)} %pad_add_fusion.at, bf16[2,768,1216]{2,1,0:T(8,128)(2,1)} %all-gather.5.cloned.1.call-done.tokens, bf16[2,1216,608]{2,1,0:T(8,128)(2,1)} %bitcast.36.weights), custom_call_target="tpu_custom_call" | custom-call | flops 2271215616 | bytes 8560640 | tf_op jit(solution)/shard_map/pallas_call | solution.py:95
  102.0 4.8 %all-to-all-done.1.terms = bf16[16,304,128]{2,1,0:T(8,128)(2,1)} async-done(((bf16[16,304,128]{2,1,0:T(8,128)(2,1)}), bf16[16,304,128]{2,1,0:T(8,128)(2,1)}, u32[]{:S(2)}, u32[]{:S(2)}) %all-to-all-start.1) | async-done | bytes 1245216 | tf_op jit(solution)/shard_map/all_to_all | solution.py:80
  106.8 3.2 %shard_map.142 = (bf16[2,4,2,2,48,128]{5,4,3,2,1,0:T(8,128)(2,1)}, bf16[608,64]{1,0:T(8,128)(2,1)}) custom-call(s32[4]{0:T(128)} %pad_add_fusion.at, bf16[768,608]{1,0:T(8,128)(2,1)} %get-tuple-element.26.hidden, bf16[16,304,128]{2,1,0:T(8,128)(2,1)} %all-to-all-done.1.terms, f32[96,64]{1,0:T(8,128)} %fusion.10.own_part), custom_call_target="tpu_custom_call" | custom-call | flops 59768832 | bytes 933888 | tf_op jit(solution)/shard_map/pallas_call | solution.py:95
  110.0 11.6 %all_to_all.25.parts = bf16[16,2,48,128]{3,2,1,0:T(8,128)(2,1)S(1)} all-to-all(bf16[16,2,48,128]{3,2,1,0:T(8,128)(2,1)} %bitcast.95), channel_id=1, replica_groups=mesh['near'=2,'z'=4,'far'=2,'y'=4,'core'=2] {'near','y','core'}, dimensions={0} | all-to-all | bytes 786432 | tf_op jit(solution)/shard_map/all_to_all | solution.py:80
  121.6 3.7 %shard_map.143 = (bf16[192,1280]{1,0:T(8,128)(2,1)S(1)}, f32[48,1280]{1,0:T(8,128)S(1)}, f32[48,2048]{1,0:T(8,128)S(1)}) custom-call(s32[4]{0:T(128)S(1)} %copy-done.16, bf16[16,2,48,128]{3,2,1,0:T(8,128)(2,1)S(1)} %all_to_all.25.parts, bf16[64,2048]{1,0:T(8,128)(2,1)S(1)} %copy-done.7, bf16[2048,768]{1,0:T(8,128)(2,1)S(1)} %copy-done.1, ...), custom_call_target="tpu_custom_call" | custom-call | flops 1031798784 | bytes 5111808 | tf_op jit(solution)/shard_map/pallas_call | solution.py:95
  126.1 5.1 %shard_map.144 = (f32[192,640]{1,0:T(8,128)S(1)}, f32[192,640]{1,0:T(8,128)S(1)}, bf16[192,1280]{1,0:T(8,128)(2,1)S(1)}) custom-call(bf16[192,1280]{1,0:T(8,128)(2,1)S(1)} %get-tuple-element.31.normed, bf16[1280,640]{1,0:T(8,128)(2,1)} %v1a.3, bf16[1280,640]{1,0:T(8,128)(2,1)} %collective-permute-done.7.v1b, bf16[640,1280]{1,0:T(8,128)(2,1)} %v2a.3, ...), custom_call_target="tpu_custom_call" | custom-call | flops 1258291200 | bytes 6553600 | tf_op jit(solution)/shard_map/pallas_call | solution.py:95
  135.4 4.1 %collective-permute-start.10 = (bf16[48,1280]{1,0:T(8,128)(2,1)}, bf16[48,1280]{1,0:T(8,128)(2,1)}, u32[]{:S(2)}, u32[]{:S(2)}) collective-permute-start(bf16[48,1280]{1,0:T(8,128)(2,1)} %get-tuple-element.65), channel_id=1, source_target_pairs={{0,4},{2,6},{4,0},{6,2},{1,5},{3,7},{5,1},{7,3},{8,12},{10,14},{12... | collective-permute-start | bytes 368648 | tf_op jit(solution)/shard_map/ppermute | solution.py:64
  140.5 2.9 %collective-permute-start.20 = (bf16[96,1216]{1,0:T(8,128)(2,1)}, bf16[96,1216]{1,0:T(8,128)(2,1)}, u32[]{:S(2)}, u32[]{:S(2)}) collective-permute-start(bf16[96,1216]{1,0:T(8,128)(2,1)} %slice_bitcast_fusion), channel_id=1, source_target_pairs={{0,8},{8,0},{1,9},{9,1},{2,10},{10,2},{3,11},{11,3},{4,12},{12,4},... | collective-permute-start | bytes 700424 | tf_op jit(solution)/shard_map/ppermute | solution.py:64
  146.0 2.1 fusion.13
  148.9 2.3 collective-permute-start.13
  153.0 2.9 %collective-permute-start.18 = (bf16[768,640]{1,0:T(8,128)(2,1)}, bf16[768,640]{1,0:T(8,128)(2,1)S(1)}, u32[]{:S(2)}, u32[]{:S(2)}) collective-permute-start(bf16[768,640]{1,0:T(8,128)(2,1)} %get-tuple-element.36.slope), channel_id=1, source_target_pairs={{0,8},{8,0},{1,9},{9,1},{2,10},{10,2},{3,11},{11,3},{4,12},{12,4},... | collective-permute-start | bytes 2949128 | tf_op jit(solution)/shard_map/ppermute | solution.py:64
  160.7 5.6 %shard_map.145 = bf16[192,1280]{1,0:T(8,128)(2,1)S(1)} custom-call(bf16[192,1280]{1,0:T(8,128)(2,1)S(1)} %pad_maximum_fusion.2.grad, bf16[1280,640]{1,0:T(8,128)(2,1)} %v1a.3, bf16[1280,640]{1,0:T(8,128)(2,1)} %collective-permute-done.7.v1b, bf16[640,1280]{1,0:T(8,128)(2,1)} %v2a.3, bf16[640,1280]{1,0:T(8,128)(2,1)} %collective-permute-done.8.v2b, ...), custom_call_target="tpu_custom_call" | custom-call | flops 1258291200 | bytes 6553600 | tf_op jit(solution)/shard_map/pallas_call | solution.py:95
  168.0 3.3 %collective-permute-start.16 = (bf16[48,1280]{1,0:T(8,128)(2,1)S(1)}, bf16[48,1280]{1,0:T(8,128)(2,1)S(1)}, u32[]{:S(2)}, u32[]{:S(2)}) collective-permute-start(bf16[48,1280]{1,0:T(8,128)(2,1)S(1)} %get-tuple-element.62), channel_id=1, source_target_pairs={{0,4},{2,6},{4,0},{6,2},{1,5},{3,7},{5,1},{7,3},{8,12},{10,14},{12... | collective-permute-start | bytes 368648 | tf_op jit(solution)/shard_map/ppermute | solution.py:64
  171.6 3.5 %collective-permute-done.17 = bf16[48,1280]{1,0:T(8,128)(2,1)S(1)} collective-permute-done((bf16[48,1280]{1,0:T(8,128)(2,1)S(1)}, bf16[48,1280]{1,0:T(8,128)(2,1)S(1)}, u32[]{:S(2)}, u32[]{:S(2)}) %collective-permute-start.17) | collective-permute-done | bytes 122912 | tf_op jit(solution)/shard_map/ppermute | solution.py:64
  177.5 3.3 %collective-permute-done.19.through2 = bf16[608,64]{1,0:T(8,128)(2,1)S(1)} collective-permute-done((bf16[608,64]{1,0:T(8,128)(2,1)}, bf16[608,64]{1,0:T(8,128)(2,1)S(1)}, u32[]{:S(2)}, u32[]{:S(2)}) %collective-permute-start.19) | collective-permute-done | bytes 77856 | tf_op jit(solution)/shard_map/ppermute | solution.py:64
  181.3 2.3 convolution_convert_fusion
  183.5 2.3 fusion.6
  185.9 14.7 %all_to_all.26 = bf16[32,48,128]{2,1,0:T(8,128)(2,1)S(1)} all-to-all(bf16[32,48,128]{2,1,0:T(8,128)(2,1)S(1)} %broadcast_in_dim.61), channel_id=1, replica_groups=mesh['near'=2,'z'=4,'far'=2,'y'=4,'core'=2] {'far','near','y','core'}, dimensions={0} | all-to-all | bytes 786432 | tf_op jit(solution)/shard_map/all_to_all | solution.py:80
  204.2 7.3 %shard_map.147 = bf16[1216,608]{1,0:T(8,128)(2,1)} custom-call(bf16[768,128]{1,0:T(8,128)(2,1)} %copy-done.14, bf16[608,64]{1,0:T(8,128)(2,1)} %get-tuple-element.37.through, bf16[768,640]{1,0:T(8,128)(2,1)} %get-tuple-element.36.slope, bf16[2,768,1216]{2,1,0:T(8,128)(2,1)} %all-gather.5.cloned.1.call-done.tokens, bf16[768,128]{1,0:T(8,128)(2,1)} %copy-done.15, ...), custom_call_target="tpu_custom_call" | custom-call | flops 2271215616 | bytes 7081984 | tf_op jit(solution)/shard_map/pallas_call | solution.py:95
  214.8 3.6 %all-to-all-start.4 = ((bf16[8,280,608]{2,1,0:T(8,128)(2,1)}), bf16[8,280,608]{2,1,0:T(8,128)(2,1)S(1)}, u32[]{:S(2)}, u32[]{:S(2)}) async-start(bf16[8,280,608]{2,1,0:T(8,128)(2,1)} %pad_maximum_fusion), calls=%async_computation.4 | async-start | bytes 5734400 | tf_op jit(solution)/shard_map/all_to_all | solution.py:80
  220.1 5.3 %rev.7 = bf16[152,4,2,64]{3,2,1,0:T(2,128)(2,1)} reverse(bf16[152,4,2,64]{3,2,1,0:T(2,128)(2,1)} %multiply_convert_fusion), dimensions={2} | reverse | bytes 311296 | tf_op jit(solution)/shard_map/rev | solution.py:586
  228.1 25.4 %all-to-all-done.4 = bf16[8,280,608]{2,1,0:T(8,128)(2,1)S(1)} async-done(((bf16[8,280,608]{2,1,0:T(8,128)(2,1)}), bf16[8,280,608]{2,1,0:T(8,128)(2,1)S(1)}, u32[]{:S(2)}, u32[]{:S(2)}) %all-to-all-start.4) | async-done | bytes 2723872 | tf_op jit(solution)/shard_map/all_to_all | solution.py:80
  (151 shorter events, 53.7 us)
Async XLA Ops:
  7.2 78.1 %copy-start = (bf16[1,96,1280]{2,1,0:T(8,128)(2,1)S(1)}, bf16[1,96,1280]{2,1,0:T(8,128)(2,1)}, u32[]{:S(2)}) copy-start(bf16[1,96,1280]{2,1,0:T(8,128)(2,1)} %param.16) | copy-start | bytes 737284
  7.2 86.8 %all-gather.5.cloned.1.call-start = ((), (), s32[]{:S(2)}) async-start(), calls=%async_computation.5 | async-start | bytes 4423680 | tf_op jit(solution)/shard_map/all_gather | solution.py:512
  14.1 15.1 %collective-permute-start.6 = (s32[1]{0:T(128)}, s32[1]{0:T(128)}, u32[]{:S(2)}, u32[]{:S(2)}) collective-permute-start(s32[1]{0:T(128)} %param.14), channel_id=1, source_target_pairs={{0,8},{8,16},{16,24},{24,32},{32,40},{40,48},{48,56},{56,0},{1,9},... | collective-permute-start | bytes 20 | tf_op jit(solution)/shard_map/ppermute | solution.py:64
  17.2 13.1 %collective-permute-start.5 = (s32[1]{0:T(128)}, s32[1]{0:T(128)}, u32[]{:S(2)}, u32[]{:S(2)}) collective-permute-start(s32[1]{0:T(128)} %param.14), channel_id=1, source_target_pairs={{0,16},{8,24},{16,32},{24,40},{32,48},{40,56},{48,0},{56,8},{1,17}... | collective-permute-start | bytes 20 | tf_op jit(solution)/shard_map/ppermute | solution.py:64
  19.1 11.2 %collective-permute-start.4 = (s32[1]{0:T(128)}, s32[1]{0:T(128)}, u32[]{:S(2)}, u32[]{:S(2)}) collective-permute-start(s32[1]{0:T(128)} %param.14), channel_id=1, source_target_pairs={{0,24},{8,32},{16,40},{24,48},{32,56},{40,0},{48,8},{56,16},{1,25}... | collective-permute-start | bytes 20 | tf_op jit(solution)/shard_map/ppermute | solution.py:64
  22.0 8.3 %collective-permute-start.3 = (s32[1]{0:T(128)}, s32[1]{0:T(128)}, u32[]{:S(2)}, u32[]{:S(2)}) collective-permute-start(s32[1]{0:T(128)} %param.14), channel_id=1, source_target_pairs={{0,32},{8,40},{16,48},{24,56},{32,0},{40,8},{48,16},{56,24},{1,33}... | collective-permute-start | bytes 20 | tf_op jit(solution)/shard_map/ppermute | solution.py:64
  23.2 7.1 %collective-permute-start.2 = (s32[1]{0:T(128)}, s32[1]{0:T(128)}, u32[]{:S(2)}, u32[]{:S(2)}) collective-permute-start(s32[1]{0:T(128)} %param.14), channel_id=1, source_target_pairs={{0,40},{8,48},{16,56},{24,0},{32,8},{40,16},{48,24},{56,32},{1,41}... | collective-permute-start | bytes 20 | tf_op jit(solution)/shard_map/ppermute | solution.py:64
  29.2 3.8 %collective-permute-start.1 = (s32[1]{0:T(128)}, s32[1]{0:T(128)}, u32[]{:S(2)}, u32[]{:S(2)}) collective-permute-start(s32[1]{0:T(128)} %param.14), channel_id=1, source_target_pairs={{0,48},{8,56},{16,0},{24,8},{32,16},{40,24},{48,32},{56,40},{1,49}... | collective-permute-start | bytes 20 | tf_op jit(solution)/shard_map/ppermute | solution.py:64
  30.3 5.1 %collective-permute-start = (s32[1]{0:T(128)}, s32[1]{0:T(128)}, u32[]{:S(2)}, u32[]{:S(2)}) collective-permute-start(s32[1]{0:T(128)} %param.14), channel_id=1, source_target_pairs={{0,56},{8,0},{16,8},{24,16},{32,24},{40,32},{48,40},{56,48},{1,57}... | collective-permute-start | bytes 20 | tf_op jit(solution)/shard_map/ppermute | solution.py:64
  41.9 43.4 %all-to-all-start = ((bf16[16,152,608]{2,1,0:T(8,128)(2,1)}), bf16[16,152,608]{2,1,0:T(8,128)(2,1)}, u32[]{:S(2)}, u32[]{:S(2)}) async-start(bf16[16,152,608]{2,1,0:T(8,128)(2,1)} %bitcast.10), calls=%async_computation | async-start | bytes 6225920 | tf_op jit(solution)/shard_map/all_to_all | solution.py:80
  85.2 21.6 %all-to-all-start.1 = ((bf16[16,304,128]{2,1,0:T(8,128)(2,1)}), bf16[16,304,128]{2,1,0:T(8,128)(2,1)}, u32[]{:S(2)}, u32[]{:S(2)}) async-start(bf16[16,304,128]{2,1,0:T(8,128)(2,1)} %bitcast.88), calls=%async_computation.1 | async-start | bytes 2490368 | tf_op jit(solution)/shard_map/all_to_all | solution.py:80
  91.0 55.0 %all-gather.9.cloned.1.call-start = ((), (), s32[]{:S(2)}) async-start(), calls=%async_computation.7 | async-start | bytes 1290240 | tf_op jit(solution)/shard_map/all_gather | solution.py:535
  91.0 35.0 %collective-permute-start.7 = (bf16[1280,640]{1,0:T(8,128)(2,1)}, bf16[1280,640]{1,0:T(8,128)(2,1)}, u32[]{:S(2)}, u32[]{:S(2)}) collective-permute-start(bf16[1280,640]{1,0:T(8,128)(2,1)} %v1a.3), channel_id=1, source_target_pairs={{0,1},{1,0},{2,3},{3,2},{4,5},{5,4},{6,7},{7,6},{8,9},{9,8},{10,11... | collective-permute-start | bytes 4915208 | tf_op jit(solution)/shard_map/ppermute | solution.py:64
  91.1 34.9 %collective-permute-start.8 = (bf16[640,1280]{1,0:T(8,128)(2,1)}, bf16[640,1280]{1,0:T(8,128)(2,1)}, u32[]{:S(2)}, u32[]{:S(2)}) collective-permute-start(bf16[640,1280]{1,0:T(8,128)(2,1)} %v2a.3), channel_id=1, source_target_pairs={{0,1},{1,0},{2,3},{3,2},{4,5},{5,4},{6,7},{7,6},{8,9},{9,8},{10,11... | collective-permute-start | bytes 4915208 | tf_op jit(solution)/shard_map/ppermute | solution.py:64
  92.3 111.9 %all-gather.7.cloned.1.call-start = ((), (), s32[]{:S(2)}) async-start(), calls=%async_computation.6 | async-start | bytes 2211840 | tf_op jit(solution)/shard_map/all_gather | solution.py:513
  93.9 27.6 %copy-start.1 = (bf16[2048,768]{1,0:T(8,128)(2,1)S(1)}, bf16[2048,768]{1,0:T(8,128)(2,1)}, u32[]{:S(2)}) copy-start(bf16[2048,768]{1,0:T(8,128)(2,1)} %w_dec2.1) | copy-start | bytes 9437188
  102.0 19.6 %copy-start.16 = (s32[4]{0:T(128)S(1)}, s32[4]{0:T(128)}, u32[]{:S(2)}) copy-start(s32[4]{0:T(128)} %pad_add_fusion.at) | copy-start | bytes 52
  134.3 11.7 %collective-permute-start.11 = (bf16[48,1280]{1,0:T(8,128)(2,1)}, bf16[48,1280]{1,0:T(8,128)(2,1)}, u32[]{:S(2)}, u32[]{:S(2)}) collective-permute-start(bf16[48,1280]{1,0:T(8,128)(2,1)} %get-tuple-element.64), channel_id=1, source_target_pairs={{0,2},{2,4},{4,6},{6,0},{1,3},{3,5},{5,7},{7,1},{8,10},{10,12},{12... | collective-permute-start | bytes 368648 | tf_op jit(solution)/shard_map/ppermute | solution.py:64
  135.4 10.6 %collective-permute-start.10 = (bf16[48,1280]{1,0:T(8,128)(2,1)}, bf16[48,1280]{1,0:T(8,128)(2,1)}, u32[]{:S(2)}, u32[]{:S(2)}) collective-permute-start(bf16[48,1280]{1,0:T(8,128)(2,1)} %get-tuple-element.65), channel_id=1, source_target_pairs={{0,4},{2,6},{4,0},{6,2},{1,5},{3,7},{5,1},{7,3},{8,12},{10,14},{12... | collective-permute-start | bytes 368648 | tf_op jit(solution)/shard_map/ppermute | solution.py:64
  139.5 6.5 %collective-permute-start.9 = (bf16[48,1280]{1,0:T(8,128)(2,1)}, bf16[48,1280]{1,0:T(8,128)(2,1)}, u32[]{:S(2)}, u32[]{:S(2)}) collective-permute-start(bf16[48,1280]{1,0:T(8,128)(2,1)} %get-tuple-element.63), channel_id=1, source_target_pairs={{0,6},{2,0},{4,2},{6,4},{1,7},{3,1},{5,3},{7,5},{8,14},{10,8},{12,... | collective-permute-start | bytes 368648 | tf_op jit(solution)/shard_map/ppermute | solution.py:64
  140.5 12.4 %collective-permute-start.20 = (bf16[96,1216]{1,0:T(8,128)(2,1)}, bf16[96,1216]{1,0:T(8,128)(2,1)}, u32[]{:S(2)}, u32[]{:S(2)}) collective-permute-start(bf16[96,1216]{1,0:T(8,128)(2,1)} %slice_bitcast_fusion), channel_id=1, source_target_pairs={{0,8},{8,0},{1,9},{9,1},{2,10},{10,2},{3,11},{11,3},{4,12},{12,4},... | collective-permute-start | bytes 700424 | tf_op jit(solution)/shard_map/ppermute | solution.py:64
  148.1 8.5 %collective-permute-start.14 = (bf16[48,1280]{1,0:T(8,128)(2,1)}, bf16[48,1280]{1,0:T(8,128)(2,1)}, u32[]{:S(2)}, u32[]{:S(2)}) collective-permute-start(bf16[48,1280]{1,0:T(8,128)(2,1)} %get-tuple-element.66), channel_id=1, source_target_pairs={{0,6},{2,0},{4,2},{6,4},{1,7},{3,1},{5,3},{7,5},{8,14},{10,8},{12,... | collective-permute-start | bytes 368648 | tf_op jit(solution)/shard_map/ppermute | solution.py:64
  148.9 7.7 %collective-permute-start.13 = (bf16[48,1280]{1,0:T(8,128)(2,1)}, bf16[48,1280]{1,0:T(8,128)(2,1)}, u32[]{:S(2)}, u32[]{:S(2)}) collective-permute-start(bf16[48,1280]{1,0:T(8,128)(2,1)} %get-tuple-element.66), channel_id=1, source_target_pairs={{0,4},{2,6},{4,0},{6,2},{1,5},{3,7},{5,1},{7,3},{8,12},{10,14},{12... | collective-permute-start | bytes 368648 | tf_op jit(solution)/shard_map/ppermute | solution.py:64
  151.3 6.2 %collective-permute-start.12 = (bf16[48,1280]{1,0:T(8,128)(2,1)}, bf16[48,1280]{1,0:T(8,128)(2,1)}, u32[]{:S(2)}, u32[]{:S(2)}) collective-permute-start(bf16[48,1280]{1,0:T(8,128)(2,1)} %get-tuple-element.66), channel_id=1, source_target_pairs={{0,2},{2,4},{4,6},{6,0},{1,3},{3,5},{5,7},{7,1},{8,10},{10,12},{12... | collective-permute-start | bytes 368648 | tf_op jit(solution)/shard_map/ppermute | solution.py:64
  153.0 27.8 %collective-permute-start.18 = (bf16[768,640]{1,0:T(8,128)(2,1)}, bf16[768,640]{1,0:T(8,128)(2,1)S(1)}, u32[]{:S(2)}, u32[]{:S(2)}) collective-permute-start(bf16[768,640]{1,0:T(8,128)(2,1)} %get-tuple-element.36.slope), channel_id=1, source_target_pairs={{0,8},{8,0},{1,9},{9,1},{2,10},{10,2},{3,11},{11,3},{4,12},{12,4},... | collective-permute-start | bytes 2949128 | tf_op jit(solution)/shard_map/ppermute | solution.py:64
  156.0 24.8 %collective-permute-start.19 = (bf16[608,64]{1,0:T(8,128)(2,1)}, bf16[608,64]{1,0:T(8,128)(2,1)S(1)}, u32[]{:S(2)}, u32[]{:S(2)}) collective-permute-start(bf16[608,64]{1,0:T(8,128)(2,1)} %get-tuple-element.37.through), channel_id=1, source_target_pairs={{0,8},{8,0},{1,9},{9,1},{2,10},{10,2},{3,11},{11,3},{4,12},{12,4},... | collective-permute-start | bytes 233480 | tf_op jit(solution)/shard_map/ppermute | solution.py:64
  160.7 20.1 %copy-start.6 = (f32[48,1280]{1,0:T(8,128)S(1)}, f32[48,1280]{1,0:T(8,128)}, u32[]{:S(2)}) copy-start(f32[48,1280]{1,0:T(8,128)} %copy-done.5) | copy-start | bytes 737284
  166.4 8.8 %collective-permute-start.17 = (bf16[48,1280]{1,0:T(8,128)(2,1)S(1)}, bf16[48,1280]{1,0:T(8,128)(2,1)S(1)}, u32[]{:S(2)}, u32[]{:S(2)}) collective-permute-start(bf16[48,1280]{1,0:T(8,128)(2,1)S(1)} %get-tuple-element.61), channel_id=1, source_target_pairs={{0,2},{2,4},{4,6},{6,0},{1,3},{3,5},{5,7},{7,1},{8,10},{10,12},{12... | collective-permute-start | bytes 368648 | tf_op jit(solution)/shard_map/ppermute | solution.py:64
  168.0 8.9 %collective-permute-start.16 = (bf16[48,1280]{1,0:T(8,128)(2,1)S(1)}, bf16[48,1280]{1,0:T(8,128)(2,1)S(1)}, u32[]{:S(2)}, u32[]{:S(2)}) collective-permute-start(bf16[48,1280]{1,0:T(8,128)(2,1)S(1)} %get-tuple-element.62), channel_id=1, source_target_pairs={{0,4},{2,6},{4,0},{6,2},{1,5},{3,7},{5,1},{7,3},{8,12},{10,14},{12... | collective-permute-start | bytes 368648 | tf_op jit(solution)/shard_map/ppermute | solution.py:64
  171.3 6.1 %collective-permute-start.15 = (bf16[48,1280]{1,0:T(8,128)(2,1)S(1)}, bf16[48,1280]{1,0:T(8,128)(2,1)S(1)}, u32[]{:S(2)}, u32[]{:S(2)}) collective-permute-start(bf16[48,1280]{1,0:T(8,128)(2,1)S(1)} %get-tuple-element.60), channel_id=1, source_target_pairs={{0,6},{2,0},{4,2},{6,4},{1,7},{3,1},{5,3},{7,5},{8,14},{10,8},{12,... | collective-permute-start | bytes 368648 | tf_op jit(solution)/shard_map/ppermute | solution.py:64
  202.9 8.6 %collective-permute-start.21 = (bf16[64,608]{1,0:T(8,128)(2,1)S(1)}, bf16[64,608]{1,0:T(8,128)(2,1)S(1)}, u32[]{:S(2)}, u32[]{:S(2)}) collective-permute-start(bf16[64,608]{1,0:T(8,128)(2,1)S(1)} %get-tuple-element.43), channel_id=1, source_target_pairs={{0,8},{8,0},{1,9},{9,1},{2,10},{10,2},{3,11},{11,3},{4,12},{12,4},... | collective-permute-start | bytes 233480 | tf_op jit(solution)/shard_map/ppermute | solution.py:64
  214.8 38.7 %all-to-all-start.4 = ((bf16[8,280,608]{2,1,0:T(8,128)(2,1)}), bf16[8,280,608]{2,1,0:T(8,128)(2,1)S(1)}, u32[]{:S(2)}, u32[]{:S(2)}) async-start(bf16[8,280,608]{2,1,0:T(8,128)(2,1)} %pad_maximum_fusion), calls=%async_computation.4 | async-start | bytes 5734400 | tf_op jit(solution)/shard_map/all_to_all | solution.py:80
  (23 other events, 137.5 us)
Sparse Core Ops, SparseCore 0:
  14.2 32.2 all-gather.4
  94.1 48.6 all-gather.8
  153.1 24.2 all-gather.6

commit v7 on v6

--- a/solution.py
+++ b/solution.py
@@ -219,17 +219,17 @@
     )
 
 
-def inner_kernel(at, spread, hidden, grads, far_grads, inner):
-    _, n_near, n_mp, mine, _ = spread.shape
-    for image, result in ((at[0], grads), (1 - at[0], far_grads)):
+def inner_kernel(spread, hidden, grads, far_grads, inner):
+    n_near, n_mp, _, mine, _ = spread.shape
+    for image, result in ((0, grads), (1, far_grads)):
         for place in range(n_mp):
             for near in range(n_near):
                 start = (place * n_near + near) * mine
-                result[start : start + mine] = spread[image, near, place]
+                result[start : start + mine] = spread[near, place, image]
     inner[...] = matmul_tn(grads[:, : inner.shape[0]], hidden[...]).astype(BF16)
 
 
-def inner_products(at, spread, hidden, lat):
+def inner_products(spread, hidden, lat):
     rows, columns = hidden.shape
     shapes = [
         jax.ShapeDtypeStruct((rows, spread.shape[-1]), BF16),
@@ -239,14 +239,13 @@
     return call(
         inner_kernel,
         1,
-        [SCALARS, whole(spread), whole(hidden)],
+        [whole(spread), whole(hidden)],
         [whole(shape) for shape in shapes],
         shapes,
         [],
         2 * rows * columns * lat,
         2 * rows * columns,
         SMALL,
-        at,
         spread,
         hidden,
     )
@@ -489,16 +488,14 @@
 
     at = jnp.stack([far, near, lax.axis_index(("y", "core")), lax.axis_index("y")]).astype(jnp.int32)
 
-    turned_steps = from_all(timestep, IMAGE)
-    images = lax.iota(jnp.int32, n_images)
-    all_steps = jnp.zeros_like(images)
-    for step, value in enumerate(turned_steps):
-        all_steps = jnp.where(images == (my_image - step) % n_images, value[0], all_steps)
+    far_step = turned(timestep, "far", 1)
+    pair_steps = jnp.where(far == 0, jnp.stack([timestep, far_step]), jnp.stack([far_step, timestep]))
+    turned_steps = from_all(pair_steps, "z")
 
     split_in = jnp.moveaxis(w_in.reshape(d_dev, n_near, half), 1, 0)
     split_in = jnp.broadcast_to(split_in[None, :, None], (n_far, n_near, n_z, d_dev, half))
     split_in = split_in.reshape(n_rows, d_dev, half)
-    split_in, all_steps = lax.optimization_barrier((split_in, all_steps))
+    split_in, turned_steps = lax.optimization_barrier((split_in, turned_steps))
     full_in = exchanged(split_in, FAR_FIRST).reshape(n_far, wide, half)
 
     noise_rows = latent_noise[0]
@@ -511,6 +508,13 @@
     modulated = jnp.where(far == 0, modulated, modulated[::-1])
     token_rows = lax.all_gather(modulated, ("y", "core"), axis=1, tiled=True)
     far_rows = lax.all_gather(turned(modulated[1], "far", 1), ("y", "core"), axis=0, tiled=True)
+
+    all_steps = jnp.zeros((n_z, n_far), jnp.int32)
+    for step, value in enumerate(turned_steps):
+        owner = (lax.axis_index("z") - step) % n_z
+        here = lax.broadcasted_iota(jnp.int32, (n_z, n_far), 0) == owner
+        all_steps = jnp.where(here, value.reshape(1, n_far), all_steps)
+    all_steps = all_steps.reshape(n_images)
 
     first = lax.axis_index(ROWS_AT) * d_dev
     my_final = lax.dynamic_slice_in_dim(w_final, first, d_dev, 0).astype(F32)
@@ -559,11 +563,11 @@
     latent_grad = matmul_nt(dec_pre_grad, w_dec1).astype(BF16)
 
     latent_grad = jnp.pad(latent_grad, ((0, 0), (0, lanes(lat) - lat)))
-    spread = jnp.broadcast_to(latent_grad, (n_far * n_tokens,) + latent_grad.shape)
-    spread = exchanged(spread, ("far",) + TOKENS_AT)
-    spread = spread.reshape((n_far, n_near, n_y * n_core) + latent_grad.shape)
-
-    latent_rows, far_latent_rows, inner = inner_products(at, spread, hidden, lat)
+    latent_grad = jnp.stack([latent_grad, turned(latent_grad, "far", 1)])
+    spread = exchanged(jnp.broadcast_to(latent_grad, (n_tokens,) + latent_grad.shape), TOKENS_AT)
+    spread = spread.reshape((n_near, n_y * n_core) + latent_grad.shape)
+
+    latent_rows, far_latent_rows, inner = inner_products(spread, hidden, lat)
     far_inner = turned(inner, "far", 1)
     term_in = block_backward(
         latent_rows,

time: 268 us -> 262 us (0.978)
  blocking collectives: 26.3 us -> 21.7 us
  other arithmetic: 19.4 us -> 15.7 us
    all_to_all x2, blocking collectives: 26.3 us -> 21.7 us  [exchanged(): return lax.all_to_all(blocks, axis, 0, 0, tiled=True)]
    select_n x1 -> x2, other arithmetic: 4.48 us -> 0.79 us  [the longest x1 0.71 us: on_device(): jnp.where(far == 0, jnp.stack([timestep, far_step]), jnp.stack([far_step,...]
    ppermute x22 -> x20, waiting for transfers between devices: 15.1 us -> 16.4 us  [turned(): lax.ppermute(value, axis, [(at, (at + steps) % count) for at in range(cou...]
    ppermute x22 -> x20, starting transfers between devices: 39.6 us -> 39.4 us  [turned(): lax.ppermute(value, axis, [(at, (at + steps) % count) for at in range(cou...]
  transfers between devices with their start and end apart: 28 -> 26, of which waited for: 10 -> 12; matrix products, arithmetic and copies ran while one was open for 12% -> 11% of each run, Pallas kernels for 14% -> 14%
where the time goes in v7:
time: 262 us; the launch traced here: 258 us
  waiting for transfers between devices  64.1 us (24%)
  starting transfers between devices  54.9 us (21%)
  Pallas kernels  36.4 us (14%)
  between operations  31.6 us (12%)
  local copies, waits for them, and re-layouts  27.7 us (11%)
  blocking collectives  21.7 us (8%)
  other arithmetic  15.7 us (6%)
  matrix products  6.07 us (2%)
    all_to_all x3, waiting for transfers between devices, exchanged(): return lax.all_to_all(blocks, axis, 0, 0, tiled=True)  47.6 us
    ppermute x20, starting transfers between devices, turned(): lax.ppermute(value, axis, [(at, (at + steps) % count) for at in range(cou...  39.4 us
    pallas_call x8, Pallas kernels, call(): pl.pallas_call(kernel, grid=(grid,), in_specs=in_specs, out_specs=out_spe...  36.4 us
    all_to_all x2, blocking collectives, exchanged(): return lax.all_to_all(blocks, axis, 0, 0, tiled=True)  21.7 us
    ppermute x20, waiting for transfers between devices, turned(): lax.ppermute(value, axis, [(at, (at + steps) % count) for at in range(cou...  16.4 us
    all_to_all x3, starting transfers between devices, exchanged(): return lax.all_to_all(blocks, axis, 0, 0, tiled=True)  15.4 us
    unnamed x55, local copies, waits for them, and re-layouts  9.29 us
    rev x1, local copies, waits for them, and re-layouts, on_device(): my_gated[:, :, ::-1]  5.31 us
  transfers between devices with their start and end apart: 26, of which 12 were waited for; matrix products, arithmetic and copies ran while one was open for 11% of the time, Pallas kernels for 14%

profile of v7, /device:TPU:8, one launch (start us, length us, event | category | flops | bytes accessed | tf_op | source)
XLA Modules:
  0.0 258.3 jit_solution(4468959461689270340)
XLA Ops:
  14.1 3.1 %collective-permute-start = (s32[1]{0:T(128)}, s32[1]{0:T(128)}, u32[]{:S(2)}, u32[]{:S(2)}) collective-permute-start(s32[1]{0:T(128)} %param.14), channel_id=1, source_target_pairs={{0,8},{8,0},{1,9},{9,1},{2,10},{10,2},{3,11},{11,3},{4,12},{12,4},... | collective-permute-start | bytes 20 | tf_op jit(solution)/shard_map/ppermute | solution.py:64
  22.1 3.6 %collective-permute-start.2 = (s32[2,1]{0,1:T(1,128)S(1)}, s32[2,1]{0,1:T(1,128)S(1)}, u32[]{:S(2)}, u32[]{:S(2)}) collective-permute-start(s32[2,1]{0,1:T(1,128)S(1)} %broadcast_select_fusion.1), channel_id=1, source_target_pairs={{0,32},{16,48},{32,0},{48,16},{1,33},{17,49},{33,1},{49,17},{2,34}... | collective-permute-start | bytes 32 | tf_op jit(solution)/shard_map/ppermute | solution.py:64
  27.2 2.0 collective-permute-done.3
  29.2 2.0 broadcast_in_dim.56
  31.2 6.2 %all-to-all-start = ((bf16[16,152,608]{2,1,0:T(8,128)(2,1)}), bf16[16,152,608]{2,1,0:T(8,128)(2,1)}, u32[]{:S(2)}, u32[]{:S(2)}) async-start(bf16[16,152,608]{2,1,0:T(8,128)(2,1)} %bitcast.10), calls=%async_computation | async-start | bytes 6225920 | tf_op jit(solution)/shard_map/all_to_all | solution.py:80
  55.7 3.2 %shard_map.140 = bf16[2,8,304,128]{3,2,1,0:T(8,128)(2,1)} custom-call(bf16[152,1216]{1,0:T(8,128)(2,1)} %w_out.1, bf16[152,512]{1,0:T(8,128)(2,1)} %convert_element_type.87.gated), custom_call_target="tpu_custom_call" | custom-call | flops 189267968 | bytes 369664 | tf_op jit(solution)/shard_map/pallas_call | solution.py:95
  58.9 16.5 %all-to-all-done = bf16[16,152,608]{2,1,0:T(8,128)(2,1)} async-done(((bf16[16,152,608]{2,1,0:T(8,128)(2,1)}), bf16[16,152,608]{2,1,0:T(8,128)(2,1)}, u32[]{:S(2)}, u32[]{:S(2)}) %all-to-all-start) | async-done | bytes 2957344 | tf_op jit(solution)/shard_map/all_to_all | solution.py:80
  75.4 5.3 %all-to-all-start.1 = ((bf16[16,304,128]{2,1,0:T(8,128)(2,1)}), bf16[16,304,128]{2,1,0:T(8,128)(2,1)}, u32[]{:S(2)}, u32[]{:S(2)}) async-start(bf16[16,304,128]{2,1,0:T(8,128)(2,1)} %bitcast.90), calls=%async_computation.1 | async-start | bytes 2490368 | tf_op jit(solution)/shard_map/all_to_all | solution.py:80
  83.7 8.0 %shard_map.141 = (bf16[768,608]{1,0:T(8,128)(2,1)}, bf16[768,640]{1,0:T(8,128)(2,1)}) custom-call(s32[4]{0:T(128)} %pad_add_fusion.at, bf16[2,768,1216]{2,1,0:T(8,128)(2,1)} %all-gather.5.cloned.1.call-done.tokens, bf16[2,1216,608]{2,1,0:T(8,128)(2,1)} %bitcast.35.weights), custom_call_target="tpu_custom_call" | custom-call | flops 2271215616 | bytes 8560640 | tf_op jit(solution)/shard_map/pallas_call | solution.py:95
  91.7 6.1 %all-to-all-done.1.terms = bf16[16,304,128]{2,1,0:T(8,128)(2,1)} async-done(((bf16[16,304,128]{2,1,0:T(8,128)(2,1)}), bf16[16,304,128]{2,1,0:T(8,128)(2,1)}, u32[]{:S(2)}, u32[]{:S(2)}) %all-to-all-start.1) | async-done | bytes 1245216 | tf_op jit(solution)/shard_map/all_to_all | solution.py:80
  97.8 3.2 %shard_map.142 = (bf16[2,4,2,2,48,128]{5,4,3,2,1,0:T(8,128)(2,1)}, bf16[608,64]{1,0:T(8,128)(2,1)}) custom-call(s32[4]{0:T(128)} %pad_add_fusion.at, bf16[768,608]{1,0:T(8,128)(2,1)} %get-tuple-element.32.hidden, bf16[16,304,128]{2,1,0:T(8,128)(2,1)} %all-to-all-done.1.terms, f32[96,64]{1,0:T(8,128)} %fusion.10.own_part), custom_call_target="tpu_custom_call" | custom-call | flops 59768832 | bytes 933888 | tf_op jit(solution)/shard_map/pallas_call | solution.py:95
  101.0 11.4 %all_to_all.25.parts = bf16[16,2,48,128]{3,2,1,0:T(8,128)(2,1)S(1)} all-to-all(bf16[16,2,48,128]{3,2,1,0:T(8,128)(2,1)} %bitcast.97), channel_id=1, replica_groups=mesh['near'=2,'z'=4,'far'=2,'y'=4,'core'=2] {'near','y','core'}, dimensions={0} | all-to-all | bytes 786432 | tf_op jit(solution)/shard_map/all_to_all | solution.py:80
  112.4 3.7 %shard_map.143 = (bf16[192,1280]{1,0:T(8,128)(2,1)S(1)}, f32[48,1280]{1,0:T(8,128)S(1)}, f32[48,2048]{1,0:T(8,128)S(1)}) custom-call(s32[4]{0:T(128)S(1)} %copy-done.16, bf16[16,2,48,128]{3,2,1,0:T(8,128)(2,1)S(1)} %all_to_all.25.parts, bf16[64,2048]{1,0:T(8,128)(2,1)S(1)} %copy-done.7, bf16[2048,768]{1,0:T(8,128)(2,1)S(1)} %copy-done.1, ...), custom_call_target="tpu_custom_call" | custom-call | flops 1031798784 | bytes 5111808 | tf_op jit(solution)/shard_map/pallas_call | solution.py:95
  116.9 5.1 %shard_map.144 = (f32[192,640]{1,0:T(8,128)S(1)}, f32[192,640]{1,0:T(8,128)S(1)}, bf16[192,1280]{1,0:T(8,128)(2,1)S(1)}) custom-call(bf16[192,1280]{1,0:T(8,128)(2,1)S(1)} %get-tuple-element.37.normed, bf16[1280,640]{1,0:T(8,128)(2,1)} %v1a.3, bf16[1280,640]{1,0:T(8,128)(2,1)} %collective-permute-done.4.v1b, bf16[640,1280]{1,0:T(8,128)(2,1)} %v2a.3, ...), custom_call_target="tpu_custom_call" | custom-call | flops 1258291200 | bytes 6553600 | tf_op jit(solution)/shard_map/pallas_call | solution.py:95
  126.0 4.2 %collective-permute-start.7 = (bf16[48,1280]{1,0:T(8,128)(2,1)}, bf16[48,1280]{1,0:T(8,128)(2,1)}, u32[]{:S(2)}, u32[]{:S(2)}) collective-permute-start(bf16[48,1280]{1,0:T(8,128)(2,1)} %get-tuple-element.71), channel_id=1, source_target_pairs={{0,4},{2,6},{4,0},{6,2},{1,5},{3,7},{5,1},{7,3},{8,12},{10,14},{12... | collective-permute-start | bytes 368648 | tf_op jit(solution)/shard_map/ppermute | solution.py:64
  131.3 3.4 %collective-permute-start.18 = (bf16[96,1216]{1,0:T(8,128)(2,1)}, bf16[96,1216]{1,0:T(8,128)(2,1)}, u32[]{:S(2)}, u32[]{:S(2)}) collective-permute-start(bf16[96,1216]{1,0:T(8,128)(2,1)} %slice_bitcast_fusion), channel_id=1, source_target_pairs={{0,8},{8,0},{1,9},{9,1},{2,10},{10,2},{3,11},{11,3},{4,12},{12,4},... | collective-permute-start | bytes 700424 | tf_op jit(solution)/shard_map/ppermute | solution.py:64
  137.0 2.1 fusion.13
  140.0 2.3 collective-permute-start.10
  143.8 3.5 %collective-permute-start.15 = (bf16[768,640]{1,0:T(8,128)(2,1)}, bf16[768,640]{1,0:T(8,128)(2,1)S(1)}, u32[]{:S(2)}, u32[]{:S(2)}) collective-permute-start(bf16[768,640]{1,0:T(8,128)(2,1)} %get-tuple-element.42.slope), channel_id=1, source_target_pairs={{0,8},{8,0},{1,9},{9,1},{2,10},{10,2},{3,11},{11,3},{4,12},{12,4},... | collective-permute-start | bytes 2949128 | tf_op jit(solution)/shard_map/ppermute | solution.py:64
  151.5 5.6 %shard_map.145 = bf16[192,1280]{1,0:T(8,128)(2,1)S(1)} custom-call(bf16[192,1280]{1,0:T(8,128)(2,1)S(1)} %pad_maximum_fusion.2.grad, bf16[1280,640]{1,0:T(8,128)(2,1)} %v1a.3, bf16[1280,640]{1,0:T(8,128)(2,1)} %collective-permute-done.4.v1b, bf16[640,1280]{1,0:T(8,128)(2,1)} %v2a.3, bf16[640,1280]{1,0:T(8,128)(2,1)} %collective-permute-done.5.v2b, ...), custom_call_target="tpu_custom_call" | custom-call | flops 1258291200 | bytes 6553600 | tf_op jit(solution)/shard_map/pallas_call | solution.py:95
  158.7 3.4 %collective-permute-start.13 = (bf16[48,1280]{1,0:T(8,128)(2,1)S(1)}, bf16[48,1280]{1,0:T(8,128)(2,1)S(1)}, u32[]{:S(2)}, u32[]{:S(2)}) collective-permute-start(bf16[48,1280]{1,0:T(8,128)(2,1)S(1)} %get-tuple-element.68), channel_id=1, source_target_pairs={{0,4},{2,6},{4,0},{6,2},{1,5},{3,7},{5,1},{7,3},{8,12},{10,14},{12... | collective-permute-start | bytes 368648 | tf_op jit(solution)/shard_map/ppermute | solution.py:64
  162.4 3.8 %collective-permute-done.14 = bf16[48,1280]{1,0:T(8,128)(2,1)S(1)} collective-permute-done((bf16[48,1280]{1,0:T(8,128)(2,1)S(1)}, bf16[48,1280]{1,0:T(8,128)(2,1)S(1)}, u32[]{:S(2)}, u32[]{:S(2)}) %collective-permute-start.14) | collective-permute-done | bytes 122912 | tf_op jit(solution)/shard_map/ppermute | solution.py:64
  168.2 3.5 %collective-permute-done.16.through2 = bf16[608,64]{1,0:T(8,128)(2,1)S(1)} collective-permute-done((bf16[608,64]{1,0:T(8,128)(2,1)}, bf16[608,64]{1,0:T(8,128)(2,1)S(1)}, u32[]{:S(2)}, u32[]{:S(2)}) %collective-permute-start.16) | collective-permute-done | bytes 77856 | tf_op jit(solution)/shard_map/ppermute | solution.py:64
  172.2 2.3 convolution_convert_fusion
  174.5 2.3 fusion.6
  176.8 3.3 %collective-permute-start.17 = (bf16[48,128]{1,0:T(8,128)(2,1)S(1)}, bf16[48,128]{1,0:T(8,128)(2,1)S(1)}, u32[]{:S(2)}, u32[]{:S(2)}) collective-permute-start(bf16[48,128]{1,0:T(8,128)(2,1)S(1)} %get-tuple-element.75), channel_id=1, source_target_pairs={{0,8},{8,0},{1,9},{9,1},{2,10},{10,2},{3,11},{11,3},{4,12},{12,4},... | collective-permute-start | bytes 36872 | tf_op jit(solution)/shard_map/ppermute | solution.py:64
  182.2 10.3 %all_to_all.26 = bf16[16,2,48,128]{3,2,1,0:T(8,128)(2,1)S(1)} all-to-all(bf16[16,2,48,128]{3,2,1,0:T(8,128)(2,1)S(1)} %broadcast_in_dim.67), channel_id=1, replica_groups=mesh['near'=2,'z'=4,'far'=2,'y'=4,'core'=2] {'near','y','core'}, dimensions={0} | all-to-all | bytes 786432 | tf_op jit(solution)/shard_map/all_to_all | solution.py:80
  194.2 3.4 %collective-permute-start.19 = (bf16[64,608]{1,0:T(8,128)(2,1)S(1)}, bf16[64,608]{1,0:T(8,128)(2,1)S(1)}, u32[]{:S(2)}, u32[]{:S(2)}) collective-permute-start(bf16[64,608]{1,0:T(8,128)(2,1)S(1)} %get-tuple-element.49), channel_id=1, source_target_pairs={{0,8},{8,0},{1,9},{9,1},{2,10},{10,2},{3,11},{11,3},{4,12},{12,4},... | collective-permute-start | bytes 233480 | tf_op jit(solution)/shard_map/ppermute | solution.py:64
  197.6 7.4 %shard_map.147 = bf16[1216,608]{1,0:T(8,128)(2,1)} custom-call(bf16[768,128]{1,0:T(8,128)(2,1)} %copy-done.14, bf16[608,64]{1,0:T(8,128)(2,1)} %get-tuple-element.43.through, bf16[768,640]{1,0:T(8,128)(2,1)} %get-tuple-element.42.slope, bf16[2,768,1216]{2,1,0:T(8,128)(2,1)} %all-gather.5.cloned.1.call-done.tokens, bf16[768,128]{1,0:T(8,128)(2,1)} %copy-done.15, ...), custom_call_target="tpu_custom_call" | custom-call | flops 2271215616 | bytes 7081984 | tf_op jit(solution)/shard_map/pallas_call | solution.py:95
  208.1 3.9 %all-to-all-start.4 = ((bf16[8,280,608]{2,1,0:T(8,128)(2,1)}), bf16[8,280,608]{2,1,0:T(8,128)(2,1)S(1)}, u32[]{:S(2)}, u32[]{:S(2)}) async-start(bf16[8,280,608]{2,1,0:T(8,128)(2,1)} %pad_maximum_fusion), calls=%async_computation.4 | async-start | bytes 5734400 | tf_op jit(solution)/shard_map/all_to_all | solution.py:80
  213.7 5.3 %rev.7 = bf16[152,4,2,64]{3,2,1,0:T(2,128)(2,1)} reverse(bf16[152,4,2,64]{3,2,1,0:T(2,128)(2,1)} %multiply_convert_fusion), dimensions={2} | reverse | bytes 311296 | tf_op jit(solution)/shard_map/rev | solution.py:590
  221.7 25.1 %all-to-all-done.4 = bf16[8,280,608]{2,1,0:T(8,128)(2,1)S(1)} async-done(((bf16[8,280,608]{2,1,0:T(8,128)(2,1)}), bf16[8,280,608]{2,1,0:T(8,128)(2,1)S(1)}, u32[]{:S(2)}, u32[]{:S(2)}) %all-to-all-start.4) | async-done | bytes 2723872 | tf_op jit(solution)/shard_map/all_to_all | solution.py:80
  (152 shorter events, 52.4 us)
Async XLA Ops:
  7.2 68.2 %copy-start = (bf16[1,96,1280]{2,1,0:T(8,128)(2,1)S(1)}, bf16[1,96,1280]{2,1,0:T(8,128)(2,1)}, u32[]{:S(2)}) copy-start(bf16[1,96,1280]{2,1,0:T(8,128)(2,1)} %param.16) | copy-start | bytes 737284
  7.2 76.5 %all-gather.5.cloned.1.call-start = ((), (), s32[]{:S(2)}) async-start(), calls=%async_computation.5 | async-start | bytes 4423680 | tf_op jit(solution)/shard_map/all_gather | solution.py:509
  14.1 5.4 %collective-permute-start = (s32[1]{0:T(128)}, s32[1]{0:T(128)}, u32[]{:S(2)}, u32[]{:S(2)}) collective-permute-start(s32[1]{0:T(128)} %param.14), channel_id=1, source_target_pairs={{0,8},{8,0},{1,9},{9,1},{2,10},{10,2},{3,11},{11,3},{4,12},{12,4},... | collective-permute-start | bytes 20 | tf_op jit(solution)/shard_map/ppermute | solution.py:64
  20.2 6.5 %collective-permute-start.1 = (s32[2,1]{0,1:T(1,128)S(1)}, s32[2,1]{0,1:T(1,128)S(1)}, u32[]{:S(2)}, u32[]{:S(2)}) collective-permute-start(s32[2,1]{0,1:T(1,128)S(1)} %broadcast_select_fusion.1), channel_id=1, source_target_pairs={{0,16},{16,32},{32,48},{48,0},{1,17},{17,33},{33,49},{49,1},{2,18}... | collective-permute-start | bytes 32 | tf_op jit(solution)/shard_map/ppermute | solution.py:64
  22.1 5.1 %collective-permute-start.2 = (s32[2,1]{0,1:T(1,128)S(1)}, s32[2,1]{0,1:T(1,128)S(1)}, u32[]{:S(2)}, u32[]{:S(2)}) collective-permute-start(s32[2,1]{0,1:T(1,128)S(1)} %broadcast_select_fusion.1), channel_id=1, source_target_pairs={{0,32},{16,48},{32,0},{48,16},{1,33},{17,49},{33,1},{49,17},{2,34}... | collective-permute-start | bytes 32 | tf_op jit(solution)/shard_map/ppermute | solution.py:64
  25.7 3.5 %collective-permute-start.3 = (s32[2,1]{0,1:T(1,128)S(1)}, s32[2,1]{0,1:T(1,128)S(1)}, u32[]{:S(2)}, u32[]{:S(2)}) collective-permute-start(s32[2,1]{0,1:T(1,128)S(1)} %broadcast_select_fusion.1), channel_id=1, source_target_pairs={{0,48},{16,0},{32,16},{48,32},{1,49},{17,1},{33,17},{49,33},{2,50}... | collective-permute-start | bytes 32 | tf_op jit(solution)/shard_map/ppermute | solution.py:64
  31.2 44.2 %all-to-all-start = ((bf16[16,152,608]{2,1,0:T(8,128)(2,1)}), bf16[16,152,608]{2,1,0:T(8,128)(2,1)}, u32[]{:S(2)}, u32[]{:S(2)}) async-start(bf16[16,152,608]{2,1,0:T(8,128)(2,1)} %bitcast.10), calls=%async_computation | async-start | bytes 6225920 | tf_op jit(solution)/shard_map/all_to_all | solution.py:80
  75.4 22.4 %all-to-all-start.1 = ((bf16[16,304,128]{2,1,0:T(8,128)(2,1)}), bf16[16,304,128]{2,1,0:T(8,128)(2,1)}, u32[]{:S(2)}, u32[]{:S(2)}) async-start(bf16[16,304,128]{2,1,0:T(8,128)(2,1)} %bitcast.90), calls=%async_computation.1 | async-start | bytes 2490368 | tf_op jit(solution)/shard_map/all_to_all | solution.py:80
  80.7 56.2 %all-gather.9.cloned.1.call-start = ((), (), s32[]{:S(2)}) async-start(), calls=%async_computation.7 | async-start | bytes 1290240 | tf_op jit(solution)/shard_map/all_gather | solution.py:539
  80.7 36.1 %collective-permute-start.4 = (bf16[1280,640]{1,0:T(8,128)(2,1)}, bf16[1280,640]{1,0:T(8,128)(2,1)}, u32[]{:S(2)}, u32[]{:S(2)}) collective-permute-start(bf16[1280,640]{1,0:T(8,128)(2,1)} %v1a.3), channel_id=1, source_target_pairs={{0,1},{1,0},{2,3},{3,2},{4,5},{5,4},{6,7},{7,6},{8,9},{9,8},{10,11... | collective-permute-start | bytes 4915208 | tf_op jit(solution)/shard_map/ppermute | solution.py:64
  80.8 36.0 %collective-permute-start.5 = (bf16[640,1280]{1,0:T(8,128)(2,1)}, bf16[640,1280]{1,0:T(8,128)(2,1)}, u32[]{:S(2)}, u32[]{:S(2)}) collective-permute-start(bf16[640,1280]{1,0:T(8,128)(2,1)} %v2a.3), channel_id=1, source_target_pairs={{0,1},{1,0},{2,3},{3,2},{4,5},{5,4},{6,7},{7,6},{8,9},{9,8},{10,11... | collective-permute-start | bytes 4915208 | tf_op jit(solution)/shard_map/ppermute | solution.py:64
  82.0 115.5 %all-gather.7.cloned.1.call-start = ((), (), s32[]{:S(2)}) async-start(), calls=%async_computation.6 | async-start | bytes 2211840 | tf_op jit(solution)/shard_map/all_gather | solution.py:510
  83.6 28.7 %copy-start.1 = (bf16[2048,768]{1,0:T(8,128)(2,1)S(1)}, bf16[2048,768]{1,0:T(8,128)(2,1)}, u32[]{:S(2)}) copy-start(bf16[2048,768]{1,0:T(8,128)(2,1)} %w_dec2.1) | copy-start | bytes 9437188
  91.7 20.7 %copy-start.16 = (s32[4]{0:T(128)S(1)}, s32[4]{0:T(128)}, u32[]{:S(2)}) copy-start(s32[4]{0:T(128)} %pad_add_fusion.at) | copy-start | bytes 52
  116.9 17.9 %copy-start.26 = (s32[8]{0:T(128)S(1)}, s32[8]{0:T(128)}, u32[]{:S(2)}) copy-start(s32[8]{0:T(128)} %param.15) | copy-start | bytes 100
  125.1 11.9 %collective-permute-start.8 = (bf16[48,1280]{1,0:T(8,128)(2,1)}, bf16[48,1280]{1,0:T(8,128)(2,1)}, u32[]{:S(2)}, u32[]{:S(2)}) collective-permute-start(bf16[48,1280]{1,0:T(8,128)(2,1)} %get-tuple-element.70), channel_id=1, source_target_pairs={{0,2},{2,4},{4,6},{6,0},{1,3},{3,5},{5,7},{7,1},{8,10},{10,12},{12... | collective-permute-start | bytes 368648 | tf_op jit(solution)/shard_map/ppermute | solution.py:64
  126.0 10.9 %collective-permute-start.7 = (bf16[48,1280]{1,0:T(8,128)(2,1)}, bf16[48,1280]{1,0:T(8,128)(2,1)}, u32[]{:S(2)}, u32[]{:S(2)}) collective-permute-start(bf16[48,1280]{1,0:T(8,128)(2,1)} %get-tuple-element.71), channel_id=1, source_target_pairs={{0,4},{2,6},{4,0},{6,2},{1,5},{3,7},{5,1},{7,3},{8,12},{10,14},{12... | collective-permute-start | bytes 368648 | tf_op jit(solution)/shard_map/ppermute | solution.py:64
  130.2 6.7 %collective-permute-start.6 = (bf16[48,1280]{1,0:T(8,128)(2,1)}, bf16[48,1280]{1,0:T(8,128)(2,1)}, u32[]{:S(2)}, u32[]{:S(2)}) collective-permute-start(bf16[48,1280]{1,0:T(8,128)(2,1)} %get-tuple-element.69), channel_id=1, source_target_pairs={{0,6},{2,0},{4,2},{6,4},{1,7},{3,1},{5,3},{7,5},{8,14},{10,8},{12,... | collective-permute-start | bytes 368648 | tf_op jit(solution)/shard_map/ppermute | solution.py:64
  131.3 12.5 %collective-permute-start.18 = (bf16[96,1216]{1,0:T(8,128)(2,1)}, bf16[96,1216]{1,0:T(8,128)(2,1)}, u32[]{:S(2)}, u32[]{:S(2)}) collective-permute-start(bf16[96,1216]{1,0:T(8,128)(2,1)} %slice_bitcast_fusion), channel_id=1, source_target_pairs={{0,8},{8,0},{1,9},{9,1},{2,10},{10,2},{3,11},{11,3},{4,12},{12,4},... | collective-permute-start | bytes 700424 | tf_op jit(solution)/shard_map/ppermute | solution.py:64
  139.1 8.4 %collective-permute-start.11 = (bf16[48,1280]{1,0:T(8,128)(2,1)}, bf16[48,1280]{1,0:T(8,128)(2,1)}, u32[]{:S(2)}, u32[]{:S(2)}) collective-permute-start(bf16[48,1280]{1,0:T(8,128)(2,1)} %get-tuple-element.72), channel_id=1, source_target_pairs={{0,6},{2,0},{4,2},{6,4},{1,7},{3,1},{5,3},{7,5},{8,14},{10,8},{12,... | collective-permute-start | bytes 368648 | tf_op jit(solution)/shard_map/ppermute | solution.py:64
  140.0 7.5 %collective-permute-start.10 = (bf16[48,1280]{1,0:T(8,128)(2,1)}, bf16[48,1280]{1,0:T(8,128)(2,1)}, u32[]{:S(2)}, u32[]{:S(2)}) collective-permute-start(bf16[48,1280]{1,0:T(8,128)(2,1)} %get-tuple-element.72), channel_id=1, source_target_pairs={{0,4},{2,6},{4,0},{6,2},{1,5},{3,7},{5,1},{7,3},{8,12},{10,14},{12... | collective-permute-start | bytes 368648 | tf_op jit(solution)/shard_map/ppermute | solution.py:64
  142.3 6.1 %collective-permute-start.9 = (bf16[48,1280]{1,0:T(8,128)(2,1)}, bf16[48,1280]{1,0:T(8,128)(2,1)}, u32[]{:S(2)}, u32[]{:S(2)}) collective-permute-start(bf16[48,1280]{1,0:T(8,128)(2,1)} %get-tuple-element.72), channel_id=1, source_target_pairs={{0,2},{2,4},{4,6},{6,0},{1,3},{3,5},{5,7},{7,1},{8,10},{10,12},{12... | collective-permute-start | bytes 368648 | tf_op jit(solution)/shard_map/ppermute | solution.py:64
  143.8 27.9 %collective-permute-start.15 = (bf16[768,640]{1,0:T(8,128)(2,1)}, bf16[768,640]{1,0:T(8,128)(2,1)S(1)}, u32[]{:S(2)}, u32[]{:S(2)}) collective-permute-start(bf16[768,640]{1,0:T(8,128)(2,1)} %get-tuple-element.42.slope), channel_id=1, source_target_pairs={{0,8},{8,0},{1,9},{9,1},{2,10},{10,2},{3,11},{11,3},{4,12},{12,4},... | collective-permute-start | bytes 2949128 | tf_op jit(solution)/shard_map/ppermute | solution.py:64
  147.3 24.4 %collective-permute-start.16 = (bf16[608,64]{1,0:T(8,128)(2,1)}, bf16[608,64]{1,0:T(8,128)(2,1)S(1)}, u32[]{:S(2)}, u32[]{:S(2)}) collective-permute-start(bf16[608,64]{1,0:T(8,128)(2,1)} %get-tuple-element.43.through), channel_id=1, source_target_pairs={{0,8},{8,0},{1,9},{9,1},{2,10},{10,2},{3,11},{11,3},{4,12},{12,4},... | collective-permute-start | bytes 233480 | tf_op jit(solution)/shard_map/ppermute | solution.py:64
  151.5 20.2 %copy-start.6 = (f32[48,1280]{1,0:T(8,128)S(1)}, f32[48,1280]{1,0:T(8,128)}, u32[]{:S(2)}) copy-start(f32[48,1280]{1,0:T(8,128)} %copy-done.5) | copy-start | bytes 737284
  157.2 9.1 %collective-permute-start.14 = (bf16[48,1280]{1,0:T(8,128)(2,1)S(1)}, bf16[48,1280]{1,0:T(8,128)(2,1)S(1)}, u32[]{:S(2)}, u32[]{:S(2)}) collective-permute-start(bf16[48,1280]{1,0:T(8,128)(2,1)S(1)} %get-tuple-element.67), channel_id=1, source_target_pairs={{0,2},{2,4},{4,6},{6,0},{1,3},{3,5},{5,7},{7,1},{8,10},{10,12},{12... | collective-permute-start | bytes 368648 | tf_op jit(solution)/shard_map/ppermute | solution.py:64
  158.7 8.8 %collective-permute-start.13 = (bf16[48,1280]{1,0:T(8,128)(2,1)S(1)}, bf16[48,1280]{1,0:T(8,128)(2,1)S(1)}, u32[]{:S(2)}, u32[]{:S(2)}) collective-permute-start(bf16[48,1280]{1,0:T(8,128)(2,1)S(1)} %get-tuple-element.68), channel_id=1, source_target_pairs={{0,4},{2,6},{4,0},{6,2},{1,5},{3,7},{5,1},{7,3},{8,12},{10,14},{12... | collective-permute-start | bytes 368648 | tf_op jit(solution)/shard_map/ppermute | solution.py:64
  162.1 6.0 %collective-permute-start.12 = (bf16[48,1280]{1,0:T(8,128)(2,1)S(1)}, bf16[48,1280]{1,0:T(8,128)(2,1)S(1)}, u32[]{:S(2)}, u32[]{:S(2)}) collective-permute-start(bf16[48,1280]{1,0:T(8,128)(2,1)S(1)} %get-tuple-element.66), channel_id=1, source_target_pairs={{0,6},{2,0},{4,2},{6,4},{1,7},{3,1},{5,3},{7,5},{8,14},{10,8},{12,... | collective-permute-start | bytes 368648 | tf_op jit(solution)/shard_map/ppermute | solution.py:64
  176.8 15.7 %copy-start.4 = (bf16[768,608]{1,0:T(8,128)(2,1)S(1)}, bf16[768,608]{1,0:T(8,128)(2,1)}, u32[]{:S(2)}) copy-start(bf16[768,608]{1,0:T(8,128)(2,1)} %get-tuple-element.32.hidden) | copy-start | bytes 2801668
  176.8 5.3 %collective-permute-start.17 = (bf16[48,128]{1,0:T(8,128)(2,1)S(1)}, bf16[48,128]{1,0:T(8,128)(2,1)S(1)}, u32[]{:S(2)}, u32[]{:S(2)}) collective-permute-start(bf16[48,128]{1,0:T(8,128)(2,1)S(1)} %get-tuple-element.75), channel_id=1, source_target_pairs={{0,8},{8,0},{1,9},{9,1},{2,10},{10,2},{3,11},{11,3},{4,12},{12,4},... | collective-permute-start | bytes 36872 | tf_op jit(solution)/shard_map/ppermute | solution.py:64
  194.2 10.7 %collective-permute-start.19 = (bf16[64,608]{1,0:T(8,128)(2,1)S(1)}, bf16[64,608]{1,0:T(8,128)(2,1)S(1)}, u32[]{:S(2)}, u32[]{:S(2)}) collective-permute-start(bf16[64,608]{1,0:T(8,128)(2,1)S(1)} %get-tuple-element.49), channel_id=1, source_target_pairs={{0,8},{8,0},{1,9},{9,1},{2,10},{10,2},{3,11},{11,3},{4,12},{12,4},... | collective-permute-start | bytes 233480 | tf_op jit(solution)/shard_map/ppermute | solution.py:64
  208.1 38.6 %all-to-all-start.4 = ((bf16[8,280,608]{2,1,0:T(8,128)(2,1)}), bf16[8,280,608]{2,1,0:T(8,128)(2,1)S(1)}, u32[]{:S(2)}, u32[]{:S(2)}) async-start(bf16[8,280,608]{2,1,0:T(8,128)(2,1)} %pad_maximum_fusion), calls=%async_computation.4 | async-start | bytes 5734400 | tf_op jit(solution)/shard_map/all_to_all | solution.py:80
  (21 other events, 95.5 us)
Sparse Core Ops, SparseCore 0:
  14.2 32.2 all-gather.4
  83.9 48.6 all-gather.8
  143.9 23.8 all-gather.6

commit v8 on v6

--- a/solution.py
+++ b/solution.py
@@ -489,16 +489,14 @@
 
     at = jnp.stack([far, near, lax.axis_index(("y", "core")), lax.axis_index("y")]).astype(jnp.int32)
 
-    turned_steps = from_all(timestep, IMAGE)
-    images = lax.iota(jnp.int32, n_images)
-    all_steps = jnp.zeros_like(images)
-    for step, value in enumerate(turned_steps):
-        all_steps = jnp.where(images == (my_image - step) % n_images, value[0], all_steps)
+    far_step = turned(timestep, "far", 1)
+    pair_steps = jnp.where(far == 0, jnp.stack([timestep, far_step]), jnp.stack([far_step, timestep]))
+    turned_steps = from_all(pair_steps, "z")
 
     split_in = jnp.moveaxis(w_in.reshape(d_dev, n_near, half), 1, 0)
     split_in = jnp.broadcast_to(split_in[None, :, None], (n_far, n_near, n_z, d_dev, half))
     split_in = split_in.reshape(n_rows, d_dev, half)
-    split_in, all_steps = lax.optimization_barrier((split_in, all_steps))
+    split_in, turned_steps = lax.optimization_barrier((split_in, turned_steps))
     full_in = exchanged(split_in, FAR_FIRST).reshape(n_far, wide, half)
 
     noise_rows = latent_noise[0]
@@ -511,6 +509,13 @@
     modulated = jnp.where(far == 0, modulated, modulated[::-1])
     token_rows = lax.all_gather(modulated, ("y", "core"), axis=1, tiled=True)
     far_rows = lax.all_gather(turned(modulated[1], "far", 1), ("y", "core"), axis=0, tiled=True)
+
+    all_steps = jnp.zeros((n_z, n_far), jnp.int32)
+    for step, value in enumerate(turned_steps):
+        owner = (lax.axis_index("z") - step) % n_z
+        here = lax.broadcasted_iota(jnp.int32, (n_z, n_far), 0) == owner
+        all_steps = jnp.where(here, value.reshape(1, n_far), all_steps)
+    all_steps = all_steps.reshape(n_images)
 
     first = lax.axis_index(ROWS_AT) * d_dev
     my_final = lax.dynamic_slice_in_dim(w_final, first, d_dev, 0).astype(F32)

time: 268 us -> 259 us (0.966)
  starting transfers between devices: 53.7 us -> 49.7 us
  other arithmetic: 19.4 us -> 15.7 us
    ppermute x22 -> x19, starting transfers between devices: 39.6 us -> 33.6 us  [turned(): lax.ppermute(value, axis, [(at, (at + steps) % count) for at in range(cou...]
    select_n x1 -> x2, other arithmetic: 4.48 us -> 0.78 us  [the longest x1 0.7 us: on_device(): jnp.where(far == 0, jnp.stack([timestep, far_step]), jnp.stack([far_step,...]
    ppermute x22 -> x19, waiting for transfers between devices: 15.1 us -> 14.2 us  [turned(): lax.ppermute(value, axis, [(at, (at + steps) % count) for at in range(cou...]
  transfers between devices with their start and end apart: 28 -> 25, of which waited for: 10 -> 11; matrix products, arithmetic and copies ran while one was open for 12% -> 11% of each run, Pallas kernels for 14% -> 14%
where the time goes in v8:
time: 259 us; the launch traced here: 256 us
  waiting for transfers between devices  61.6 us (24%)
  starting transfers between devices  49.7 us (19%)
  Pallas kernels  36.9 us (14%)
  between operations  31.6 us (12%)
  local copies, waits for them, and re-layouts  27.8 us (11%)
  blocking collectives  26.2 us (10%)
  other arithmetic  15.7 us (6%)
  matrix products  6.06 us (2%)
    all_to_all x3, waiting for transfers between devices, exchanged(): return lax.all_to_all(blocks, axis, 0, 0, tiled=True)  47.4 us
    pallas_call x8, Pallas kernels, call(): pl.pallas_call(kernel, grid=(grid,), in_specs=in_specs, out_specs=out_spe...  36.9 us
    ppermute x19, starting transfers between devices, turned(): lax.ppermute(value, axis, [(at, (at + steps) % count) for at in range(cou...  33.6 us
    all_to_all x2, blocking collectives, exchanged(): return lax.all_to_all(blocks, axis, 0, 0, tiled=True)  26.2 us
    all_to_all x3, starting transfers between devices, exchanged(): return lax.all_to_all(blocks, axis, 0, 0, tiled=True)  15.9 us
    ppermute x19, waiting for transfers between devices, turned(): lax.ppermute(value, axis, [(at, (at + steps) % count) for at in range(cou...  14.2 us
    unnamed x55, local copies, waits for them, and re-layouts  9.26 us
    rev x1, local copies, waits for them, and re-layouts, on_device(): my_gated[:, :, ::-1]  5.31 us
  transfers between devices with their start and end apart: 25, of which 11 were waited for; matrix products, arithmetic and copies ran while one was open for 11% of the time, Pallas kernels for 14%

profile of v8, /device:TPU:8, one launch (start us, length us, event | category | flops | bytes accessed | tf_op | source)
XLA Modules:
  0.0 255.7 jit_solution(13816365586093497214)
XLA Ops:
  14.1 3.1 %collective-permute-start = (s32[1]{0:T(128)}, s32[1]{0:T(128)}, u32[]{:S(2)}, u32[]{:S(2)}) collective-permute-start(s32[1]{0:T(128)} %param.14), channel_id=1, source_target_pairs={{0,8},{8,0},{1,9},{9,1},{2,10},{10,2},{3,11},{11,3},{4,12},{12,4},... | collective-permute-start | bytes 20 | tf_op jit(solution)/shard_map/ppermute | solution.py:64
  20.0 1.9 collective-permute-start.1
  21.9 3.6 %collective-permute-start.2 = (s32[2,1]{0,1:T(1,128)S(1)}, s32[2,1]{0,1:T(1,128)S(1)}, u32[]{:S(2)}, u32[]{:S(2)}) collective-permute-start(s32[2,1]{0,1:T(1,128)S(1)} %broadcast_select_fusion.1), channel_id=1, source_target_pairs={{0,32},{16,48},{32,0},{48,16},{1,33},{17,49},{33,1},{49,17},{2,34}... | collective-permute-start | bytes 32 | tf_op jit(solution)/shard_map/ppermute | solution.py:64
  27.0 2.0 collective-permute-done.3
  29.0 2.0 broadcast_in_dim.56
  31.0 6.2 %all-to-all-start = ((bf16[16,152,608]{2,1,0:T(8,128)(2,1)}), bf16[16,152,608]{2,1,0:T(8,128)(2,1)}, u32[]{:S(2)}, u32[]{:S(2)}) async-start(bf16[16,152,608]{2,1,0:T(8,128)(2,1)} %bitcast.10), calls=%async_computation | async-start | bytes 6225920 | tf_op jit(solution)/shard_map/all_to_all | solution.py:80
  55.4 3.1 %shard_map.140 = bf16[2,8,304,128]{3,2,1,0:T(8,128)(2,1)} custom-call(bf16[152,1216]{1,0:T(8,128)(2,1)} %w_out.1, bf16[152,512]{1,0:T(8,128)(2,1)} %convert_element_type.87.gated), custom_call_target="tpu_custom_call" | custom-call | flops 189267968 | bytes 369664 | tf_op jit(solution)/shard_map/pallas_call | solution.py:95
  58.5 17.1 %all-to-all-done = bf16[16,152,608]{2,1,0:T(8,128)(2,1)} async-done(((bf16[16,152,608]{2,1,0:T(8,128)(2,1)}), bf16[16,152,608]{2,1,0:T(8,128)(2,1)}, u32[]{:S(2)}, u32[]{:S(2)}) %all-to-all-start) | async-done | bytes 2957344 | tf_op jit(solution)/shard_map/all_to_all | solution.py:80
  75.6 5.8 %all-to-all-start.1 = ((bf16[16,304,128]{2,1,0:T(8,128)(2,1)}), bf16[16,304,128]{2,1,0:T(8,128)(2,1)}, u32[]{:S(2)}, u32[]{:S(2)}) async-start(bf16[16,304,128]{2,1,0:T(8,128)(2,1)} %bitcast.87), calls=%async_computation.1 | async-start | bytes 2490368 | tf_op jit(solution)/shard_map/all_to_all | solution.py:80
  84.4 8.0 %shard_map.141 = (bf16[768,608]{1,0:T(8,128)(2,1)}, bf16[768,640]{1,0:T(8,128)(2,1)}) custom-call(s32[4]{0:T(128)} %pad_add_fusion.at, bf16[2,768,1216]{2,1,0:T(8,128)(2,1)} %all-gather.5.cloned.1.call-done.tokens, bf16[2,1216,608]{2,1,0:T(8,128)(2,1)} %bitcast.35.weights), custom_call_target="tpu_custom_call" | custom-call | flops 2271215616 | bytes 8560640 | tf_op jit(solution)/shard_map/pallas_call | solution.py:95
  92.4 5.2 %all-to-all-done.1.terms = bf16[16,304,128]{2,1,0:T(8,128)(2,1)} async-done(((bf16[16,304,128]{2,1,0:T(8,128)(2,1)}), bf16[16,304,128]{2,1,0:T(8,128)(2,1)}, u32[]{:S(2)}, u32[]{:S(2)}) %all-to-all-start.1) | async-done | bytes 1245216 | tf_op jit(solution)/shard_map/all_to_all | solution.py:80
  97.5 3.2 %shard_map.142 = (bf16[2,4,2,2,48,128]{5,4,3,2,1,0:T(8,128)(2,1)}, bf16[608,64]{1,0:T(8,128)(2,1)}) custom-call(s32[4]{0:T(128)} %pad_add_fusion.at, bf16[768,608]{1,0:T(8,128)(2,1)} %get-tuple-element.32.hidden, bf16[16,304,128]{2,1,0:T(8,128)(2,1)} %all-to-all-done.1.terms, f32[96,64]{1,0:T(8,128)} %fusion.10.own_part), custom_call_target="tpu_custom_call" | custom-call | flops 59768832 | bytes 933888 | tf_op jit(solution)/shard_map/pallas_call | solution.py:95
  100.7 11.5 %all_to_all.25.parts = bf16[16,2,48,128]{3,2,1,0:T(8,128)(2,1)S(1)} all-to-all(bf16[16,2,48,128]{3,2,1,0:T(8,128)(2,1)} %bitcast.94), channel_id=1, replica_groups=mesh['near'=2,'z'=4,'far'=2,'y'=4,'core'=2] {'near','y','core'}, dimensions={0} | all-to-all | bytes 786432 | tf_op jit(solution)/shard_map/all_to_all | solution.py:80
  112.2 3.7 %shard_map.143 = (bf16[192,1280]{1,0:T(8,128)(2,1)S(1)}, f32[48,1280]{1,0:T(8,128)S(1)}, f32[48,2048]{1,0:T(8,128)S(1)}) custom-call(s32[4]{0:T(128)S(1)} %copy-done.16, bf16[16,2,48,128]{3,2,1,0:T(8,128)(2,1)S(1)} %all_to_all.25.parts, bf16[64,2048]{1,0:T(8,128)(2,1)S(1)} %copy-done.7, bf16[2048,768]{1,0:T(8,128)(2,1)S(1)} %copy-done.1, ...), custom_call_target="tpu_custom_call" | custom-call | flops 1031798784 | bytes 5111808 | tf_op jit(solution)/shard_map/pallas_call | solution.py:95
  116.7 5.1 %shard_map.144 = (f32[192,640]{1,0:T(8,128)S(1)}, f32[192,640]{1,0:T(8,128)S(1)}, bf16[192,1280]{1,0:T(8,128)(2,1)S(1)}) custom-call(bf16[192,1280]{1,0:T(8,128)(2,1)S(1)} %get-tuple-element.37.normed, bf16[1280,640]{1,0:T(8,128)(2,1)} %v1a.3, bf16[1280,640]{1,0:T(8,128)(2,1)} %collective-permute-done.4.v1b, bf16[640,1280]{1,0:T(8,128)(2,1)} %v2a.3, ...), custom_call_target="tpu_custom_call" | custom-call | flops 1258291200 | bytes 6553600 | tf_op jit(solution)/shard_map/pallas_call | solution.py:95
  125.9 4.1 %collective-permute-start.7 = (bf16[48,1280]{1,0:T(8,128)(2,1)}, bf16[48,1280]{1,0:T(8,128)(2,1)}, u32[]{:S(2)}, u32[]{:S(2)}) collective-permute-start(bf16[48,1280]{1,0:T(8,128)(2,1)} %get-tuple-element.71), channel_id=1, source_target_pairs={{0,4},{2,6},{4,0},{6,2},{1,5},{3,7},{5,1},{7,3},{8,12},{10,14},{12... | collective-permute-start | bytes 368648 | tf_op jit(solution)/shard_map/ppermute | solution.py:64
  131.2 3.0 %collective-permute-start.17 = (bf16[96,1216]{1,0:T(8,128)(2,1)}, bf16[96,1216]{1,0:T(8,128)(2,1)}, u32[]{:S(2)}, u32[]{:S(2)}) collective-permute-start(bf16[96,1216]{1,0:T(8,128)(2,1)} %slice_bitcast_fusion), channel_id=1, source_target_pairs={{0,8},{8,0},{1,9},{9,1},{2,10},{10,2},{3,11},{11,3},{4,12},{12,4},... | collective-permute-start | bytes 700424 | tf_op jit(solution)/shard_map/ppermute | solution.py:64
  136.7 2.1 fusion.13
  139.6 2.3 collective-permute-start.10
  143.6 3.0 %collective-permute-start.15 = (bf16[768,640]{1,0:T(8,128)(2,1)}, bf16[768,640]{1,0:T(8,128)(2,1)S(1)}, u32[]{:S(2)}, u32[]{:S(2)}) collective-permute-start(bf16[768,640]{1,0:T(8,128)(2,1)} %get-tuple-element.42.slope), channel_id=1, source_target_pairs={{0,8},{8,0},{1,9},{9,1},{2,10},{10,2},{3,11},{11,3},{4,12},{12,4},... | collective-permute-start | bytes 2949128 | tf_op jit(solution)/shard_map/ppermute | solution.py:64
  151.3 5.6 %shard_map.145 = bf16[192,1280]{1,0:T(8,128)(2,1)S(1)} custom-call(bf16[192,1280]{1,0:T(8,128)(2,1)S(1)} %pad_maximum_fusion.2.grad, bf16[1280,640]{1,0:T(8,128)(2,1)} %v1a.3, bf16[1280,640]{1,0:T(8,128)(2,1)} %collective-permute-done.4.v1b, bf16[640,1280]{1,0:T(8,128)(2,1)} %v2a.3, bf16[640,1280]{1,0:T(8,128)(2,1)} %collective-permute-done.5.v2b, ...), custom_call_target="tpu_custom_call" | custom-call | flops 1258291200 | bytes 6553600 | tf_op jit(solution)/shard_map/pallas_call | solution.py:95
  158.6 3.3 %collective-permute-start.13 = (bf16[48,1280]{1,0:T(8,128)(2,1)S(1)}, bf16[48,1280]{1,0:T(8,128)(2,1)S(1)}, u32[]{:S(2)}, u32[]{:S(2)}) collective-permute-start(bf16[48,1280]{1,0:T(8,128)(2,1)S(1)} %get-tuple-element.68), channel_id=1, source_target_pairs={{0,4},{2,6},{4,0},{6,2},{1,5},{3,7},{5,1},{7,3},{8,12},{10,14},{12... | collective-permute-start | bytes 368648 | tf_op jit(solution)/shard_map/ppermute | solution.py:64
  162.2 4.0 %collective-permute-done.14 = bf16[48,1280]{1,0:T(8,128)(2,1)S(1)} collective-permute-done((bf16[48,1280]{1,0:T(8,128)(2,1)S(1)}, bf16[48,1280]{1,0:T(8,128)(2,1)S(1)}, u32[]{:S(2)}, u32[]{:S(2)}) %collective-permute-start.14) | collective-permute-done | bytes 122912 | tf_op jit(solution)/shard_map/ppermute | solution.py:64
  167.9 3.4 %collective-permute-done.16.through2 = bf16[608,64]{1,0:T(8,128)(2,1)S(1)} collective-permute-done((bf16[608,64]{1,0:T(8,128)(2,1)}, bf16[608,64]{1,0:T(8,128)(2,1)S(1)}, u32[]{:S(2)}, u32[]{:S(2)}) %collective-permute-start.16) | collective-permute-done | bytes 77856 | tf_op jit(solution)/shard_map/ppermute | solution.py:64
  171.9 2.3 convolution_convert_fusion
  174.2 2.3 fusion.6
  176.6 14.8 %all_to_all.26 = bf16[32,48,128]{2,1,0:T(8,128)(2,1)S(1)} all-to-all(bf16[32,48,128]{2,1,0:T(8,128)(2,1)S(1)} %broadcast_in_dim.67), channel_id=1, replica_groups=mesh['near'=2,'z'=4,'far'=2,'y'=4,'core'=2] {'far','near','y','core'}, dimensions={0} | all-to-all | bytes 786432 | tf_op jit(solution)/shard_map/all_to_all | solution.py:80
  194.9 7.3 %shard_map.147 = bf16[1216,608]{1,0:T(8,128)(2,1)} custom-call(bf16[768,128]{1,0:T(8,128)(2,1)} %copy-done.14, bf16[608,64]{1,0:T(8,128)(2,1)} %get-tuple-element.43.through, bf16[768,640]{1,0:T(8,128)(2,1)} %get-tuple-element.42.slope, bf16[2,768,1216]{2,1,0:T(8,128)(2,1)} %all-gather.5.cloned.1.call-done.tokens, bf16[768,128]{1,0:T(8,128)(2,1)} %copy-done.15, ...), custom_call_target="tpu_custom_call" | custom-call | flops 2271215616 | bytes 7081984 | tf_op jit(solution)/shard_map/pallas_call | solution.py:95
  203.6 1.8 pad_maximum_fusion
  205.5 3.9 %all-to-all-start.4 = ((bf16[8,280,608]{2,1,0:T(8,128)(2,1)}), bf16[8,280,608]{2,1,0:T(8,128)(2,1)S(1)}, u32[]{:S(2)}, u32[]{:S(2)}) async-start(bf16[8,280,608]{2,1,0:T(8,128)(2,1)} %pad_maximum_fusion), calls=%async_computation.4 | async-start | bytes 5734400 | tf_op jit(solution)/shard_map/all_to_all | solution.py:80
  211.0 5.3 %rev.7 = bf16[152,4,2,64]{3,2,1,0:T(2,128)(2,1)} reverse(bf16[152,4,2,64]{3,2,1,0:T(2,128)(2,1)} %multiply_convert_fusion), dimensions={2} | reverse | bytes 311296 | tf_op jit(solution)/shard_map/rev | solution.py:591
  219.0 25.1 %all-to-all-done.4 = bf16[8,280,608]{2,1,0:T(8,128)(2,1)S(1)} async-done(((bf16[8,280,608]{2,1,0:T(8,128)(2,1)}), bf16[8,280,608]{2,1,0:T(8,128)(2,1)S(1)}, u32[]{:S(2)}, u32[]{:S(2)}) %all-to-all-start.4) | async-done | bytes 2723872 | tf_op jit(solution)/shard_map/all_to_all | solution.py:80
  (149 shorter events, 48.9 us)
Async XLA Ops:
  7.2 68.5 %copy-start = (bf16[1,96,1280]{2,1,0:T(8,128)(2,1)S(1)}, bf16[1,96,1280]{2,1,0:T(8,128)(2,1)}, u32[]{:S(2)}) copy-start(bf16[1,96,1280]{2,1,0:T(8,128)(2,1)} %param.16) | copy-start | bytes 737284
  7.2 77.2 %all-gather.5.cloned.1.call-start = ((), (), s32[]{:S(2)}) async-start(), calls=%async_computation.5 | async-start | bytes 4423680 | tf_op jit(solution)/shard_map/all_gather | solution.py:510
  14.1 5.2 %collective-permute-start = (s32[1]{0:T(128)}, s32[1]{0:T(128)}, u32[]{:S(2)}, u32[]{:S(2)}) collective-permute-start(s32[1]{0:T(128)} %param.14), channel_id=1, source_target_pairs={{0,8},{8,0},{1,9},{9,1},{2,10},{10,2},{3,11},{11,3},{4,12},{12,4},... | collective-permute-start | bytes 20 | tf_op jit(solution)/shard_map/ppermute | solution.py:64
  20.0 6.5 %collective-permute-start.1 = (s32[2,1]{0,1:T(1,128)S(1)}, s32[2,1]{0,1:T(1,128)S(1)}, u32[]{:S(2)}, u32[]{:S(2)}) collective-permute-start(s32[2,1]{0,1:T(1,128)S(1)} %broadcast_select_fusion.1), channel_id=1, source_target_pairs={{0,16},{16,32},{32,48},{48,0},{1,17},{17,33},{33,49},{49,1},{2,18}... | collective-permute-start | bytes 32 | tf_op jit(solution)/shard_map/ppermute | solution.py:64
  21.9 5.1 %collective-permute-start.2 = (s32[2,1]{0,1:T(1,128)S(1)}, s32[2,1]{0,1:T(1,128)S(1)}, u32[]{:S(2)}, u32[]{:S(2)}) collective-permute-start(s32[2,1]{0,1:T(1,128)S(1)} %broadcast_select_fusion.1), channel_id=1, source_target_pairs={{0,32},{16,48},{32,0},{48,16},{1,33},{17,49},{33,1},{49,17},{2,34}... | collective-permute-start | bytes 32 | tf_op jit(solution)/shard_map/ppermute | solution.py:64
  25.5 3.5 %collective-permute-start.3 = (s32[2,1]{0,1:T(1,128)S(1)}, s32[2,1]{0,1:T(1,128)S(1)}, u32[]{:S(2)}, u32[]{:S(2)}) collective-permute-start(s32[2,1]{0,1:T(1,128)S(1)} %broadcast_select_fusion.1), channel_id=1, source_target_pairs={{0,48},{16,0},{32,16},{48,32},{1,49},{17,1},{33,17},{49,33},{2,50}... | collective-permute-start | bytes 32 | tf_op jit(solution)/shard_map/ppermute | solution.py:64
  31.0 44.6 %all-to-all-start = ((bf16[16,152,608]{2,1,0:T(8,128)(2,1)}), bf16[16,152,608]{2,1,0:T(8,128)(2,1)}, u32[]{:S(2)}, u32[]{:S(2)}) async-start(bf16[16,152,608]{2,1,0:T(8,128)(2,1)} %bitcast.10), calls=%async_computation | async-start | bytes 6225920 | tf_op jit(solution)/shard_map/all_to_all | solution.py:80
  75.6 21.9 %all-to-all-start.1 = ((bf16[16,304,128]{2,1,0:T(8,128)(2,1)}), bf16[16,304,128]{2,1,0:T(8,128)(2,1)}, u32[]{:S(2)}, u32[]{:S(2)}) async-start(bf16[16,304,128]{2,1,0:T(8,128)(2,1)} %bitcast.87), calls=%async_computation.1 | async-start | bytes 2490368 | tf_op jit(solution)/shard_map/all_to_all | solution.py:80
  81.5 55.2 %all-gather.9.cloned.1.call-start = ((), (), s32[]{:S(2)}) async-start(), calls=%async_computation.7 | async-start | bytes 1290240 | tf_op jit(solution)/shard_map/all_gather | solution.py:540
  81.5 35.2 %collective-permute-start.4 = (bf16[1280,640]{1,0:T(8,128)(2,1)}, bf16[1280,640]{1,0:T(8,128)(2,1)}, u32[]{:S(2)}, u32[]{:S(2)}) collective-permute-start(bf16[1280,640]{1,0:T(8,128)(2,1)} %v1a.3), channel_id=1, source_target_pairs={{0,1},{1,0},{2,3},{3,2},{4,5},{5,4},{6,7},{7,6},{8,9},{9,8},{10,11... | collective-permute-start | bytes 4915208 | tf_op jit(solution)/shard_map/ppermute | solution.py:64
  81.6 35.1 %collective-permute-start.5 = (bf16[640,1280]{1,0:T(8,128)(2,1)}, bf16[640,1280]{1,0:T(8,128)(2,1)}, u32[]{:S(2)}, u32[]{:S(2)}) collective-permute-start(bf16[640,1280]{1,0:T(8,128)(2,1)} %v2a.3), channel_id=1, source_target_pairs={{0,1},{1,0},{2,3},{3,2},{4,5},{5,4},{6,7},{7,6},{8,9},{9,8},{10,11... | collective-permute-start | bytes 4915208 | tf_op jit(solution)/shard_map/ppermute | solution.py:64
  82.8 112.1 %all-gather.7.cloned.1.call-start = ((), (), s32[]{:S(2)}) async-start(), calls=%async_computation.6 | async-start | bytes 2211840 | tf_op jit(solution)/shard_map/all_gather | solution.py:511
  84.4 27.8 %copy-start.1 = (bf16[2048,768]{1,0:T(8,128)(2,1)S(1)}, bf16[2048,768]{1,0:T(8,128)(2,1)}, u32[]{:S(2)}) copy-start(bf16[2048,768]{1,0:T(8,128)(2,1)} %w_dec2.1) | copy-start | bytes 9437188
  92.4 19.8 %copy-start.16 = (s32[4]{0:T(128)S(1)}, s32[4]{0:T(128)}, u32[]{:S(2)}) copy-start(s32[4]{0:T(128)} %pad_add_fusion.at) | copy-start | bytes 52
  116.7 17.4 %copy-start.26 = (s32[8]{0:T(128)S(1)}, s32[8]{0:T(128)}, u32[]{:S(2)}) copy-start(s32[8]{0:T(128)} %param.15) | copy-start | bytes 100
  124.9 11.8 %collective-permute-start.8 = (bf16[48,1280]{1,0:T(8,128)(2,1)}, bf16[48,1280]{1,0:T(8,128)(2,1)}, u32[]{:S(2)}, u32[]{:S(2)}) collective-permute-start(bf16[48,1280]{1,0:T(8,128)(2,1)} %get-tuple-element.70), channel_id=1, source_target_pairs={{0,2},{2,4},{4,6},{6,0},{1,3},{3,5},{5,7},{7,1},{8,10},{10,12},{12... | collective-permute-start | bytes 368648 | tf_op jit(solution)/shard_map/ppermute | solution.py:64
  125.9 10.7 %collective-permute-start.7 = (bf16[48,1280]{1,0:T(8,128)(2,1)}, bf16[48,1280]{1,0:T(8,128)(2,1)}, u32[]{:S(2)}, u32[]{:S(2)}) collective-permute-start(bf16[48,1280]{1,0:T(8,128)(2,1)} %get-tuple-element.71), channel_id=1, source_target_pairs={{0,4},{2,6},{4,0},{6,2},{1,5},{3,7},{5,1},{7,3},{8,12},{10,14},{12... | collective-permute-start | bytes 368648 | tf_op jit(solution)/shard_map/ppermute | solution.py:64
  130.1 6.6 %collective-permute-start.6 = (bf16[48,1280]{1,0:T(8,128)(2,1)}, bf16[48,1280]{1,0:T(8,128)(2,1)}, u32[]{:S(2)}, u32[]{:S(2)}) collective-permute-start(bf16[48,1280]{1,0:T(8,128)(2,1)} %get-tuple-element.69), channel_id=1, source_target_pairs={{0,6},{2,0},{4,2},{6,4},{1,7},{3,1},{5,3},{7,5},{8,14},{10,8},{12,... | collective-permute-start | bytes 368648 | tf_op jit(solution)/shard_map/ppermute | solution.py:64
  131.2 12.4 %collective-permute-start.17 = (bf16[96,1216]{1,0:T(8,128)(2,1)}, bf16[96,1216]{1,0:T(8,128)(2,1)}, u32[]{:S(2)}, u32[]{:S(2)}) collective-permute-start(bf16[96,1216]{1,0:T(8,128)(2,1)} %slice_bitcast_fusion), channel_id=1, source_target_pairs={{0,8},{8,0},{1,9},{9,1},{2,10},{10,2},{3,11},{11,3},{4,12},{12,4},... | collective-permute-start | bytes 700424 | tf_op jit(solution)/shard_map/ppermute | solution.py:64
  138.8 8.5 %collective-permute-start.11 = (bf16[48,1280]{1,0:T(8,128)(2,1)}, bf16[48,1280]{1,0:T(8,128)(2,1)}, u32[]{:S(2)}, u32[]{:S(2)}) collective-permute-start(bf16[48,1280]{1,0:T(8,128)(2,1)} %get-tuple-element.72), channel_id=1, source_target_pairs={{0,6},{2,0},{4,2},{6,4},{1,7},{3,1},{5,3},{7,5},{8,14},{10,8},{12,... | collective-permute-start | bytes 368648 | tf_op jit(solution)/shard_map/ppermute | solution.py:64
  139.6 7.6 %collective-permute-start.10 = (bf16[48,1280]{1,0:T(8,128)(2,1)}, bf16[48,1280]{1,0:T(8,128)(2,1)}, u32[]{:S(2)}, u32[]{:S(2)}) collective-permute-start(bf16[48,1280]{1,0:T(8,128)(2,1)} %get-tuple-element.72), channel_id=1, source_target_pairs={{0,4},{2,6},{4,0},{6,2},{1,5},{3,7},{5,1},{7,3},{8,12},{10,14},{12... | collective-permute-start | bytes 368648 | tf_op jit(solution)/shard_map/ppermute | solution.py:64
  141.9 6.2 %collective-permute-start.9 = (bf16[48,1280]{1,0:T(8,128)(2,1)}, bf16[48,1280]{1,0:T(8,128)(2,1)}, u32[]{:S(2)}, u32[]{:S(2)}) collective-permute-start(bf16[48,1280]{1,0:T(8,128)(2,1)} %get-tuple-element.72), channel_id=1, source_target_pairs={{0,2},{2,4},{4,6},{6,0},{1,3},{3,5},{5,7},{7,1},{8,10},{10,12},{12... | collective-permute-start | bytes 368648 | tf_op jit(solution)/shard_map/ppermute | solution.py:64
  143.6 27.8 %collective-permute-start.15 = (bf16[768,640]{1,0:T(8,128)(2,1)}, bf16[768,640]{1,0:T(8,128)(2,1)S(1)}, u32[]{:S(2)}, u32[]{:S(2)}) collective-permute-start(bf16[768,640]{1,0:T(8,128)(2,1)} %get-tuple-element.42.slope), channel_id=1, source_target_pairs={{0,8},{8,0},{1,9},{9,1},{2,10},{10,2},{3,11},{11,3},{4,12},{12,4},... | collective-permute-start | bytes 2949128 | tf_op jit(solution)/shard_map/ppermute | solution.py:64
  146.6 24.7 %collective-permute-start.16 = (bf16[608,64]{1,0:T(8,128)(2,1)}, bf16[608,64]{1,0:T(8,128)(2,1)S(1)}, u32[]{:S(2)}, u32[]{:S(2)}) collective-permute-start(bf16[608,64]{1,0:T(8,128)(2,1)} %get-tuple-element.43.through), channel_id=1, source_target_pairs={{0,8},{8,0},{1,9},{9,1},{2,10},{10,2},{3,11},{11,3},{4,12},{12,4},... | collective-permute-start | bytes 233480 | tf_op jit(solution)/shard_map/ppermute | solution.py:64
  151.3 20.1 %copy-start.6 = (f32[48,1280]{1,0:T(8,128)S(1)}, f32[48,1280]{1,0:T(8,128)}, u32[]{:S(2)}) copy-start(f32[48,1280]{1,0:T(8,128)} %copy-done.5) | copy-start | bytes 737284
  156.9 14.9 %copy-start.3 = (bf16[768,1280]{1,0:T(8,128)(2,1)S(1)}, bf16[768,1280]{1,0:T(8,128)(2,1)}, u32[]{:S(2)}) copy-start(bf16[768,1280]{1,0:T(8,128)(2,1)} %w_patch.1) | copy-start | bytes 5898244
  157.0 9.2 %collective-permute-start.14 = (bf16[48,1280]{1,0:T(8,128)(2,1)S(1)}, bf16[48,1280]{1,0:T(8,128)(2,1)S(1)}, u32[]{:S(2)}, u32[]{:S(2)}) collective-permute-start(bf16[48,1280]{1,0:T(8,128)(2,1)S(1)} %get-tuple-element.67), channel_id=1, source_target_pairs={{0,2},{2,4},{4,6},{6,0},{1,3},{3,5},{5,7},{7,1},{8,10},{10,12},{12... | collective-permute-start | bytes 368648 | tf_op jit(solution)/shard_map/ppermute | solution.py:64
  158.6 8.9 %collective-permute-start.13 = (bf16[48,1280]{1,0:T(8,128)(2,1)S(1)}, bf16[48,1280]{1,0:T(8,128)(2,1)S(1)}, u32[]{:S(2)}, u32[]{:S(2)}) collective-permute-start(bf16[48,1280]{1,0:T(8,128)(2,1)S(1)} %get-tuple-element.68), channel_id=1, source_target_pairs={{0,4},{2,6},{4,0},{6,2},{1,5},{3,7},{5,1},{7,3},{8,12},{10,14},{12... | collective-permute-start | bytes 368648 | tf_op jit(solution)/shard_map/ppermute | solution.py:64
  161.9 6.0 %collective-permute-start.12 = (bf16[48,1280]{1,0:T(8,128)(2,1)S(1)}, bf16[48,1280]{1,0:T(8,128)(2,1)S(1)}, u32[]{:S(2)}, u32[]{:S(2)}) collective-permute-start(bf16[48,1280]{1,0:T(8,128)(2,1)S(1)} %get-tuple-element.66), channel_id=1, source_target_pairs={{0,6},{2,0},{4,2},{6,4},{1,7},{3,1},{5,3},{7,5},{8,14},{10,8},{12,... | collective-permute-start | bytes 368648 | tf_op jit(solution)/shard_map/ppermute | solution.py:64
  176.5 14.8 %copy-start.4 = (bf16[768,608]{1,0:T(8,128)(2,1)S(1)}, bf16[768,608]{1,0:T(8,128)(2,1)}, u32[]{:S(2)}) copy-start(bf16[768,608]{1,0:T(8,128)(2,1)} %get-tuple-element.32.hidden) | copy-start | bytes 2801668
  193.6 8.7 %collective-permute-start.18 = (bf16[64,608]{1,0:T(8,128)(2,1)S(1)}, bf16[64,608]{1,0:T(8,128)(2,1)S(1)}, u32[]{:S(2)}, u32[]{:S(2)}) collective-permute-start(bf16[64,608]{1,0:T(8,128)(2,1)S(1)} %get-tuple-element.49), channel_id=1, source_target_pairs={{0,8},{8,0},{1,9},{9,1},{2,10},{10,2},{3,11},{11,3},{4,12},{12,4},... | collective-permute-start | bytes 233480 | tf_op jit(solution)/shard_map/ppermute | solution.py:64
  205.5 38.7 %all-to-all-start.4 = ((bf16[8,280,608]{2,1,0:T(8,128)(2,1)}), bf16[8,280,608]{2,1,0:T(8,128)(2,1)S(1)}, u32[]{:S(2)}, u32[]{:S(2)}) async-start(bf16[8,280,608]{2,1,0:T(8,128)(2,1)} %pad_maximum_fusion), calls=%async_computation.4 | async-start | bytes 5734400 | tf_op jit(solution)/shard_map/all_to_all | solution.py:80
  (20 other events, 80.5 us)
Sparse Core Ops, SparseCore 0:
  14.2 32.2 all-gather.4
  84.6 48.6 all-gather.8
  143.8 23.9 all-gather.6

commit v9 on v8

--- a/solution.py
+++ b/solution.py
@@ -491,6 +491,7 @@
 
     far_step = turned(timestep, "far", 1)
     pair_steps = jnp.where(far == 0, jnp.stack([timestep, far_step]), jnp.stack([far_step, timestep]))
+    pair_steps, noise_rows = lax.optimization_barrier((pair_steps, latent_noise[0]))
     turned_steps = from_all(pair_steps, "z")
 
     split_in = jnp.moveaxis(w_in.reshape(d_dev, n_near, half), 1, 0)
@@ -499,7 +500,6 @@
     split_in, turned_steps = lax.optimization_barrier((split_in, turned_steps))
     full_in = exchanged(split_in, FAR_FIRST).reshape(n_far, wide, half)
 
-    noise_rows = latent_noise[0]
     modulate = modulation[timestep[0]]
     modulated = (
         layer_norm(noise_rows.astype(F32)) * (1.0 + modulate[1]) + modulate[0]

time: 259 us -> 260 us (level)
  blocking collectives: 26.2 us -> 14.9 us
  starting transfers between devices: 49.7 us -> 54.4 us
  waiting for transfers between devices: 61.6 us -> 65.8 us
  local copies, waits for them, and re-layouts: 27.8 us -> 30.7 us
    all_to_all x2 -> x1, blocking collectives: 26.2 us -> 14.9 us  [exchanged(): return lax.all_to_all(blocks, axis, 0, 0, tiled=True)]
    all_to_all x3 -> x4, waiting for transfers between devices: 47.4 us -> 51.3 us  [exchanged(): return lax.all_to_all(blocks, axis, 0, 0, tiled=True)]
    all_to_all x3 -> x4, starting transfers between devices: 15.9 us -> 19.8 us  [exchanged(): return lax.all_to_all(blocks, axis, 0, 0, tiled=True)]
    unnamed x55 -> x53, local copies, waits for them, and re-layouts: 9.26 us -> 12.4 us
  transfers between devices with their start and end apart: 25 -> 26, of which waited for: 11 -> 13; matrix products, arithmetic and copies ran while one was open for 11% -> 12% of each run, Pallas kernels for 14% -> 15%
where the time goes in v9:
time: 260 us; the launch traced here: 256 us
  waiting for transfers between devices  65.8 us (25%)
  starting transfers between devices  54.4 us (21%)
  Pallas kernels  37.2 us (14%)
  between operations  31.8 us (12%)
  local copies, waits for them, and re-layouts  30.7 us (12%)
  other arithmetic  15.5 us (6%)
  blocking collectives  14.9 us (6%)
  matrix products  6.12 us (2%)
    all_to_all x4, waiting for transfers between devices, exchanged(): return lax.all_to_all(blocks, axis, 0, 0, tiled=True)  51.3 us
    pallas_call x8, Pallas kernels, call(): pl.pallas_call(kernel, grid=(grid,), in_specs=in_specs, out_specs=out_spe...  37.2 us
    ppermute x19, starting transfers between devices, turned(): lax.ppermute(value, axis, [(at, (at + steps) % count) for at in range(cou...  34.3 us
    all_to_all x4, starting transfers between devices, exchanged(): return lax.all_to_all(blocks, axis, 0, 0, tiled=True)  19.8 us
    all_to_all x1, blocking collectives, exchanged(): return lax.all_to_all(blocks, axis, 0, 0, tiled=True)  14.9 us
    ppermute x19, waiting for transfers between devices, turned(): lax.ppermute(value, axis, [(at, (at + steps) % count) for at in range(cou...  14.5 us
    unnamed x53, local copies, waits for them, and re-layouts  12.4 us
    rev x1, local copies, waits for them, and re-layouts, on_device(): my_gated[:, :, ::-1]  5.31 us
  transfers between devices with their start and end apart: 26, of which 13 were waited for; matrix products, arithmetic and copies ran while one was open for 12% of the time, Pallas kernels for 15%

profile of v9, /device:TPU:8, one launch (start us, length us, event | category | flops | bytes accessed | tf_op | source)
XLA Modules:
  0.0 256.5 jit_solution(15063958784782007007)
XLA Ops:
  7.2 3.1 %collective-permute-start = (s32[1]{0:T(128)}, s32[1]{0:T(128)}, u32[]{:S(2)}, u32[]{:S(2)}) collective-permute-start(s32[1]{0:T(128)} %param.14), channel_id=1, source_target_pairs={{0,8},{8,0},{1,9},{9,1},{2,10},{10,2},{3,11},{11,3},{4,12},{12,4},... | collective-permute-start | bytes 20 | tf_op jit(solution)/shard_map/ppermute | solution.py:64
  17.9 2.0 collective-permute-start.1
  19.8 3.6 %collective-permute-start.2 = (s32[2,1]{0,1:T(1,128)S(1)}, s32[2,1]{0,1:T(1,128)S(1)}, u32[]{:S(2)}, u32[]{:S(2)}) collective-permute-start(s32[2,1]{0,1:T(1,128)S(1)} %broadcast_select_fusion.1), channel_id=1, source_target_pairs={{0,32},{16,48},{32,0},{48,16},{1,33},{17,49},{33,1},{49,17},{2,34}... | collective-permute-start | bytes 32 | tf_op jit(solution)/shard_map/ppermute | solution.py:64
  24.9 2.0 collective-permute-done.3
  27.0 2.0 broadcast_in_dim.56
  28.9 5.3 %all-to-all-start = ((bf16[16,152,608]{2,1,0:T(8,128)(2,1)}), bf16[16,152,608]{2,1,0:T(8,128)(2,1)}, u32[]{:S(2)}, u32[]{:S(2)}) async-start(bf16[16,152,608]{2,1,0:T(8,128)(2,1)} %bitcast.84), calls=%async_computation | async-start | bytes 6225920 | tf_op jit(solution)/shard_map/all_to_all | solution.py:80
  52.7 3.2 %shard_map.140 = bf16[2,8,304,128]{3,2,1,0:T(8,128)(2,1)} custom-call(bf16[152,1216]{1,0:T(8,128)(2,1)} %w_out.1, bf16[152,512]{1,0:T(8,128)(2,1)} %convert_element_type.78.gated), custom_call_target="tpu_custom_call" | custom-call | flops 189267968 | bytes 369664 | tf_op jit(solution)/shard_map/pallas_call | solution.py:95
  55.8 17.1 %all-to-all-done = bf16[16,152,608]{2,1,0:T(8,128)(2,1)} async-done(((bf16[16,152,608]{2,1,0:T(8,128)(2,1)}), bf16[16,152,608]{2,1,0:T(8,128)(2,1)}, u32[]{:S(2)}, u32[]{:S(2)}) %all-to-all-start) | async-done | bytes 2957344 | tf_op jit(solution)/shard_map/all_to_all | solution.py:80
  73.0 5.8 %all-to-all-start.1 = ((bf16[16,304,128]{2,1,0:T(8,128)(2,1)}), bf16[16,304,128]{2,1,0:T(8,128)(2,1)}, u32[]{:S(2)}, u32[]{:S(2)}) async-start(bf16[16,304,128]{2,1,0:T(8,128)(2,1)} %bitcast.88), calls=%async_computation.1 | async-start | bytes 2490368 | tf_op jit(solution)/shard_map/all_to_all | solution.py:80
  81.7 8.0 %shard_map.141 = (bf16[768,608]{1,0:T(8,128)(2,1)}, bf16[768,640]{1,0:T(8,128)(2,1)}) custom-call(s32[4]{0:T(128)} %pad_add_fusion.at, bf16[2,768,1216]{2,1,0:T(8,128)(2,1)} %all-gather.5.cloned.1.call-done.tokens, bf16[2,1216,608]{2,1,0:T(8,128)(2,1)} %bitcast.35.weights), custom_call_target="tpu_custom_call" | custom-call | flops 2271215616 | bytes 8560640 | tf_op jit(solution)/shard_map/pallas_call | solution.py:95
  89.7 4.9 %all-to-all-done.1.terms = bf16[16,304,128]{2,1,0:T(8,128)(2,1)} async-done(((bf16[16,304,128]{2,1,0:T(8,128)(2,1)}), bf16[16,304,128]{2,1,0:T(8,128)(2,1)}, u32[]{:S(2)}, u32[]{:S(2)}) %all-to-all-start.1) | async-done | bytes 1245216 | tf_op jit(solution)/shard_map/all_to_all | solution.py:80
  94.6 3.0 %shard_map.142 = (bf16[2,4,2,2,48,128]{5,4,3,2,1,0:T(8,128)(2,1)}, bf16[608,64]{1,0:T(8,128)(2,1)}) custom-call(s32[4]{0:T(128)} %pad_add_fusion.at, bf16[768,608]{1,0:T(8,128)(2,1)} %get-tuple-element.36.hidden, bf16[16,304,128]{2,1,0:T(8,128)(2,1)} %all-to-all-done.1.terms, f32[96,64]{1,0:T(8,128)} %fusion.27.own_part), custom_call_target="tpu_custom_call" | custom-call | flops 59768832 | bytes 933888 | tf_op jit(solution)/shard_map/pallas_call | solution.py:95
  97.7 5.1 %all-to-all-start.2 = ((bf16[16,2,48,128]{3,2,1,0:T(8,128)(2,1)}), bf16[16,2,48,128]{3,2,1,0:T(8,128)(2,1)}, u32[]{:S(2)}, u32[]{:S(2)}) async-start(bf16[16,2,48,128]{3,2,1,0:T(8,128)(2,1)} %bitcast.95), calls=%async_computation.2 | async-start | bytes 786432 | tf_op jit(solution)/shard_map/all_to_all | solution.py:80
  105.5 3.9 %all-to-all-done.2.parts = bf16[16,2,48,128]{3,2,1,0:T(8,128)(2,1)} async-done(((bf16[16,2,48,128]{3,2,1,0:T(8,128)(2,1)}), bf16[16,2,48,128]{3,2,1,0:T(8,128)(2,1)}, u32[]{:S(2)}, u32[]{:S(2)}) %all-to-all-start.2) | async-done | bytes 393248 | tf_op jit(solution)/shard_map/all_to_all | solution.py:80
  111.8 4.1 %shard_map.143 = (bf16[192,1280]{1,0:T(8,128)(2,1)S(1)}, f32[48,1280]{1,0:T(8,128)S(1)}, f32[48,2048]{1,0:T(8,128)S(1)}) custom-call(s32[4]{0:T(128)S(1)} %copy-done.16, bf16[16,2,48,128]{3,2,1,0:T(8,128)(2,1)} %all-to-all-done.2.parts, bf16[64,2048]{1,0:T(8,128)(2,1)S(1)} %copy-done.7, bf16[2048,768]{1,0:T(8,128)(2,1)S(1)} %copy-done.1, ...), custom_call_target="tpu_custom_call" | custom-call | flops 1031798784 | bytes 5111808 | tf_op jit(solution)/shard_map/pallas_call | solution.py:95
  117.4 5.0 %shard_map.144 = (f32[192,640]{1,0:T(8,128)S(1)}, f32[192,640]{1,0:T(8,128)S(1)}, bf16[192,1280]{1,0:T(8,128)(2,1)S(1)}) custom-call(bf16[192,1280]{1,0:T(8,128)(2,1)S(1)} %get-tuple-element.41.normed, bf16[1280,640]{1,0:T(8,128)(2,1)} %v1a.3, bf16[1280,640]{1,0:T(8,128)(2,1)} %collective-permute-done.4.v1b, bf16[640,1280]{1,0:T(8,128)(2,1)} %v2a.3, ...), custom_call_target="tpu_custom_call" | custom-call | flops 1258291200 | bytes 6553600 | tf_op jit(solution)/shard_map/pallas_call | solution.py:95
  126.5 4.2 %collective-permute-start.7 = (bf16[48,1280]{1,0:T(8,128)(2,1)}, bf16[48,1280]{1,0:T(8,128)(2,1)}, u32[]{:S(2)}, u32[]{:S(2)}) collective-permute-start(bf16[48,1280]{1,0:T(8,128)(2,1)} %get-tuple-element.75), channel_id=1, source_target_pairs={{0,4},{2,6},{4,0},{6,2},{1,5},{3,7},{5,1},{7,3},{8,12},{10,14},{12... | collective-permute-start | bytes 368648 | tf_op jit(solution)/shard_map/ppermute | solution.py:64
  131.9 2.9 %collective-permute-start.17 = (bf16[96,1216]{1,0:T(8,128)(2,1)}, bf16[96,1216]{1,0:T(8,128)(2,1)}, u32[]{:S(2)}, u32[]{:S(2)}) collective-permute-start(bf16[96,1216]{1,0:T(8,128)(2,1)} %slice_bitcast_fusion), channel_id=1, source_target_pairs={{0,8},{8,0},{1,9},{9,1},{2,10},{10,2},{3,11},{11,3},{4,12},{12,4},... | collective-permute-start | bytes 700424 | tf_op jit(solution)/shard_map/ppermute | solution.py:64
  136.7 2.1 fusion.10
  141.7 2.5 collective-permute-start.9
  144.3 3.0 %collective-permute-start.15 = (bf16[768,640]{1,0:T(8,128)(2,1)}, bf16[768,640]{1,0:T(8,128)(2,1)S(1)}, u32[]{:S(2)}, u32[]{:S(2)}) collective-permute-start(bf16[768,640]{1,0:T(8,128)(2,1)} %get-tuple-element.46.slope), channel_id=1, source_target_pairs={{0,8},{8,0},{1,9},{9,1},{2,10},{10,2},{3,11},{11,3},{4,12},{12,4},... | collective-permute-start | bytes 2949128 | tf_op jit(solution)/shard_map/ppermute | solution.py:64
  152.0 5.6 %shard_map.145 = bf16[192,1280]{1,0:T(8,128)(2,1)S(1)} custom-call(bf16[192,1280]{1,0:T(8,128)(2,1)S(1)} %pad_maximum_fusion.2.grad, bf16[1280,640]{1,0:T(8,128)(2,1)} %v1a.3, bf16[1280,640]{1,0:T(8,128)(2,1)} %collective-permute-done.4.v1b, bf16[640,1280]{1,0:T(8,128)(2,1)} %v2a.3, bf16[640,1280]{1,0:T(8,128)(2,1)} %collective-permute-done.5.v2b, ...), custom_call_target="tpu_custom_call" | custom-call | flops 1258291200 | bytes 6553600 | tf_op jit(solution)/shard_map/pallas_call | solution.py:95
  159.2 3.3 %collective-permute-start.13 = (bf16[48,1280]{1,0:T(8,128)(2,1)S(1)}, bf16[48,1280]{1,0:T(8,128)(2,1)S(1)}, u32[]{:S(2)}, u32[]{:S(2)}) collective-permute-start(bf16[48,1280]{1,0:T(8,128)(2,1)S(1)} %get-tuple-element.72), channel_id=1, source_target_pairs={{0,4},{2,6},{4,0},{6,2},{1,5},{3,7},{5,1},{7,3},{8,12},{10,14},{12... | collective-permute-start | bytes 368648 | tf_op jit(solution)/shard_map/ppermute | solution.py:64
  162.8 3.8 %collective-permute-done.14 = bf16[48,1280]{1,0:T(8,128)(2,1)S(1)} collective-permute-done((bf16[48,1280]{1,0:T(8,128)(2,1)S(1)}, bf16[48,1280]{1,0:T(8,128)(2,1)S(1)}, u32[]{:S(2)}, u32[]{:S(2)}) %collective-permute-start.14) | collective-permute-done | bytes 122912 | tf_op jit(solution)/shard_map/ppermute | solution.py:64
  169.1 3.0 %collective-permute-done.16.through2 = bf16[608,64]{1,0:T(8,128)(2,1)S(1)} collective-permute-done((bf16[608,64]{1,0:T(8,128)(2,1)}, bf16[608,64]{1,0:T(8,128)(2,1)S(1)}, u32[]{:S(2)}, u32[]{:S(2)}) %collective-permute-start.16) | collective-permute-done | bytes 77856 | tf_op jit(solution)/shard_map/ppermute | solution.py:64
  172.5 2.3 convolution_convert_fusion
  174.8 2.3 fusion.8
  177.2 14.9 %all_to_all.25 = bf16[32,48,128]{2,1,0:T(8,128)(2,1)S(1)} all-to-all(bf16[32,48,128]{2,1,0:T(8,128)(2,1)S(1)} %broadcast_in_dim.67), channel_id=1, replica_groups=mesh['near'=2,'z'=4,'far'=2,'y'=4,'core'=2] {'far','near','y','core'}, dimensions={0} | all-to-all | bytes 786432 | tf_op jit(solution)/shard_map/all_to_all | solution.py:80
  195.7 7.3 %shard_map.147 = bf16[1216,608]{1,0:T(8,128)(2,1)} custom-call(bf16[768,128]{1,0:T(8,128)(2,1)} %copy-done.14, bf16[608,64]{1,0:T(8,128)(2,1)} %get-tuple-element.47.through, bf16[768,640]{1,0:T(8,128)(2,1)} %get-tuple-element.46.slope, bf16[2,768,1216]{2,1,0:T(8,128)(2,1)} %all-gather.5.cloned.1.call-done.tokens, bf16[768,128]{1,0:T(8,128)(2,1)} %copy-done.15, ...), custom_call_target="tpu_custom_call" | custom-call | flops 2271215616 | bytes 7081984 | tf_op jit(solution)/shard_map/pallas_call | solution.py:95
  206.3 3.6 %all-to-all-start.4 = ((bf16[8,280,608]{2,1,0:T(8,128)(2,1)}), bf16[8,280,608]{2,1,0:T(8,128)(2,1)S(1)}, u32[]{:S(2)}, u32[]{:S(2)}) async-start(bf16[8,280,608]{2,1,0:T(8,128)(2,1)} %pad_maximum_fusion), calls=%async_computation.4 | async-start | bytes 5734400 | tf_op jit(solution)/shard_map/all_to_all | solution.py:80
  211.6 5.3 %rev.7 = bf16[152,4,2,64]{3,2,1,0:T(2,128)(2,1)} reverse(bf16[152,4,2,64]{3,2,1,0:T(2,128)(2,1)} %multiply_convert_fusion), dimensions={2} | reverse | bytes 311296 | tf_op jit(solution)/shard_map/rev | solution.py:591
  219.6 25.4 %all-to-all-done.4 = bf16[8,280,608]{2,1,0:T(8,128)(2,1)S(1)} async-done(((bf16[8,280,608]{2,1,0:T(8,128)(2,1)}), bf16[8,280,608]{2,1,0:T(8,128)(2,1)S(1)}, u32[]{:S(2)}, u32[]{:S(2)}) %all-to-all-start.4) | async-done | bytes 2723872 | tf_op jit(solution)/shard_map/all_to_all | solution.py:80
  (146 shorter events, 54.9 us)
Async XLA Ops:
  7.2 65.8 %copy-start = (bf16[1,96,1280]{2,1,0:T(8,128)(2,1)S(1)}, bf16[1,96,1280]{2,1,0:T(8,128)(2,1)}, u32[]{:S(2)}) copy-start(bf16[1,96,1280]{2,1,0:T(8,128)(2,1)} %param.16) | copy-start | bytes 737284
  7.2 74.5 %all-gather.5.cloned.1.call-start = ((), (), s32[]{:S(2)}) async-start(), calls=%async_computation.5 | async-start | bytes 4423680 | tf_op jit(solution)/shard_map/all_gather | solution.py:510
  7.2 6.1 %collective-permute-start = (s32[1]{0:T(128)}, s32[1]{0:T(128)}, u32[]{:S(2)}, u32[]{:S(2)}) collective-permute-start(s32[1]{0:T(128)} %param.14), channel_id=1, source_target_pairs={{0,8},{8,0},{1,9},{9,1},{2,10},{10,2},{3,11},{11,3},{4,12},{12,4},... | collective-permute-start | bytes 20 | tf_op jit(solution)/shard_map/ppermute | solution.py:64
  17.9 6.6 %collective-permute-start.1 = (s32[2,1]{0,1:T(1,128)S(1)}, s32[2,1]{0,1:T(1,128)S(1)}, u32[]{:S(2)}, u32[]{:S(2)}) collective-permute-start(s32[2,1]{0,1:T(1,128)S(1)} %broadcast_select_fusion.1), channel_id=1, source_target_pairs={{0,16},{16,32},{32,48},{48,0},{1,17},{17,33},{33,49},{49,1},{2,18}... | collective-permute-start | bytes 32 | tf_op jit(solution)/shard_map/ppermute | solution.py:64
  19.8 5.1 %collective-permute-start.2 = (s32[2,1]{0,1:T(1,128)S(1)}, s32[2,1]{0,1:T(1,128)S(1)}, u32[]{:S(2)}, u32[]{:S(2)}) collective-permute-start(s32[2,1]{0,1:T(1,128)S(1)} %broadcast_select_fusion.1), channel_id=1, source_target_pairs={{0,32},{16,48},{32,0},{48,16},{1,33},{17,49},{33,1},{49,17},{2,34}... | collective-permute-start | bytes 32 | tf_op jit(solution)/shard_map/ppermute | solution.py:64
  23.4 3.5 %collective-permute-start.3 = (s32[2,1]{0,1:T(1,128)S(1)}, s32[2,1]{0,1:T(1,128)S(1)}, u32[]{:S(2)}, u32[]{:S(2)}) collective-permute-start(s32[2,1]{0,1:T(1,128)S(1)} %broadcast_select_fusion.1), channel_id=1, source_target_pairs={{0,48},{16,0},{32,16},{48,32},{1,49},{17,1},{33,17},{49,33},{2,50}... | collective-permute-start | bytes 32 | tf_op jit(solution)/shard_map/ppermute | solution.py:64
  28.9 44.0 %all-to-all-start = ((bf16[16,152,608]{2,1,0:T(8,128)(2,1)}), bf16[16,152,608]{2,1,0:T(8,128)(2,1)}, u32[]{:S(2)}, u32[]{:S(2)}) async-start(bf16[16,152,608]{2,1,0:T(8,128)(2,1)} %bitcast.84), calls=%async_computation | async-start | bytes 6225920 | tf_op jit(solution)/shard_map/all_to_all | solution.py:80
  73.0 21.7 %all-to-all-start.1 = ((bf16[16,304,128]{2,1,0:T(8,128)(2,1)}), bf16[16,304,128]{2,1,0:T(8,128)(2,1)}, u32[]{:S(2)}, u32[]{:S(2)}) async-start(bf16[16,304,128]{2,1,0:T(8,128)(2,1)} %bitcast.88), calls=%async_computation.1 | async-start | bytes 2490368 | tf_op jit(solution)/shard_map/all_to_all | solution.py:80
  78.7 56.0 %all-gather.9.cloned.1.call-start = ((), (), s32[]{:S(2)}) async-start(), calls=%async_computation.7 | async-start | bytes 1290240 | tf_op jit(solution)/shard_map/all_gather | solution.py:540
  78.8 38.6 %collective-permute-start.4 = (bf16[1280,640]{1,0:T(8,128)(2,1)}, bf16[1280,640]{1,0:T(8,128)(2,1)}, u32[]{:S(2)}, u32[]{:S(2)}) collective-permute-start(bf16[1280,640]{1,0:T(8,128)(2,1)} %v1a.3), channel_id=1, source_target_pairs={{0,1},{1,0},{2,3},{3,2},{4,5},{5,4},{6,7},{7,6},{8,9},{9,8},{10,11... | collective-permute-start | bytes 4915208 | tf_op jit(solution)/shard_map/ppermute | solution.py:64
  78.9 38.5 %collective-permute-start.5 = (bf16[640,1280]{1,0:T(8,128)(2,1)}, bf16[640,1280]{1,0:T(8,128)(2,1)}, u32[]{:S(2)}, u32[]{:S(2)}) collective-permute-start(bf16[640,1280]{1,0:T(8,128)(2,1)} %v2a.3), channel_id=1, source_target_pairs={{0,1},{1,0},{2,3},{3,2},{4,5},{5,4},{6,7},{7,6},{8,9},{9,8},{10,11... | collective-permute-start | bytes 4915208 | tf_op jit(solution)/shard_map/ppermute | solution.py:64
  81.7 27.6 %copy-start.1 = (bf16[2048,768]{1,0:T(8,128)(2,1)S(1)}, bf16[2048,768]{1,0:T(8,128)(2,1)}, u32[]{:S(2)}) copy-start(bf16[2048,768]{1,0:T(8,128)(2,1)} %w_dec2.1) | copy-start | bytes 9437188
  89.7 19.6 %copy-start.16 = (s32[4]{0:T(128)S(1)}, s32[4]{0:T(128)}, u32[]{:S(2)}) copy-start(s32[4]{0:T(128)} %pad_add_fusion.at) | copy-start | bytes 52
  97.7 11.6 %all-to-all-start.2 = ((bf16[16,2,48,128]{3,2,1,0:T(8,128)(2,1)}), bf16[16,2,48,128]{3,2,1,0:T(8,128)(2,1)}, u32[]{:S(2)}, u32[]{:S(2)}) async-start(bf16[16,2,48,128]{3,2,1,0:T(8,128)(2,1)} %bitcast.95), calls=%async_computation.2 | async-start | bytes 786432 | tf_op jit(solution)/shard_map/all_to_all | solution.py:80
  102.8 92.9 %all-gather.7.cloned.1.call-start = ((), (), s32[]{:S(2)}) async-start(), calls=%async_computation.6 | async-start | bytes 2211840 | tf_op jit(solution)/shard_map/all_gather | solution.py:511
  125.6 9.2 %collective-permute-start.8 = (bf16[48,1280]{1,0:T(8,128)(2,1)}, bf16[48,1280]{1,0:T(8,128)(2,1)}, u32[]{:S(2)}, u32[]{:S(2)}) collective-permute-start(bf16[48,1280]{1,0:T(8,128)(2,1)} %get-tuple-element.74), channel_id=1, source_target_pairs={{0,2},{2,4},{4,6},{6,0},{1,3},{3,5},{5,7},{7,1},{8,10},{10,12},{12... | collective-permute-start | bytes 368648 | tf_op jit(solution)/shard_map/ppermute | solution.py:64
  126.5 8.8 %collective-permute-start.7 = (bf16[48,1280]{1,0:T(8,128)(2,1)}, bf16[48,1280]{1,0:T(8,128)(2,1)}, u32[]{:S(2)}, u32[]{:S(2)}) collective-permute-start(bf16[48,1280]{1,0:T(8,128)(2,1)} %get-tuple-element.75), channel_id=1, source_target_pairs={{0,4},{2,6},{4,0},{6,2},{1,5},{3,7},{5,1},{7,3},{8,12},{10,14},{12... | collective-permute-start | bytes 368648 | tf_op jit(solution)/shard_map/ppermute | solution.py:64
  130.8 5.9 %collective-permute-start.6 = (bf16[48,1280]{1,0:T(8,128)(2,1)}, bf16[48,1280]{1,0:T(8,128)(2,1)}, u32[]{:S(2)}, u32[]{:S(2)}) collective-permute-start(bf16[48,1280]{1,0:T(8,128)(2,1)} %get-tuple-element.73), channel_id=1, source_target_pairs={{0,6},{2,0},{4,2},{6,4},{1,7},{3,1},{5,3},{7,5},{8,14},{10,8},{12,... | collective-permute-start | bytes 368648 | tf_op jit(solution)/shard_map/ppermute | solution.py:64
  131.9 12.4 %collective-permute-start.17 = (bf16[96,1216]{1,0:T(8,128)(2,1)}, bf16[96,1216]{1,0:T(8,128)(2,1)}, u32[]{:S(2)}, u32[]{:S(2)}) collective-permute-start(bf16[96,1216]{1,0:T(8,128)(2,1)} %slice_bitcast_fusion), channel_id=1, source_target_pairs={{0,8},{8,0},{1,9},{9,1},{2,10},{10,2},{3,11},{11,3},{4,12},{12,4},... | collective-permute-start | bytes 700424 | tf_op jit(solution)/shard_map/ppermute | solution.py:64
  138.8 9.1 %collective-permute-start.11 = (bf16[48,1280]{1,0:T(8,128)(2,1)}, bf16[48,1280]{1,0:T(8,128)(2,1)}, u32[]{:S(2)}, u32[]{:S(2)}) collective-permute-start(bf16[48,1280]{1,0:T(8,128)(2,1)} %get-tuple-element.76), channel_id=1, source_target_pairs={{0,6},{2,0},{4,2},{6,4},{1,7},{3,1},{5,3},{7,5},{8,14},{10,8},{12,... | collective-permute-start | bytes 368648 | tf_op jit(solution)/shard_map/ppermute | solution.py:64
  140.1 7.8 %collective-permute-start.10 = (bf16[48,1280]{1,0:T(8,128)(2,1)}, bf16[48,1280]{1,0:T(8,128)(2,1)}, u32[]{:S(2)}, u32[]{:S(2)}) collective-permute-start(bf16[48,1280]{1,0:T(8,128)(2,1)} %get-tuple-element.76), channel_id=1, source_target_pairs={{0,4},{2,6},{4,0},{6,2},{1,5},{3,7},{5,1},{7,3},{8,12},{10,14},{12... | collective-permute-start | bytes 368648 | tf_op jit(solution)/shard_map/ppermute | solution.py:64
  141.7 7.0 %collective-permute-start.9 = (bf16[48,1280]{1,0:T(8,128)(2,1)}, bf16[48,1280]{1,0:T(8,128)(2,1)}, u32[]{:S(2)}, u32[]{:S(2)}) collective-permute-start(bf16[48,1280]{1,0:T(8,128)(2,1)} %get-tuple-element.76), channel_id=1, source_target_pairs={{0,2},{2,4},{4,6},{6,0},{1,3},{3,5},{5,7},{7,1},{8,10},{10,12},{12... | collective-permute-start | bytes 368648 | tf_op jit(solution)/shard_map/ppermute | solution.py:64
  144.3 27.7 %collective-permute-start.15 = (bf16[768,640]{1,0:T(8,128)(2,1)}, bf16[768,640]{1,0:T(8,128)(2,1)S(1)}, u32[]{:S(2)}, u32[]{:S(2)}) collective-permute-start(bf16[768,640]{1,0:T(8,128)(2,1)} %get-tuple-element.46.slope), channel_id=1, source_target_pairs={{0,8},{8,0},{1,9},{9,1},{2,10},{10,2},{3,11},{11,3},{4,12},{12,4},... | collective-permute-start | bytes 2949128 | tf_op jit(solution)/shard_map/ppermute | solution.py:64
  147.4 24.7 %collective-permute-start.16 = (bf16[608,64]{1,0:T(8,128)(2,1)}, bf16[608,64]{1,0:T(8,128)(2,1)S(1)}, u32[]{:S(2)}, u32[]{:S(2)}) collective-permute-start(bf16[608,64]{1,0:T(8,128)(2,1)} %get-tuple-element.47.through), channel_id=1, source_target_pairs={{0,8},{8,0},{1,9},{9,1},{2,10},{10,2},{3,11},{11,3},{4,12},{12,4},... | collective-permute-start | bytes 233480 | tf_op jit(solution)/shard_map/ppermute | solution.py:64
  152.0 20.1 %copy-start.6 = (f32[48,1280]{1,0:T(8,128)S(1)}, f32[48,1280]{1,0:T(8,128)}, u32[]{:S(2)}) copy-start(f32[48,1280]{1,0:T(8,128)} %copy-done.5) | copy-start | bytes 737284
  157.6 14.9 %copy-start.3 = (bf16[768,1280]{1,0:T(8,128)(2,1)S(1)}, bf16[768,1280]{1,0:T(8,128)(2,1)}, u32[]{:S(2)}) copy-start(bf16[768,1280]{1,0:T(8,128)(2,1)} %w_patch.1) | copy-start | bytes 5898244
  157.6 9.0 %collective-permute-start.14 = (bf16[48,1280]{1,0:T(8,128)(2,1)S(1)}, bf16[48,1280]{1,0:T(8,128)(2,1)S(1)}, u32[]{:S(2)}, u32[]{:S(2)}) collective-permute-start(bf16[48,1280]{1,0:T(8,128)(2,1)S(1)} %get-tuple-element.71), channel_id=1, source_target_pairs={{0,2},{2,4},{4,6},{6,0},{1,3},{3,5},{5,7},{7,1},{8,10},{10,12},{12... | collective-permute-start | bytes 368648 | tf_op jit(solution)/shard_map/ppermute | solution.py:64
  159.2 8.9 %collective-permute-start.13 = (bf16[48,1280]{1,0:T(8,128)(2,1)S(1)}, bf16[48,1280]{1,0:T(8,128)(2,1)S(1)}, u32[]{:S(2)}, u32[]{:S(2)}) collective-permute-start(bf16[48,1280]{1,0:T(8,128)(2,1)S(1)} %get-tuple-element.72), channel_id=1, source_target_pairs={{0,4},{2,6},{4,0},{6,2},{1,5},{3,7},{5,1},{7,3},{8,12},{10,14},{12... | collective-permute-start | bytes 368648 | tf_op jit(solution)/shard_map/ppermute | solution.py:64
  162.6 6.4 %collective-permute-start.12 = (bf16[48,1280]{1,0:T(8,128)(2,1)S(1)}, bf16[48,1280]{1,0:T(8,128)(2,1)S(1)}, u32[]{:S(2)}, u32[]{:S(2)}) collective-permute-start(bf16[48,1280]{1,0:T(8,128)(2,1)S(1)} %get-tuple-element.70), channel_id=1, source_target_pairs={{0,6},{2,0},{4,2},{6,4},{1,7},{3,1},{5,3},{7,5},{8,14},{10,8},{12,... | collective-permute-start | bytes 368648 | tf_op jit(solution)/shard_map/ppermute | solution.py:64
  177.1 15.0 %copy-start.4 = (bf16[768,608]{1,0:T(8,128)(2,1)S(1)}, bf16[768,608]{1,0:T(8,128)(2,1)}, u32[]{:S(2)}) copy-start(bf16[768,608]{1,0:T(8,128)(2,1)} %get-tuple-element.36.hidden) | copy-start | bytes 2801668
  194.4 8.6 %collective-permute-start.18 = (bf16[64,608]{1,0:T(8,128)(2,1)S(1)}, bf16[64,608]{1,0:T(8,128)(2,1)S(1)}, u32[]{:S(2)}, u32[]{:S(2)}) collective-permute-start(bf16[64,608]{1,0:T(8,128)(2,1)S(1)} %get-tuple-element.53), channel_id=1, source_target_pairs={{0,8},{8,0},{1,9},{9,1},{2,10},{10,2},{3,11},{11,3},{4,12},{12,4},... | collective-permute-start | bytes 233480 | tf_op jit(solution)/shard_map/ppermute | solution.py:64
  206.3 38.7 %all-to-all-start.4 = ((bf16[8,280,608]{2,1,0:T(8,128)(2,1)}), bf16[8,280,608]{2,1,0:T(8,128)(2,1)S(1)}, u32[]{:S(2)}, u32[]{:S(2)}) async-start(bf16[8,280,608]{2,1,0:T(8,128)(2,1)} %pad_maximum_fusion), calls=%async_computation.4 | async-start | bytes 5734400 | tf_op jit(solution)/shard_map/all_to_all | solution.py:80
  (20 other events, 53.8 us)
Sparse Core Ops, SparseCore 0:
  17.5 31.3 all-gather.4
  81.9 48.6 all-gather.8
  144.4 23.7 all-gather.6
